TPU v7x, 32 devices: a whole 2x2x4 slice. The times are simulated.
32 devices in a mesh: dp: 32 (over z, y, x, core).
Axes of the slice: x: 2, y: 2, z: 4, core: 2. Of those that a mesh axis runs over, the one named last changes fastest.
Arguments:
- embedded: bfloat16 [8192, 768], P('dp'), may hold values from -6 to 6
- doc_ids: int32 [32, 256], P('dp'), may hold values from 0 to 3, never falling along the last dimension, each value on 1 to 170 neighbouring positions
- step_ids: int32 [32, 4], P('dp'), may hold values from 0 to 1023
- step_table: bfloat16 [1024, 768], P('dp'), may hold values from -3 to 3
- qkv_weight: bfloat16 [2, 768, 2304], P(None, 'dp'), may hold values from -0.21875 to 0.21875
- qv_bias: bfloat16 [2, 1536], P(None, 'dp'), may hold values from -3 to 3
- out_weight: bfloat16 [2, 768, 768], P(None, 'dp'), may hold values from -0.625 to 0.625
- out_bias: bfloat16 [2, 768], P(None, 'dp'), may hold values from -2 to 2
- first_gain: bfloat16 [2, 768], P(None, 'dp'), may hold values from 0.5 to 1.5
- first_shift: bfloat16 [2, 768], P(None, 'dp'), may hold values from -2 to 2
- up_weight: bfloat16 [2, 768, 3072], P(None, 'dp'), may hold values from -0.21875 to 0.21875
- up_bias: bfloat16 [2, 3072], P(None, 'dp'), may hold values from -3 to 3
- down_weight: bfloat16 [2, 3072, 768], P(None, 'dp'), may hold values from -0.109375 to 0.109375
- down_bias: bfloat16 [2, 768], P(None, 'dp'), may hold values from -2 to 2
- second_gain: bfloat16 [2, 768], P(None, 'dp'), may hold values from 0.5 to 1.5
- second_shift: bfloat16 [2, 768], P(None, 'dp'), may hold values from -2 to 2
- cotangent: bfloat16 [8192, 768], P('dp'), may hold values from -6 to 6
Outputs:
- block_output: bfloat16 [8192, 768], P('dp')
- input_grad: float32 [8192, 768], P('dp')
- table_grad: float32 [1024, 768], P('dp')
- qkv_weight_grad: float32 [2, 768, 2304], P(None, 'dp')
- qv_bias_grad: float32 [2, 1536], P(None, 'dp')
- out_weight_grad: float32 [2, 768, 768], P(None, 'dp')
- out_bias_grad: float32 [2, 768], P(None, 'dp')
- first_gain_grad: float32 [2, 768], P(None, 'dp')
- first_shift_grad: float32 [2, 768], P(None, 'dp')
- up_weight_grad: float32 [2, 768, 3072], P(None, 'dp')
- up_bias_grad: float32 [2, 3072], P(None, 'dp')
- down_weight_grad: float32 [2, 3072, 768], P(None, 'dp')
- down_bias_grad: float32 [2, 768], P(None, 'dp')
- second_gain_grad: float32 [2, 768], P(None, 'dp')
- second_shift_grad: float32 [2, 768], P(None, 'dp')
Inputs may be any that keep to these rules, and one draw needn't show every extreme that they name: `doc_ids`: document numbers never fall along a row of 256 tokens; each of the 4 documents of a row holds 1 to 170 tokens.
All inputs are finite; a program needn't handle non-finite values.
Results may differ from a plain program's by a relative error of at most 0.013.
Values may be sent and summed in bfloat16 or wider, within the bound.
No kernel may reach another device: no remote copies, remote signals or barrier semaphores. Data moves between devices by JAX's collectives and lax.ppermute only.
A program may use at most 256 MiB of HBM per device.

v0:
```python
import math

import jax
import jax.numpy as jnp
from jax import lax
from jax.sharding import PartitionSpec as P

HEADS = 12
HEAD_DIM = 64


EPSILON = 1e-05


def shortened(value):
    return jax.tree.map(lambda a: a.astype(jnp.bfloat16) if a.dtype == jnp.float32 else a, value)


def partner(value, axis, stride):
    return lax.ppermute(value, axis, [(i, i ^ 1 << stride) for i in range(lax.axis_size(axis))])


def norm_rows(hidden, gain_vec, shift_vec):
    average = jnp.mean(hidden, axis=-1, keepdims=True)
    centred = hidden - average
    variance = jnp.mean(centred * centred, axis=-1, keepdims=True)
    inverse = lax.rsqrt(variance + EPSILON)
    unit_rows = centred * inverse
    normed = unit_rows * gain_vec.astype(jnp.float32) + shift_vec.astype(jnp.float32)
    return (normed, unit_rows, inverse)


def norm_back(grad_rows, unit_rows, inverse, gain_vec):
    scaled = grad_rows * gain_vec.astype(jnp.float32)
    first_mean = jnp.mean(scaled, axis=-1, keepdims=True)
    second_mean = jnp.mean(scaled * unit_rows, axis=-1, keepdims=True)
    return inverse * (scaled - first_mean - unit_rows * second_mean)


def smooth_gate(lifted):
    return jax.nn.gelu(lifted, approximate=True)


def halving_sum(members, send_fn):
    levels = lax.axis_size("dp").bit_length() - 1
    position = lax.axis_index("dp")
    current = tuple(members)
    for level in range(levels - 1, -1, -1):
        upper_side = position // (1 << level) % 2 == 1
        kept_list = []
        sent_list = []
        for member in current:
            half = member.shape[0] // 2
            lower_part = member[:half]
            upper_part = member[half:]
            kept_list.append(jnp.where(upper_side, upper_part, lower_part))
            sent_list.append(jnp.where(upper_side, lower_part, upper_part))
        received = send_fn(tuple(sent_list), level)
        current = tuple((kept + came for kept, came in zip(kept_list, received)))
    return current


def layer_apply(hidden, params, same_doc):
    qkv_w, qv_b, out_w, out_b, gain_a, shift_a, up_w, up_b, down_w, down_b, gain_b, shift_b = params
    width = out_w.shape[0]
    tok_count = hidden.shape[0]
    scale = 1.0 / math.sqrt(HEAD_DIM)
    normed_a, unit_a, inverse_a = norm_rows(hidden, gain_a, shift_a)
    normed_a = normed_a.astype(jnp.bfloat16)
    qv_float = qv_b.astype(jnp.float32)
    bias_full = jnp.concatenate(
        [qv_float[:width], jnp.zeros((width,), jnp.float32), qv_float[width:]]
    )
    packed = (jnp.dot(normed_a, qkv_w, preferred_element_type=jnp.float32) + bias_full).astype(
        jnp.bfloat16
    )
    queries = packed[:, :width].reshape(tok_count, HEADS, HEAD_DIM)
    key_rows = packed[:, width : 2 * width].reshape(tok_count, HEADS, HEAD_DIM)
    value_rows = packed[:, 2 * width :].reshape(tok_count, HEADS, HEAD_DIM)
    scores = (
        jnp.einsum("qhd,khd->hqk", queries, key_rows, preferred_element_type=jnp.float32) * scale
    )
    masked = jnp.where(same_doc[None], scores, -1e30)
    top_score = jnp.max(masked, axis=-1, keepdims=True)
    expo_rows = jnp.exp(masked - top_score)
    probs = expo_rows / jnp.sum(expo_rows, axis=-1, keepdims=True)
    probs_low = probs.astype(jnp.bfloat16)
    mixed = jnp.einsum("hqk,khd->qhd", probs_low, value_rows, preferred_element_type=jnp.float32)
    mixed = mixed.reshape(tok_count, width).astype(jnp.bfloat16)
    middle = (
        hidden
        + jnp.dot(mixed, out_w, preferred_element_type=jnp.float32)
        + out_b.astype(jnp.float32)
    )
    normed_b, unit_b, inverse_b = norm_rows(middle, gain_b, shift_b)
    normed_b = normed_b.astype(jnp.bfloat16)
    lifted = jnp.dot(normed_b, up_w, preferred_element_type=jnp.float32) + up_b.astype(jnp.float32)
    activated = smooth_gate(lifted).astype(jnp.bfloat16)
    output = (
        middle
        + jnp.dot(activated, down_w, preferred_element_type=jnp.float32)
        + down_b.astype(jnp.float32)
    )
    saved = (
        unit_a,
        inverse_a,
        normed_a,
        queries,
        key_rows,
        value_rows,
        probs,
        probs_low,
        mixed,
        unit_b,
        inverse_b,
        normed_b,
        lifted,
        activated,
    )
    return (output, saved)


def layer_back(hidden, params, same_doc, grad_top):
    qkv_w, qv_b, out_w, out_b, gain_a, shift_a, up_w, up_b, down_w, down_b, gain_b, shift_b = params
    unused_output, saved = layer_apply(hidden, params, same_doc)
    (
        unit_a,
        inverse_a,
        normed_a,
        queries,
        key_rows,
        value_rows,
        probs,
        probs_low,
        mixed,
        unit_b,
        inverse_b,
        normed_b,
        lifted,
        activated,
    ) = saved
    width = out_w.shape[0]
    tok_count = hidden.shape[0]
    scale = 1.0 / math.sqrt(HEAD_DIM)
    grad_down = grad_top.astype(jnp.bfloat16)
    down_b_grad = jnp.sum(grad_down.astype(jnp.float32), axis=0)
    down_w_grad = jnp.einsum("tf,td->fd", activated, grad_down, preferred_element_type=jnp.float32)
    grad_act = jnp.einsum("td,fd->tf", grad_down, down_w, preferred_element_type=jnp.float32)
    unused_gate, gate_pull = jax.vjp(smooth_gate, lifted)
    grad_lift = gate_pull(grad_act)[0].astype(jnp.bfloat16)
    up_b_grad = jnp.sum(grad_lift.astype(jnp.float32), axis=0)
    up_w_grad = jnp.einsum("td,tf->df", normed_b, grad_lift, preferred_element_type=jnp.float32)
    grad_nb = jnp.einsum("tf,df->td", grad_lift, up_w, preferred_element_type=jnp.float32)
    gain_b_grad = jnp.sum(grad_nb * unit_b, axis=0)
    shift_b_grad = jnp.sum(grad_nb, axis=0)
    grad_mid = grad_top + norm_back(grad_nb, unit_b, inverse_b, gain_b)
    grad_branch = grad_mid.astype(jnp.bfloat16)
    out_b_grad = jnp.sum(grad_branch.astype(jnp.float32), axis=0)
    out_w_grad = jnp.einsum("te,td->ed", mixed, grad_branch, preferred_element_type=jnp.float32)
    grad_mixed = jnp.einsum("td,ed->te", grad_branch, out_w, preferred_element_type=jnp.float32)
    grad_mixed = grad_mixed.astype(jnp.bfloat16).reshape(tok_count, HEADS, HEAD_DIM)
    grad_probs = jnp.einsum(
        "qhd,khd->hqk", grad_mixed, value_rows, preferred_element_type=jnp.float32
    )
    grad_values = jnp.einsum(
        "hqk,qhd->khd", probs_low, grad_mixed, preferred_element_type=jnp.float32
    )
    grad_scores = probs * (grad_probs - jnp.sum(probs * grad_probs, axis=-1, keepdims=True))
    scores_low = grad_scores.astype(jnp.bfloat16)
    grad_queries = (
        jnp.einsum("hqk,khd->qhd", scores_low, key_rows, preferred_element_type=jnp.float32) * scale
    )
    grad_keys = (
        jnp.einsum("hqk,qhd->khd", scores_low, queries, preferred_element_type=jnp.float32) * scale
    )
    grad_packed = jnp.concatenate(
        [
            grad_queries.reshape(tok_count, width),
            grad_keys.reshape(tok_count, width),
            grad_values.reshape(tok_count, width),
        ],
        axis=1,
    ).astype(jnp.bfloat16)
    packed_sums = jnp.sum(grad_packed.astype(jnp.float32), axis=0)
    qv_b_grad = jnp.concatenate([packed_sums[:width], packed_sums[2 * width :]])
    qkv_w_grad = jnp.einsum("td,te->de", normed_a, grad_packed, preferred_element_type=jnp.float32)
    grad_na = jnp.einsum("te,de->td", grad_packed, qkv_w, preferred_element_type=jnp.float32)
    gain_a_grad = jnp.sum(grad_na * unit_a, axis=0)
    shift_a_grad = jnp.sum(grad_na, axis=0)
    grad_in = grad_mid + norm_back(grad_na, unit_a, inverse_a, gain_a)
    grads = (
        qkv_w_grad,
        qv_b_grad,
        out_w_grad,
        out_b_grad,
        gain_a_grad,
        shift_a_grad,
        up_w_grad,
        up_b_grad,
        down_w_grad,
        down_b_grad,
        gain_b_grad,
        shift_b_grad,
    )
    return (grad_in, grads)


def local(
    embedded,
    doc_ids,
    step_ids,
    step_table,
    qkv_weight,
    qv_bias,
    out_weight,
    out_bias,
    first_gain,
    first_shift,
    up_weight,
    up_bias,
    down_weight,
    down_bias,
    second_gain,
    second_shift,
    cotangent,
):
    docs_row = doc_ids[0]
    same_doc = docs_row[:, None] == docs_row[None, :]
    doc_count = step_ids.shape[1]
    doc_hot = (docs_row[:, None] == jnp.arange(doc_count, dtype=jnp.int32)[None, :]).astype(
        jnp.float32
    )
    gathered_first = (
        lax.all_gather(qkv_weight[0], "dp", axis=0, tiled=True),
        lax.all_gather(qv_bias[0], "dp", axis=0, tiled=True),
        lax.all_gather(out_weight[0], "dp", axis=0, tiled=True),
        lax.all_gather(out_bias[0], "dp", axis=0, tiled=True),
        lax.all_gather(first_gain[0], "dp", axis=0, tiled=True),
        lax.all_gather(first_shift[0], "dp", axis=0, tiled=True),
        lax.all_gather(up_weight[0], "dp", axis=0, tiled=True),
        lax.all_gather(up_bias[0], "dp", axis=0, tiled=True),
        lax.all_gather(down_weight[0], "dp", axis=0, tiled=True),
        lax.all_gather(down_bias[0], "dp", axis=0, tiled=True),
        lax.all_gather(second_gain[0], "dp", axis=0, tiled=True),
        lax.all_gather(second_shift[0], "dp", axis=0, tiled=True),
        lax.all_gather(step_table, "dp", axis=0, tiled=True),
    )
    params_lower = gathered_first[:12]
    table_whole = gathered_first[12]
    step_hot = step_ids[0][:, None] == jnp.arange(table_whole.shape[0], dtype=jnp.int32)[None, :]
    doc_rows = jnp.dot(
        step_hot.astype(jnp.bfloat16), table_whole, preferred_element_type=jnp.float32
    )
    start = embedded.astype(jnp.float32) + jnp.dot(
        doc_hot, doc_rows, precision=lax.Precision.HIGHEST
    )
    middle_hidden, unused_lower = layer_apply(start, params_lower, same_doc)
    params_upper = (
        lax.all_gather(qkv_weight[1], "dp", axis=0, tiled=True),
        lax.all_gather(qv_bias[1], "dp", axis=0, tiled=True),
        lax.all_gather(out_weight[1], "dp", axis=0, tiled=True),
        lax.all_gather(out_bias[1], "dp", axis=0, tiled=True),
        lax.all_gather(first_gain[1], "dp", axis=0, tiled=True),
        lax.all_gather(first_shift[1], "dp", axis=0, tiled=True),
        lax.all_gather(up_weight[1], "dp", axis=0, tiled=True),
        lax.all_gather(up_bias[1], "dp", axis=0, tiled=True),
        lax.all_gather(down_weight[1], "dp", axis=0, tiled=True),
        lax.all_gather(down_bias[1], "dp", axis=0, tiled=True),
        lax.all_gather(second_gain[1], "dp", axis=0, tiled=True),
        lax.all_gather(second_shift[1], "dp", axis=0, tiled=True),
    )
    final_hidden, unused_upper = layer_apply(middle_hidden, params_upper, same_doc)
    block_output = final_hidden.astype(jnp.bfloat16)

    def weights_for(layer_index):
        return (
            lax.all_gather(qkv_weight[layer_index], "dp", axis=0, tiled=True),
            lax.all_gather(qv_bias[layer_index], "dp", axis=0, tiled=True),
            lax.all_gather(out_weight[layer_index], "dp", axis=0, tiled=True),
            lax.all_gather(out_bias[layer_index], "dp", axis=0, tiled=True),
            lax.all_gather(first_gain[layer_index], "dp", axis=0, tiled=True),
            lax.all_gather(first_shift[layer_index], "dp", axis=0, tiled=True),
            lax.all_gather(up_weight[layer_index], "dp", axis=0, tiled=True),
            lax.all_gather(up_bias[layer_index], "dp", axis=0, tiled=True),
            lax.all_gather(down_weight[layer_index], "dp", axis=0, tiled=True),
            lax.all_gather(down_bias[layer_index], "dp", axis=0, tiled=True),
            lax.all_gather(second_gain[layer_index], "dp", axis=0, tiled=True),
            lax.all_gather(second_shift[layer_index], "dp", axis=0, tiled=True),
        )

    grad_upper_in, upper_grads = layer_back(
        middle_hidden, weights_for(1), same_doc, cotangent.astype(jnp.float32)
    )

    def send_upper(sent, level):
        return jax.tree.map(
            lambda part, own: part.astype(own.dtype), partner(shortened(sent), "dp", level), sent
        )

    upper_shards = halving_sum(upper_grads, send_upper)
    input_grad, lower_grads = layer_back(start, weights_for(0), same_doc, grad_upper_in)
    doc_grads = jnp.einsum("ts,td->sd", doc_hot, input_grad, precision=lax.Precision.HIGHEST)
    table_full_grad = jnp.einsum(
        "sn,sd->nd", step_hot.astype(jnp.float32), doc_grads, precision=lax.Precision.HIGHEST
    )

    def send_lower(sent, level):
        return jax.tree.map(
            lambda part, own: part.astype(own.dtype), partner(shortened(sent), "dp", level), sent
        )

    lower_all = halving_sum(tuple(lower_grads) + (table_full_grad,), send_lower)
    lower_shards = lower_all[:12]
    table_shard = lower_all[12]
    stacked = [jnp.stack([lower_shards[index], upper_shards[index]], axis=0) for index in range(12)]
    return (
        block_output,
        input_grad,
        table_shard,
        stacked[0],
        stacked[1],
        stacked[2],
        stacked[3],
        stacked[4],
        stacked[5],
        stacked[6],
        stacked[7],
        stacked[8],
        stacked[9],
        stacked[10],
        stacked[11],
    )


def solution(mesh):
    in_specs = (
        P("dp", None),
        P("dp", None),
        P("dp", None),
        P("dp", None),
        P(None, "dp", None),
        P(None, "dp"),
        P(None, "dp", None),
        P(None, "dp"),
        P(None, "dp"),
        P(None, "dp"),
        P(None, "dp", None),
        P(None, "dp"),
        P(None, "dp", None),
        P(None, "dp"),
        P(None, "dp"),
        P(None, "dp"),
        P("dp", None),
    )
    out_specs = (
        P("dp", None),
        P("dp", None),
        P("dp", None),
        P(None, "dp", None),
        P(None, "dp"),
        P(None, "dp", None),
        P(None, "dp"),
        P(None, "dp"),
        P(None, "dp"),
        P(None, "dp", None),
        P(None, "dp"),
        P(None, "dp", None),
        P(None, "dp"),
        P(None, "dp"),
        P(None, "dp"),
    )
    return jax.shard_map(local, mesh=mesh, in_specs=in_specs, out_specs=out_specs, check_vma=False)
```

profile of v0, /device:TPU:0, one launch (start us, length us, event | category | flops | bytes accessed | tf_op | source)
XLA Modules:
  0.0 1694.2 jit_solution(2194229519670627036)
XLA Ops:
  21.4 43.2 %all-reduce.16 = (bf16[1536]{0:T(1024)(128)(2,1)S(1)}, bf16[768]{0:T(1024)(128)(2,1)S(1)}, bf16[768]{0:T(1024)(128)(2,1)S(1)}, bf16[768]{0:T(1024)(128)(2,1)S(1)...) all-reduce(bf16[1536]{0:T(1024)(128)(2,1)S(1)} %dynamic-update-slic, ...), channel_id=5, replica_groups=mesh['dp'=32] {'dp'}, use_global_device_ids=true, to_apply=%add.2 | all-reduce | flops 18432 | bytes 73728
  71.5 59.8 %all-gather.36.cloned.1.call-done = bf16[1,768,2304]{2,1,0:T(8,128)(2,1)} async-done(((bf16[1,24,2304]{2,1,0:T(8,128)(2,1)}), bf16[1,768,2304]{2,1,0:T(8,128)(2,1)}) %all-gather.36.cloned.1.call-update) | async-done | bytes 3538960 | tf_op jit(solution)/shard_map/all_gather | solution.py:234
  140.4 46.7 %all-gather.38.cloned.1.call-done = bf16[1,768,768]{2,1,0:T(8,128)(2,1)} async-done(((bf16[1,24,768]{2,1,0:T(8,128)(2,1)}), bf16[1,768,768]{2,1,0:T(8,128)(2,1)}) %all-gather.38.cloned.1.call-update) | async-done | bytes 1179664 | tf_op jit(solution)/shard_map/all_gather | solution.py:236
  189.2 63.8 %all-gather.40.cloned.1.call-done = bf16[1,768,3072]{2,1,0:T(8,128)(2,1)} async-done(((bf16[1,24,3072]{2,1,0:T(8,128)(2,1)}), bf16[1,768,3072]{2,1,0:T(8,128)(2,1)}) %all-gather.40.cloned.1.call-update) | async-done | bytes 4718608 | tf_op jit(solution)/shard_map/all_gather | solution.py:240
  253.0 5.4 fusion.18
  258.5 60.4 %all-gather.42.cloned.1.call-done = bf16[1,3072,768]{2,1,0:T(8,128)(2,1)} async-done(((bf16[1,96,768]{2,1,0:T(8,128)(2,1)}), bf16[1,3072,768]{2,1,0:T(8,128)(2,1)}) %all-gather.42.cloned.1.call-update) | async-done | bytes 4718608 | tf_op jit(solution)/shard_map/all_gather | solution.py:242
  318.8 5.3 fusion.227
  324.4 56.6 %all-gather.44.cloned.1.call-done = bf16[1,768,2304]{2,1,0:T(8,128)(2,1)} async-done(((bf16[1,24,2304]{2,1,0:T(8,128)(2,1)}), bf16[1,768,2304]{2,1,0:T(8,128)(2,1)}) %all-gather.44.cloned.1.call-update) | async-done | bytes 3538960 | tf_op jit(solution)/shard_map/all_gather | solution.py:259
  385.6 4.4 fusion.228
  392.4 45.0 %all-gather.46.cloned.1.call-done = bf16[1,768,768]{2,1,0:T(8,128)(2,1)} async-done(((bf16[1,24,768]{2,1,0:T(8,128)(2,1)}), bf16[1,768,768]{2,1,0:T(8,128)(2,1)}) %all-gather.46.cloned.1.call-update) | async-done | bytes 1179664 | tf_op jit(solution)/shard_map/all_gather | solution.py:261
  439.6 63.4 %all-gather.48.cloned.1.call-done = bf16[1,768,3072]{2,1,0:T(8,128)(2,1)} async-done(((bf16[1,24,3072]{2,1,0:T(8,128)(2,1)}), bf16[1,768,3072]{2,1,0:T(8,128)(2,1)}) %all-gather.48.cloned.1.call-update) | async-done | bytes 4718608 | tf_op jit(solution)/shard_map/all_gather | solution.py:265
  502.9 5.8 fusion.21
  508.7 60.2 %all-gather.50.cloned.1.call-done = bf16[1,3072,768]{2,1,0:T(8,128)(2,1)} async-done(((bf16[1,96,768]{2,1,0:T(8,128)(2,1)}), bf16[1,3072,768]{2,1,0:T(8,128)(2,1)}) %all-gather.50.cloned.1.call-update) | async-done | bytes 4718608 | tf_op jit(solution)/shard_map/all_gather | solution.py:267
  568.9 7.5 convert_reduce_fusion
  591.9 3.8 convert_reduce_fusion.1
  606.5 4.2 fusion.214
  617.7 5.2 fusion.216
  622.9 5.2 fusion.215
  632.8 3.4 multiply_reduce_fusion.5
  642.0 4.6 select_convert_fusion.4
  655.3 5.6 select_convert_fusion.2
  661.0 5.6 select_convert_fusion.3
  670.4 6.5 fusion.72
  676.8 152.6 %collective-permute-done.40 = bf16[384]{0:T(512)(128)(2,1)S(1)} collective-permute-done((bf16[384]{0:T(512)(128)(2,1)S(1)}, bf16[384]{0:T(512)(128)(2,1)S(1)}, u32[]{:S(2)}, u32[]{:S(2)}) %collective-permute-start.40) | collective-permute-done | bytes 800 | tf_op jit(solution)/shard_map/ppermute | solution.py:20
  829.5 4.4 collective-permute-done.35
  834.0 4.4 collective-permute-done.50
  838.5 4.4 collective-permute-done.45
  842.9 4.4 collective-permute-done.60
  847.4 4.4 collective-permute-done.55
  851.9 4.4 collective-permute-done.100
  856.4 4.4 collective-permute-done.95
  860.8 4.4 collective-permute-done.110
  865.3 4.4 collective-permute-done.105
  869.8 4.4 collective-permute-done.120
  874.2 4.4 collective-permute-done.115
  878.7 3.5 collective-permute-done.41
  882.3 3.4 collective-permute-done.36
  885.9 3.4 collective-permute-done.51
  1024.1 11.8 collective-permute-done.21
  1092.9 76.4 %collective-permute-done.25 = bf16[384,768]{1,0:T(8,128)(2,1)S(1)} collective-permute-done((bf16[384,768]{1,0:T(8,128)(2,1)S(1)}, bf16[384,768]{1,0:T(8,128)(2,1)S(1)}, u32[]{:S(2)}, u32[]{:S(2)}) %collective-permute-start.25) | collective-permute-done | bytes 589856 | tf_op jit(solution)/shard_map/ppermute | solution.py:20
  1173.8 51.7 %collective-permute-done.31 = bf16[192,768]{1,0:T(8,128)(2,1)S(1)} collective-permute-done((bf16[192,768]{1,0:T(8,128)(2,1)S(1)}, bf16[192,768]{1,0:T(8,128)(2,1)S(1)}, u32[]{:S(2)}, u32[]{:S(2)}) %collective-permute-start.31) | collective-permute-done | bytes 294944 | tf_op jit(solution)/shard_map/ppermute | solution.py:20
  1228.1 98.5 %collective-permute-done.26 = bf16[192,768]{1,0:T(8,128)(2,1)S(1)} collective-permute-done((bf16[192,768]{1,0:T(8,128)(2,1)S(1)}, bf16[192,768]{1,0:T(8,128)(2,1)S(1)}, u32[]{:S(2)}, u32[]{:S(2)}) %collective-permute-start.26) | collective-permute-done | bytes 294944 | tf_op jit(solution)/shard_map/ppermute | solution.py:20
  1328.2 4.2 collective-permute-done.32
  1333.9 3.6 collective-permute-done.27
  1346.8 7.7 collective-permute-done.1
  1357.2 5.5 collective-permute-done.2
  1365.4 3.4 collective-permute-done.3
  1373.7 4.1 convert_add_fusion.4
  1379.5 3.9 convert_add_fusion.5
  1388.5 5.6 convert_add_fusion.2
  1395.5 8.1 convert_add_fusion.3
  1403.6 3.6 select_convert_fusion.9
  1407.2 118.1 %collective-permute-done.90 = bf16[1536,768]{1,0:T(8,128)(2,1)} collective-permute-done((bf16[1536,768]{1,0:T(8,128)(2,1)}, bf16[1536,768]{1,0:T(8,128)(2,1)}, u32[]{:S(2)}, u32[]{:S(2)}) %collective-permute-start.90) | collective-permute-done | bytes 2359328 | tf_op jit(solution)/shard_map/ppermute | solution.py:20
  1525.3 4.7 convert_add_fusion
  1530.0 3.7 select_convert_fusion.6
  1533.7 42.2 %collective-permute-done.85 = bf16[1536,768]{1,0:T(8,128)(2,1)} collective-permute-done((bf16[1536,768]{1,0:T(8,128)(2,1)}, bf16[1536,768]{1,0:T(8,128)(2,1)}, u32[]{:S(2)}, u32[]{:S(2)}) %collective-permute-start.85) | collective-permute-done | bytes 2359328 | tf_op jit(solution)/shard_map/ppermute | solution.py:20
  1585.4 8.8 collective-permute-done.12
  1595.9 9.3 collective-permute-done.7
  1606.8 4.3 collective-permute-done.13
  1612.7 4.4 collective-permute-done.8
  1630.5 21.1 %collective-permute-done.86 = bf16[768,768]{1,0:T(8,128)(2,1)S(1)} collective-permute-done((bf16[768,768]{1,0:T(8,128)(2,1)S(1)}, bf16[768,768]{1,0:T(8,128)(2,1)S(1)}, u32[]{:S(2)}, u32[]{:S(2)}) %collective-permute-start.86) | collective-permute-done | bytes 1179680 | tf_op jit(solution)/shard_map/ppermute | solution.py:20
  1656.3 8.3 collective-permute-done.92
  1666.3 10.1 collective-permute-done.87
  1679.3 5.7 collective-permute-done.88
  (865 shorter events, 366.2 us)
Async XLA Ops:
  7.3 61.6 %all-gather.34.cloned.1.call-start = ((), (), s32[]{:S(2)}) async-start(), calls=%async_computation | async-start | bytes 1622016 | tf_op jit(solution)/shard_map/all_gather | solution.py:246
  8.0 123.3 %all-gather.36.cloned.1.call-start = ((), (), s32[]{:S(2)}) async-start(), calls=%async_computation.1 | async-start | bytes 3649536 | tf_op jit(solution)/shard_map/all_gather | solution.py:234
  9.7 177.4 %all-gather.38.cloned.1.call-start = ((), (), s32[]{:S(2)}) async-start(), calls=%async_computation.2 | async-start | bytes 1216512 | tf_op jit(solution)/shard_map/all_gather | solution.py:236
  11.3 241.8 %all-gather.40.cloned.1.call-start = ((), (), s32[]{:S(2)}) async-start(), calls=%async_computation.3 | async-start | bytes 4866048 | tf_op jit(solution)/shard_map/all_gather | solution.py:240
  13.1 305.8 %all-gather.42.cloned.1.call-start = ((), (), s32[]{:S(2)}) async-start(), calls=%async_computation.4 | async-start | bytes 4866048 | tf_op jit(solution)/shard_map/all_gather | solution.py:242
  14.8 366.2 %all-gather.44.cloned.1.call-start = ((), (), s32[]{:S(2)}) async-start(), calls=%async_computation.5 | async-start | bytes 3649536 | tf_op jit(solution)/shard_map/all_gather | solution.py:259
  15.4 422.0 %all-gather.46.cloned.1.call-start = ((), (), s32[]{:S(2)}) async-start(), calls=%async_computation.6 | async-start | bytes 1216512 | tf_op jit(solution)/shard_map/all_gather | solution.py:261
  16.2 486.7 %all-gather.48.cloned.1.call-start = ((), (), s32[]{:S(2)}) async-start(), calls=%async_computation.7 | async-start | bytes 4866048 | tf_op jit(solution)/shard_map/all_gather | solution.py:265
  16.9 552.0 %all-gather.50.cloned.1.call-start = ((), (), s32[]{:S(2)}) async-start(), calls=%async_computation.8 | async-start | bytes 4866048 | tf_op jit(solution)/shard_map/all_gather | solution.py:267
  639.9 529.7 %collective-permute-start = (bf16[512,768]{1,0:T(8,128)(2,1)}, bf16[512,768]{1,0:T(8,128)(2,1)}, u32[]{:S(2)}, u32[]{:S(2)}) collective-permute-start(bf16[512,768]{1,0:T(8,128)(2,1)} %select_convert_fusion.12), channel_id=1, source_target_pairs={{0,16},{1,17},{2,18},{3,19},{4,20},{5,21},{6,22},{7,23},{8,24},{9,... | collective-permute-start | bytes 2359304 | tf_op jit(solution)/shard_map/ppermute | solution.py:20
  646.6 724.8 %collective-permute-start.10 = (bf16[384,2304]{1,0:T(8,128)(2,1)}, bf16[384,2304]{1,0:T(8,128)(2,1)}, u32[]{:S(2)}, u32[]{:S(2)}) collective-permute-start(bf16[384,2304]{1,0:T(8,128)(2,1)} %select_convert_fusion.4), channel_id=1, source_target_pairs={{0,16},{1,17},{2,18},{3,19},{4,20},{5,21},{6,22},{7,23},{8,24},{9,... | collective-permute-start | bytes 5308424 | tf_op jit(solution)/shard_map/ppermute | solution.py:20
  649.0 730.4 %collective-permute-start.5 = (bf16[384,2304]{1,0:T(8,128)(2,1)}, bf16[384,2304]{1,0:T(8,128)(2,1)}, u32[]{:S(2)}, u32[]{:S(2)}) collective-permute-start(bf16[384,2304]{1,0:T(8,128)(2,1)} %select_convert_fusion.5), channel_id=1, source_target_pairs={{0,16},{1,17},{2,18},{3,19},{4,20},{5,21},{6,22},{7,23},{8,24},{9,... | collective-permute-start | bytes 5308424 | tf_op jit(solution)/shard_map/ppermute | solution.py:20
  651.2 369.7 %collective-permute-start.20 = (bf16[768]{0:T(1024)(128)(2,1)S(1)}, bf16[768]{0:T(1024)(128)(2,1)S(1)}, u32[]{:S(2)}, u32[]{:S(2)}) collective-permute-start(bf16[768]{0:T(1024)(128)(2,1)S(1)} %select_convert_fusion.49), channel_id=1, source_target_pairs={{0,16},{1,17},{2,18},{3,19},{4,20},{5,21},{6,22},{7,23},{8,24},{9,... | collective-permute-start | bytes 4616 | tf_op jit(solution)/shard_map/ppermute | solution.py:20
  653.0 176.4 %collective-permute-start.40 = (bf16[384]{0:T(512)(128)(2,1)S(1)}, bf16[384]{0:T(512)(128)(2,1)S(1)}, u32[]{:S(2)}, u32[]{:S(2)}) collective-permute-start(bf16[384]{0:T(512)(128)(2,1)S(1)} %select_convert_fusion.63), channel_id=1, source_target_pairs={{0,16},{1,17},{2,18},{3,19},{4,20},{5,21},{6,22},{7,23},{8,24},{9,... | collective-permute-start | bytes 2312 | tf_op jit(solution)/shard_map/ppermute | solution.py:20
  829.5 4.5 collective-permute-start.35
  833.9 4.5 collective-permute-start.50
  838.4 4.5 collective-permute-start.45
  842.9 4.5 collective-permute-start.60
  847.3 4.5 collective-permute-start.55
  851.8 4.5 collective-permute-start.100
  856.3 4.5 collective-permute-start.95
  860.7 4.5 collective-permute-start.110
  865.2 4.5 collective-permute-start.105
  869.7 4.5 collective-permute-start.120
  874.1 4.5 collective-permute-start.115
  1019.6 4.5 collective-permute-start.15
  1020.9 71.4 %collective-permute-start.30 = (bf16[384,768]{1,0:T(8,128)(2,1)S(1)}, bf16[384,768]{1,0:T(8,128)(2,1)S(1)}, u32[]{:S(2)}, u32[]{:S(2)}) collective-permute-start(bf16[384,768]{1,0:T(8,128)(2,1)S(1)} %copy-done.48), channel_id=1, source_target_pairs={{0,16},{1,17},{2,18},{3,19},{4,20},{5,21},{6,22},{7,23},{8,24},{9,... | collective-permute-start | bytes 1769480 | tf_op jit(solution)/shard_map/ppermute | solution.py:20
  1024.0 11.9 collective-permute-start.21
  1056.4 4.5 collective-permute-start.80
  1060.9 4.5 collective-permute-start.75
  1089.1 80.3 %collective-permute-start.25 = (bf16[384,768]{1,0:T(8,128)(2,1)S(1)}, bf16[384,768]{1,0:T(8,128)(2,1)S(1)}, u32[]{:S(2)}, u32[]{:S(2)}) collective-permute-start(bf16[384,768]{1,0:T(8,128)(2,1)S(1)} %select_convert_fusion.18), channel_id=1, source_target_pairs={{0,16},{1,17},{2,18},{3,19},{4,20},{5,21},{6,22},{7,23},{8,24},{9,... | collective-permute-start | bytes 1769480 | tf_op jit(solution)/shard_map/ppermute | solution.py:20
  1092.3 294.3 %collective-permute-start.70 = (bf16[384,3072]{1,0:T(8,128)(2,1)}, bf16[384,3072]{1,0:T(8,128)(2,1)}, u32[]{:S(2)}, u32[]{:S(2)}) collective-permute-start(bf16[384,3072]{1,0:T(8,128)(2,1)} %select_convert_fusion.2), channel_id=1, source_target_pairs={{0,16},{1,17},{2,18},{3,19},{4,20},{5,21},{6,22},{7,23},{8,24},{9,... | collective-permute-start | bytes 7077896 | tf_op jit(solution)/shard_map/ppermute | solution.py:20
  1169.3 226.0 %collective-permute-start.65 = (bf16[384,3072]{1,0:T(8,128)(2,1)}, bf16[384,3072]{1,0:T(8,128)(2,1)}, u32[]{:S(2)}, u32[]{:S(2)}) collective-permute-start(bf16[384,3072]{1,0:T(8,128)(2,1)} %select_convert_fusion.3), channel_id=1, source_target_pairs={{0,16},{1,17},{2,18},{3,19},{4,20},{5,21},{6,22},{7,23},{8,24},{9,... | collective-permute-start | bytes 7077896 | tf_op jit(solution)/shard_map/ppermute | solution.py:20
  1169.6 55.9 %collective-permute-start.31 = (bf16[192,768]{1,0:T(8,128)(2,1)S(1)}, bf16[192,768]{1,0:T(8,128)(2,1)S(1)}, u32[]{:S(2)}, u32[]{:S(2)}) collective-permute-start(bf16[192,768]{1,0:T(8,128)(2,1)S(1)} %select_convert_fusion.26), channel_id=1, source_target_pairs={{0,8},{1,9},{2,10},{3,11},{4,12},{5,13},{6,14},{7,15},{8,0},{9,1},... | collective-permute-start | bytes 884744 | tf_op jit(solution)/shard_map/ppermute | solution.py:20
  1225.5 101.1 %collective-permute-start.26 = (bf16[192,768]{1,0:T(8,128)(2,1)S(1)}, bf16[192,768]{1,0:T(8,128)(2,1)S(1)}, u32[]{:S(2)}, u32[]{:S(2)}) collective-permute-start(bf16[192,768]{1,0:T(8,128)(2,1)S(1)} %select_convert_fusion.27), channel_id=1, source_target_pairs={{0,8},{1,9},{2,10},{3,11},{4,12},{5,13},{6,14},{7,15},{8,0},{9,1},... | collective-permute-start | bytes 884744 | tf_op jit(solution)/shard_map/ppermute | solution.py:20
  1326.6 5.8 collective-permute-start.32
  1332.4 5.1 collective-permute-start.27
  1337.5 4.9 collective-permute-start.33
  1346.8 7.8 collective-permute-start.1
  1355.8 7.0 collective-permute-start.2
  1363.9 4.9 collective-permute-start.3
  1370.2 155.2 %collective-permute-start.90 = (bf16[1536,768]{1,0:T(8,128)(2,1)}, bf16[1536,768]{1,0:T(8,128)(2,1)}, u32[]{:S(2)}, u32[]{:S(2)}) collective-permute-start(bf16[1536,768]{1,0:T(8,128)(2,1)} %select_convert_fusion), channel_id=1, source_target_pairs={{0,16},{1,17},{2,18},{3,19},{4,20},{5,21},{6,22},{7,23},{8,24},{9,... | collective-permute-start | bytes 7077896 | tf_op jit(solution)/shard_map/ppermute | solution.py:20
  1371.4 204.5 %collective-permute-start.85 = (bf16[1536,768]{1,0:T(8,128)(2,1)}, bf16[1536,768]{1,0:T(8,128)(2,1)}, u32[]{:S(2)}, u32[]{:S(2)}) collective-permute-start(bf16[1536,768]{1,0:T(8,128)(2,1)} %select_convert_fusion.1), channel_id=1, source_target_pairs={{0,16},{1,17},{2,18},{3,19},{4,20},{5,21},{6,22},{7,23},{8,24},{9,... | collective-permute-start | bytes 7077896 | tf_op jit(solution)/shard_map/ppermute | solution.py:20
  1379.4 199.3 %collective-permute-start.11 = (bf16[192,2304]{1,0:T(8,128)(2,1)}, bf16[192,2304]{1,0:T(8,128)(2,1)}, u32[]{:S(2)}, u32[]{:S(2)}) collective-permute-start(bf16[192,2304]{1,0:T(8,128)(2,1)} %select_convert_fusion.10), channel_id=1, source_target_pairs={{0,8},{1,9},{2,10},{3,11},{4,12},{5,13},{6,14},{7,15},{8,0},{9,1},... | collective-permute-start | bytes 2654216 | tf_op jit(solution)/shard_map/ppermute | solution.py:20
  1386.6 195.8 %collective-permute-start.6 = (bf16[192,2304]{1,0:T(8,128)(2,1)}, bf16[192,2304]{1,0:T(8,128)(2,1)}, u32[]{:S(2)}, u32[]{:S(2)}) collective-permute-start(bf16[192,2304]{1,0:T(8,128)(2,1)} %select_convert_fusion.11), channel_id=1, source_target_pairs={{0,8},{1,9},{2,10},{3,11},{4,12},{5,13},{6,14},{7,15},{8,0},{9,1},... | collective-permute-start | bytes 2654216 | tf_op jit(solution)/shard_map/ppermute | solution.py:20
  1395.3 225.3 %collective-permute-start.71 = (bf16[192,3072]{1,0:T(8,128)(2,1)}, bf16[192,3072]{1,0:T(8,128)(2,1)}, u32[]{:S(2)}, u32[]{:S(2)}) collective-permute-start(bf16[192,3072]{1,0:T(8,128)(2,1)} %select_convert_fusion.8), channel_id=1, source_target_pairs={{0,8},{1,9},{2,10},{3,11},{4,12},{5,13},{6,14},{7,15},{8,0},{9,1},... | collective-permute-start | bytes 3538952 | tf_op jit(solution)/shard_map/ppermute | solution.py:20
  1525.3 99.3 %collective-permute-start.66 = (bf16[192,3072]{1,0:T(8,128)(2,1)}, bf16[192,3072]{1,0:T(8,128)(2,1)}, u32[]{:S(2)}, u32[]{:S(2)}) collective-permute-start(bf16[192,3072]{1,0:T(8,128)(2,1)} %select_convert_fusion.9), channel_id=1, source_target_pairs={{0,8},{1,9},{2,10},{3,11},{4,12},{5,13},{6,14},{7,15},{8,0},{9,1},... | collective-permute-start | bytes 3538952 | tf_op jit(solution)/shard_map/ppermute | solution.py:20
  1575.9 51.6 %collective-permute-start.91 = (bf16[768,768]{1,0:T(8,128)(2,1)}, bf16[768,768]{1,0:T(8,128)(2,1)}, u32[]{:S(2)}, u32[]{:S(2)}) collective-permute-start(bf16[768,768]{1,0:T(8,128)(2,1)} %select_convert_fusion.6), channel_id=1, source_target_pairs={{0,8},{1,9},{2,10},{3,11},{4,12},{5,13},{6,14},{7,15},{8,0},{9,1},... | collective-permute-start | bytes 3538952 | tf_op jit(solution)/shard_map/ppermute | solution.py:20
  1578.7 72.8 %collective-permute-start.86 = (bf16[768,768]{1,0:T(8,128)(2,1)S(1)}, bf16[768,768]{1,0:T(8,128)(2,1)S(1)}, u32[]{:S(2)}, u32[]{:S(2)}) collective-permute-start(bf16[768,768]{1,0:T(8,128)(2,1)S(1)} %select_convert_fusion.7), channel_id=1, source_target_pairs={{0,8},{1,9},{2,10},{3,11},{4,12},{5,13},{6,14},{7,15},{8,0},{9,1},... | collective-permute-start | bytes 3538952 | tf_op jit(solution)/shard_map/ppermute | solution.py:20
  1582.4 11.8 collective-permute-start.12
  1594.2 11.0 collective-permute-start.7
  1605.2 5.9 collective-permute-start.13
  1611.1 5.9 collective-permute-start.8
  1623.0 30.6 %collective-permute-start.72 = (bf16[96,3072]{1,0:T(8,128)(2,1)S(1)}, bf16[96,3072]{1,0:T(8,128)(2,1)S(1)}, u32[]{:S(2)}, u32[]{:S(2)}) collective-permute-start(bf16[96,3072]{1,0:T(8,128)(2,1)S(1)} %select_convert_fusion.15), channel_id=1, source_target_pairs={{0,4},{1,5},{2,6},{3,7},{4,0},{5,1},{6,2},{7,3},{8,12},{9,13},{10,... | collective-permute-start | bytes 1769480 | tf_op jit(solution)/shard_map/ppermute | solution.py:20
  1626.5 28.0 %collective-permute-start.67 = (bf16[96,3072]{1,0:T(8,128)(2,1)S(1)}, bf16[96,3072]{1,0:T(8,128)(2,1)S(1)}, u32[]{:S(2)}, u32[]{:S(2)}) collective-permute-start(bf16[96,3072]{1,0:T(8,128)(2,1)S(1)} %select_convert_fusion.16), channel_id=1, source_target_pairs={{0,4},{1,5},{2,6},{3,7},{4,0},{5,1},{6,2},{7,3},{8,12},{9,13},{10,... | collective-permute-start | bytes 1769480 | tf_op jit(solution)/shard_map/ppermute | solution.py:20
  1629.3 35.3 %collective-permute-start.92 = (bf16[384,768]{1,0:T(8,128)(2,1)S(1)}, bf16[384,768]{1,0:T(8,128)(2,1)S(1)}, u32[]{:S(2)}, u32[]{:S(2)}) collective-permute-start(bf16[384,768]{1,0:T(8,128)(2,1)S(1)} %select_convert_fusion.13), channel_id=1, source_target_pairs={{0,4},{1,5},{2,6},{3,7},{4,0},{5,1},{6,2},{7,3},{8,12},{9,13},{10,... | collective-permute-start | bytes 1769480 | tf_op jit(solution)/shard_map/ppermute | solution.py:20
  1652.1 24.3 %collective-permute-start.87 = (bf16[384,768]{1,0:T(8,128)(2,1)S(1)}, bf16[384,768]{1,0:T(8,128)(2,1)S(1)}, u32[]{:S(2)}, u32[]{:S(2)}) collective-permute-start(bf16[384,768]{1,0:T(8,128)(2,1)S(1)} %select_convert_fusion.14), channel_id=1, source_target_pairs={{0,4},{1,5},{2,6},{3,7},{4,0},{5,1},{6,2},{7,3},{8,12},{9,13},{10,... | collective-permute-start | bytes 1769480 | tf_op jit(solution)/shard_map/ppermute | solution.py:20
  1653.9 24.3 %collective-permute-start.73 = (bf16[48,3072]{1,0:T(8,128)(2,1)S(1)}, bf16[48,3072]{1,0:T(8,128)(2,1)S(1)}, u32[]{:S(2)}, u32[]{:S(2)}) collective-permute-start(bf16[48,3072]{1,0:T(8,128)(2,1)S(1)} %select_convert_fusion.24), channel_id=1, source_target_pairs={{0,2},{1,3},{2,0},{3,1},{4,6},{5,7},{6,4},{7,5},{8,10},{9,11},{10,... | collective-permute-start | bytes 884744 | tf_op jit(solution)/shard_map/ppermute | solution.py:20
  1654.7 23.6 %collective-permute-start.68 = (bf16[48,3072]{1,0:T(8,128)(2,1)S(1)}, bf16[48,3072]{1,0:T(8,128)(2,1)S(1)}, u32[]{:S(2)}, u32[]{:S(2)}) collective-permute-start(bf16[48,3072]{1,0:T(8,128)(2,1)S(1)} %select_convert_fusion.25), channel_id=1, source_target_pairs={{0,2},{1,3},{2,0},{3,1},{4,6},{5,7},{6,4},{7,5},{8,10},{9,11},{10,... | collective-permute-start | bytes 884744 | tf_op jit(solution)/shard_map/ppermute | solution.py:20
  1664.8 14.2 collective-permute-start.93
  1676.7 8.3 collective-permute-start.88
  1678.3 6.9 collective-permute-start.74
  1678.5 6.7 collective-permute-start.69
  1679.2 7.0 collective-permute-start.94
  (191 other events, 3482.6 us)
Sparse Core Ops, SparseCore 0:
  11.0 57.8 all-gather.33
  72.4 58.9 all-gather.35
  134.2 52.8 all-gather.37
  190.4 62.5 all-gather.39
  256.4 62.4 all-gather.41
  322.2 58.8 all-gather.43
  384.5 52.8 all-gather.45
  440.3 62.5 all-gather.47
  506.4 62.4 all-gather.49
where the time goes:
time: 1700 us; the launch traced here: 1690 us
  waiting for transfers between devices  1290 us (76%)
  starting transfers between devices  114 us (7%)
  other arithmetic  107 us (6%)
  matrix products  102 us (6%)
  blocking collectives  43.2 us (3%)
  local copies, waits for them, and re-layouts  20.5 us (1%)
    ppermute x125, waiting for transfers between devices, partner(): lax.ppermute(value, axis, [(i, i ^ 1 << stride) for i in range(lax.axis_s...  830 us
    ppermute x125, starting transfers between devices, partner(): lax.ppermute(value, axis, [(i, i ^ 1 << stride) for i in range(lax.axis_s...  113 us
    all_gather x1, waiting for transfers between devices, local(): lax.all_gather(up_weight[0], 'dp', axis=0, tiled=True)  63.8 us
    all_gather x1, waiting for transfers between devices, local(): lax.all_gather(up_weight[1], 'dp', axis=0, tiled=True)  63.4 us
    all_gather x1, waiting for transfers between devices, local(): lax.all_gather(down_weight[0], 'dp', axis=0, tiled=True)  60.4 us
    all_gather x1, waiting for transfers between devices, local(): lax.all_gather(down_weight[1], 'dp', axis=0, tiled=True)  60.2 us
    all_gather x1, waiting for transfers between devices, local(): lax.all_gather(qkv_weight[0], 'dp', axis=0, tiled=True)  59.8 us
    all_gather x1, waiting for transfers between devices, local(): lax.all_gather(qkv_weight[1], 'dp', axis=0, tiled=True)  56.6 us
  transfers between devices with their start and end apart: 134, of which 114 were waited for; matrix products, arithmetic and copies ran while one was open for 9% of the time, Pallas kernels for 0%

commit v1 on v0

--- a/solution.py
+++ b/solution.py
@@ -3,21 +3,38 @@
 import jax
 import jax.numpy as jnp
 from jax import lax
+from jax.experimental import pallas as pl
+from jax.experimental.pallas import tpu as pltpu
 from jax.sharding import PartitionSpec as P
 
 HEADS = 12
 HEAD_DIM = 64
-
-
 EPSILON = 1e-05
-
-
-def shortened(value):
-    return jax.tree.map(lambda a: a.astype(jnp.bfloat16) if a.dtype == jnp.float32 else a, value)
-
-
-def partner(value, axis, stride):
-    return lax.ppermute(value, axis, [(i, i ^ 1 << stride) for i in range(lax.axis_size(axis))])
+BF = jnp.bfloat16
+F32 = jnp.float32
+
+TUNED = 32
+CORE, ALONG_X, ALONG_Y, ALONG_Z, MIDDLE = 1, 2, 4, 8, 24
+SLAB = 48
+HALF = 384
+SMALL_SIZES = (48, 24, 24, 24, 96, 24, 24, 24)
+
+
+def swap(value, stride):
+    return lax.ppermute(value, "dp", [(i, i ^ stride) for i in range(TUNED)])
+
+
+def swap_from(value, stride, zs):
+    return lax.ppermute(value, "dp", [(i, i ^ stride) for i in range(TUNED) if i // 8 in zs])
+
+
+def after(done, waiting):
+    return lax.optimization_barrier((done, waiting))
+
+
+def place():
+    index = lax.axis_index("dp")
+    return index % 2, index // 2, index // 8
 
 
 def norm_rows(hidden, gain_vec, shift_vec):
@@ -39,6 +56,170 @@
 
 def smooth_gate(lifted):
     return jax.nn.gelu(lifted, approximate=True)
+
+
+def layer_apply(hidden, params, same_doc):
+    qkv_w, qv_b, out_w, out_b, gain_a, shift_a, up_w, up_b, down_w, down_b, gain_b, shift_b = params
+    width = out_w.shape[0]
+    tok_count = hidden.shape[0]
+    scale = 1.0 / math.sqrt(HEAD_DIM)
+    normed_a, unit_a, inverse_a = norm_rows(hidden, gain_a, shift_a)
+    normed_a = normed_a.astype(jnp.bfloat16)
+    qv_float = qv_b.astype(jnp.float32)
+    bias_full = jnp.concatenate(
+        [qv_float[:width], jnp.zeros((width,), jnp.float32), qv_float[width:]]
+    )
+    packed = (jnp.dot(normed_a, qkv_w, preferred_element_type=jnp.float32) + bias_full).astype(
+        jnp.bfloat16
+    )
+    queries = packed[:, :width].reshape(tok_count, HEADS, HEAD_DIM)
+    key_rows = packed[:, width : 2 * width].reshape(tok_count, HEADS, HEAD_DIM)
+    value_rows = packed[:, 2 * width :].reshape(tok_count, HEADS, HEAD_DIM)
+    scores = (
+        jnp.einsum("qhd,khd->hqk", queries, key_rows, preferred_element_type=jnp.float32) * scale
+    )
+    masked = jnp.where(same_doc[None], scores, -1e30)
+    top_score = jnp.max(masked, axis=-1, keepdims=True)
+    expo_rows = jnp.exp(masked - top_score)
+    probs = expo_rows / jnp.sum(expo_rows, axis=-1, keepdims=True)
+    probs_low = probs.astype(jnp.bfloat16)
+    mixed = jnp.einsum("hqk,khd->qhd", probs_low, value_rows, preferred_element_type=jnp.float32)
+    mixed = mixed.reshape(tok_count, width).astype(jnp.bfloat16)
+    middle = (
+        hidden
+        + jnp.dot(mixed, out_w, preferred_element_type=jnp.float32)
+        + out_b.astype(jnp.float32)
+    )
+    normed_b, unit_b, inverse_b = norm_rows(middle, gain_b, shift_b)
+    normed_b = normed_b.astype(jnp.bfloat16)
+    lifted = jnp.dot(normed_b, up_w, preferred_element_type=jnp.float32) + up_b.astype(jnp.float32)
+    activated = smooth_gate(lifted).astype(jnp.bfloat16)
+    output = (
+        middle
+        + jnp.dot(activated, down_w, preferred_element_type=jnp.float32)
+        + down_b.astype(jnp.float32)
+    )
+    saved = (
+        unit_a,
+        inverse_a,
+        normed_a,
+        queries,
+        key_rows,
+        value_rows,
+        probs,
+        probs_low,
+        mixed,
+        unit_b,
+        inverse_b,
+        normed_b,
+        lifted,
+        activated,
+    )
+    return (output, saved)
+
+
+def half_sums(rows, grads, core):
+    count = grads.shape[1] // 2
+    return [
+        jnp.einsum(
+            "td,te->de",
+            rows,
+            lax.dynamic_slice_in_dim(grads, side * count, count, 1),
+            preferred_element_type=jnp.float32,
+        ).astype(BF)
+        for side in (core, 1 - core)
+    ]
+
+
+def layer_back(params, saved, grad_top, core):
+    qkv_w, qv_b, out_w, out_b, gain_a, shift_a, up_w, up_b, down_w, down_b, gain_b, shift_b = params
+    (
+        unit_a,
+        inverse_a,
+        normed_a,
+        queries,
+        key_rows,
+        value_rows,
+        probs,
+        probs_low,
+        mixed,
+        unit_b,
+        inverse_b,
+        normed_b,
+        lifted,
+        activated,
+    ) = saved
+    width = out_w.shape[0]
+    tok_count = grad_top.shape[0]
+    scale = 1.0 / math.sqrt(HEAD_DIM)
+    grad_down = grad_top.astype(jnp.bfloat16)
+    down_b_grad = jnp.sum(grad_down.astype(jnp.float32), axis=0)
+    down_w_grad = [
+        part.reshape(16, 4, SLAB, HALF).transpose(0, 2, 1, 3).reshape(width, 4 * HALF)
+        for part in half_sums(activated, grad_down, core)
+    ]
+    grad_act = jnp.einsum("td,fd->tf", grad_down, down_w, preferred_element_type=jnp.float32)
+    unused_gate, gate_pull = jax.vjp(smooth_gate, lifted)
+    grad_lift = gate_pull(grad_act)[0].astype(jnp.bfloat16)
+    up_b_grad = jnp.sum(grad_lift.astype(jnp.float32), axis=0)
+    up_w_grad = half_sums(normed_b, grad_lift, core)
+    mlp_grads = [jnp.concatenate(pair, axis=1) for pair in zip(up_w_grad, down_w_grad)]
+    grad_nb = jnp.einsum("tf,df->td", grad_lift, up_w, preferred_element_type=jnp.float32)
+    gain_b_grad = jnp.sum(grad_nb * unit_b, axis=0)
+    shift_b_grad = jnp.sum(grad_nb, axis=0)
+    grad_mid = grad_top + norm_back(grad_nb, unit_b, inverse_b, gain_b)
+    grad_branch = grad_mid.astype(jnp.bfloat16)
+    out_b_grad = jnp.sum(grad_branch.astype(jnp.float32), axis=0)
+    out_w_grad = half_sums(mixed, grad_branch, core)
+    grad_mixed = jnp.einsum("td,ed->te", grad_branch, out_w, preferred_element_type=jnp.float32)
+    grad_mixed = grad_mixed.astype(jnp.bfloat16).reshape(tok_count, HEADS, HEAD_DIM)
+    grad_probs = jnp.einsum(
+        "qhd,khd->hqk", grad_mixed, value_rows, preferred_element_type=jnp.float32
+    )
+    grad_values = jnp.einsum(
+        "hqk,qhd->khd", probs_low, grad_mixed, preferred_element_type=jnp.float32
+    )
+    grad_scores = probs * (grad_probs - jnp.sum(probs * grad_probs, axis=-1, keepdims=True))
+    scores_low = grad_scores.astype(jnp.bfloat16)
+    grad_queries = (
+        jnp.einsum("hqk,khd->qhd", scores_low, key_rows, preferred_element_type=jnp.float32) * scale
+    )
+    grad_keys = (
+        jnp.einsum("hqk,qhd->khd", scores_low, queries, preferred_element_type=jnp.float32) * scale
+    )
+    grad_packed = jnp.concatenate(
+        [
+            grad_queries.reshape(tok_count, width),
+            grad_keys.reshape(tok_count, width),
+            grad_values.reshape(tok_count, width),
+        ],
+        axis=1,
+    ).astype(jnp.bfloat16)
+    packed_sums = jnp.sum(grad_packed.astype(jnp.float32), axis=0)
+    qv_b_grad = jnp.concatenate([packed_sums[:width], packed_sums[2 * width :]])
+    qkv_w_grad = half_sums(normed_a, grad_packed, core)
+    attn_grads = [jnp.concatenate(pair, axis=1) for pair in zip(qkv_w_grad, out_w_grad)]
+    grad_na = jnp.einsum("te,de->td", grad_packed, qkv_w, preferred_element_type=jnp.float32)
+    gain_a_grad = jnp.sum(grad_na * unit_a, axis=0)
+    shift_a_grad = jnp.sum(grad_na, axis=0)
+    grad_in = grad_mid + norm_back(grad_na, unit_a, inverse_a, gain_a)
+    small_grads = (
+        qv_b_grad,
+        out_b_grad,
+        gain_a_grad,
+        shift_a_grad,
+        up_b_grad,
+        down_b_grad,
+        gain_b_grad,
+        shift_b_grad,
+    )
+    return (grad_in, (mlp_grads, attn_grads), small_grads)
+def shortened(value):
+    return jax.tree.map(lambda a: a.astype(jnp.bfloat16) if a.dtype == jnp.float32 else a, value)
+
+
+def partner(value, axis, stride):
+    return lax.ppermute(value, axis, [(i, i ^ 1 << stride) for i in range(lax.axis_size(axis))])
 
 
 def halving_sum(members, send_fn):
@@ -60,67 +241,7 @@
     return current
 
 
-def layer_apply(hidden, params, same_doc):
-    qkv_w, qv_b, out_w, out_b, gain_a, shift_a, up_w, up_b, down_w, down_b, gain_b, shift_b = params
-    width = out_w.shape[0]
-    tok_count = hidden.shape[0]
-    scale = 1.0 / math.sqrt(HEAD_DIM)
-    normed_a, unit_a, inverse_a = norm_rows(hidden, gain_a, shift_a)
-    normed_a = normed_a.astype(jnp.bfloat16)
-    qv_float = qv_b.astype(jnp.float32)
-    bias_full = jnp.concatenate(
-        [qv_float[:width], jnp.zeros((width,), jnp.float32), qv_float[width:]]
-    )
-    packed = (jnp.dot(normed_a, qkv_w, preferred_element_type=jnp.float32) + bias_full).astype(
-        jnp.bfloat16
-    )
-    queries = packed[:, :width].reshape(tok_count, HEADS, HEAD_DIM)
-    key_rows = packed[:, width : 2 * width].reshape(tok_count, HEADS, HEAD_DIM)
-    value_rows = packed[:, 2 * width :].reshape(tok_count, HEADS, HEAD_DIM)
-    scores = (
-        jnp.einsum("qhd,khd->hqk", queries, key_rows, preferred_element_type=jnp.float32) * scale
-    )
-    masked = jnp.where(same_doc[None], scores, -1e30)
-    top_score = jnp.max(masked, axis=-1, keepdims=True)
-    expo_rows = jnp.exp(masked - top_score)
-    probs = expo_rows / jnp.sum(expo_rows, axis=-1, keepdims=True)
-    probs_low = probs.astype(jnp.bfloat16)
-    mixed = jnp.einsum("hqk,khd->qhd", probs_low, value_rows, preferred_element_type=jnp.float32)
-    mixed = mixed.reshape(tok_count, width).astype(jnp.bfloat16)
-    middle = (
-        hidden
-        + jnp.dot(mixed, out_w, preferred_element_type=jnp.float32)
-        + out_b.astype(jnp.float32)
-    )
-    normed_b, unit_b, inverse_b = norm_rows(middle, gain_b, shift_b)
-    normed_b = normed_b.astype(jnp.bfloat16)
-    lifted = jnp.dot(normed_b, up_w, preferred_element_type=jnp.float32) + up_b.astype(jnp.float32)
-    activated = smooth_gate(lifted).astype(jnp.bfloat16)
-    output = (
-        middle
-        + jnp.dot(activated, down_w, preferred_element_type=jnp.float32)
-        + down_b.astype(jnp.float32)
-    )
-    saved = (
-        unit_a,
-        inverse_a,
-        normed_a,
-        queries,
-        key_rows,
-        value_rows,
-        probs,
-        probs_low,
-        mixed,
-        unit_b,
-        inverse_b,
-        normed_b,
-        lifted,
-        activated,
-    )
-    return (output, saved)
-
-
-def layer_back(hidden, params, same_doc, grad_top):
+def plain_back(hidden, params, same_doc, grad_top):
     qkv_w, qv_b, out_w, out_b, gain_a, shift_a, up_w, up_b, down_w, down_b, gain_b, shift_b = params
     unused_output, saved = layer_apply(hidden, params, same_doc)
     (
@@ -205,7 +326,7 @@
     return (grad_in, grads)
 
 
-def local(
+def plain(
     embedded,
     doc_ids,
     step_ids,
@@ -288,7 +409,7 @@
             lax.all_gather(second_shift[layer_index], "dp", axis=0, tiled=True),
         )
 
-    grad_upper_in, upper_grads = layer_back(
+    grad_upper_in, upper_grads = plain_back(
         middle_hidden, weights_for(1), same_doc, cotangent.astype(jnp.float32)
     )
 
@@ -298,7 +419,7 @@
         )
 
     upper_shards = halving_sum(upper_grads, send_upper)
-    input_grad, lower_grads = layer_back(start, weights_for(0), same_doc, grad_upper_in)
+    input_grad, lower_grads = plain_back(start, weights_for(0), same_doc, grad_upper_in)
     doc_grads = jnp.einsum("ts,td->sd", doc_hot, input_grad, precision=lax.Precision.HIGHEST)
     table_full_grad = jnp.einsum(
         "sn,sd->nd", step_hot.astype(jnp.float32), doc_grads, precision=lax.Precision.HIGHEST
@@ -332,7 +453,342 @@
     )
 
 
+def is_middle():
+    level = lax.axis_index("dp") // 8
+    return (level == 1) | (level == 2)
+
+
+def middle_column(value):
+    return value.shape[-1] // 256 * 128
+
+
+def gather_parts(own):
+    middle = is_middle()
+    first = swap(own, ALONG_Z)
+    third_middle = swap_from(own, MIDDLE, (1, 2))
+    second_middle = swap_from(first, MIDDLE, (1, 2))
+    second_end = swap_from(third_middle, ALONG_Z, (1, 2))
+    third_end = swap_from(second_middle, ALONG_Z, (1, 2))
+    levels = [
+        own,
+        first,
+        jnp.where(middle, second_middle, second_end),
+        jnp.where(middle, third_middle, third_end),
+    ]
+    cut = middle_column(own)
+    parts = []
+    for level in levels:
+        by_x = swap(level, ALONG_X)
+        by_y = swap(level, ALONG_Y)
+        by_both = jnp.concatenate([swap(by_x[:, :cut], ALONG_Y), swap(by_y[:, cut:], ALONG_X)], axis=1)
+        parts.append(jnp.stack([level, by_x, by_y, by_both]))
+    return parts
+
+
+def reduce_parts(parts):
+    def add(*values):
+        return sum(v.astype(F32) for v in values).astype(BF)
+
+    cut = middle_column(parts[0][0])
+    levels = [None] * 4
+    for distance in (3, 2, 1, 0):
+        own, by_x, by_y, by_both = parts[distance]
+        back_y = swap(by_both[:, :cut], ALONG_Y)
+        back_x = swap(by_both[:, cut:], ALONG_X)
+        to_x = jnp.concatenate([add(by_x[:, :cut], back_y), by_x[:, cut:]], axis=1)
+        to_y = jnp.concatenate([by_y[:, :cut], add(by_y[:, cut:], back_x)], axis=1)
+        levels[distance] = add(own, swap(to_x, ALONG_X), swap(to_y, ALONG_Y))
+    own, first, second, third = levels
+    end_third = swap_from(third, ALONG_Z, (0, 3))
+    end_second = swap_from(second, ALONG_Z, (0, 3))
+    across_second = swap_from(add(second, end_third), MIDDLE, (1, 2))
+    across_third = swap_from(add(third, end_second), MIDDLE, (1, 2))
+    last = swap(add(first, across_second), ALONG_Z)
+    return sum(v.astype(F32) for v in (own, across_third, last))
+
+
+def layout(with_extra):
+    names = [("qkv", 1152), ("out", 384), ("up", 1536), ("down", 1536)]
+    return names + [("extra", 768)] if with_extra else names
+
+
+def assemble(mine, other, with_extra):
+    names = layout(with_extra)
+    shapes = {"qkv": (768, 2304), "out": (768, 768), "up": (768, 3072), "down": (3072, 768), "extra": (768, 1536)}
+
+    def body(*refs):
+        sources = refs[:8]
+        outputs = refs[8 : 8 + len(names)]
+        held = refs[8 + len(names) : 8 + 2 * len(names)]
+        targets = dict(zip([name for name, _ in names], held))
+        sems, out_sems = refs[-2:]
+        index = lax.axis_index("dp")
+        core, chip = index % 2, index // 2
+        copies = []
+        for which in range(8):
+            half = core if which < 4 else 1 - core
+            for step in range(4):
+                there = chip ^ (4 * (which % 4) + step)
+                start = 0
+                for name, width in names:
+                    target = targets[name]
+                    if name == "down":
+                        for block in range(4):
+                            copies.append(
+                                (
+                                    sources[which].at[step, :, pl.ds(start + block * HALF, HALF)],
+                                    target.at[
+                                        pl.ds(pl.multiple_of(there * 192 + block * SLAB, SLAB), SLAB),
+                                        pl.ds(pl.multiple_of(half * HALF, HALF), HALF),
+                                    ],
+                                )
+                            )
+                    else:
+                        copies.append(
+                            (
+                                sources[which].at[step, :, pl.ds(start, width)],
+                                target.at[
+                                    pl.ds(pl.multiple_of(there * SLAB, SLAB), SLAB),
+                                    pl.ds(pl.multiple_of(half * width, 128), width),
+                                ],
+                            )
+                        )
+                    start += width
+        started = [pltpu.make_async_copy(a, b, sems.at[n]) for n, (a, b) in enumerate(copies)]
+        for copy in started:
+            copy.start()
+        for copy in started:
+            copy.wait()
+        written = [pltpu.make_async_copy(a, b, out_sems.at[n]) for n, (a, b) in enumerate(zip(held, outputs))]
+        for copy in written:
+            copy.start()
+        for copy in written:
+            copy.wait()
+
+    count = 32 * (8 if with_extra else 7)
+    return pl.pallas_call(
+        body,
+        out_shape=[jax.ShapeDtypeStruct(shapes[name], BF) for name, _ in names],
+        in_specs=[pl.BlockSpec(memory_space=pl.ANY)] * 8,
+        out_specs=[pl.BlockSpec(memory_space=pl.ANY)] * len(names),
+        scratch_shapes=[pltpu.VMEM(shapes[name], BF) for name, _ in names]
+        + [pltpu.SemaphoreType.DMA((count,)), pltpu.SemaphoreType.DMA((len(names),))],
+        compiler_params=pltpu.CompilerParams(vmem_limit_bytes=24 * 2**20),
+        cost_estimate=pl.CostEstimate(flops=0, bytes_accessed=2 * 14 * 2**20, transcendentals=0),
+    )(*mine, *other)
+
+
+def chip_share(layer_weights, extra):
+    qkv, out, up, down = layer_weights
+    core, _, _ = place()
+
+    def halves(half):
+        narrow = jnp.concatenate(
+            [qkv[:, half * 1152 : half * 1152 + 1152], out[:, half * 384 : half * 384 + 384], up[:, half * 1536 : half * 1536 + 1536]],
+            axis=1,
+        )
+        low = down[:, half * HALF : half * HALF + HALF]
+        wide = [low[:SLAB], low[SLAB:]]
+        if extra is not None:
+            wide.append(extra[:, half * HALF : half * HALF + HALF])
+        wide = jnp.concatenate(wide, axis=1)
+        return jnp.concatenate([narrow, wide[:24], wide[24:]], axis=1)
+
+    left, right = halves(0), halves(1)
+    kept = jnp.where(core == 0, left, right)
+    came = swap(jnp.where(core == 0, right, left), CORE)
+    lower = jnp.where(core == 0, kept, came)
+    upper = jnp.where(core == 0, came, kept)
+    wide = (lower.shape[1] - 3072) // 2
+
+    def wide_of(part):
+        return jnp.concatenate([part[:, 3072 : 3072 + wide], part[:, 3072 + wide :]], axis=0)
+
+    low_wide, high_wide = wide_of(lower), wide_of(upper)
+    columns = [jnp.concatenate([lower[:, :3072], upper[:, :3072]], axis=0), low_wide[:, :768], high_wide[:, :768]]
+    if extra is not None:
+        columns += [low_wide[:, 768:], high_wide[:, 768:]]
+    return jnp.concatenate(columns, axis=1)
+
+
+def fetch_layer(layer_weights, extra):
+    share = chip_share(layer_weights, extra)
+    mine = gather_parts(share)
+    other = [swap(part, CORE) for part in mine]
+    return assemble(mine, other, extra is not None)
+
+
+def reduce_chunk(kept, sent):
+    _, chip, level = place()
+    came = swap(sent, CORE)
+    columns = kept.shape[1]
+    both = [v.reshape(4, 4, SLAB, columns) for v in (kept, came)]
+    parts = []
+    for distance in range(4):
+        planes = [lax.dynamic_index_in_dim(v, level ^ distance, 0, keepdims=False) for v in both]
+        part = []
+        for step in range(4):
+            pair = [lax.dynamic_index_in_dim(v, (chip % 4) ^ step, 0, keepdims=False) for v in planes]
+            part.append((pair[0].astype(F32) + pair[1].astype(F32)).astype(BF))
+        parts.append(part)
+    return reduce_parts(parts)
+
+
+def split_small(row, layer_count_width):
+    pieces = []
+    start = 0
+    for size in SMALL_SIZES:
+        pieces.append(row[:, start : start + size].reshape(-1))
+        start += size
+    return pieces
+
+
+def tuned(
+    embedded,
+    doc_ids,
+    step_ids,
+    step_table,
+    qkv_weight,
+    qv_bias,
+    out_weight,
+    out_bias,
+    first_gain,
+    first_shift,
+    up_weight,
+    up_bias,
+    down_weight,
+    down_bias,
+    second_gain,
+    second_shift,
+    cotangent,
+):
+    core, chip, level = place()
+    docs_row = doc_ids[0]
+    same_doc = docs_row[:, None] == docs_row[None, :]
+    doc_count = step_ids.shape[1]
+    doc_hot = (docs_row[:, None] == jnp.arange(doc_count, dtype=jnp.int32)[None, :]).astype(jnp.float32)
+    smalls = (qv_bias, out_bias, first_gain, first_shift, up_bias, down_bias, second_gain, second_shift)
+    small_rows = [jnp.pad(jnp.concatenate([v[layer] for v in smalls]), (0, HALF - 288)) for layer in range(2)]
+    extra = jnp.concatenate(
+        [step_table, jnp.concatenate(small_rows)[None], jnp.zeros((SLAB - 33, 768), BF)], axis=0
+    )
+    lower_w = fetch_layer((qkv_weight[0], out_weight[0], up_weight[0], down_weight[0]), extra)
+    upper_w = fetch_layer((qkv_weight[1], out_weight[1], up_weight[1], down_weight[1]), None)
+    extra_all = lower_w[4].reshape(16, SLAB, 2, 2, HALF)
+    table_whole = extra_all[:, :32].transpose(0, 3, 1, 2, 4).reshape(1024, 768)
+    small_all = extra_all[:, 32].transpose(1, 0, 2, 3).reshape(2, TUNED, HALF)
+
+    def with_smalls(layer, weights):
+        qv_b, out_b, gain_a, shift_a, up_b, down_b, gain_b, shift_b = split_small(small_all[layer], HALF)
+        qkv_w, out_w, up_w, down_w = weights[:4]
+        return (qkv_w, qv_b, out_w, out_b, gain_a, shift_a, up_w, up_b, down_w, down_b, gain_b, shift_b)
+
+    params_lower = with_smalls(0, lower_w)
+    params_upper = with_smalls(1, upper_w)
+    step_hot = step_ids[0][:, None] == jnp.arange(table_whole.shape[0], dtype=jnp.int32)[None, :]
+    doc_rows = jnp.dot(step_hot.astype(BF), table_whole, preferred_element_type=F32)
+    start = embedded.astype(F32) + jnp.dot(doc_hot, doc_rows, precision=lax.Precision.HIGHEST)
+    middle_hidden, lower_saved = layer_apply(start, params_lower, same_doc)
+    final_hidden, upper_saved = layer_apply(middle_hidden, params_upper, same_doc)
+    block_output = final_hidden.astype(BF)
+    grad_upper_in, upper_grads, upper_small = layer_back(
+        params_upper, upper_saved, cotangent.astype(F32), core
+    )
+    upper_mlp = reduce_chunk(*upper_grads[0])
+    upper_attn = reduce_chunk(*upper_grads[1])
+    input_grad, lower_grads, lower_small = layer_back(params_lower, lower_saved, grad_upper_in, core)
+    lower_mlp = reduce_chunk(*lower_grads[0])
+    doc_grads = jnp.einsum("ts,td->sd", doc_hot, input_grad, precision=lax.Precision.HIGHEST)
+    table_full = jnp.einsum("sn,sd->nd", step_hot.astype(F32), doc_grads, precision=lax.Precision.HIGHEST)
+    table_full = table_full.astype(BF).reshape(16, 2, 32, 2, HALF).transpose(3, 0, 2, 1, 4).reshape(2, 16, 32, 768)
+
+    def small_columns(pieces):
+        rows = [p.reshape(TUNED, size) for p, size in zip(pieces, SMALL_SIZES)]
+        row = jnp.pad(jnp.concatenate(rows, axis=1), ((0, 0), (0, HALF - 288)))
+        return row.astype(BF).reshape(16, 1, 768)
+
+    small_full = jnp.stack([small_columns(lower_small), small_columns(upper_small)])
+    extra_grad = jnp.concatenate([table_full, small_full, jnp.zeros((2, 16, SLAB - 33, 768), BF)], axis=2)
+    extra_grad = extra_grad.reshape(2, 768, 768)
+    extra_kept = lax.dynamic_index_in_dim(extra_grad, core, 0, keepdims=False)
+    extra_sent = lax.dynamic_index_in_dim(extra_grad, 1 - core, 0, keepdims=False)
+    lower_attn = reduce_chunk(
+        jnp.concatenate([lower_grads[1][0], extra_kept], axis=1),
+        jnp.concatenate([lower_grads[1][1], extra_sent], axis=1),
+    )
+
+    def finish(attn, mlp):
+        pieces = [attn[:, :1152], attn[:, 1152:1536], mlp[:, :1536]]
+        return jnp.concatenate(pieces, axis=1), mlp[:, 1536:]
+
+    def exchange(narrow, wide):
+        mine_n = lax.dynamic_slice_in_dim(narrow, core * 24, 24, 0)
+        theirs_n = lax.dynamic_slice_in_dim(narrow, (1 - core) * 24, 24, 0)
+        m = wide.shape[1] // 2
+        mine_w = lax.dynamic_slice_in_dim(wide, core * m, m, 1)
+        theirs_w = lax.dynamic_slice_in_dim(wide, (1 - core) * m, m, 1)
+        send = jnp.concatenate([theirs_n, theirs_w[:24], theirs_w[24:]], axis=1).astype(BF)
+        came = swap(send, CORE).astype(F32)
+        n = narrow.shape[1]
+        came_n = came[:, :n]
+        came_w = jnp.concatenate([came[:, n : n + m], came[:, n + m :]], axis=0)
+
+        def ordered(mine, other):
+            return jnp.where(core == 0, mine, other), jnp.where(core == 0, other, mine)
+
+        return ordered(mine_n, came_n), ordered(mine_w, came_w)
+
+    def natural(attn, mlp, extra_part):
+        narrow, wide = finish(attn, mlp)
+        if extra_part is not None:
+            wide = jnp.concatenate([wide[:, :768], extra_part[:, :HALF], wide[:, 768:], extra_part[:, HALF:]], axis=1)
+        (left, right), (wide_left, wide_right) = exchange(narrow, wide)
+        qkv = jnp.concatenate([left[:, :1152], right[:, :1152]], axis=1)
+        out = jnp.concatenate([left[:, 1152:1536], right[:, 1152:1536]], axis=1)
+        up = jnp.concatenate([left[:, 1536:], right[:, 1536:]], axis=1)
+        down = jnp.concatenate(
+            [
+                jnp.concatenate([w[:, :HALF], w[:, HALF:768]], axis=0) for w in (wide_left, wide_right)
+            ],
+            axis=1,
+        )
+        if extra_part is None:
+            return qkv, out, up, down
+        return qkv, out, up, down, wide_left[:, 768:], wide_right[:, 768:]
+
+    upper_out = natural(upper_attn, upper_mlp, None)
+    lower_out = natural(lower_attn[:, :1536], lower_mlp, lower_attn[:, 1536:])
+    extra_left, extra_right = lower_out[4:]
+    table_shard = jnp.concatenate([extra_left[:32], extra_right[:32]], axis=1)
+    small_out = jnp.stack([extra_left[32], extra_right[32]])
+    pieces = []
+    begin = 0
+    for size in SMALL_SIZES:
+        pieces.append(small_out[:, begin : begin + size])
+        begin += size
+    qv_g, out_b_g, gain_a_g, shift_a_g, up_b_g, down_b_g, gain_b_g, shift_b_g = pieces
+    qkv_g, out_g, up_g, down_g = [jnp.stack([a, b]) for a, b in zip(lower_out[:4], upper_out)]
+    return (
+        block_output,
+        input_grad,
+        table_shard,
+        qkv_g,
+        qv_g,
+        out_g,
+        out_b_g,
+        gain_a_g,
+        shift_a_g,
+        up_g,
+        up_b_g,
+        down_g,
+        down_b_g,
+        gain_b_g,
+        shift_b_g,
+    )
+
+
 def solution(mesh):
+    local = tuned if mesh.shape["dp"] == TUNED else plain
     in_specs = (
         P("dp", None),
         P("dp", None),

time: 1700 us -> 639 us (0.38)
  waiting for transfers between devices: 1290 us -> 178 us
  local copies, waits for them, and re-layouts: 20.5 us -> 102 us
  starting transfers between devices: 114 us -> 190 us
  other arithmetic: 107 us -> 54.5 us
  blocking collectives: 43.2 us -> 0 us
  Pallas kernels: 0 us -> 19.6 us
  matrix products: 102 us -> 83.7 us
    ppermute x125 -> x142, waiting for transfers between devices: 830 us -> 178 us  [the longest x118 125 us: swap(): return lax.ppermute(value, 'dp', [(i, i ^ stride) for i in range(TUNED)])]
    all_gather x9 -> x0, waiting for transfers between devices: 458 us -> none  [the longest x1 63.8 us: local(): lax.all_gather(up_weight[0], 'dp', axis=0, tiled=True)]
    ppermute x125 -> x142, starting transfers between devices: 113 us -> 190 us  [the longest x118 147 us: swap(): return lax.ppermute(value, 'dp', [(i, i ^ stride) for i in range(TUNED)])]
    unnamed x1 -> x0, blocking collectives: 43.2 us -> none
    add x101 -> x4, other arithmetic: 45.8 us -> 2.77 us  [reduce_parts(): return sum((v.astype(F32) for v in (own, across_third, last)))]
    unnamed x282 -> x223, local copies, waits for them, and re-layouts: 11.6 us -> 42.8 us
    convert_element_type x133 -> x58, other arithmetic: 44.2 us -> 16.6 us  [the longest x48 8.98 us: add(): return sum((v.astype(F32) for v in values)).astype(BF)]
    reshape x0 -> x20, local copies, waits for them, and re-layouts: none -> 21 us  [the longest x3 9.53 us: tuned(): table_full.astype(BF).reshape(16, 2, 32, 2, HALF).transpose(3, 0, 2, 1, 4)]
  transfers between devices with their start and end apart: 134 -> 142, of which waited for: 114 -> 58; matrix products, arithmetic and copies ran while one was open for 9% -> 12% of each run, Pallas kernels for 0% -> 1%
where the time goes in v1:
time: 639 us; the launch traced here: 632 us
  starting transfers between devices  190 us (30%)
  waiting for transfers between devices  178 us (28%)
  local copies, waits for them, and re-layouts  102 us (16%)
  matrix products  83.7 us (13%)
  other arithmetic  54.5 us (9%)
  Pallas kernels  19.6 us (3%)
    ppermute x118, starting transfers between devices, swap(): return lax.ppermute(value, 'dp', [(i, i ^ stride) for i in range(TUNED)])  147 us
    ppermute x118, waiting for transfers between devices, swap(): return lax.ppermute(value, 'dp', [(i, i ^ stride) for i in range(TUNED)])  125 us
    ppermute x24, waiting for transfers between devices, swap_from(): lax.ppermute(value, 'dp', [(i, i ^ stride) for i in range(TUNED) if i //...  53 us
    ppermute x24, starting transfers between devices, swap_from(): lax.ppermute(value, 'dp', [(i, i ^ stride) for i in range(TUNED) if i //...  43.2 us
    unnamed x223, local copies, waits for them, and re-layouts  42.8 us
    dot_general x16, matrix products, half_sums(): jnp.einsum('td,te->de', rows, lax.dynamic_slice_in_dim(grads, side * coun...  32.8 us
    pallas_call x2, Pallas kernels, assemble(): pl.pallas_call(body, out_shape=[jax.ShapeDtypeStruct(shapes[name], BF) fo...  19.6 us
  transfers between devices with their start and end apart: 142, of which 58 were waited for; matrix products, arithmetic and copies ran while one was open for 12% of the time, Pallas kernels for 1%

profile of v1, /device:TPU:0, one launch (start us, length us, event | category | flops | bytes accessed | tf_op | source)
XLA Modules:
  0.0 632.1 jit_solution(11977857558320999977)
XLA Ops:
  6.6 3.0 collective-permute-start.28
  12.4 8.2 %collective-permute-done.28 = bf16[48,4608]{1,0:T(8,128)(2,1)S(1)} collective-permute-done((bf16[48,4608]{1,0:T(8,128)(2,1)S(1)}, bf16[48,4608]{1,0:T(8,128)(2,1)S(1)}, u32[]{:S(2)}, u32[]{:S(2)}) %collective-permute-start.28) | collective-permute-done | bytes 442400 | tf_op jit(solution)/shard_map/ppermute | solution.py:24
  26.0 5.7 collective-permute-done.2
  34.5 2.8 collective-permute-done.30
  39.5 3.6 collective-permute-start.5
  47.9 6.4 %collective-permute-done.5 = bf16[48,5376]{1,0:T(8,128)(2,1)S(1)} collective-permute-done((bf16[48,5376]{1,0:T(8,128)(2,1)S(1)}, bf16[48,5376]{1,0:T(8,128)(2,1)S(1)}, u32[]{:S(2)}, u32[]{:S(2)}) %collective-permute-start.5) | collective-permute-done | bytes 516128 | tf_op jit(solution)/shard_map/ppermute | solution.py:24
  56.4 5.3 collective-permute-done.38
  64.4 14.7 %collective-permute-done.12 = bf16[48,5376]{1,0:T(8,128)(2,1)S(1)} collective-permute-done((bf16[48,5376]{1,0:T(8,128)(2,1)S(1)}, bf16[48,5376]{1,0:T(8,128)(2,1)S(1)}, u32[]{:S(2)}, u32[]{:S(2)}) %collective-permute-start.12) | collective-permute-done | bytes 516128 | tf_op jit(solution)/shard_map/ppermute | solution.py:28
  83.5 4.1 collective-permute-done.35
  90.6 7.3 %collective-permute-done.43 = bf16[48,4608]{1,0:T(8,128)(2,1)S(1)} collective-permute-done((bf16[48,4608]{1,0:T(8,128)(2,1)S(1)}, bf16[48,4608]{1,0:T(8,128)(2,1)S(1)}, u32[]{:S(2)}, u32[]{:S(2)}) %collective-permute-start.43) | collective-permute-done | bytes 442400 | tf_op jit(solution)/shard_map/ppermute | solution.py:28
  107.0 9.4 %collective-permute-done.42 = bf16[48,2304]{1,0:T(8,128)(2,1)S(1)} collective-permute-done((bf16[48,2304]{1,0:T(8,128)(2,1)S(1)}, bf16[48,2304]{1,0:T(8,128)(2,1)S(1)}, u32[]{:S(2)}, u32[]{:S(2)}) %collective-permute-start.42) | collective-permute-done | bytes 221216 | tf_op jit(solution)/shard_map/ppermute | solution.py:24
  121.0 6.4 %collective-permute-done.17 = bf16[48,5376]{1,0:T(8,128)(2,1)S(1)} collective-permute-done((bf16[48,5376]{1,0:T(8,128)(2,1)S(1)}, bf16[48,5376]{1,0:T(8,128)(2,1)S(1)}, u32[]{:S(2)}, u32[]{:S(2)}) %collective-permute-start.17) | collective-permute-done | bytes 516128 | tf_op jit(solution)/shard_map/ppermute | solution.py:28
  130.9 2.7 collective-permute-start.18
  133.6 2.8 collective-permute-done.16
  142.5 2.7 collective-permute-done.19
  148.9 5.3 collective-permute-done.21
  162.3 7.2 %collective-permute-done.51.refs_7_ = bf16[4,48,4608]{2,1,0:T(8,128)(2,1)} collective-permute-done((bf16[4,48,4608]{2,1,0:T(8,128)(2,1)}, bf16[4,48,4608]{2,1,0:T(8,128)(2,1)}, u32[]{:S(2)}, u32[]{:S(2)}) %collective-permute-start.51) | collective-permute-done | bytes 1769504 | tf_op jit(solution)/shard_map/ppermute | solution.py:24
  178.4 8.1 %shard_map.281 = (bf16[768,2304]{1,0:T(8,128)(2,1)S(1)}, bf16[768,768]{1,0:T(8,128)(2,1)S(1)}, bf16[768,3072]{1,0:T(8,128)(2,1)S(1)}, bf16[3072,768]{1,0:T(8,128)(2,1)S(1)}) custom-call(bf16[4,48,4608]{2,1,0:T(8,128)(2,1)S(1)} %copy-done.1, bf16[4,48,4608]{2,1,0:T(8,128)(2,1)S(1)} %copy-done.3, bf16[4,48,4608]{2,1,0:T(8,128)(2,1)S(1)} %copy-done.5, ...), custom_call_target="tpu_custom_call" | custom-call | bytes 29360128 | tf_op jit(solution)/shard_map/pallas_call | solution.py:569
  193.8 11.5 %shard_map.280 = (bf16[768,2304]{1,0:T(8,128)(2,1)S(1)}, bf16[768,768]{1,0:T(8,128)(2,1)S(1)}, bf16[768,3072]{1,0:T(8,128)(2,1)S(1)}, bf16[3072,768]{1,0:T(8,128)(2,1)}, bf16[768,1536]{1,0:T(8,128)(2,1)S(1)}) custom-call(bf16[4,48,5376]{2,1,0:T(8,128)(2,1)S(1)} %pad_maximum_fusion.6.refs_0_, bf16[4,48,5376]{2,1,0:T(8,128)(2,1)} %pad_maximum_fusion.7.refs_1_, ...), custom_call_target="tpu_custom_call" | custom-call | bytes 29360128 | tf_op jit(solution)/shard_map/pallas_call | solution.py:569
  210.6 6.3 reshape.1027
  228.2 2.8 fusion.290
  231.0 2.6 convolution_convert_fusion.22
  247.0 4.2 fusion.293
  251.1 2.6 convolution_convert_fusion.21
  256.7 3.1 fusion.295
  265.2 2.9 convolution_convert_fusion.1
  269.2 2.8 convolution_convert_fusion
  274.0 2.8 convolution_convert_fusion.19
  284.3 3.5 fusion.242
  294.5 2.9 convolution_convert_fusion.3
  297.4 2.9 convolution_convert_fusion.2
  305.2 2.6 convolution_convert_fusion.17
  318.4 2.8 copy.89
  324.2 3.3 convolution_convert_fusion.7
  338.4 4.3 copy.106
  342.6 3.9 reshape.1048
  355.6 3.0 pad_maximum_fusion.1
  359.7 2.7 pad_maximum_fusion
  365.6 2.7 fusion.30
  392.6 3.5 collective-permute-start.110
  400.0 4.5 collective-permute-start.116
  404.5 2.6 collective-permute-done.116
  411.4 7.0 %collective-permute-start.118 = (bf16[48,1536]{1,0:T(8,128)(2,1)S(1)}, bf16[48,1536]{1,0:T(8,128)(2,1)S(1)}, u32[]{:S(2)}, u32[]{:S(2)}) collective-permute-start(bf16[48,1536]{1,0:T(8,128)(2,1)S(1)} %add_convert_fusion.69), channel_id=1, source_target_pairs={{0,8},{1,9},{2,10},{3,11},{4,12},{5,13},{6,14},{7,15},{8,0},{9,1},... | collective-permute-start | bytes 442376 | tf_op jit(solution)/shard_map/ppermute | solution.py:24
  423.4 5.0 concatenate.411
  428.4 4.3 copy.80
  432.7 5.0 concatenate.361
  439.3 3.2 fusion.154
  446.0 2.6 collective-permute-done.89
  451.7 2.7 collective-permute-done.85
  462.5 5.8 collective-permute-done.86
  477.2 4.4 collective-permute-start.93
  481.7 3.4 collective-permute-done.93
  490.0 10.5 %collective-permute-start.95 = (bf16[48,2304]{1,0:T(8,128)(2,1)S(1)}, bf16[48,2304]{1,0:T(8,128)(2,1)S(1)}, u32[]{:S(2)}, u32[]{:S(2)}) collective-permute-start(bf16[48,2304]{1,0:T(8,128)(2,1)S(1)} %add_convert_fusion.42), channel_id=1, source_target_pairs={{0,8},{1,9},{2,10},{3,11},{4,12},{5,13},{6,14},{7,15},{8,0},{9,1},... | collective-permute-start | bytes 663560 | tf_op jit(solution)/shard_map/ppermute | solution.py:24
  535.8 13.3 %collective-permute-done.64 = bf16[48,3072]{1,0:T(8,128)(2,1)S(1)} collective-permute-done((bf16[48,3072]{1,0:T(8,128)(2,1)S(1)}, bf16[48,3072]{1,0:T(8,128)(2,1)S(1)}, u32[]{:S(2)}, u32[]{:S(2)}) %collective-permute-start.64) | collective-permute-done | bytes 294944 | tf_op jit(solution)/shard_map/ppermute | solution.py:24
  551.2 7.8 %collective-permute-done.131 = bf16[48,3072]{1,0:T(8,128)(2,1)S(1)} collective-permute-done((bf16[48,3072]{1,0:T(8,128)(2,1)S(1)}, bf16[48,3072]{1,0:T(8,128)(2,1)S(1)}, u32[]{:S(2)}, u32[]{:S(2)}) %collective-permute-start.131) | collective-permute-done | bytes 294944 | tf_op jit(solution)/shard_map/ppermute | solution.py:24
  564.3 2.7 collective-permute-done.65
  567.1 4.4 collective-permute-start.132
  575.7 4.4 collective-permute-start.71
  580.3 4.0 collective-permute-done.71
  584.3 4.4 collective-permute-start.138
  588.7 4.1 collective-permute-done.138
  596.4 4.0 collective-permute-done.137
  603.8 10.5 %collective-permute-start.73 = (bf16[48,3072]{1,0:T(8,128)(2,1)S(1)}, bf16[48,3072]{1,0:T(8,128)(2,1)S(1)}, u32[]{:S(2)}, u32[]{:S(2)}) collective-permute-start(bf16[48,3072]{1,0:T(8,128)(2,1)S(1)} %add_convert_fusion.23), channel_id=1, source_target_pairs={{0,8},{1,9},{2,10},{3,11},{4,12},{5,13},{6,14},{7,15},{8,0},{9,1},... | collective-permute-start | bytes 884744 | tf_op jit(solution)/shard_map/ppermute | solution.py:24
  616.0 2.8 collective-permute-start.140
  (896 shorter events, 318.9 us)
Async XLA Ops:
  6.6 14.0 %collective-permute-start.28 = (bf16[48,4608]{1,0:T(8,128)(2,1)S(1)}, bf16[48,4608]{1,0:T(8,128)(2,1)S(1)}, u32[]{:S(2)}, u32[]{:S(2)}) collective-permute-start(bf16[48,4608]{1,0:T(8,128)(2,1)S(1)} %maximum_maximum_fusion.1), channel_id=1, source_target_pairs={{0,4},{1,5},{2,6},{3,7},{4,0},{5,1},{6,2},{7,3},{8,12},{9,13},{10,... | collective-permute-start | bytes 1327112 | tf_op jit(solution)/shard_map/ppermute | solution.py:24
  9.6 13.1 %collective-permute-start.27 = (bf16[48,4608]{1,0:T(8,128)(2,1)S(1)}, bf16[48,4608]{1,0:T(8,128)(2,1)S(1)}, u32[]{:S(2)}, u32[]{:S(2)}) collective-permute-start(bf16[48,4608]{1,0:T(8,128)(2,1)S(1)} %maximum_maximum_fusion.1), channel_id=1, source_target_pairs={{0,2},{1,3},{2,0},{3,1},{4,6},{5,7},{6,4},{7,5},{8,10},{9,11},{10,... | collective-permute-start | bytes 1327112 | tf_op jit(solution)/shard_map/ppermute | solution.py:24
  11.3 20.3 %collective-permute-start.2 = (bf16[48,5376]{1,0:T(8,128)(2,1)S(1)}, bf16[48,5376]{1,0:T(8,128)(2,1)S(1)}, u32[]{:S(2)}, u32[]{:S(2)}) collective-permute-start(bf16[48,5376]{1,0:T(8,128)(2,1)S(1)} %constant_dynamic-update-slice_fusion.2), channel_id=1, source_target_pairs={{0,4},{1,5},{2,6},{3,7},{4,0},{5,1},{6,2},{7,3},{8,12},{9,13},{10,... | collective-permute-start | bytes 1548296 | tf_op jit(solution)/shard_map/ppermute | solution.py:24
  11.9 21.8 %collective-permute-start.1 = (bf16[48,5376]{1,0:T(8,128)(2,1)S(1)}, bf16[48,5376]{1,0:T(8,128)(2,1)S(1)}, u32[]{:S(2)}, u32[]{:S(2)}) collective-permute-start(bf16[48,5376]{1,0:T(8,128)(2,1)S(1)} %constant_dynamic-update-slice_fusion.2), channel_id=1, source_target_pairs={{0,2},{1,3},{2,0},{3,1},{4,6},{5,7},{6,4},{7,5},{8,10},{9,11},{10,... | collective-permute-start | bytes 1548296 | tf_op jit(solution)/shard_map/ppermute | solution.py:24
  20.6 16.7 %collective-permute-start.30 = (bf16[48,2304]{1,0:T(8,128)(2,1)S(1)}, bf16[48,2304]{1,0:T(8,128)(2,1)S(1)}, u32[]{:S(2)}, u32[]{:S(2)}) collective-permute-start(bf16[48,2304]{1,0:T(8,128)(2,1)S(1)} %slice.1224), channel_id=1, source_target_pairs={{0,2},{1,3},{2,0},{3,1},{4,6},{5,7},{6,4},{7,5},{8,10},{9,11},{10,... | collective-permute-start | bytes 663560 | tf_op jit(solution)/shard_map/ppermute | solution.py:24
  22.7 16.0 %collective-permute-start.29 = (bf16[48,2304]{1,0:T(8,128)(2,1)S(1)}, bf16[48,2304]{1,0:T(8,128)(2,1)S(1)}, u32[]{:S(2)}, u32[]{:S(2)}) collective-permute-start(bf16[48,2304]{1,0:T(8,128)(2,1)S(1)} %slice.1223), channel_id=1, source_target_pairs={{0,4},{1,5},{2,6},{3,7},{4,0},{5,1},{6,2},{7,3},{8,12},{9,13},{10,... | collective-permute-start | bytes 663560 | tf_op jit(solution)/shard_map/ppermute | solution.py:24
  24.3 15.2 %collective-permute-start.31 = (bf16[48,4608]{1,0:T(8,128)(2,1)S(1)}, bf16[48,4608]{1,0:T(8,128)(2,1)S(1)}, u32[]{:S(2)}, u32[]{:S(2)}) collective-permute-start(bf16[48,4608]{1,0:T(8,128)(2,1)S(1)} %maximum_maximum_fusion.1), channel_id=1, source_target_pairs={{0,8},{1,9},{2,10},{3,11},{4,12},{5,13},{6,14},{7,15},{8,0},{9,1},... | collective-permute-start | bytes 1327112 | tf_op jit(solution)/shard_map/ppermute | solution.py:24
  31.6 11.5 %collective-permute-start.37 = (bf16[48,4608]{1,0:T(8,128)(2,1)S(1)}, bf16[48,4608]{1,0:T(8,128)(2,1)S(1)}, u32[]{:S(2)}, u32[]{:S(2)}) collective-permute-start(bf16[48,4608]{1,0:T(8,128)(2,1)S(1)} %maximum_maximum_fusion.1), channel_id=1, source_target_pairs={{8,16},{9,17},{10,18},{11,19},{12,20},{13,21},{14,22},{15,23},{16,... | collective-permute-start | bytes 1327112 | tf_op jit(solution)/shard_map/ppermute | solution.py:28
  33.7 13.9 %collective-permute-start.11 = (bf16[48,5376]{1,0:T(8,128)(2,1)S(1)}, bf16[48,5376]{1,0:T(8,128)(2,1)S(1)}, u32[]{:S(2)}, u32[]{:S(2)}) collective-permute-start(bf16[48,5376]{1,0:T(8,128)(2,1)S(1)} %constant_dynamic-update-slice_fusion.2), channel_id=1, source_target_pairs={{8,16},{9,17},{10,18},{11,19},{12,20},{13,21},{14,22},{15,23},{16,... | collective-permute-start | bytes 1548296 | tf_op jit(solution)/shard_map/ppermute | solution.py:28
  39.5 14.8 %collective-permute-start.5 = (bf16[48,5376]{1,0:T(8,128)(2,1)S(1)}, bf16[48,5376]{1,0:T(8,128)(2,1)S(1)}, u32[]{:S(2)}, u32[]{:S(2)}) collective-permute-start(bf16[48,5376]{1,0:T(8,128)(2,1)S(1)} %constant_dynamic-update-slice_fusion.2), channel_id=1, source_target_pairs={{0,8},{1,9},{2,10},{3,11},{4,12},{5,13},{6,14},{7,15},{8,0},{9,1},... | collective-permute-start | bytes 1548296 | tf_op jit(solution)/shard_map/ppermute | solution.py:24
  43.1 11.9 %collective-permute-start.36 = (bf16[48,4608]{1,0:T(8,128)(2,1)S(1)}, bf16[48,4608]{1,0:T(8,128)(2,1)S(1)}, u32[]{:S(2)}, u32[]{:S(2)}) collective-permute-start(bf16[48,4608]{1,0:T(8,128)(2,1)S(1)} %collective-permute-done.31), channel_id=1, source_target_pairs={{8,16},{9,17},{10,18},{11,19},{12,20},{13,21},{14,22},{15,23},{16,... | collective-permute-start | bytes 1327112 | tf_op jit(solution)/shard_map/ppermute | solution.py:28
  44.3 18.8 %collective-permute-start.33 = (bf16[48,4608]{1,0:T(8,128)(2,1)S(1)}, bf16[48,4608]{1,0:T(8,128)(2,1)S(1)}, u32[]{:S(2)}, u32[]{:S(2)}) collective-permute-start(bf16[48,4608]{1,0:T(8,128)(2,1)S(1)} %collective-permute-done.31), channel_id=1, source_target_pairs={{0,4},{1,5},{2,6},{3,7},{4,0},{5,1},{6,2},{7,3},{8,12},{9,13},{10,... | collective-permute-start | bytes 1327112 | tf_op jit(solution)/shard_map/ppermute | solution.py:24
  46.1 15.6 %collective-permute-start.38 = (bf16[48,4608]{1,0:T(8,128)(2,1)S(1)}, bf16[48,4608]{1,0:T(8,128)(2,1)S(1)}, u32[]{:S(2)}, u32[]{:S(2)}) collective-permute-start(bf16[48,4608]{1,0:T(8,128)(2,1)S(1)} %collective-permute-done.37), channel_id=1, source_target_pairs={{8,0},{9,1},{10,2},{11,3},{12,4},{13,5},{14,6},{15,7},{16,24},{17,... | collective-permute-start | bytes 1327112 | tf_op jit(solution)/shard_map/ppermute | solution.py:28
  47.7 16.6 %collective-permute-start.32 = (bf16[48,4608]{1,0:T(8,128)(2,1)S(1)}, bf16[48,4608]{1,0:T(8,128)(2,1)S(1)}, u32[]{:S(2)}, u32[]{:S(2)}) collective-permute-start(bf16[48,4608]{1,0:T(8,128)(2,1)S(1)} %collective-permute-done.31), channel_id=1, source_target_pairs={{0,2},{1,3},{2,0},{3,1},{4,6},{5,7},{6,4},{7,5},{8,10},{9,11},{10,... | collective-permute-start | bytes 1327112 | tf_op jit(solution)/shard_map/ppermute | solution.py:24
  54.3 26.3 %collective-permute-start.10 = (bf16[48,5376]{1,0:T(8,128)(2,1)S(1)}, bf16[48,5376]{1,0:T(8,128)(2,1)S(1)}, u32[]{:S(2)}, u32[]{:S(2)}) collective-permute-start(bf16[48,5376]{1,0:T(8,128)(2,1)S(1)} %collective-permute-done.5), channel_id=1, source_target_pairs={{8,16},{9,17},{10,18},{11,19},{12,20},{13,21},{14,22},{15,23},{16,... | collective-permute-start | bytes 1548296 | tf_op jit(solution)/shard_map/ppermute | solution.py:28
  55.0 26.2 %collective-permute-start.7 = (bf16[48,5376]{1,0:T(8,128)(2,1)S(1)}, bf16[48,5376]{1,0:T(8,128)(2,1)S(1)}, u32[]{:S(2)}, u32[]{:S(2)}) collective-permute-start(bf16[48,5376]{1,0:T(8,128)(2,1)S(1)} %collective-permute-done.5), channel_id=1, source_target_pairs={{0,4},{1,5},{2,6},{3,7},{4,0},{5,1},{6,2},{7,3},{8,12},{9,13},{10,... | collective-permute-start | bytes 1548296 | tf_op jit(solution)/shard_map/ppermute | solution.py:24
  61.7 17.5 %collective-permute-start.12 = (bf16[48,5376]{1,0:T(8,128)(2,1)S(1)}, bf16[48,5376]{1,0:T(8,128)(2,1)S(1)}, u32[]{:S(2)}, u32[]{:S(2)}) collective-permute-start(bf16[48,5376]{1,0:T(8,128)(2,1)S(1)} %collective-permute-done.11), channel_id=1, source_target_pairs={{8,0},{9,1},{10,2},{11,3},{12,4},{13,5},{14,6},{15,7},{16,24},{17,... | collective-permute-start | bytes 1548296 | tf_op jit(solution)/shard_map/ppermute | solution.py:28
  63.1 19.8 %collective-permute-start.6 = (bf16[48,5376]{1,0:T(8,128)(2,1)S(1)}, bf16[48,5376]{1,0:T(8,128)(2,1)S(1)}, u32[]{:S(2)}, u32[]{:S(2)}) collective-permute-start(bf16[48,5376]{1,0:T(8,128)(2,1)S(1)} %collective-permute-done.5), channel_id=1, source_target_pairs={{0,2},{1,3},{2,0},{3,1},{4,6},{5,7},{6,4},{7,5},{8,10},{9,11},{10,... | collective-permute-start | bytes 1548296 | tf_op jit(solution)/shard_map/ppermute | solution.py:24
  64.3 92.9 %collective-permute-start.48 = (bf16[4,48,4608]{2,1,0:T(8,128)(2,1)S(1)}, bf16[4,48,4608]{2,1,0:T(8,128)(2,1)S(1)}, u32[]{:S(2)}, u32[]{:S(2)}) collective-permute-start(bf16[4,48,4608]{2,1,0:T(8,128)(2,1)S(1)} %pad_maximum_fusion.10.refs_0_), channel_id=1, source_target_pairs={{0,1},{1,0},{2,3},{3,2},{4,5},{5,4},{6,7},{7,6},{8,9},{9,8},{10,11... | collective-permute-start | bytes 5308424 | tf_op jit(solution)/shard_map/ppermute | solution.py:24
  81.2 17.3 %collective-permute-start.40 = (bf16[48,4608]{1,0:T(8,128)(2,1)S(1)}, bf16[48,4608]{1,0:T(8,128)(2,1)S(1)}, u32[]{:S(2)}, u32[]{:S(2)}) collective-permute-start(bf16[48,4608]{1,0:T(8,128)(2,1)S(1)} %broadcast_select_fusion.3), channel_id=1, source_target_pairs={{0,4},{1,5},{2,6},{3,7},{4,0},{5,1},{6,2},{7,3},{8,12},{9,13},{10,... | collective-permute-start | bytes 1327112 | tf_op jit(solution)/shard_map/ppermute | solution.py:24
  82.8 17.3 %collective-permute-start.39 = (bf16[48,4608]{1,0:T(8,128)(2,1)S(1)}, bf16[48,4608]{1,0:T(8,128)(2,1)S(1)}, u32[]{:S(2)}, u32[]{:S(2)}) collective-permute-start(bf16[48,4608]{1,0:T(8,128)(2,1)S(1)} %broadcast_select_fusion.3), channel_id=1, source_target_pairs={{0,2},{1,3},{2,0},{3,1},{4,6},{5,7},{6,4},{7,5},{8,10},{9,11},{10,... | collective-permute-start | bytes 1327112 | tf_op jit(solution)/shard_map/ppermute | solution.py:24
  88.8 13.8 %collective-permute-start.9 = (bf16[48,2688]{1,0:T(8,128)(2,1)S(1)}, bf16[48,2688]{1,0:T(8,128)(2,1)S(1)}, u32[]{:S(2)}, u32[]{:S(2)}) collective-permute-start(bf16[48,2688]{1,0:T(8,128)(2,1)S(1)} %slice.1179), channel_id=1, source_target_pairs={{0,2},{1,3},{2,0},{3,1},{4,6},{5,7},{6,4},{7,5},{8,10},{9,11},{10,... | collective-permute-start | bytes 774152 | tf_op jit(solution)/shard_map/ppermute | solution.py:24
  98.5 19.9 %collective-permute-start.14 = (bf16[48,5376]{1,0:T(8,128)(2,1)S(1)}, bf16[48,5376]{1,0:T(8,128)(2,1)S(1)}, u32[]{:S(2)}, u32[]{:S(2)}) collective-permute-start(bf16[48,5376]{1,0:T(8,128)(2,1)S(1)} %broadcast_select_fusion.1), channel_id=1, source_target_pairs={{0,4},{1,5},{2,6},{3,7},{4,0},{5,1},{6,2},{7,3},{8,12},{9,13},{10,... | collective-permute-start | bytes 1548296 | tf_op jit(solution)/shard_map/ppermute | solution.py:24
  100.1 20.8 %collective-permute-start.13 = (bf16[48,5376]{1,0:T(8,128)(2,1)S(1)}, bf16[48,5376]{1,0:T(8,128)(2,1)S(1)}, u32[]{:S(2)}, u32[]{:S(2)}) collective-permute-start(bf16[48,5376]{1,0:T(8,128)(2,1)S(1)} %broadcast_select_fusion.1), channel_id=1, source_target_pairs={{0,2},{1,3},{2,0},{3,1},{4,6},{5,7},{6,4},{7,5},{8,10},{9,11},{10,... | collective-permute-start | bytes 1548296 | tf_op jit(solution)/shard_map/ppermute | solution.py:24
  102.7 13.8 %collective-permute-start.42 = (bf16[48,2304]{1,0:T(8,128)(2,1)S(1)}, bf16[48,2304]{1,0:T(8,128)(2,1)S(1)}, u32[]{:S(2)}, u32[]{:S(2)}) collective-permute-start(bf16[48,2304]{1,0:T(8,128)(2,1)S(1)} %slice.1228), channel_id=1, source_target_pairs={{0,2},{1,3},{2,0},{3,1},{4,6},{5,7},{6,4},{7,5},{8,10},{9,11},{10,... | collective-permute-start | bytes 663560 | tf_op jit(solution)/shard_map/ppermute | solution.py:24
  104.9 13.0 %collective-permute-start.41 = (bf16[48,2304]{1,0:T(8,128)(2,1)S(1)}, bf16[48,2304]{1,0:T(8,128)(2,1)S(1)}, u32[]{:S(2)}, u32[]{:S(2)}) collective-permute-start(bf16[48,2304]{1,0:T(8,128)(2,1)S(1)} %slice.1227), channel_id=1, source_target_pairs={{0,4},{1,5},{2,6},{3,7},{4,0},{5,1},{6,2},{7,3},{8,12},{9,13},{10,... | collective-permute-start | bytes 663560 | tf_op jit(solution)/shard_map/ppermute | solution.py:24
  117.9 11.8 %collective-permute-start.45 = (bf16[48,4608]{1,0:T(8,128)(2,1)S(1)}, bf16[48,4608]{1,0:T(8,128)(2,1)S(1)}, u32[]{:S(2)}, u32[]{:S(2)}) collective-permute-start(bf16[48,4608]{1,0:T(8,128)(2,1)S(1)} %broadcast_select_fusion.2), channel_id=1, source_target_pairs={{0,4},{1,5},{2,6},{3,7},{4,0},{5,1},{6,2},{7,3},{8,12},{9,13},{10,... | collective-permute-start | bytes 1327112 | tf_op jit(solution)/shard_map/ppermute | solution.py:24
  118.4 12.5 %collective-permute-start.44 = (bf16[48,4608]{1,0:T(8,128)(2,1)S(1)}, bf16[48,4608]{1,0:T(8,128)(2,1)S(1)}, u32[]{:S(2)}, u32[]{:S(2)}) collective-permute-start(bf16[48,4608]{1,0:T(8,128)(2,1)S(1)} %broadcast_select_fusion.2), channel_id=1, source_target_pairs={{0,2},{1,3},{2,0},{3,1},{4,6},{5,7},{6,4},{7,5},{8,10},{9,11},{10,... | collective-permute-start | bytes 1327112 | tf_op jit(solution)/shard_map/ppermute | solution.py:24
  120.9 15.5 %collective-permute-start.16 = (bf16[48,2688]{1,0:T(8,128)(2,1)S(1)}, bf16[48,2688]{1,0:T(8,128)(2,1)S(1)}, u32[]{:S(2)}, u32[]{:S(2)}) collective-permute-start(bf16[48,2688]{1,0:T(8,128)(2,1)S(1)} %slice.1181), channel_id=1, source_target_pairs={{0,2},{1,3},{2,0},{3,1},{4,6},{5,7},{6,4},{7,5},{8,10},{9,11},{10,... | collective-permute-start | bytes 774152 | tf_op jit(solution)/shard_map/ppermute | solution.py:24
  129.8 15.5 %collective-permute-start.19 = (bf16[48,5376]{1,0:T(8,128)(2,1)S(1)}, bf16[48,5376]{1,0:T(8,128)(2,1)S(1)}, u32[]{:S(2)}, u32[]{:S(2)}) collective-permute-start(bf16[48,5376]{1,0:T(8,128)(2,1)S(1)} %broadcast_select_fusion), channel_id=1, source_target_pairs={{0,4},{1,5},{2,6},{3,7},{4,0},{5,1},{6,2},{7,3},{8,12},{9,13},{10,... | collective-permute-start | bytes 1548296 | tf_op jit(solution)/shard_map/ppermute | solution.py:24
  130.9 14.4 %collective-permute-start.18 = (bf16[48,5376]{1,0:T(8,128)(2,1)S(1)}, bf16[48,5376]{1,0:T(8,128)(2,1)S(1)}, u32[]{:S(2)}, u32[]{:S(2)}) collective-permute-start(bf16[48,5376]{1,0:T(8,128)(2,1)S(1)} %broadcast_select_fusion), channel_id=1, source_target_pairs={{0,2},{1,3},{2,0},{3,1},{4,6},{5,7},{6,4},{7,5},{8,10},{9,11},{10,... | collective-permute-start | bytes 1548296 | tf_op jit(solution)/shard_map/ppermute | solution.py:24
  145.3 48.5 %collective-permute-start.22 = (bf16[4,48,5376]{2,1,0:T(8,128)(2,1)S(1)}, bf16[4,48,5376]{2,1,0:T(8,128)(2,1)}, u32[]{:S(2)}, u32[]{:S(2)}) collective-permute-start(bf16[4,48,5376]{2,1,0:T(8,128)(2,1)S(1)} %pad_maximum_fusion.6.refs_0_), channel_id=1, source_target_pairs={{0,1},{1,0},{2,3},{3,2},{4,5},{5,4},{6,7},{7,6},{8,9},{9,8},{10,11... | collective-permute-start | bytes 6193160 | tf_op jit(solution)/shard_map/ppermute | solution.py:24
  145.3 12.4 %collective-permute-start.49 = (bf16[4,48,4608]{2,1,0:T(8,128)(2,1)S(1)}, bf16[4,48,4608]{2,1,0:T(8,128)(2,1)S(1)}, u32[]{:S(2)}, u32[]{:S(2)}) collective-permute-start(bf16[4,48,4608]{2,1,0:T(8,128)(2,1)S(1)} %pad_maximum_fusion.11.refs_1_), channel_id=1, source_target_pairs={{0,1},{1,0},{2,3},{3,2},{4,5},{5,4},{6,7},{7,6},{8,9},{9,8},{10,11... | collective-permute-start | bytes 5308424 | tf_op jit(solution)/shard_map/ppermute | solution.py:24
  154.1 39.6 %collective-permute-start.23 = (bf16[4,48,5376]{2,1,0:T(8,128)(2,1)}, bf16[4,48,5376]{2,1,0:T(8,128)(2,1)}, u32[]{:S(2)}, u32[]{:S(2)}) collective-permute-start(bf16[4,48,5376]{2,1,0:T(8,128)(2,1)} %pad_maximum_fusion.7.refs_1_), channel_id=1, source_target_pairs={{0,1},{1,0},{2,3},{3,2},{4,5},{5,4},{6,7},{7,6},{8,9},{9,8},{10,11... | collective-permute-start | bytes 6193160 | tf_op jit(solution)/shard_map/ppermute | solution.py:24
  157.2 36.5 %collective-permute-start.24 = (bf16[4,48,5376]{2,1,0:T(8,128)(2,1)}, bf16[4,48,5376]{2,1,0:T(8,128)(2,1)}, u32[]{:S(2)}, u32[]{:S(2)}) collective-permute-start(bf16[4,48,5376]{2,1,0:T(8,128)(2,1)} %pad_maximum_fusion.8.refs_2_), channel_id=1, source_target_pairs={{0,1},{1,0},{2,3},{3,2},{4,5},{5,4},{6,7},{7,6},{8,9},{9,8},{10,11... | collective-permute-start | bytes 6193160 | tf_op jit(solution)/shard_map/ppermute | solution.py:24
  157.7 36.0 %collective-permute-start.25 = (bf16[4,48,5376]{2,1,0:T(8,128)(2,1)}, bf16[4,48,5376]{2,1,0:T(8,128)(2,1)}, u32[]{:S(2)}, u32[]{:S(2)}) collective-permute-start(bf16[4,48,5376]{2,1,0:T(8,128)(2,1)} %pad_maximum_fusion.9.refs_3_), channel_id=1, source_target_pairs={{0,1},{1,0},{2,3},{3,2},{4,5},{5,4},{6,7},{7,6},{8,9},{9,8},{10,11... | collective-permute-start | bytes 6193160 | tf_op jit(solution)/shard_map/ppermute | solution.py:24
  332.5 35.8 %collective-permute-start.97 = (bf16[768,1536]{1,0:T(8,128)(2,1)}, bf16[768,1536]{1,0:T(8,128)(2,1)}, u32[]{:S(2)}, u32[]{:S(2)}) collective-permute-start(bf16[768,1536]{1,0:T(8,128)(2,1)} %pad_maximum_fusion.5), channel_id=1, source_target_pairs={{0,1},{1,0},{2,3},{3,2},{4,5},{5,4},{6,7},{7,6},{8,9},{9,8},{10,11... | collective-permute-start | bytes 7077896 | tf_op jit(solution)/shard_map/ppermute | solution.py:24
  351.0 88.3 %collective-permute-start.74 = (bf16[768,2304]{1,0:T(8,128)(2,1)}, bf16[768,2304]{1,0:T(8,128)(2,1)}, u32[]{:S(2)}, u32[]{:S(2)}) collective-permute-start(bf16[768,2304]{1,0:T(8,128)(2,1)} %pad_maximum_fusion.3), channel_id=1, source_target_pairs={{0,1},{1,0},{2,3},{3,2},{4,5},{5,4},{6,7},{7,6},{8,9},{9,8},{10,11... | collective-permute-start | bytes 10616840 | tf_op jit(solution)/shard_map/ppermute | solution.py:24
  377.8 22.2 %collective-permute-start.98 = (bf16[48,768]{1,0:T(8,128)(2,1)S(1)}, bf16[48,768]{1,0:T(8,128)(2,1)S(1)}, u32[]{:S(2)}, u32[]{:S(2)}) collective-permute-start(bf16[48,768]{1,0:T(8,128)(2,1)S(1)} %get-tuple-element.197), channel_id=1, source_target_pairs={{0,4},{1,5},{2,6},{3,7},{4,0},{5,1},{6,2},{7,3},{8,12},{9,13},{10,... | collective-permute-start | bytes 221192 | tf_op jit(solution)/shard_map/ppermute | solution.py:24
  382.1 13.9 %collective-permute-start.105 = (bf16[48,1536]{1,0:T(8,128)(2,1)S(1)}, bf16[48,1536]{1,0:T(8,128)(2,1)S(1)}, u32[]{:S(2)}, u32[]{:S(2)}) collective-permute-start(bf16[48,1536]{1,0:T(8,128)(2,1)S(1)} %pad_maximum_fusion.50), channel_id=1, source_target_pairs={{0,4},{1,5},{2,6},{3,7},{4,0},{5,1},{6,2},{7,3},{8,12},{9,13},{10,... | collective-permute-start | bytes 442376 | tf_op jit(solution)/shard_map/ppermute | solution.py:24
  396.0 41.7 %collective-permute-start.101 = (bf16[48,1536]{1,0:T(8,128)(2,1)S(1)}, bf16[48,1536]{1,0:T(8,128)(2,1)S(1)}, u32[]{:S(2)}, u32[]{:S(2)}) collective-permute-start(bf16[48,1536]{1,0:T(8,128)(2,1)S(1)} %pad_maximum_fusion.48), channel_id=1, source_target_pairs={{0,4},{1,5},{2,6},{3,7},{4,0},{5,1},{6,2},{7,3},{8,12},{9,13},{10,... | collective-permute-start | bytes 442376 | tf_op jit(solution)/shard_map/ppermute | solution.py:24
  407.9 29.8 %collective-permute-start.99 = (bf16[48,1536]{1,0:T(8,128)(2,1)S(1)}, bf16[48,1536]{1,0:T(8,128)(2,1)S(1)}, u32[]{:S(2)}, u32[]{:S(2)}) collective-permute-start(bf16[48,1536]{1,0:T(8,128)(2,1)S(1)} %pad_maximum_fusion.47), channel_id=1, source_target_pairs={{0,2},{1,3},{2,0},{3,1},{4,6},{5,7},{6,4},{7,5},{8,10},{9,11},{10,... | collective-permute-start | bytes 442376 | tf_op jit(solution)/shard_map/ppermute | solution.py:24
  409.7 28.5 %collective-permute-start.111 = (bf16[48,1536]{1,0:T(8,128)(2,1)S(1)}, bf16[48,1536]{1,0:T(8,128)(2,1)S(1)}, u32[]{:S(2)}, u32[]{:S(2)}) collective-permute-start(bf16[48,1536]{1,0:T(8,128)(2,1)S(1)} %get-tuple-element.49), channel_id=1, source_target_pairs={{8,16},{9,17},{10,18},{11,19},{12,20},{13,21},{14,22},{15,23},{16,... | collective-permute-start | bytes 442376 | tf_op jit(solution)/shard_map/ppermute | solution.py:28
  411.4 26.8 %collective-permute-start.118 = (bf16[48,1536]{1,0:T(8,128)(2,1)S(1)}, bf16[48,1536]{1,0:T(8,128)(2,1)S(1)}, u32[]{:S(2)}, u32[]{:S(2)}) collective-permute-start(bf16[48,1536]{1,0:T(8,128)(2,1)S(1)} %add_convert_fusion.69), channel_id=1, source_target_pairs={{0,8},{1,9},{2,10},{3,11},{4,12},{5,13},{6,14},{7,15},{8,0},{9,1},... | collective-permute-start | bytes 442376 | tf_op jit(solution)/shard_map/ppermute | solution.py:24
  437.7 52.3 %collective-permute-start.52 = (bf16[768,3072]{1,0:T(8,128)(2,1)}, bf16[768,3072]{1,0:T(8,128)(2,1)S(1)}, u32[]{:S(2)}, u32[]{:S(2)}) collective-permute-start(bf16[768,3072]{1,0:T(8,128)(2,1)} %pad_maximum_fusion), channel_id=1, source_target_pairs={{0,1},{1,0},{2,3},{3,2},{4,5},{5,4},{6,7},{7,6},{8,9},{9,8},{10,11... | collective-permute-start | bytes 14155784 | tf_op jit(solution)/shard_map/ppermute | solution.py:24
  437.7 63.9 %collective-permute-start.119 = (bf16[768,3072]{1,0:T(8,128)(2,1)}, bf16[768,3072]{1,0:T(8,128)(2,1)S(1)}, u32[]{:S(2)}, u32[]{:S(2)}) collective-permute-start(bf16[768,3072]{1,0:T(8,128)(2,1)} %pad_maximum_fusion.1), channel_id=1, source_target_pairs={{0,1},{1,0},{2,3},{3,2},{4,5},{5,4},{6,7},{7,6},{8,9},{9,8},{10,11... | collective-permute-start | bytes 14155784 | tf_op jit(solution)/shard_map/ppermute | solution.py:24
  456.7 16.0 %collective-permute-start.82 = (bf16[48,2304]{1,0:T(8,128)(2,1)S(1)}, bf16[48,2304]{1,0:T(8,128)(2,1)S(1)}, u32[]{:S(2)}, u32[]{:S(2)}) collective-permute-start(bf16[48,2304]{1,0:T(8,128)(2,1)S(1)} %pad_maximum_fusion.40), channel_id=1, source_target_pairs={{0,4},{1,5},{2,6},{3,7},{4,0},{5,1},{6,2},{7,3},{8,12},{9,13},{10,... | collective-permute-start | bytes 663560 | tf_op jit(solution)/shard_map/ppermute | solution.py:24
  472.6 13.2 %collective-permute-start.92 = (bf16[48,2304]{1,0:T(8,128)(2,1)S(1)}, bf16[48,2304]{1,0:T(8,128)(2,1)S(1)}, u32[]{:S(2)}, u32[]{:S(2)}) collective-permute-start(bf16[48,2304]{1,0:T(8,128)(2,1)S(1)} %pad_maximum_fusion.44), channel_id=1, source_target_pairs={{0,4},{1,5},{2,6},{3,7},{4,0},{5,1},{6,2},{7,3},{8,12},{9,13},{10,... | collective-permute-start | bytes 663560 | tf_op jit(solution)/shard_map/ppermute | solution.py:24
  474.4 12.6 %collective-permute-start.90 = (bf16[48,2304]{1,0:T(8,128)(2,1)S(1)}, bf16[48,2304]{1,0:T(8,128)(2,1)S(1)}, u32[]{:S(2)}, u32[]{:S(2)}) collective-permute-start(bf16[48,2304]{1,0:T(8,128)(2,1)S(1)} %pad_maximum_fusion.43), channel_id=1, source_target_pairs={{0,2},{1,3},{2,0},{3,1},{4,6},{5,7},{6,4},{7,5},{8,10},{9,11},{10,... | collective-permute-start | bytes 663560 | tf_op jit(solution)/shard_map/ppermute | solution.py:24
  485.8 19.8 %collective-permute-start.78 = (bf16[48,2304]{1,0:T(8,128)(2,1)S(1)}, bf16[48,2304]{1,0:T(8,128)(2,1)S(1)}, u32[]{:S(2)}, u32[]{:S(2)}) collective-permute-start(bf16[48,2304]{1,0:T(8,128)(2,1)S(1)} %pad_maximum_fusion.38), channel_id=1, source_target_pairs={{0,4},{1,5},{2,6},{3,7},{4,0},{5,1},{6,2},{7,3},{8,12},{9,13},{10,... | collective-permute-start | bytes 663560 | tf_op jit(solution)/shard_map/ppermute | solution.py:24
  487.0 19.7 %collective-permute-start.76 = (bf16[48,2304]{1,0:T(8,128)(2,1)S(1)}, bf16[48,2304]{1,0:T(8,128)(2,1)S(1)}, u32[]{:S(2)}, u32[]{:S(2)}) collective-permute-start(bf16[48,2304]{1,0:T(8,128)(2,1)S(1)} %pad_maximum_fusion.37), channel_id=1, source_target_pairs={{0,2},{1,3},{2,0},{3,1},{4,6},{5,7},{6,4},{7,5},{8,10},{9,11},{10,... | collective-permute-start | bytes 663560 | tf_op jit(solution)/shard_map/ppermute | solution.py:24
  487.9 19.7 %collective-permute-start.88 = (bf16[48,2304]{1,0:T(8,128)(2,1)S(1)}, bf16[48,2304]{1,0:T(8,128)(2,1)S(1)}, u32[]{:S(2)}, u32[]{:S(2)}) collective-permute-start(bf16[48,2304]{1,0:T(8,128)(2,1)S(1)} %get-tuple-element.55), channel_id=1, source_target_pairs={{8,16},{9,17},{10,18},{11,19},{12,20},{13,21},{14,22},{15,23},{16,... | collective-permute-start | bytes 663560 | tf_op jit(solution)/shard_map/ppermute | solution.py:28
  490.0 18.7 %collective-permute-start.95 = (bf16[48,2304]{1,0:T(8,128)(2,1)S(1)}, bf16[48,2304]{1,0:T(8,128)(2,1)S(1)}, u32[]{:S(2)}, u32[]{:S(2)}) collective-permute-start(bf16[48,2304]{1,0:T(8,128)(2,1)S(1)} %add_convert_fusion.42), channel_id=1, source_target_pairs={{0,8},{1,9},{2,10},{3,11},{4,12},{5,13},{6,14},{7,15},{8,0},{9,1},... | collective-permute-start | bytes 663560 | tf_op jit(solution)/shard_map/ppermute | solution.py:24
  529.0 85.5 %collective-permute-start.56 = (bf16[48,3072]{1,0:T(8,128)(2,1)S(1)}, bf16[48,3072]{1,0:T(8,128)(2,1)S(1)}, u32[]{:S(2)}, u32[]{:S(2)}) collective-permute-start(bf16[48,3072]{1,0:T(8,128)(2,1)S(1)} %pad_maximum_fusion.21), channel_id=1, source_target_pairs={{0,4},{1,5},{2,6},{3,7},{4,0},{5,1},{6,2},{7,3},{8,12},{9,13},{10,... | collective-permute-start | bytes 884744 | tf_op jit(solution)/shard_map/ppermute | solution.py:24
  530.3 32.1 %collective-permute-start.60 = (bf16[48,3072]{1,0:T(8,128)(2,1)S(1)}, bf16[48,3072]{1,0:T(8,128)(2,1)S(1)}, u32[]{:S(2)}, u32[]{:S(2)}) collective-permute-start(bf16[48,3072]{1,0:T(8,128)(2,1)S(1)} %pad_maximum_fusion.23), channel_id=1, source_target_pairs={{0,4},{1,5},{2,6},{3,7},{4,0},{5,1},{6,2},{7,3},{8,12},{9,13},{10,... | collective-permute-start | bytes 884744 | tf_op jit(solution)/shard_map/ppermute | solution.py:24
  531.4 32.1 %collective-permute-start.58 = (bf16[48,3072]{1,0:T(8,128)(2,1)S(1)}, bf16[48,3072]{1,0:T(8,128)(2,1)S(1)}, u32[]{:S(2)}, u32[]{:S(2)}) collective-permute-start(bf16[48,3072]{1,0:T(8,128)(2,1)S(1)} %pad_maximum_fusion.22), channel_id=1, source_target_pairs={{0,2},{1,3},{2,0},{3,1},{4,6},{5,7},{6,4},{7,5},{8,10},{9,11},{10,... | collective-permute-start | bytes 884744 | tf_op jit(solution)/shard_map/ppermute | solution.py:24
  532.9 16.2 %collective-permute-start.64 = (bf16[48,3072]{1,0:T(8,128)(2,1)S(1)}, bf16[48,3072]{1,0:T(8,128)(2,1)S(1)}, u32[]{:S(2)}, u32[]{:S(2)}) collective-permute-start(bf16[48,3072]{1,0:T(8,128)(2,1)S(1)} %pad_maximum_fusion.25), channel_id=1, source_target_pairs={{0,4},{1,5},{2,6},{3,7},{4,0},{5,1},{6,2},{7,3},{8,12},{9,13},{10,... | collective-permute-start | bytes 884744 | tf_op jit(solution)/shard_map/ppermute | solution.py:24
  534.7 15.5 %collective-permute-start.62 = (bf16[48,3072]{1,0:T(8,128)(2,1)S(1)}, bf16[48,3072]{1,0:T(8,128)(2,1)S(1)}, u32[]{:S(2)}, u32[]{:S(2)}) collective-permute-start(bf16[48,3072]{1,0:T(8,128)(2,1)S(1)} %pad_maximum_fusion.24), channel_id=1, source_target_pairs={{0,2},{1,3},{2,0},{3,1},{4,6},{5,7},{6,4},{7,5},{8,10},{9,11},{10,... | collective-permute-start | bytes 884744 | tf_op jit(solution)/shard_map/ppermute | solution.py:24
  559.0 34.6 %collective-permute-start.70 = (bf16[48,3072]{1,0:T(8,128)(2,1)S(1)}, bf16[48,3072]{1,0:T(8,128)(2,1)S(1)}, u32[]{:S(2)}, u32[]{:S(2)}) collective-permute-start(bf16[48,3072]{1,0:T(8,128)(2,1)S(1)} %pad_maximum_fusion.27), channel_id=1, source_target_pairs={{0,4},{1,5},{2,6},{3,7},{4,0},{5,1},{6,2},{7,3},{8,12},{9,13},{10,... | collective-permute-start | bytes 884744 | tf_op jit(solution)/shard_map/ppermute | solution.py:24
  571.7 22.9 %collective-permute-start.68 = (bf16[48,3072]{1,0:T(8,128)(2,1)S(1)}, bf16[48,3072]{1,0:T(8,128)(2,1)S(1)}, u32[]{:S(2)}, u32[]{:S(2)}) collective-permute-start(bf16[48,3072]{1,0:T(8,128)(2,1)S(1)} %pad_maximum_fusion.26), channel_id=1, source_target_pairs={{0,2},{1,3},{2,0},{3,1},{4,6},{5,7},{6,4},{7,5},{8,10},{9,11},{10,... | collective-permute-start | bytes 884744 | tf_op jit(solution)/shard_map/ppermute | solution.py:24
  573.4 41.8 %collective-permute-start.54 = (bf16[48,3072]{1,0:T(8,128)(2,1)S(1)}, bf16[48,3072]{1,0:T(8,128)(2,1)S(1)}, u32[]{:S(2)}, u32[]{:S(2)}) collective-permute-start(bf16[48,3072]{1,0:T(8,128)(2,1)S(1)} %pad_maximum_fusion.20), channel_id=1, source_target_pairs={{0,2},{1,3},{2,0},{3,1},{4,6},{5,7},{6,4},{7,5},{8,10},{9,11},{10,... | collective-permute-start | bytes 884744 | tf_op jit(solution)/shard_map/ppermute | solution.py:24
  600.4 19.0 %collective-permute-start.123 = (bf16[48,3072]{1,0:T(8,128)(2,1)S(1)}, bf16[48,3072]{1,0:T(8,128)(2,1)S(1)}, u32[]{:S(2)}, u32[]{:S(2)}) collective-permute-start(bf16[48,3072]{1,0:T(8,128)(2,1)S(1)} %pad_maximum_fusion.29), channel_id=1, source_target_pairs={{0,4},{1,5},{2,6},{3,7},{4,0},{5,1},{6,2},{7,3},{8,12},{9,13},{10,... | collective-permute-start | bytes 884744 | tf_op jit(solution)/shard_map/ppermute | solution.py:24
  603.1 12.8 %collective-permute-start.66 = (bf16[48,3072]{1,0:T(8,128)(2,1)S(1)}, bf16[48,3072]{1,0:T(8,128)(2,1)S(1)}, u32[]{:S(2)}, u32[]{:S(2)}) collective-permute-start(bf16[48,3072]{1,0:T(8,128)(2,1)S(1)} %get-tuple-element.53), channel_id=1, source_target_pairs={{8,16},{9,17},{10,18},{11,19},{12,20},{13,21},{14,22},{15,23},{16,... | collective-permute-start | bytes 884744 | tf_op jit(solution)/shard_map/ppermute | solution.py:28
  603.8 15.2 %collective-permute-start.73 = (bf16[48,3072]{1,0:T(8,128)(2,1)S(1)}, bf16[48,3072]{1,0:T(8,128)(2,1)S(1)}, u32[]{:S(2)}, u32[]{:S(2)}) collective-permute-start(bf16[48,3072]{1,0:T(8,128)(2,1)S(1)} %add_convert_fusion.23), channel_id=1, source_target_pairs={{0,8},{1,9},{2,10},{3,11},{4,12},{5,13},{6,14},{7,15},{8,0},{9,1},... | collective-permute-start | bytes 884744 | tf_op jit(solution)/shard_map/ppermute | solution.py:24
  (185 other events, 1309.7 us)

commit v2 on v0

--- a/solution.py
+++ b/solution.py
@@ -2,14 +2,856 @@
 
 import jax
 import jax.numpy as jnp
+import numpy as np
 from jax import lax
+from jax.experimental import pallas as pl
+from jax.experimental.pallas import tpu as pltpu
 from jax.sharding import PartitionSpec as P
 
 HEADS = 12
 HEAD_DIM = 64
-
-
 EPSILON = 1e-05
+BF = jnp.bfloat16
+F32 = jnp.float32
+
+TUNED = 32
+CORE, ALONG_X, ALONG_Y, ALONG_Z, MIDDLE = 1, 2, 4, 8, 24
+SLAB = 48
+HALF = 384
+
+
+def swap(value, stride):
+    return lax.ppermute(value, "dp", [(i, i ^ stride) for i in range(TUNED)])
+
+
+def swap_from(value, stride, zs):
+    return lax.ppermute(value, "dp", [(i, i ^ stride) for i in range(TUNED) if i // 8 in zs])
+
+
+def after(done, waiting):
+    return lax.optimization_barrier((done, waiting))
+
+
+def place():
+    index = lax.axis_index("dp")
+    return index % 2, index // 2
+
+
+WIDTH = HEADS * HEAD_DIM
+HIDDEN = 4 * WIDTH
+PAIR = 2 * HEAD_DIM
+ANY = pl.BlockSpec(memory_space=pl.ANY)
+WHOLE = pl.BlockSpec(memory_space=pltpu.VMEM)
+ATTN = {"qkv": 1152, "out": 384}
+MLP = {"up": 1536, "down": 1536}
+SHAPES = {"qkv": (768, 2304), "out": (768, 768), "up": (768, 3072), "down": (3072, 768), "extra": (768, 1536)}
+
+
+SPOTS = {"gain_a": 0, "shift_a": 768, "out_b": 1536, "gain_b": 2304, "shift_b": 3072, "down_b": 3840}
+BIAS_AT, UP_AT, ROW_LENGTH = 4608, 6912, 9984
+
+
+def spot(ref, name):
+    return ref[:, SPOTS[name] : SPOTS[name] + WIDTH]
+
+
+class Part:
+    def __init__(self, array, entries, first, own):
+        self.array, self.entries, self.first, self.own = array, entries, first, own
+
+
+def fetch(parts, refs, starts, targets, sems):
+    index = lax.axis_index("dp")
+    core, chip = index % 2, index // 2
+    for part, ref in zip(parts, refs):
+        half = core if part.own else 1 - core
+        last = part.first + part.array.shape[-1]
+        for name, target in targets.items():
+            begin = starts[name]
+            if name == "down":
+                pieces = [(begin + block * HALF, HALF, block) for block in range(4)]
+            else:
+                pieces = [(begin, target.shape[1] // 2, None)]
+            for start, width, block in pieces:
+                low, high = max(start, part.first), min(start + width, last)
+                if low >= high:
+                    continue
+                columns = pl.ds(pl.multiple_of(half * width + (low - start), 128), high - low)
+                for leading, code in part.entries:
+                    there = chip ^ code
+                    row = there * SLAB if block is None else there * (4 * SLAB) + block * SLAB
+                    pltpu.make_async_copy(
+                        ref.at[leading + (slice(None), pl.ds(low - part.first, high - low))],
+                        target.at[pl.ds(pl.multiple_of(row, SLAB), SLAB), columns],
+                        sems[name],
+                    ).start()
+
+
+NATURAL = {"qkv": 0, "out": 2304, "up": 3072, "down": 6144}
+
+
+def natural_pieces(array, name, whole):
+    if name == "down":
+        for block in range(4):
+            columns = pl.ds(NATURAL[name] + block * WIDTH, WIDTH)
+            yield array.at[:, columns], whole.at[pl.ds(block * WIDTH, WIDTH), :]
+    else:
+        yield array.at[:, pl.ds(NATURAL[name], whole.shape[1])], whole
+
+
+def start_fetch(weights, refs, starts, targets, sems):
+    if isinstance(weights, list):
+        return fetch(weights, refs, starts, targets, sems)
+    for name, target in targets.items():
+        for piece, place_of in natural_pieces(refs[0], name, target):
+            pltpu.make_async_copy(piece, place_of, sems[name]).start()
+
+
+def arrays_of(weights):
+    return [p.array for p in weights] if isinstance(weights, list) else [weights]
+
+
+def arrived(target, sem):
+    pltpu.make_async_copy(target, target, sem).wait()
+
+
+def dot(left, right, contract):
+    return lax.dot_general(left, right, ((contract[:1], contract[1:]), ((), ())), preferred_element_type=F32)
+
+
+def unit_of(hidden):
+    average = jnp.mean(hidden, axis=-1, keepdims=True)
+    centred = hidden - average
+    inverse = lax.rsqrt(jnp.mean(centred * centred, axis=-1, keepdims=True) + EPSILON)
+    return centred * inverse, inverse
+
+
+def back_of_norm(grad_rows, unit_rows, inverse, gain):
+    scaled = grad_rows * gain
+    first_mean = jnp.mean(scaled, axis=-1, keepdims=True)
+    second_mean = jnp.mean(scaled * unit_rows, axis=-1, keepdims=True)
+    return inverse * (scaled - first_mean - unit_rows * second_mean)
+
+
+def gelu_pair(value):
+    factor = math.sqrt(2.0 / math.pi)
+    square = value * value
+    bend = jnp.tanh(factor * value * (1.0 + 0.044715 * square))
+    half_up = 0.5 * (1.0 + bend)
+    slope = half_up + 0.5 * value * (1.0 - bend * bend) * factor * (1.0 + 3.0 * 0.044715 * square)
+    return value * half_up, slope
+
+
+def softmax_rows(query, keys, same):
+    scores = dot(query, keys, (1, 1)) * (1.0 / math.sqrt(HEAD_DIM))
+    masked = jnp.where(same, scores, -1e30)
+    expo = jnp.exp(masked - jnp.max(masked, axis=-1, keepdims=True))
+    return expo / jnp.sum(expo, axis=-1, keepdims=True)
+
+
+def head_lanes(count):
+    return lax.broadcasted_iota(jnp.int32, (count, PAIR), 1) < HEAD_DIM
+
+
+def pair_slice(pair, block):
+    return pl.ds(pl.multiple_of(block * WIDTH + pair * PAIR, PAIR), PAIR)
+
+
+def attn_forward(hidden, row, docs, weights, starts):
+    arrays = arrays_of(weights)
+    tokens = hidden.shape[0]
+
+    def body(hidden_ref, row_ref, down_docs, across_docs, *rest):
+        refs, rest = rest[: len(arrays)], rest[len(arrays) :]
+        packed_ref, mixed_ref, middle_ref, qkv_ref, out_ref, sems = rest
+        targets = {"qkv": qkv_ref, "out": out_ref}
+        named = {"qkv": sems.at[0], "out": sems.at[1]}
+        start_fetch(weights, refs, starts, targets, named)
+        unit, _ = unit_of(hidden_ref[...])
+        normed = (unit * spot(row_ref, "gain_a") + spot(row_ref, "shift_a")).astype(BF)
+        arrived(qkv_ref, named["qkv"])
+        for block in range(3):
+            columns = slice(block * WIDTH, (block + 1) * WIDTH)
+            packed_ref[:, columns] = (
+                dot(normed, qkv_ref[:, columns], (1, 0))
+                + row_ref[:, BIAS_AT + block * WIDTH : BIAS_AT + (block + 1) * WIDTH]
+            ).astype(BF)
+        same = down_docs[...] == across_docs[...]
+        first_head = head_lanes(tokens)
+
+        def one_pair(pair, carry):
+            query = packed_ref[:, pair_slice(pair, 0)]
+            keys = packed_ref[:, pair_slice(pair, 1)]
+            values = packed_ref[:, pair_slice(pair, 2)]
+            blank = jnp.zeros_like(query)
+            mixes = []
+            for own in (jnp.where(first_head, query, blank), jnp.where(first_head, blank, query)):
+                mixes.append(dot(softmax_rows(own, keys, same).astype(BF), values, (1, 0)))
+            mixed_ref[:, pair_slice(pair, 0)] = jnp.where(first_head, mixes[0], mixes[1]).astype(BF)
+            return carry
+
+        lax.fori_loop(0, HEADS // 2, one_pair, 0)
+        arrived(out_ref, named["out"])
+        middle_ref[...] = hidden_ref[...] + dot(mixed_ref[...], out_ref[...], (1, 0)) + spot(row_ref, "out_b")
+
+    return pl.pallas_call(
+        body,
+        out_shape=[
+            jax.ShapeDtypeStruct((tokens, 3 * WIDTH), BF),
+            jax.ShapeDtypeStruct((tokens, WIDTH), BF),
+            jax.ShapeDtypeStruct((tokens, WIDTH), F32),
+        ],
+        in_specs=[WHOLE] * 4 + [ANY] * len(arrays),
+        out_specs=[WHOLE] * 3,
+        scratch_shapes=[pltpu.VMEM(SHAPES["qkv"], BF), pltpu.VMEM(SHAPES["out"], BF), pltpu.SemaphoreType.DMA((2,))],
+        compiler_params=pltpu.CompilerParams(vmem_limit_bytes=40 * 2**20),
+        cost_estimate=pl.CostEstimate(flops=1, bytes_accessed=1, transcendentals=1),
+        name="attn_forward",
+    )(hidden, row, docs.reshape(-1, 1), docs.reshape(1, -1), *arrays)
+
+
+def mlp_forward(middle, row, weights, starts):
+    arrays = arrays_of(weights)
+    tokens = middle.shape[0]
+
+    def body(middle_ref, row_ref, *rest):
+        refs, rest = rest[: len(arrays)], rest[len(arrays) :]
+        top_ref, up_ref, down_ref, sems = rest
+        named = {"up": sems.at[0], "down": sems.at[1]}
+        start_fetch(weights, refs, starts, {"up": up_ref, "down": down_ref}, named)
+        unit, _ = unit_of(middle_ref[...])
+        normed = (unit * spot(row_ref, "gain_b") + spot(row_ref, "shift_b")).astype(BF)
+        total = middle_ref[...] + spot(row_ref, "down_b")
+        arrived(up_ref, named["up"])
+        arrived(down_ref, named["down"])
+        for tile in range(4):
+            columns = slice(tile * WIDTH, (tile + 1) * WIDTH)
+            lifted = dot(normed, up_ref[:, columns], (1, 0))
+            lifted = lifted + row_ref[:, UP_AT + tile * WIDTH : UP_AT + (tile + 1) * WIDTH]
+            active, _ = gelu_pair(lifted)
+            total = total + dot(active.astype(BF), down_ref[columns, :], (1, 0))
+        top_ref[...] = total
+
+    return pl.pallas_call(
+        body,
+        out_shape=jax.ShapeDtypeStruct((tokens, WIDTH), F32),
+        in_specs=[WHOLE] * 2 + [ANY] * len(arrays),
+        out_specs=WHOLE,
+        scratch_shapes=[pltpu.VMEM(SHAPES["up"], BF), pltpu.VMEM(SHAPES["down"], BF), pltpu.SemaphoreType.DMA((2,))],
+        compiler_params=pltpu.CompilerParams(vmem_limit_bytes=40 * 2**20),
+        cost_estimate=pl.CostEstimate(flops=1, bytes_accessed=1, transcendentals=1),
+        name="mlp_forward",
+    )(middle, row, *arrays)
+
+
+def send_rows(source, rows, columns, targets, half, first, sem):
+    index = lax.axis_index("dp")
+    core, chip = index % 2, index // 2
+    for side, target in enumerate(targets):
+
+        @pl.when(core == half ^ side)
+        def _(target=target):
+            for there, row in rows:
+                pltpu.make_async_copy(
+                    source.at[pl.ds(row, SLAB), columns],
+                    target.at[chip ^ there, :, pl.ds(first, columns.size)],
+                    sem,
+                ).start()
+
+
+def mlp_backward(middle, grad_top, row, weights, starts, with_top):
+    natural = not isinstance(weights, list)
+    arrays = arrays_of(weights)
+    tokens = middle.shape[0]
+
+    def body(middle_ref, grad_ref, row_ref, *rest):
+        refs, rest = rest[: len(arrays)], rest[len(arrays) :]
+        grads_ref, rest = rest[:2], rest[2:]
+        mid_ref, small_ref = rest[:2]
+        top_ref = rest[2] if with_top else None
+        up_ref, down_ref, up_stage, down_stage, sems = rest[-5:]
+        named = {"up": sems.at[0], "down": sems.at[1]}
+        tiles = [slice(tile * WIDTH, (tile + 1) * WIDTH) for tile in range(4)]
+        start_fetch(weights, refs, starts, {"up": up_ref, "down": down_ref}, named)
+        unit, inverse = unit_of(middle_ref[...])
+        normed = (unit * spot(row_ref, "gain_b") + spot(row_ref, "shift_b")).astype(BF)
+        grad_top_rows = grad_ref[...].astype(F32)
+        grad_down = grad_top_rows.astype(BF)
+        small_ref[:, HIDDEN : HIDDEN + WIDTH] = jnp.sum(grad_down.astype(F32), axis=0, keepdims=True)
+        grad_nb = jnp.zeros((tokens, WIDTH), F32)
+        total = middle_ref[...] + spot(row_ref, "down_b") if with_top else None
+        arrived(up_ref, named["up"])
+        arrived(down_ref, named["down"])
+        for tile, columns in enumerate(tiles):
+            lifted = dot(normed, up_ref[:, columns], (1, 0))
+            lifted = lifted + row_ref[:, UP_AT + tile * WIDTH : UP_AT + (tile + 1) * WIDTH]
+            active, slope = gelu_pair(lifted)
+            active = active.astype(BF)
+            if with_top:
+                total = total + dot(active, down_ref[columns, :], (1, 0))
+            grad_act = dot(grad_down, down_ref[columns, :], (1, 1))
+            grad_lift = (grad_act * slope).astype(BF)
+            small_ref[:, columns] = jnp.sum(grad_lift.astype(F32), axis=0, keepdims=True)
+            grad_nb = grad_nb + dot(grad_lift, up_ref[:, columns], (1, 1))
+            up_stage[:, columns] = dot(normed, grad_lift, (0, 0)).astype(BF)
+            down_stage[columns, :] = dot(active, grad_down, (0, 0)).astype(BF)
+            send_rows(
+                up_stage,
+                [(there, there * SLAB) for there in range(16)],
+                pl.ds(tile * WIDTH, WIDTH),
+                grads_ref,
+                tile // 2,
+                tile % 2 * WIDTH,
+                sems.at[2],
+            )
+            if natural:
+                pieces = [(tile, [(there, tile * WIDTH + there * SLAB) for there in range(16)])]
+            else:
+                chips = range(4 * tile, 4 * tile + 4)
+                pieces = [(b, [(there, there * 4 * SLAB + b * SLAB) for there in chips]) for b in range(4)]
+            for half in range(2):
+                for block, rows in pieces:
+                    send_rows(
+                        down_stage,
+                        rows,
+                        pl.ds(half * HALF, HALF),
+                        grads_ref,
+                        half,
+                        4 * HALF + block * HALF,
+                        sems.at[3],
+                    )
+        if with_top:
+            top_ref[...] = total.astype(BF)
+        small_ref[:, HIDDEN + WIDTH : HIDDEN + 2 * WIDTH] = jnp.sum(grad_nb * unit, axis=0, keepdims=True)
+        small_ref[:, HIDDEN + 2 * WIDTH :] = jnp.sum(grad_nb, axis=0, keepdims=True)
+        mid_ref[...] = grad_top_rows + back_of_norm(grad_nb, unit, inverse, spot(row_ref, "gain_b"))
+        arrived(up_stage, sems.at[2])
+        arrived(down_stage, sems.at[3])
+
+    sums = [(16, SLAB, HIDDEN)] * 2
+    outs = [jax.ShapeDtypeStruct(shape, BF) for shape in sums] + [
+        jax.ShapeDtypeStruct((tokens, WIDTH), F32),
+        jax.ShapeDtypeStruct((1, HIDDEN + 3 * WIDTH), F32),
+    ]
+    if with_top:
+        outs.append(jax.ShapeDtypeStruct((tokens, WIDTH), BF))
+    return pl.pallas_call(
+        body,
+        out_shape=outs,
+        in_specs=[WHOLE] * 3 + [ANY] * len(arrays),
+        out_specs=[ANY] * len(sums) + [WHOLE] * (len(outs) - len(sums)),
+        scratch_shapes=[pltpu.VMEM(SHAPES["up"], BF), pltpu.VMEM(SHAPES["down"], BF)] * 2
+        + [pltpu.SemaphoreType.DMA((4,))],
+        compiler_params=pltpu.CompilerParams(vmem_limit_bytes=50 * 2**20),
+        cost_estimate=pl.CostEstimate(flops=1, bytes_accessed=1, transcendentals=1),
+        name="mlp_backward",
+    )(middle, grad_top, row, *arrays)
+
+
+def attn_backward(hidden, grad_mid, packed, mixed, row, docs, weights, starts, steps):
+    arrays = arrays_of(weights)
+    tokens = hidden.shape[0]
+    scale = 1.0 / math.sqrt(HEAD_DIM)
+
+    def body(hidden_ref, mid_ref, packed_ref, mixed_ref, row_ref, down_docs, across_docs, *rest):
+        if steps is not None:
+            steps_ref, rest = rest[0], rest[1:]
+        refs, rest = rest[: len(arrays)], rest[len(arrays) :]
+        grads_ref, rest = rest[:2], rest[2:]
+        in_ref, small_ref = rest[:2]
+        qkv_ref, out_ref, qkv_stage, out_stage, gm_ref, gp_ref, sems = rest[2:9]
+        named = {"qkv": sems.at[0], "out": sems.at[1]}
+        start_fetch(weights, refs, starts, {"qkv": qkv_ref, "out": out_ref}, named)
+        unit, inverse = unit_of(hidden_ref[...])
+        normed = (unit * spot(row_ref, "gain_a") + spot(row_ref, "shift_a")).astype(BF)
+        grad_branch = mid_ref[...].astype(BF)
+        small_ref[:, 2 * WIDTH : 3 * WIDTH] = jnp.sum(grad_branch.astype(F32), axis=0, keepdims=True)
+        out_stage[...] = dot(mixed_ref[...], grad_branch, (0, 0)).astype(BF)
+        chips = [(there, there * SLAB) for there in range(16)]
+        for half in range(2):
+            send_rows(out_stage, chips, pl.ds(half * HALF, HALF), grads_ref, half, 3 * HALF, sems.at[2])
+        arrived(out_ref, named["out"])
+        gm_ref[...] = dot(grad_branch, out_ref[...], (1, 1)).astype(BF)
+        same = down_docs[...] == across_docs[...]
+        first_head = head_lanes(tokens)
+
+        def one_pair(pair, carry):
+            query = packed_ref[:, pair_slice(pair, 0)]
+            keys = packed_ref[:, pair_slice(pair, 1)]
+            values = packed_ref[:, pair_slice(pair, 2)]
+            grad_mixed = gm_ref[:, pair_slice(pair, 0)]
+            blank = jnp.zeros_like(query)
+            results = []
+            for head in range(2):
+                lanes = first_head if head == 0 else jnp.logical_not(first_head)
+                probs = softmax_rows(jnp.where(lanes, query, blank), keys, same)
+                low = probs.astype(BF)
+                grad_probs = dot(jnp.where(lanes, grad_mixed, blank), values, (1, 1))
+                grad_scores = probs * (grad_probs - jnp.sum(probs * grad_probs, axis=-1, keepdims=True))
+                scores_low = grad_scores.astype(BF)
+                results.append(
+                    (
+                        dot(scores_low, keys, (1, 0)) * scale,
+                        dot(scores_low, query, (0, 0)) * scale,
+                        dot(low, grad_mixed, (0, 0)),
+                    )
+                )
+            for block in range(3):
+                gp_ref[:, pair_slice(pair, block)] = jnp.where(
+                    first_head, results[0][block], results[1][block]
+                ).astype(BF)
+            return carry
+
+        lax.fori_loop(0, HEADS // 2, one_pair, 0)
+        arrived(qkv_ref, named["qkv"])
+        grad_na = jnp.zeros((tokens, WIDTH), F32)
+        for block in range(3):
+            columns = slice(block * WIDTH, (block + 1) * WIDTH)
+            piece = gp_ref[:, columns]
+            sums = jnp.sum(piece.astype(F32), axis=0, keepdims=True)
+            if block != 1:
+                small_ref[:, block // 2 * WIDTH : (block // 2 + 1) * WIDTH] = sums
+            qkv_stage[:, columns] = dot(normed, piece, (0, 0)).astype(BF)
+            grad_na = grad_na + dot(piece, qkv_ref[:, columns], (1, 1))
+        for half in range(2):
+            send_rows(qkv_stage, chips, pl.ds(half * 3 * HALF, 3 * HALF), grads_ref, half, 0, sems.at[3])
+        small_ref[:, 3 * WIDTH : 4 * WIDTH] = jnp.sum(grad_na * unit, axis=0, keepdims=True)
+        small_ref[:, 4 * WIDTH :] = jnp.sum(grad_na, axis=0, keepdims=True)
+        grad_in = mid_ref[...] + back_of_norm(grad_na, unit, inverse, spot(row_ref, "gain_a"))
+        in_ref[...] = grad_in
+        if steps is not None:
+            sums_ref, table_stages = rest[9], rest[10:]
+            index = lax.axis_index("dp")
+            core, chip = index % 2, index // 2
+            for doc in range(8):
+                sums_ref[doc : doc + 1, :] = (
+                    jnp.sum(jnp.where(down_docs[...] == doc, grad_in, 0.0), axis=0, keepdims=True)
+                    if doc < steps.shape[1]
+                    else jnp.zeros((1, WIDTH), F32)
+                )
+            spots = [lax.broadcasted_iota(jnp.int32, (16, SLAB, 8), axis) for axis in range(2)]
+            for side, half in enumerate((core, 1 - core)):
+                sums = sums_ref[:, pl.ds(pl.multiple_of(half * HALF, HALF), HALF)].astype(BF)
+                for owner in range(2):
+                    line = ((chip ^ spots[0]) * 2 + owner) * 32 + spots[1]
+                    line = jnp.where(spots[1] < 32, line, -1)
+                    hot = jnp.where(line == steps_ref[...][None], 1.0, 0.0).reshape(16 * SLAB, 8).astype(BF)
+                    block = dot(hot, sums, (1, 0)).astype(BF).reshape(16, SLAB, HALF)
+                    stage = table_stages[side]
+                    stage[:, :, owner * HALF : (owner + 1) * HALF] = block
+                pltpu.make_async_copy(
+                    table_stages[side], grads_ref[side].at[:, :, pl.ds(1536, 2 * HALF)], sems.at[4 + side]
+                ).start()
+            for side in range(2):
+                arrived(table_stages[side], sems.at[4 + side])
+        arrived(out_stage, sems.at[2])
+        arrived(qkv_stage, sems.at[3])
+
+    sums = [(16, SLAB, 1536 if steps is None else 2304)] * 2
+    outs = [jax.ShapeDtypeStruct(shape, BF) for shape in sums] + [
+        jax.ShapeDtypeStruct((tokens, WIDTH), F32),
+        jax.ShapeDtypeStruct((1, 5 * WIDTH), F32),
+    ]
+    operands = [hidden, grad_mid, packed, mixed, row, docs.reshape(-1, 1), docs.reshape(1, -1)]
+    scratch = [pltpu.VMEM(SHAPES["qkv"], BF), pltpu.VMEM(SHAPES["out"], BF)] * 2 + [
+        pltpu.VMEM((tokens, WIDTH), BF),
+        pltpu.VMEM((tokens, 3 * WIDTH), BF),
+        pltpu.SemaphoreType.DMA((6,)),
+    ]
+    if steps is not None:
+        operands.append(jnp.pad(steps, ((0, 0), (0, 8 - steps.shape[1])), constant_values=-2))
+        scratch += [pltpu.VMEM((8, WIDTH), F32)] + [pltpu.VMEM((16, SLAB, 2 * HALF), BF)] * 2
+    return pl.pallas_call(
+        body,
+        out_shape=outs,
+        in_specs=[WHOLE] * len(operands) + [ANY] * len(arrays),
+        out_specs=[ANY] * len(sums) + [WHOLE] * (len(outs) - len(sums)),
+        scratch_shapes=scratch,
+        compiler_params=pltpu.CompilerParams(vmem_limit_bytes=50 * 2**20),
+        cost_estimate=pl.CostEstimate(flops=1, bytes_accessed=1, transcendentals=1),
+        name="attn_backward",
+    )(*operands, *arrays)
+
+
+def lay_extra(parts, first):
+    def body(*rest):
+        refs, (extra_ref, sems) = rest[: len(parts)], rest[len(parts) :]
+        named = {"extra": sems.at[0]}
+        fetch(parts, refs, {"extra": first}, {"extra": extra_ref}, named)
+        arrived(extra_ref, named["extra"])
+
+    return pl.pallas_call(
+        body,
+        out_shape=jax.ShapeDtypeStruct(SHAPES["extra"], BF),
+        in_specs=[ANY] * len(parts),
+        out_specs=WHOLE,
+        scratch_shapes=[pltpu.SemaphoreType.DMA((1,))],
+        compiler_params=pltpu.CompilerParams(vmem_limit_bytes=16 * 2**20),
+        cost_estimate=pl.CostEstimate(flops=1, bytes_accessed=1, transcendentals=1),
+        name="lay_extra",
+    )(*[p.array for p in parts])
+
+
+def is_middle():
+    level = lax.axis_index("dp") // 8
+    return (level == 1) | (level == 2)
+
+
+def cut_of(value):
+    return value.shape[-1] // 256 * 128
+
+
+def chip_share(layer_weights, extra):
+    core, _ = place()
+    down = layer_weights.get("down")
+
+    def halves(half):
+        def columns(value):
+            width = value.shape[1] // 2
+            return value[:, half * width : half * width + width]
+
+        narrow = [columns(layer_weights[name]) for name in ("qkv", "out", "up") if name in layer_weights]
+        wide = []
+        if down is not None:
+            wide += [columns(down)[:SLAB], columns(down)[SLAB:]]
+        if extra is not None:
+            wide.append(columns(extra))
+        parts = narrow
+        if wide:
+            wide = jnp.concatenate(wide, axis=1)
+            parts = parts + [wide[:24], wide[24:]]
+        return jnp.concatenate(parts, axis=1), sum(v.shape[1] for v in narrow)
+
+    (left, count), (right, _) = halves(0), halves(1)
+    kept = jnp.where(core == 0, left, right)
+    came = swap(jnp.where(core == 0, right, left), CORE)
+    lower = jnp.where(core == 0, kept, came)
+    upper = jnp.where(core == 0, came, kept)
+    columns = [jnp.concatenate([lower[:, :count], upper[:, :count]], axis=0)]
+    wide = (lower.shape[1] - count) // 2
+    if wide:
+        low, high = [
+            jnp.concatenate([v[:, count : count + wide], v[:, count + wide :]], axis=0) for v in (lower, upper)
+        ]
+        if down is not None:
+            columns += [low[:, : 2 * HALF], high[:, : 2 * HALF]]
+        if extra is not None:
+            columns += [low[:, wide - HALF :], high[:, wide - HALF :]]
+    return jnp.concatenate(columns, axis=1)
+
+
+def line_second(first, third_middle):
+    return swap_from(first, MIDDLE, (1, 2)), swap_from(third_middle, ALONG_Z, (1, 2))
+
+
+def line_third(second_middle):
+    return swap_from(second_middle, ALONG_Z, (1, 2))
+
+
+def line_first(own):
+    return swap(own, ALONG_Z), swap_from(own, MIDDLE, (1, 2))
+
+
+def by_place(middle, end):
+    return jnp.where(is_middle(), middle, end)
+
+
+def along_each(to_x, to_y):
+    return swap(to_x, ALONG_X), swap(to_y, ALONG_Y)
+
+
+def diagonal(by_x, by_y):
+    cut = cut_of(by_x)
+    return swap(by_x[..., :cut], ALONG_Y), swap(by_y[..., cut:], ALONG_X)
+
+
+def with_other_core(own, by_x, by_y, low, high, distances, first):
+    sides = jnp.stack([own, by_x, by_y])
+    across = jnp.concatenate([low, high], axis=-1)
+    parts = []
+    for array, steps in ((sides, (0, 1, 2)), (across, (3,))):
+        if len(steps) > 1:
+            entries = [((n, k), 4 * d + step) for n, step in enumerate(steps) for k, d in enumerate(distances)]
+        else:
+            entries = [((k,), 4 * d + 3) for k, d in enumerate(distances)]
+        parts.append(Part(array, entries, first, True))
+        parts.append(Part(swap(array, CORE), entries, first, False))
+    return parts
+
+
+def direct_line(levels):
+    return [swap(levels[k], ALONG_Z * k) for k in (1, 2, 3)]
+
+
+def total(*values):
+    return sum(v.astype(F32) for v in values)
+
+
+class PlaneSums:
+    def __init__(self, *pairs):
+        self.pairs = [[v.reshape(4, 4, SLAB, v.shape[-1]) for v in pair] for pair in pairs]
+        self.columns = sum(pair[0].shape[-1] for pair in pairs)
+        self.cut = self.columns // 256 * 128
+
+    def pair(self, step, first=0, last=None):
+        last = self.columns if last is None else last
+        pieces = []
+        begin = 0
+        for pair in self.pairs:
+            end = begin + pair[0].shape[-1]
+            low, high = max(first, begin) - begin, min(last, end) - begin
+            if low < high:
+                pieces.append(total(*[v[:, step, :, low:high] for v in pair]))
+            begin = end
+        return pieces[0] if len(pieces) == 1 else jnp.concatenate(pieces, axis=-1)
+
+    def diagonals(self):
+        return self.pair(3, 0, self.cut).astype(BF), self.pair(3, self.cut).astype(BF)
+
+    def sides(self, low, high):
+        room = [(0, 0)] * 2
+        low = jnp.pad(low, room + [(0, self.columns - self.cut)])
+        high = jnp.pad(high, room + [(self.cut, 0)])
+        return (self.pair(1) + low.astype(F32)).astype(BF), (self.pair(2) + high.astype(F32)).astype(BF)
+
+    def levels(self, by_x, by_y):
+        return (self.pair(0) + total(by_x, by_y)).astype(BF)
+
+
+def by_half(core, mine, other, axis):
+    return jnp.where(
+        core == 0, jnp.concatenate([mine, other], axis=axis), jnp.concatenate([other, mine], axis=axis)
+    )
+
+
+def own_rows(names, share):
+    core, _ = place()
+    widths = {"qkv": 1152, "out": 384, "up": 1536, "down": 1536, "down_by_core": 1536, "extra": 768}
+    pieces = []
+    start = 0
+    for name in names:
+        piece = share[:, start : start + widths[name]]
+        start += widths[name]
+        if name in ("down", "extra"):
+            m = widths[name] // 2
+            mine, theirs = [lax.dynamic_slice_in_dim(piece, side * m, m, 1) for side in (core, 1 - core)]
+            if name == "down":
+                mine, theirs = [jnp.concatenate([v[:, :HALF], v[:, HALF:]], axis=0) for v in (mine, theirs)]
+        else:
+            mine, theirs = [lax.dynamic_slice_in_dim(piece, side * 24, 24, 0) for side in (core, 1 - core)]
+        pieces.append((mine, theirs))
+    sizes = [theirs.shape for _, theirs in pieces]
+    packed = jnp.concatenate([theirs.astype(BF).reshape(24, -1) for _, theirs in pieces], axis=1)
+    came = swap(packed, CORE)
+    outs = []
+    start = 0
+    for (mine, _), (rows, columns) in zip(pieces, sizes):
+        count = rows * columns // 24
+        other = came[:, start : start + count].reshape(rows, columns).astype(F32)
+        start += count
+        outs.append((mine, other))
+    for n, name in enumerate(names):
+        if name == "down_by_core":
+            outs[n] = [jnp.concatenate(jnp.split(v, 4, axis=1), axis=0) for v in outs[n]]
+    return [by_half(core, mine, other, 1) for mine, other in outs]
+
+
+def small_maps(layer):
+    device = np.full(ROW_LENGTH, -1, np.int32)
+    inner = np.full(ROW_LENGTH, -1, np.int32)
+
+    def put(at, count, each, begin):
+        spots = np.arange(count)
+        device[at : at + count] = spots // each
+        inner[at : at + count] = begin + spots % each
+
+    for n, name in enumerate(WIDE_SMALLS):
+        put(SPOTS[name], WIDTH, 24, 24 * n)
+    put(BIAS_AT, 2 * WIDTH, 48, 144)
+    for array in (device, inner):
+        array[BIAS_AT + 2 * WIDTH : BIAS_AT + 3 * WIDTH] = array[BIAS_AT + WIDTH : BIAS_AT + 2 * WIDTH]
+        array[BIAS_AT + WIDTH : BIAS_AT + 2 * WIDTH] = -1
+    put(UP_AT, HIDDEN, 96, 192)
+    if layer == 1:
+        block, there, at = np.unravel_index(np.arange(HIDDEN), (4, TUNED, 24))
+        device[UP_AT:], inner[UP_AT:] = there, 192 + 24 * block + at
+    return device, inner
+
+
+WIDE_SMALLS = ("out_b", "gain_a", "shift_a", "down_b", "gain_b", "shift_b")
+GRAD_ORDER = ("up", "down_b", "gain_b", "shift_b", "query", "value", "out_b", "gain_a", "shift_a")
+
+
+def grad_maps(layer):
+    device, inner = small_maps(layer)
+    pieces = {"up": (UP_AT, HIDDEN), "query": (BIAS_AT, WIDTH), "value": (BIAS_AT + 2 * WIDTH, WIDTH)}
+    pieces.update({name: (at, WIDTH) for name, at in SPOTS.items()})
+    order = np.concatenate([np.arange(at, at + count) for at, count in (pieces[name] for name in GRAD_ORDER)])
+    return device[order], inner[order]
+
+
+def spread_smalls(gathered, layer):
+    device, inner = small_maps(layer)
+    hot = (jnp.arange(HALF, dtype=jnp.int32)[:, None] == inner[None, :]).astype(BF)
+    wide = jnp.dot(gathered, hot, preferred_element_type=F32)
+    mine = jnp.arange(TUNED, dtype=jnp.int32)[:, None] == device[None, :]
+    return jnp.sum(jnp.where(mine, wide, 0.0), axis=0, keepdims=True)
+
+
+def collect_smalls(row, layer):
+    device, inner = grad_maps(layer)
+    mine = jnp.arange(TUNED, dtype=jnp.int32)[:, None] == device[None, :]
+    masked = jnp.where(mine, row.astype(BF), jnp.zeros((), BF))
+    hot = (inner[:, None] == jnp.arange(HALF, dtype=jnp.int32)[None, :]).astype(BF)
+    return jnp.dot(masked, hot, preferred_element_type=F32).astype(BF)
+
+
+gate = lax.optimization_barrier
+
+
+def tuned(
+    embedded,
+    doc_ids,
+    step_ids,
+    step_table,
+    qkv_weight,
+    qv_bias,
+    out_weight,
+    out_bias,
+    first_gain,
+    first_shift,
+    up_weight,
+    up_bias,
+    down_weight,
+    down_bias,
+    second_gain,
+    second_shift,
+    cotangent,
+):
+    core, chip = place()
+    docs = doc_ids[0]
+    doc_count = step_ids.shape[1]
+    steps = step_ids[0]
+    smalls = (out_bias, first_gain, first_shift, down_bias, second_gain, second_shift, qv_bias, up_bias)
+    small_rows = jnp.pad(jnp.concatenate(smalls, axis=1), ((0, 0), (0, HALF - 288))).reshape(1, 2 * HALF)
+    extra = jnp.concatenate([step_table, jnp.pad(small_rows, ((0, 15), (0, 0)))], axis=0)
+    down_blocks = [down_weight[1][24 * b : 24 * b + 24] for b in range(4)]
+    up_order = up_weight[1].reshape(24, TUNED, 4, 24).transpose(0, 2, 1, 3).reshape(24, HIDDEN)
+    upper_share = jnp.concatenate([qkv_weight[1], out_weight[1], up_order] + down_blocks, axis=1)
+    lower_share = chip_share(
+        {"qkv": qkv_weight[0], "out": out_weight[0], "up": up_weight[0], "down": down_weight[0]}, extra
+    )
+    starts = {"qkv": 0, "out": 1152, "up": 1536, "down": 3072, "extra": 4608}
+    upper = lax.all_gather(upper_share, "dp", axis=0, tiled=True)
+
+    block1, block3_middle = line_first(lower_share)
+    second_middle, second_end = line_second(block1, block3_middle)
+    third_end = line_third(second_middle)
+    blocks = [lower_share, block1, by_place(second_middle, second_end), by_place(block3_middle, third_end)]
+    parts = []
+    for distance, block in enumerate(blocks):
+        by_x, by_y = along_each(block, block)
+        plane = jnp.stack([block, by_x, by_y, jnp.concatenate(diagonal(by_x, by_y), axis=1)])
+        entries = [((step,), 4 * distance + step) for step in range(4)]
+        parts += [Part(plane, entries, 0, True), Part(swap(plane, CORE), entries, 0, False)]
+
+    all_extra = lay_extra(parts, starts["extra"])
+    small_all = all_extra[32::SLAB].reshape(16, 2, 2, HALF).transpose(1, 0, 2, 3).reshape(2, TUNED, HALF)
+    rows = [spread_smalls(small_all[layer], layer) for layer in range(2)]
+    owner = steps // 32
+    row_of = (owner // 2) * SLAB + steps % 32
+    row_hot = (row_of[:, None] == jnp.arange(16 * SLAB, dtype=jnp.int32)[None, :]).astype(BF)
+    both_rows = jnp.dot(row_hot, all_extra, preferred_element_type=F32).reshape(doc_count, 2, 2, HALF)
+    doc_rows = jnp.where((owner % 2 == 0)[:, None, None], both_rows[:, :, 0], both_rows[:, :, 1])
+    doc_rows = doc_rows.reshape(doc_count, WIDTH)
+    of_doc = [(docs == s)[:, None] for s in range(doc_count)]
+    start = embedded.astype(F32) + sum(jnp.where(of_doc[s], doc_rows[s][None], 0.0) for s in range(doc_count))
+
+    packed0, mixed0, middle0 = attn_forward(start, rows[0], docs, parts, starts)
+    between = mlp_forward(middle0, rows[0], parts, starts)
+    packed1, mixed1, middle1 = attn_forward(between, rows[1], docs, upper, None)
+
+    kept_m, sent_m, mid1, small_mlp1, block_output = mlp_backward(middle1, cotangent, rows[1], upper, None, True)
+    came_m = swap(sent_m, CORE)
+    kept_t, sent_t, in1, small_attn1 = attn_backward(
+        between, mid1, packed1, mixed1, rows[1], docs, upper, None, None
+    )
+    in1, came_m, sent_t = gate((in1, came_m, sent_t))
+    came_t = swap(sent_t, CORE)
+    in1, came_t = gate((in1, came_t))
+    sums_a = PlaneSums((kept_m, came_m), (kept_t, came_t))
+    in1, to_go = gate((in1, sums_a.diagonals()))
+    low_a, high_a = swap(to_go[0], ALONG_Y), swap(to_go[1], ALONG_X)
+    kept_b, sent_b, mid0, small_mlp0 = mlp_backward(middle0, in1, rows[0], parts, starts, False)
+    mid0, low_a, high_a, sent_b = gate((mid0, low_a, high_a, sent_b))
+    mid0, to_go, sent_b, small_mlp1, small_attn1 = gate(
+        (mid0, sums_a.sides(low_a, high_a), sent_b, small_mlp1, small_attn1)
+    )
+    x_a, y_a = along_each(*to_go)
+    came_b = swap(sent_b, CORE)
+    kept_c, sent_c, input_grad, small_attn0 = attn_backward(
+        start, mid0, packed0, mixed0, rows[0], docs, parts, starts, step_ids
+    )
+    small_grads = jnp.stack(
+        [
+            collect_smalls(jnp.concatenate([small_mlp0, small_attn0], axis=1), 0),
+            collect_smalls(jnp.concatenate([small_mlp1, small_attn1], axis=1), 1),
+        ]
+    ).reshape(2, 16, 2 * HALF)
+    small_grads = small_grads[:, chip ^ jnp.arange(16, dtype=jnp.int32)][:, :, None]
+    small_grads = jnp.pad(small_grads, ((0, 0), (0, 0), (0, 15), (0, 0)))
+    kept_c, sent_c = [
+        lax.dynamic_update_slice(
+            v, lax.dynamic_index_in_dim(small_grads, side, 0, keepdims=False), (0, 32, 1536)
+        )
+        for v, side in ((kept_c, core), (sent_c, 1 - core))
+    ]
+    sums_b = PlaneSums((kept_b, came_b))
+    input_grad, kept_c, sent_c, x_a, y_a, to_go = gate((input_grad, kept_c, sent_c, x_a, y_a, sums_b.diagonals()))
+    low_b, high_b = swap(to_go[0], ALONG_Y), swap(to_go[1], ALONG_X)
+    came_c = swap(sent_c, CORE)
+    levels_a = sums_a.levels(x_a, y_a)
+    low_b, high_b, levels_a = gate((low_b, high_b, levels_a))
+    to_go, levels_a = gate((sums_b.sides(low_b, high_b), levels_a))
+    x_b, y_b = along_each(*to_go)
+    back_a = direct_line(levels_a)
+    sums_c = PlaneSums((kept_c, came_c))
+    x_b, y_b, to_go = gate((x_b, y_b, sums_c.diagonals()))
+    low_c, high_c = swap(to_go[0], ALONG_Y), swap(to_go[1], ALONG_X)
+    levels_b = sums_b.levels(x_b, y_b)
+    low_c, high_c, back_a, levels_b = gate((low_c, high_c, back_a, levels_b))
+    to_go, back_a, levels_b = gate((sums_c.sides(low_c, high_c), back_a, levels_b))
+    x_c, y_c = along_each(*to_go)
+    back_b = direct_line(levels_b)
+    x_c, y_c, back_b, back_a = gate((x_c, y_c, back_b, back_a))
+    levels_c = sums_c.levels(x_c, y_c)
+    back_c = direct_line(levels_c)
+    up_1, down_1, qkv_1, out_1 = own_rows(("up", "down_by_core", "qkv", "out"), total(levels_a[0], *back_a))
+    up_1 = up_1.reshape(24, 4, TUNED, 24).transpose(0, 2, 1, 3).reshape(24, HIDDEN)
+    up_0, down_0 = own_rows(("up", "down"), total(levels_b[0], *back_b))
+    up, down = jnp.stack([up_0, up_1]), jnp.stack([down_0, down_1])
+    up, down, qkv_1, out_1, back_c = gate((up, down, qkv_1, out_1, back_c))
+    sum_c = total(levels_c[0], *back_c)
+    qkv_0, out_0, extra_0 = own_rows(("qkv", "out", "extra"), sum_c)
+    small_out = extra_0[32].reshape(2, HALF)
+    out_b, gain_a, shift_a, down_b, gain_b, shift_b = [small_out[:, n * 24 : n * 24 + 24] for n in range(6)]
+    return (
+        block_output,
+        input_grad,
+        extra_0[:32],
+        jnp.stack([qkv_0, qkv_1]),
+        small_out[:, 144:192],
+        jnp.stack([out_0, out_1]),
+        out_b,
+        gain_a,
+        shift_a,
+        up,
+        small_out[:, 192:288],
+        down,
+        down_b,
+        gain_b,
+        shift_b,
+    )
 
 
 def shortened(value):
@@ -205,7 +1047,7 @@
     return (grad_in, grads)
 
 
-def local(
+def plain(
     embedded,
     doc_ids,
     step_ids,
@@ -333,6 +1175,7 @@
 
 
 def solution(mesh):
+    local = tuned if mesh.shape["dp"] == TUNED else plain
     in_specs = (
         P("dp", None),
         P("dp", None),

time: 1700 us -> 431 us (0.25)
  waiting for transfers between devices: 1290 us -> 162 us
  matrix products: 102 us -> 13.6 us
  Pallas kernels: 0 us -> 88.4 us
  other arithmetic: 107 us -> 51.5 us
  starting transfers between devices: 114 us -> 68.5 us
  blocking collectives: 43.2 us -> 0 us
    ppermute x125 -> x54, waiting for transfers between devices: 830 us -> 162 us  [the longest x50 146 us: swap(): return lax.ppermute(value, 'dp', [(i, i ^ stride) for i in range(TUNED)])]
    all_gather x9 -> x1, waiting for transfers between devices: 458 us -> 0.02 us  [tuned(): upper = lax.all_gather(upper_share, 'dp', axis=0, tiled=True)]
    pallas_call x0 -> x8, Pallas kernels: none -> 88.4 us  [the longest x2 33 us: attn_backward(): pl.pallas_call(body, out_shape=outs, in_specs=[WHOLE] * len(operands) + [...]
    dot_general x38 -> x5, matrix products: 95.2 us -> 13.6 us  [the longest x2 5.95 us: spread_smalls(): wide = jnp.dot(gathered, hot, preferred_element_type=F32)]
    ppermute x125 -> x54, starting transfers between devices: 113 us -> 68.4 us  [the longest x50 63.5 us: swap(): return lax.ppermute(value, 'dp', [(i, i ^ stride) for i in range(TUNED)])]
    unnamed x1 -> x0, blocking collectives: 43.2 us -> none
    add x102 -> x8, other arithmetic: 46.1 us -> 12.2 us  [the longest x6 11.9 us: total(): return sum((v.astype(F32) for v in values))]
    convert_element_type x141 -> x14, other arithmetic: 46 us -> 24.7 us  [the longest x3 7.52 us: sides(): (self.pair(2) + high.astype(F32)).astype(BF)]
  transfers between devices with their start and end apart: 134 -> 55, of which waited for: 114 -> 28; matrix products, arithmetic and copies ran while one was open for 9% -> 14% of each run, Pallas kernels for 0% -> 15%
where the time goes in v2:
time: 431 us; the launch traced here: 425 us
  waiting for transfers between devices  162 us (38%)
  Pallas kernels  88.4 us (21%)
  starting transfers between devices  68.5 us (16%)
  other arithmetic  51.5 us (12%)
  local copies, waits for them, and re-layouts  24.3 us (6%)
  between operations  16.1 us (4%)
  matrix products  13.6 us (3%)
    ppermute x50, waiting for transfers between devices, swap(): return lax.ppermute(value, 'dp', [(i, i ^ stride) for i in range(TUNED)])  146 us
    ppermute x50, starting transfers between devices, swap(): return lax.ppermute(value, 'dp', [(i, i ^ stride) for i in range(TUNED)])  63.5 us
    pallas_call x2, Pallas kernels, attn_backward(): pl.pallas_call(body, out_shape=outs, in_specs=[WHOLE] * len(operands) + [...  33 us
    pallas_call x2, Pallas kernels, mlp_backward(): pl.pallas_call(body, out_shape=outs, in_specs=[WHOLE] * 3 + [ANY] * len(a...  27.7 us
    pallas_call x2, Pallas kernels, attn_forward(): pl.pallas_call(body, out_shape=[jax.ShapeDtypeStruct((tokens, 3 * WIDTH),...  18.9 us
    ppermute x4, waiting for transfers between devices, swap_from(): lax.ppermute(value, 'dp', [(i, i ^ stride) for i in range(TUNED) if i //...  16 us
    add x6, other arithmetic, total(): return sum((v.astype(F32) for v in values))  11.9 us
  transfers between devices with their start and end apart: 55, of which 28 were waited for; matrix products, arithmetic and copies ran while one was open for 14% of the time, Pallas kernels for 15%

profile of v2, /device:TPU:0, one launch (start us, length us, event | category | flops | bytes accessed | tf_op | source)
XLA Modules:
  0.0 424.7 jit_solution(14977549437475992100)
XLA Ops:
  14.5 3.0 collective-permute-start.1
  17.4 1.5 collective-permute-start.2
  18.9 1.6 collective-permute-start.6
  22.0 10.6 %collective-permute-done.1 = bf16[48,5376]{1,0:T(8,128)(2,1)S(1)} collective-permute-done((bf16[48,5376]{1,0:T(8,128)(2,1)S(1)}, bf16[48,5376]{1,0:T(8,128)(2,1)S(1)}, u32[]{:S(2)}, u32[]{:S(2)}) %collective-permute-start.1) | collective-permute-done | bytes 516128 | tf_op jit(solution)/shard_map/ppermute | solution.py:24
  32.6 1.8 collective-permute-start.3
  34.5 1.6 collective-permute-start.4
  36.0 3.4 collective-permute-done.6
  44.4 10.5 %collective-permute-done.8 = bf16[48,5376]{1,0:T(8,128)(2,1)S(1)} collective-permute-done((bf16[48,5376]{1,0:T(8,128)(2,1)}, bf16[48,5376]{1,0:T(8,128)(2,1)S(1)}, u32[]{:S(2)}, u32[]{:S(2)}) %collective-permute-start.8) | collective-permute-done | bytes 516128 | tf_op jit(solution)/shard_map/ppermute | solution.py:24
  54.9 1.8 collective-permute-start.10
  56.7 3.1 collective-permute-done.7
  60.3 9.3 %collective-permute-done.14 = bf16[48,5376]{1,0:T(8,128)(2,1)S(1)} collective-permute-done((bf16[48,5376]{1,0:T(8,128)(2,1)}, bf16[48,5376]{1,0:T(8,128)(2,1)S(1)}, u32[]{:S(2)}, u32[]{:S(2)}) %collective-permute-start.14) | collective-permute-done | bytes 516128 | tf_op jit(solution)/shard_map/ppermute | solution.py:28
  69.7 1.6 collective-permute-start.15
  71.7 1.5 collective-permute-start.20
  73.3 2.6 pad_maximum_fusion.1.rest_2_.rest_3_
  75.9 5.9 %collective-permute-done.15 = bf16[48,5376]{1,0:T(8,128)(2,1)S(1)} collective-permute-done((bf16[48,5376]{1,0:T(8,128)(2,1)S(1)}, bf16[48,5376]{1,0:T(8,128)(2,1)S(1)}, u32[]{:S(2)}, u32[]{:S(2)}) %collective-permute-start.15) | collective-permute-done | bytes 516128 | tf_op jit(solution)/shard_map/ppermute | solution.py:24
  84.2 6.7 %collective-permute-done.20 = bf16[48,5376]{1,0:T(8,128)(2,1)S(1)} collective-permute-done((bf16[48,5376]{1,0:T(8,128)(2,1)S(1)}, bf16[48,5376]{1,0:T(8,128)(2,1)S(1)}, u32[]{:S(2)}, u32[]{:S(2)}) %collective-permute-start.20) | collective-permute-done | bytes 516128 | tf_op jit(solution)/shard_map/ppermute | solution.py:28
  91.6 1.5 collective-permute-start.22
  93.2 21.4 %collective-permute-done.21 = bf16[48,5376]{1,0:T(8,128)(2,1)S(1)} collective-permute-done((bf16[48,5376]{1,0:T(8,128)(2,1)S(1)}, bf16[48,5376]{1,0:T(8,128)(2,1)S(1)}, u32[]{:S(2)}, u32[]{:S(2)}) %collective-permute-start.21) | collective-permute-done | bytes 516128 | tf_op jit(solution)/shard_map/ppermute | solution.py:24
  116.5 1.6 pad_maximum_fusion.2.rest_4_.rest_5_
  118.1 8.4 %collective-permute-done.23 = bf16[48,2688]{1,0:T(8,128)(2,1)S(1)} collective-permute-done((bf16[48,2688]{1,0:T(8,128)(2,1)S(1)}, bf16[48,2688]{1,0:T(8,128)(2,1)S(1)}, u32[]{:S(2)}, u32[]{:S(2)}) %collective-permute-start.23) | collective-permute-done | bytes 258080 | tf_op jit(solution)/shard_map/ppermute | solution.py:24
  127.2 1.6 pad_maximum_fusion.3.rest_6_.rest_7_
  129.0 4.2 collective-permute-done.25.rest_7_.rest_8_
  133.2 1.7 lay_extra.1
  136.3 1.7 slice.488
  138.1 2.1 fusion.57
  140.5 3.0 fusion.20
  143.9 9.7 %attn_forward.2 = (bf16[256,2304]{1,0:T(8,128)(2,1)S(1)}, bf16[256,768]{1,0:T(8,128)(2,1)S(1)}, f32[256,768]{1,0:T(8,128)S(1)}) custom-call(f32[256,768]{1,0:T(8,128)S(1)} %add_add_fusion.hidden_ref, f32[1,9984]{1,0:T(1,128)S(1)} %broadcast_in_dim.132.row_ref, s32[256,1]{1,0:T(8,128)S(1)} %copy.82.down_docs, s32[1,256]{1,0:T(1,128)S(1)} %copy-done.9, ...), custom_call_target="tpu_custom_call" | custom-call | flops 1 | bytes 1 | tf_op jit(solution)/shard_map/attn_forward/pallas_call | solution.py:197
  154.6 7.1 %mlp_forward.1.hidden_ref = f32[256,768]{1,0:T(8,128)S(1)} custom-call(f32[256,768]{1,0:T(8,128)S(1)} %get-tuple-element.100.middle_ref, f32[1,9984]{1,0:T(1,128)S(1)} %broadcast_in_dim.132.row_ref, bf16[4,48,5376]{2,1,0:T(8,128)(2,1)S(1)} %pad_maximum_fusion.rest_0_.rest_1_, bf16[4,48,5376]{2,1,0:T(8,128)(2,1)} %collective-permute-done.5.rest_1_.rest_2_, ...), custom_call_target="tpu_custom_call" | custom-call | flops 1 | bytes 1 | tf_op jit(solution)/shard_map/mlp_forward/pallas_call | solution.py:235
  161.8 3.0 fusion.21
  164.8 9.2 %attn_forward.3 = (bf16[256,2304]{1,0:T(8,128)(2,1)S(1)}, bf16[256,768]{1,0:T(8,128)(2,1)S(1)}, f32[256,768]{1,0:T(8,128)S(1)}) custom-call(f32[256,768]{1,0:T(8,128)S(1)} %mlp_forward.1.hidden_ref, f32[1,9984]{1,0:T(1,128)S(1)} %broadcast_in_dim.133.row_ref, s32[256,1]{1,0:T(8,128)S(1)} %copy.82.down_docs, s32[1,256]{1,0:T(1,128)S(1)} %copy-done.9, ...), custom_call_target="tpu_custom_call" | custom-call | flops 1 | bytes 1 | tf_op jit(solution)/shard_map/attn_forward/pallas_call | solution.py:197
  174.1 15.4 %mlp_backward.2 = (bf16[16,48,3072]{2,1,0:T(8,128)(2,1)}, bf16[16,48,3072]{2,1,0:T(8,128)(2,1)}, f32[256,768]{1,0:T(8,128)S(1)}, f32[1,5376]{1,0:T(1,128)S(1)}, bf16[256,768]{1,0:T(8,128)(2,1)}) custom-call(f32[256,768]{1,0:T(8,128)S(1)} %get-tuple-element.101.middle_ref, bf16[256,768]{1,0:T(8,128)(2,1)S(1)} %copy-done.8, ...), custom_call_target="tpu_custom_call" | custom-call | flops 1 | bytes 1 | tf_op jit(solution)/shard_map/mlp_backward/pallas_call | solution.py:338
  190.2 15.0 %attn_backward.2 = (bf16[16,48,1536]{2,1,0:T(8,128)(2,1)}, bf16[16,48,1536]{2,1,0:T(8,128)(2,1)}, f32[256,768]{1,0:T(8,128)S(1)}, f32[1,3840]{1,0:T(1,128)S(1)}) custom-call(f32[256,768]{1,0:T(8,128)S(1)} %mlp_forward.1.hidden_ref, f32[256,768]{1,0:T(8,128)S(1)} %get-tuple-element.103.mid_ref, bf16[256,2304]{1,0:T(8,128)(2,1)S(1)} %get-tuple-element.104.packed_ref, ...), custom_call_target="tpu_custom_call" | custom-call | flops 1 | bytes 1 | tf_op jit(solution)/shard_map/attn_backward/pallas_call | solution.py:464
  206.5 2.3 fusion.26
  210.0 2.1 add_bitcast_fusion.3
  215.4 4.8 %add_bitcast_fusion = (f32[4,48,3072]{2,1,0:T(8,128)}, f32[4,48,3072]{2,1,0:T(8,128)S(1)}, f32[4,48,3072]{2,1,0:T(8,128)S(1)}) fusion(bf16[4,4,48,3072]{3,2,1,0:T(8,128)(2,1)} %bitcast.32, bf16[4,4,48,3072]{3,2,1,0:T(8,128)(2,1)S(1)} %bitcast.361), kind=kLoop, calls=%fused_computation.27 | loop fusion | flops 5308416 | bytes 14155776 | tf_op jit(solution)/shard_map/add | solution.py:587
  220.1 12.2 %mlp_backward.3 = (bf16[16,48,3072]{2,1,0:T(8,128)(2,1)}, bf16[16,48,3072]{2,1,0:T(8,128)(2,1)}, f32[256,768]{1,0:T(8,128)S(1)}, f32[1,5376]{1,0:T(1,128)S(1)}) custom-call(f32[256,768]{1,0:T(8,128)S(1)} %copy-done.5, f32[256,768]{1,0:T(8,128)S(1)} %get-tuple-element.116.grad_ref, f32[1,9984]{1,0:T(1,128)S(1)} %broadcast_in_dim.132.row_ref, ...), custom_call_target="tpu_custom_call" | custom-call | flops 1 | bytes 1 | tf_op jit(solution)/shard_map/mlp_backward/pallas_call | solution.py:338
  232.4 2.7 collective-permute-done.28
  236.3 2.8 fusion.11
  239.1 2.8 fusion.10
  244.0 18.0 %attn_backward.3 = (bf16[16,48,2304]{2,1,0:T(8,128)(2,1)}, bf16[16,48,2304]{2,1,0:T(8,128)(2,1)}, f32[256,768]{1,0:T(8,128)}, f32[1,3840]{1,0:T(1,128)S(1)}) custom-call(f32[256,768]{1,0:T(8,128)S(1)} %copy-done.3, f32[256,768]{1,0:T(8,128)S(1)} %get-tuple-element.127.mid_ref, bf16[256,2304]{1,0:T(8,128)(2,1)S(1)} %copy-done.7, ...), custom_call_target="tpu_custom_call" | custom-call | flops 1 | bytes 1 | tf_op jit(solution)/shard_map/attn_backward/pallas_call | solution.py:464
  262.2 2.8 fusion.25
  265.0 2.8 fusion.24
  270.5 2.2 fusion.33
  272.7 10.7 %collective-permute-done.30 = bf16[4,48,4608]{2,1,0:T(8,128)(2,1)} collective-permute-done((bf16[4,48,4608]{2,1,0:T(8,128)(2,1)}, bf16[4,48,4608]{2,1,0:T(8,128)(2,1)}, u32[]{:S(2)}, u32[]{:S(2)}) %collective-permute-start.30) | collective-permute-done | bytes 1769504 | tf_op jit(solution)/shard_map/ppermute | solution.py:24
  285.6 2.8 fusion.12
  288.4 11.4 %collective-permute-done.34 = bf16[4,48,1536]{2,1,0:T(8,128)(2,1)S(1)} collective-permute-done((bf16[4,48,1536]{2,1,0:T(8,128)(2,1)S(1)}, bf16[4,48,1536]{2,1,0:T(8,128)(2,1)S(1)}, u32[]{:S(2)}, u32[]{:S(2)}) %collective-permute-start.34) | collective-permute-done | bytes 589856 | tf_op jit(solution)/shard_map/ppermute | solution.py:24
  300.4 2.7 fusion.14
  303.9 1.5 collective-permute-start.37
  305.5 5.6 %collective-permute-start.40 = (bf16[48,4608]{1,0:T(8,128)(2,1)S(1)}, bf16[48,4608]{1,0:T(8,128)(2,1)S(1)}, u32[]{:S(2)}, u32[]{:S(2)}) collective-permute-start(bf16[48,4608]{1,0:T(8,128)(2,1)S(1)} %get-tuple-element.208), channel_id=1, source_target_pairs={{0,8},{1,9},{2,10},{3,11},{4,12},{5,13},{6,14},{7,15},{8,0},{9,1},... | collective-permute-start | bytes 1327112 | tf_op jit(solution)/shard_map/ppermute | solution.py:24
  311.1 2.9 collective-permute-start.41
  315.7 14.8 %collective-permute-done.36 = bf16[4,48,3072]{2,1,0:T(8,128)(2,1)S(1)} collective-permute-done((bf16[4,48,3072]{2,1,0:T(8,128)(2,1)S(1)}, bf16[4,48,3072]{2,1,0:T(8,128)(2,1)S(1)}, u32[]{:S(2)}, u32[]{:S(2)}) %collective-permute-start.36) | collective-permute-done | bytes 1179680 | tf_op jit(solution)/shard_map/ppermute | solution.py:24
  333.4 2.0 fusion.13
  335.4 8.7 %collective-permute-done.41 = bf16[48,4608]{1,0:T(8,128)(2,1)S(1)} collective-permute-done((bf16[48,4608]{1,0:T(8,128)(2,1)S(1)}, bf16[48,4608]{1,0:T(8,128)(2,1)S(1)}, u32[]{:S(2)}, u32[]{:S(2)}) %collective-permute-start.41) | collective-permute-done | bytes 442400 | tf_op jit(solution)/shard_map/ppermute | solution.py:24
  345.0 2.0 fusion.16
  347.5 1.7 collective-permute-start.44
  350.2 8.2 %collective-permute-start.45 = (bf16[48,3072]{1,0:T(8,128)(2,1)}, bf16[48,3072]{1,0:T(8,128)(2,1)}, u32[]{:S(2)}, u32[]{:S(2)}) collective-permute-start(bf16[48,3072]{1,0:T(8,128)(2,1)} %get-tuple-element.211), channel_id=1, source_target_pairs={{0,8},{1,9},{2,10},{3,11},{4,12},{5,13},{6,14},{7,15},{8,0},{9,1},... | collective-permute-start | bytes 884744 | tf_op jit(solution)/shard_map/ppermute | solution.py:24
  358.4 1.9 collective-permute-start.46
  361.8 5.3 %collective-permute-done.45 = bf16[48,3072]{1,0:T(8,128)(2,1)} collective-permute-done((bf16[48,3072]{1,0:T(8,128)(2,1)}, bf16[48,3072]{1,0:T(8,128)(2,1)}, u32[]{:S(2)}, u32[]{:S(2)}) %collective-permute-start.45) | collective-permute-done | bytes 294944 | tf_op jit(solution)/shard_map/ppermute | solution.py:24
  367.1 14.3 %collective-permute-done.46 = bf16[48,3072]{1,0:T(8,128)(2,1)} collective-permute-done((bf16[48,3072]{1,0:T(8,128)(2,1)}, bf16[48,3072]{1,0:T(8,128)(2,1)}, u32[]{:S(2)}, u32[]{:S(2)}) %collective-permute-start.46) | collective-permute-done | bytes 294944 | tf_op jit(solution)/shard_map/ppermute | solution.py:24
  385.6 2.4 fusion.18
  388.8 3.7 collective-permute-start.50
  392.6 1.8 collective-permute-start.51
  401.5 1.8 stack_reshape.3
  408.5 1.9 collective-permute-done.51
  (335 shorter events, 71.9 us)
Async XLA Ops:
  7.2 157.6 %all-gather.2.cloned.1.call-start = ((), (), s32[]{:S(2)}) async-start(), calls=%async_computation | async-start | bytes 14598144 | tf_op jit(solution)/shard_map/all_gather | solution.py:745
  12.6 1.7 collective-permute-start
  14.5 18.1 %collective-permute-start.1 = (bf16[48,5376]{1,0:T(8,128)(2,1)S(1)}, bf16[48,5376]{1,0:T(8,128)(2,1)S(1)}, u32[]{:S(2)}, u32[]{:S(2)}) collective-permute-start(bf16[48,5376]{1,0:T(8,128)(2,1)S(1)} %constant_dynamic-update-slice_fusion.2), channel_id=1, source_target_pairs={{0,2},{1,3},{2,0},{3,1},{4,6},{5,7},{6,4},{7,5},{8,10},{9,11},{10,... | collective-permute-start | bytes 1548296 | tf_op jit(solution)/shard_map/ppermute | solution.py:24
  17.4 17.0 %collective-permute-start.2 = (bf16[48,5376]{1,0:T(8,128)(2,1)S(1)}, bf16[48,5376]{1,0:T(8,128)(2,1)S(1)}, u32[]{:S(2)}, u32[]{:S(2)}) collective-permute-start(bf16[48,5376]{1,0:T(8,128)(2,1)S(1)} %constant_dynamic-update-slice_fusion.2), channel_id=1, source_target_pairs={{0,4},{1,5},{2,6},{3,7},{4,0},{5,1},{6,2},{7,3},{8,12},{9,13},{10,... | collective-permute-start | bytes 1548296 | tf_op jit(solution)/shard_map/ppermute | solution.py:24
  18.9 20.6 %collective-permute-start.6 = (bf16[48,5376]{1,0:T(8,128)(2,1)S(1)}, bf16[48,5376]{1,0:T(8,128)(2,1)}, u32[]{:S(2)}, u32[]{:S(2)}) collective-permute-start(bf16[48,5376]{1,0:T(8,128)(2,1)S(1)} %constant_dynamic-update-slice_fusion.2), channel_id=1, source_target_pairs={{0,8},{1,9},{2,10},{3,11},{4,12},{5,13},{6,14},{7,15},{8,0},{9,1},... | collective-permute-start | bytes 1548296 | tf_op jit(solution)/shard_map/ppermute | solution.py:24
  20.5 19.8 %collective-permute-start.13 = (bf16[48,5376]{1,0:T(8,128)(2,1)S(1)}, bf16[48,5376]{1,0:T(8,128)(2,1)}, u32[]{:S(2)}, u32[]{:S(2)}) collective-permute-start(bf16[48,5376]{1,0:T(8,128)(2,1)S(1)} %constant_dynamic-update-slice_fusion.2), channel_id=1, source_target_pairs={{8,16},{9,17},{10,18},{11,19},{12,20},{13,21},{14,22},{15,23},{16,... | collective-permute-start | bytes 1548296 | tf_op jit(solution)/shard_map/ppermute | solution.py:28
  32.6 7.7 %collective-permute-start.3 = (bf16[48,2688]{1,0:T(8,128)(2,1)S(1)}, bf16[48,2688]{1,0:T(8,128)(2,1)S(1)}, u32[]{:S(2)}, u32[]{:S(2)}) collective-permute-start(bf16[48,2688]{1,0:T(8,128)(2,1)S(1)} %slice.612), channel_id=1, source_target_pairs={{0,4},{1,5},{2,6},{3,7},{4,0},{5,1},{6,2},{7,3},{8,12},{9,13},{10,... | collective-permute-start | bytes 774152 | tf_op jit(solution)/shard_map/ppermute | solution.py:24
  34.5 8.5 %collective-permute-start.4 = (bf16[48,2688]{1,0:T(8,128)(2,1)S(1)}, bf16[48,2688]{1,0:T(8,128)(2,1)S(1)}, u32[]{:S(2)}, u32[]{:S(2)}) collective-permute-start(bf16[48,2688]{1,0:T(8,128)(2,1)S(1)} %slice.613), channel_id=1, source_target_pairs={{0,2},{1,3},{2,0},{3,1},{4,6},{5,7},{6,4},{7,5},{8,10},{9,11},{10,... | collective-permute-start | bytes 774152 | tf_op jit(solution)/shard_map/ppermute | solution.py:24
  39.5 20.8 %collective-permute-start.12 = (bf16[48,5376]{1,0:T(8,128)(2,1)}, bf16[48,5376]{1,0:T(8,128)(2,1)S(1)}, u32[]{:S(2)}, u32[]{:S(2)}) collective-permute-start(bf16[48,5376]{1,0:T(8,128)(2,1)} %collective-permute-done.6), channel_id=1, source_target_pairs={{8,16},{9,17},{10,18},{11,19},{12,20},{13,21},{14,22},{15,23},{16,... | collective-permute-start | bytes 1548296 | tf_op jit(solution)/shard_map/ppermute | solution.py:28
  40.2 14.7 %collective-permute-start.8 = (bf16[48,5376]{1,0:T(8,128)(2,1)}, bf16[48,5376]{1,0:T(8,128)(2,1)S(1)}, u32[]{:S(2)}, u32[]{:S(2)}) collective-permute-start(bf16[48,5376]{1,0:T(8,128)(2,1)} %collective-permute-done.6), channel_id=1, source_target_pairs={{0,4},{1,5},{2,6},{3,7},{4,0},{5,1},{6,2},{7,3},{8,12},{9,13},{10,... | collective-permute-start | bytes 1548296 | tf_op jit(solution)/shard_map/ppermute | solution.py:24
  40.3 19.5 %collective-permute-start.7 = (bf16[48,5376]{1,0:T(8,128)(2,1)}, bf16[48,5376]{1,0:T(8,128)(2,1)S(1)}, u32[]{:S(2)}, u32[]{:S(2)}) collective-permute-start(bf16[48,5376]{1,0:T(8,128)(2,1)} %collective-permute-done.6), channel_id=1, source_target_pairs={{0,2},{1,3},{2,0},{3,1},{4,6},{5,7},{6,4},{7,5},{8,10},{9,11},{10,... | collective-permute-start | bytes 1548296 | tf_op jit(solution)/shard_map/ppermute | solution.py:24
  40.4 29.3 %collective-permute-start.14 = (bf16[48,5376]{1,0:T(8,128)(2,1)}, bf16[48,5376]{1,0:T(8,128)(2,1)S(1)}, u32[]{:S(2)}, u32[]{:S(2)}) collective-permute-start(bf16[48,5376]{1,0:T(8,128)(2,1)} %collective-permute-done.13), channel_id=1, source_target_pairs={{8,0},{9,1},{10,2},{11,3},{12,4},{13,5},{14,6},{15,7},{16,24},{17,... | collective-permute-start | bytes 1548296 | tf_op jit(solution)/shard_map/ppermute | solution.py:28
  44.3 110.3 %copy-start = (bf16[4,48,5376]{2,1,0:T(8,128)(2,1)}, bf16[4,48,5376]{2,1,0:T(8,128)(2,1)S(1)}, u32[]{:S(2)}) copy-start(bf16[4,48,5376]{2,1,0:T(8,128)(2,1)S(1)} %pad_maximum_fusion.rest_0_.rest_1_) | copy-start | bytes 6193156
  44.3 84.7 %collective-permute-start.5 = (bf16[4,48,5376]{2,1,0:T(8,128)(2,1)S(1)}, bf16[4,48,5376]{2,1,0:T(8,128)(2,1)}, u32[]{:S(2)}, u32[]{:S(2)}) collective-permute-start(bf16[4,48,5376]{2,1,0:T(8,128)(2,1)S(1)} %pad_maximum_fusion.rest_0_.rest_1_), channel_id=1, source_target_pairs={{0,1},{1,0},{2,3},{3,2},{4,5},{5,4},{6,7},{7,6},{8,9},{9,8},{10,11... | collective-permute-start | bytes 6193160 | tf_op jit(solution)/shard_map/ppermute | solution.py:24
  54.9 16.8 %collective-permute-start.10 = (bf16[48,2688]{1,0:T(8,128)(2,1)S(1)}, bf16[48,2688]{1,0:T(8,128)(2,1)S(1)}, u32[]{:S(2)}, u32[]{:S(2)}) collective-permute-start(bf16[48,2688]{1,0:T(8,128)(2,1)S(1)} %slice.615), channel_id=1, source_target_pairs={{0,2},{1,3},{2,0},{3,1},{4,6},{5,7},{6,4},{7,5},{8,10},{9,11},{10,... | collective-permute-start | bytes 774152 | tf_op jit(solution)/shard_map/ppermute | solution.py:24
  59.8 13.5 %collective-permute-start.9 = (bf16[48,2688]{1,0:T(8,128)(2,1)S(1)}, bf16[48,2688]{1,0:T(8,128)(2,1)S(1)}, u32[]{:S(2)}, u32[]{:S(2)}) collective-permute-start(bf16[48,2688]{1,0:T(8,128)(2,1)S(1)} %slice.614), channel_id=1, source_target_pairs={{0,4},{1,5},{2,6},{3,7},{4,0},{5,1},{6,2},{7,3},{8,12},{9,13},{10,... | collective-permute-start | bytes 774152 | tf_op jit(solution)/shard_map/ppermute | solution.py:24
  69.7 12.2 %collective-permute-start.15 = (bf16[48,5376]{1,0:T(8,128)(2,1)S(1)}, bf16[48,5376]{1,0:T(8,128)(2,1)S(1)}, u32[]{:S(2)}, u32[]{:S(2)}) collective-permute-start(bf16[48,5376]{1,0:T(8,128)(2,1)S(1)} %broadcast_select_fusion.1), channel_id=1, source_target_pairs={{0,2},{1,3},{2,0},{3,1},{4,6},{5,7},{6,4},{7,5},{8,10},{9,11},{10,... | collective-permute-start | bytes 1548296 | tf_op jit(solution)/shard_map/ppermute | solution.py:24
  71.3 11.9 %collective-permute-start.16 = (bf16[48,5376]{1,0:T(8,128)(2,1)S(1)}, bf16[48,5376]{1,0:T(8,128)(2,1)S(1)}, u32[]{:S(2)}, u32[]{:S(2)}) collective-permute-start(bf16[48,5376]{1,0:T(8,128)(2,1)S(1)} %broadcast_select_fusion.1), channel_id=1, source_target_pairs={{0,4},{1,5},{2,6},{3,7},{4,0},{5,1},{6,2},{7,3},{8,12},{9,13},{10,... | collective-permute-start | bytes 1548296 | tf_op jit(solution)/shard_map/ppermute | solution.py:24
  71.7 19.2 %collective-permute-start.20 = (bf16[48,5376]{1,0:T(8,128)(2,1)S(1)}, bf16[48,5376]{1,0:T(8,128)(2,1)S(1)}, u32[]{:S(2)}, u32[]{:S(2)}) collective-permute-start(bf16[48,5376]{1,0:T(8,128)(2,1)S(1)} %collective-permute-done.12), channel_id=1, source_target_pairs={{8,0},{9,1},{10,2},{11,3},{12,4},{13,5},{14,6},{15,7},{16,24},{17,... | collective-permute-start | bytes 1548296 | tf_op jit(solution)/shard_map/ppermute | solution.py:28
  75.9 53.1 %collective-permute-start.11 = (bf16[4,48,5376]{2,1,0:T(8,128)(2,1)}, bf16[4,48,5376]{2,1,0:T(8,128)(2,1)}, u32[]{:S(2)}, u32[]{:S(2)}) collective-permute-start(bf16[4,48,5376]{2,1,0:T(8,128)(2,1)} %pad_maximum_fusion.1.rest_2_.rest_3_), channel_id=1, source_target_pairs={{0,1},{1,0},{2,3},{3,2},{4,5},{5,4},{6,7},{7,6},{8,9},{9,8},{10,11... | collective-permute-start | bytes 6193160 | tf_op jit(solution)/shard_map/ppermute | solution.py:24
  81.9 9.8 %collective-permute-start.17 = (bf16[48,2688]{1,0:T(8,128)(2,1)S(1)}, bf16[48,2688]{1,0:T(8,128)(2,1)S(1)}, u32[]{:S(2)}, u32[]{:S(2)}) collective-permute-start(bf16[48,2688]{1,0:T(8,128)(2,1)S(1)} %slice.616), channel_id=1, source_target_pairs={{0,4},{1,5},{2,6},{3,7},{4,0},{5,1},{6,2},{7,3},{8,12},{9,13},{10,... | collective-permute-start | bytes 774152 | tf_op jit(solution)/shard_map/ppermute | solution.py:24
  83.3 9.8 %collective-permute-start.18 = (bf16[48,2688]{1,0:T(8,128)(2,1)S(1)}, bf16[48,2688]{1,0:T(8,128)(2,1)S(1)}, u32[]{:S(2)}, u32[]{:S(2)}) collective-permute-start(bf16[48,2688]{1,0:T(8,128)(2,1)S(1)} %slice.617), channel_id=1, source_target_pairs={{0,2},{1,3},{2,0},{3,1},{4,6},{5,7},{6,4},{7,5},{8,10},{9,11},{10,... | collective-permute-start | bytes 774152 | tf_op jit(solution)/shard_map/ppermute | solution.py:24
  91.0 23.6 %collective-permute-start.21 = (bf16[48,5376]{1,0:T(8,128)(2,1)S(1)}, bf16[48,5376]{1,0:T(8,128)(2,1)S(1)}, u32[]{:S(2)}, u32[]{:S(2)}) collective-permute-start(bf16[48,5376]{1,0:T(8,128)(2,1)S(1)} %broadcast_select_fusion), channel_id=1, source_target_pairs={{0,2},{1,3},{2,0},{3,1},{4,6},{5,7},{6,4},{7,5},{8,10},{9,11},{10,... | collective-permute-start | bytes 1548296 | tf_op jit(solution)/shard_map/ppermute | solution.py:24
  91.6 23.6 %collective-permute-start.22 = (bf16[48,5376]{1,0:T(8,128)(2,1)S(1)}, bf16[48,5376]{1,0:T(8,128)(2,1)S(1)}, u32[]{:S(2)}, u32[]{:S(2)}) collective-permute-start(bf16[48,5376]{1,0:T(8,128)(2,1)S(1)} %broadcast_select_fusion), channel_id=1, source_target_pairs={{0,4},{1,5},{2,6},{3,7},{4,0},{5,1},{6,2},{7,3},{8,12},{9,13},{10,... | collective-permute-start | bytes 1548296 | tf_op jit(solution)/shard_map/ppermute | solution.py:24
  114.6 11.9 %collective-permute-start.23 = (bf16[48,2688]{1,0:T(8,128)(2,1)S(1)}, bf16[48,2688]{1,0:T(8,128)(2,1)S(1)}, u32[]{:S(2)}, u32[]{:S(2)}) collective-permute-start(bf16[48,2688]{1,0:T(8,128)(2,1)S(1)} %slice.618), channel_id=1, source_target_pairs={{0,4},{1,5},{2,6},{3,7},{4,0},{5,1},{6,2},{7,3},{8,12},{9,13},{10,... | collective-permute-start | bytes 774152 | tf_op jit(solution)/shard_map/ppermute | solution.py:24
  115.2 11.9 %collective-permute-start.24 = (bf16[48,2688]{1,0:T(8,128)(2,1)S(1)}, bf16[48,2688]{1,0:T(8,128)(2,1)S(1)}, u32[]{:S(2)}, u32[]{:S(2)}) collective-permute-start(bf16[48,2688]{1,0:T(8,128)(2,1)S(1)} %slice.619), channel_id=1, source_target_pairs={{0,2},{1,3},{2,0},{3,1},{4,6},{5,7},{6,4},{7,5},{8,10},{9,11},{10,... | collective-permute-start | bytes 774152 | tf_op jit(solution)/shard_map/ppermute | solution.py:24
  118.1 10.9 %collective-permute-start.19 = (bf16[4,48,5376]{2,1,0:T(8,128)(2,1)}, bf16[4,48,5376]{2,1,0:T(8,128)(2,1)}, u32[]{:S(2)}, u32[]{:S(2)}) collective-permute-start(bf16[4,48,5376]{2,1,0:T(8,128)(2,1)} %pad_maximum_fusion.2.rest_4_.rest_5_), channel_id=1, source_target_pairs={{0,1},{1,0},{2,3},{3,2},{4,5},{5,4},{6,7},{7,6},{8,9},{9,8},{10,11... | collective-permute-start | bytes 6193160 | tf_op jit(solution)/shard_map/ppermute | solution.py:24
  128.8 4.5 %collective-permute-start.25 = (bf16[4,48,5376]{2,1,0:T(8,128)(2,1)}, bf16[4,48,5376]{2,1,0:T(8,128)(2,1)}, u32[]{:S(2)}, u32[]{:S(2)}) collective-permute-start(bf16[4,48,5376]{2,1,0:T(8,128)(2,1)} %pad_maximum_fusion.3.rest_6_.rest_7_), channel_id=1, source_target_pairs={{0,1},{1,0},{2,3},{3,2},{4,5},{5,4},{6,7},{7,6},{8,9},{9,8},{10,11... | collective-permute-start | bytes 6193160 | tf_op jit(solution)/shard_map/ppermute | solution.py:24
  189.6 15.6 %collective-permute-start.26 = (bf16[16,48,3072]{2,1,0:T(8,128)(2,1)}, bf16[16,48,3072]{2,1,0:T(8,128)(2,1)}, u32[]{:S(2)}, u32[]{:S(2)}) collective-permute-start(bf16[16,48,3072]{2,1,0:T(8,128)(2,1)} %get-tuple-element.107), channel_id=1, source_target_pairs={{0,1},{1,0},{2,3},{3,2},{4,5},{5,4},{6,7},{7,6},{8,9},{9,8},{10,11... | collective-permute-start | bytes 14155784 | tf_op jit(solution)/shard_map/ppermute | solution.py:24
  190.2 15.2 %copy-start.12 = (bf16[16,48,3072]{2,1,0:T(8,128)(2,1)S(1)}, bf16[16,48,3072]{2,1,0:T(8,128)(2,1)}, u32[]{:S(2)}) copy-start(bf16[16,48,3072]{2,1,0:T(8,128)(2,1)} %get-tuple-element.112) | copy-start | bytes 14155780
  205.2 4.8 %collective-permute-start.27 = (bf16[16,48,1536]{2,1,0:T(8,128)(2,1)}, bf16[16,48,1536]{2,1,0:T(8,128)(2,1)S(1)}, u32[]{:S(2)}, u32[]{:S(2)}) collective-permute-start(bf16[16,48,1536]{2,1,0:T(8,128)(2,1)} %get-tuple-element.110), channel_id=1, source_target_pairs={{0,1},{1,0},{2,3},{3,2},{4,5},{5,4},{6,7},{7,6},{8,9},{9,8},{10,11... | collective-permute-start | bytes 7077896 | tf_op jit(solution)/shard_map/ppermute | solution.py:24
  213.1 22.0 %collective-permute-start.28 = (bf16[4,48,2304]{2,1,0:T(8,128)(2,1)}, bf16[4,48,2304]{2,1,0:T(8,128)(2,1)}, u32[]{:S(2)}, u32[]{:S(2)}) collective-permute-start(bf16[4,48,2304]{2,1,0:T(8,128)(2,1)} %fusion.26), channel_id=1, source_target_pairs={{0,4},{1,5},{2,6},{3,7},{4,0},{5,1},{6,2},{7,3},{8,12},{9,13},{10,... | collective-permute-start | bytes 2654216 | tf_op jit(solution)/shard_map/ppermute | solution.py:24
  214.6 21.8 %collective-permute-start.29 = (bf16[4,48,2304]{2,1,0:T(8,128)(2,1)}, bf16[4,48,2304]{2,1,0:T(8,128)(2,1)}, u32[]{:S(2)}, u32[]{:S(2)}) collective-permute-start(bf16[4,48,2304]{2,1,0:T(8,128)(2,1)} %pad_maximum_fusion.4), channel_id=1, source_target_pairs={{0,2},{1,3},{2,0},{3,1},{4,6},{5,7},{6,4},{7,5},{8,10},{9,11},{10,... | collective-permute-start | bytes 2654216 | tf_op jit(solution)/shard_map/ppermute | solution.py:24
  241.9 28.6 %collective-permute-start.32 = (bf16[16,48,3072]{2,1,0:T(8,128)(2,1)}, bf16[16,48,3072]{2,1,0:T(8,128)(2,1)}, u32[]{:S(2)}, u32[]{:S(2)}) collective-permute-start(bf16[16,48,3072]{2,1,0:T(8,128)(2,1)} %get-tuple-element.140), channel_id=1, source_target_pairs={{0,1},{1,0},{2,3},{3,2},{4,5},{5,4},{6,7},{7,6},{8,9},{9,8},{10,11... | collective-permute-start | bytes 14155784 | tf_op jit(solution)/shard_map/ppermute | solution.py:24
  242.0 41.4 %collective-permute-start.30 = (bf16[4,48,4608]{2,1,0:T(8,128)(2,1)}, bf16[4,48,4608]{2,1,0:T(8,128)(2,1)}, u32[]{:S(2)}, u32[]{:S(2)}) collective-permute-start(bf16[4,48,4608]{2,1,0:T(8,128)(2,1)} %fusion.10), channel_id=1, source_target_pairs={{0,2},{1,3},{2,0},{3,1},{4,6},{5,7},{6,4},{7,5},{8,10},{9,11},{10,... | collective-permute-start | bytes 5308424 | tf_op jit(solution)/shard_map/ppermute | solution.py:24
  243.0 41.0 %collective-permute-start.31 = (bf16[4,48,4608]{2,1,0:T(8,128)(2,1)}, bf16[4,48,4608]{2,1,0:T(8,128)(2,1)}, u32[]{:S(2)}, u32[]{:S(2)}) collective-permute-start(bf16[4,48,4608]{2,1,0:T(8,128)(2,1)} %fusion.11), channel_id=1, source_target_pairs={{0,4},{1,5},{2,6},{3,7},{4,0},{5,1},{6,2},{7,3},{8,12},{9,13},{10,... | collective-permute-start | bytes 5308424 | tf_op jit(solution)/shard_map/ppermute | solution.py:24
  243.9 18.2 %copy-start.42 = (s32[9216]{0:T(1024)S(1)}, s32[9216]{0:T(1024)}, u32[]{:S(2)}) copy-start(s32[9216]{0:T(1024)} %constant.181) | copy-start | bytes 110596
  244.0 18.2 %copy-start.43 = (s32[9216]{0:T(1024)S(1)}, s32[9216]{0:T(1024)}, u32[]{:S(2)}) copy-start(s32[9216]{0:T(1024)} %constant.182) | copy-start | bytes 110596
  269.6 16.0 %copy-start.10 = (f32[4,48,3072]{2,1,0:T(8,128)S(1)}, f32[4,48,3072]{2,1,0:T(8,128)}, u32[]{:S(2)}) copy-start(f32[4,48,3072]{2,1,0:T(8,128)} %get-tuple-element.193) | copy-start | bytes 7077892
  269.6 16.0 %copy-start.11 = (f32[4,48,1536]{2,1,0:T(8,128)S(1)}, f32[4,48,1536]{2,1,0:T(8,128)}, u32[]{:S(2)}) copy-start(f32[4,48,1536]{2,1,0:T(8,128)} %get-tuple-element.202) | copy-start | bytes 3538948
  270.5 29.9 %slice-start = ((s8[4718592]{0:T(1024)(128)(4,1)}), s8[4194304]{0:T(1024)(128)(4,1)S(1)}, s32[]{:S(2)}) async-start(s8[4718592]{0:T(1024)(128)(4,1)} %bitcast.363), calls=%async_computation.1 | async-start | bytes 8388608
  284.1 30.0 %collective-permute-start.33 = (bf16[16,48,2304]{2,1,0:T(8,128)(2,1)}, bf16[16,48,2304]{2,1,0:T(8,128)(2,1)S(1)}, u32[]{:S(2)}, u32[]{:S(2)}) collective-permute-start(bf16[16,48,2304]{2,1,0:T(8,128)(2,1)} %bitcast_dynamic-update-slice_fusion), channel_id=1, source_target_pairs={{0,1},{1,0},{2,3},{3,2},{4,5},{5,4},{6,7},{7,6},{8,9},{9,8},{10,11... | collective-permute-start | bytes 10616840 | tf_op jit(solution)/shard_map/ppermute | solution.py:24
  284.1 15.7 %collective-permute-start.34 = (bf16[4,48,1536]{2,1,0:T(8,128)(2,1)S(1)}, bf16[4,48,1536]{2,1,0:T(8,128)(2,1)S(1)}, u32[]{:S(2)}, u32[]{:S(2)}) collective-permute-start(bf16[4,48,1536]{2,1,0:T(8,128)(2,1)S(1)} %get-tuple-element.144), channel_id=1, source_target_pairs={{0,4},{1,5},{2,6},{3,7},{4,0},{5,1},{6,2},{7,3},{8,12},{9,13},{10,... | collective-permute-start | bytes 1769480 | tf_op jit(solution)/shard_map/ppermute | solution.py:24
  285.0 15.5 %collective-permute-start.35 = (bf16[4,48,1536]{2,1,0:T(8,128)(2,1)S(1)}, bf16[4,48,1536]{2,1,0:T(8,128)(2,1)S(1)}, u32[]{:S(2)}, u32[]{:S(2)}) collective-permute-start(bf16[4,48,1536]{2,1,0:T(8,128)(2,1)S(1)} %get-tuple-element.145), channel_id=1, source_target_pairs={{0,2},{1,3},{2,0},{3,1},{4,6},{5,7},{6,4},{7,5},{8,10},{9,11},{10,... | collective-permute-start | bytes 1769480 | tf_op jit(solution)/shard_map/ppermute | solution.py:24
  300.4 15.1 %copy-start.15 = (bf16[16,48,2304]{2,1,0:T(8,128)(2,1)S(1)}, bf16[16,48,2304]{2,1,0:T(8,128)(2,1)}, u32[]{:S(2)}) copy-start(bf16[16,48,2304]{2,1,0:T(8,128)(2,1)} %bitcast_dynamic-update-slice_fusion.1) | copy-start | bytes 10616836
  303.2 27.3 %collective-permute-start.36 = (bf16[4,48,3072]{2,1,0:T(8,128)(2,1)S(1)}, bf16[4,48,3072]{2,1,0:T(8,128)(2,1)S(1)}, u32[]{:S(2)}, u32[]{:S(2)}) collective-permute-start(bf16[4,48,3072]{2,1,0:T(8,128)(2,1)S(1)} %get-tuple-element.151), channel_id=1, source_target_pairs={{0,2},{1,3},{2,0},{3,1},{4,6},{5,7},{6,4},{7,5},{8,10},{9,11},{10,... | collective-permute-start | bytes 3538952 | tf_op jit(solution)/shard_map/ppermute | solution.py:24
  303.9 27.1 %collective-permute-start.37 = (bf16[4,48,3072]{2,1,0:T(8,128)(2,1)S(1)}, bf16[4,48,3072]{2,1,0:T(8,128)(2,1)S(1)}, u32[]{:S(2)}, u32[]{:S(2)}) collective-permute-start(bf16[4,48,3072]{2,1,0:T(8,128)(2,1)S(1)} %get-tuple-element.152), channel_id=1, source_target_pairs={{0,4},{1,5},{2,6},{3,7},{4,0},{5,1},{6,2},{7,3},{8,12},{9,13},{10,... | collective-permute-start | bytes 3538952 | tf_op jit(solution)/shard_map/ppermute | solution.py:24
  305.5 29.9 %collective-permute-start.40 = (bf16[48,4608]{1,0:T(8,128)(2,1)S(1)}, bf16[48,4608]{1,0:T(8,128)(2,1)S(1)}, u32[]{:S(2)}, u32[]{:S(2)}) collective-permute-start(bf16[48,4608]{1,0:T(8,128)(2,1)S(1)} %get-tuple-element.208), channel_id=1, source_target_pairs={{0,8},{1,9},{2,10},{3,11},{4,12},{5,13},{6,14},{7,15},{8,0},{9,1},... | collective-permute-start | bytes 1327112 | tf_op jit(solution)/shard_map/ppermute | solution.py:24
  311.1 33.0 %collective-permute-start.41 = (bf16[48,4608]{1,0:T(8,128)(2,1)S(1)}, bf16[48,4608]{1,0:T(8,128)(2,1)S(1)}, u32[]{:S(2)}, u32[]{:S(2)}) collective-permute-start(bf16[48,4608]{1,0:T(8,128)(2,1)S(1)} %get-tuple-element.207), channel_id=1, source_target_pairs={{0,16},{1,17},{2,18},{3,19},{4,20},{5,21},{6,22},{7,23},{8,24},{9,... | collective-permute-start | bytes 1327112 | tf_op jit(solution)/shard_map/ppermute | solution.py:24
  314.1 31.0 %copy-start.14 = (bf16[16,48,2304]{2,1,0:T(8,128)(2,1)}, bf16[16,48,2304]{2,1,0:T(8,128)(2,1)S(1)}, u32[]{:S(2)}) copy-start(bf16[16,48,2304]{2,1,0:T(8,128)(2,1)S(1)} %collective-permute-done.33) | copy-start | bytes 10616836
  314.1 30.1 %collective-permute-start.42 = (bf16[48,4608]{1,0:T(8,128)(2,1)S(1)}, bf16[48,4608]{1,0:T(8,128)(2,1)S(1)}, u32[]{:S(2)}, u32[]{:S(2)}) collective-permute-start(bf16[48,4608]{1,0:T(8,128)(2,1)S(1)} %get-tuple-element.206), channel_id=1, source_target_pairs={{0,24},{1,25},{2,26},{3,27},{4,28},{5,29},{6,30},{7,31},{8,16},{9,... | collective-permute-start | bytes 1327112 | tf_op jit(solution)/shard_map/ppermute | solution.py:24
  331.0 13.1 %collective-permute-start.38 = (bf16[4,48,1152]{2,1,0:T(8,128)(2,1)S(1)}, bf16[4,48,1152]{2,1,0:T(8,128)(2,1)S(1)}, u32[]{:S(2)}, u32[]{:S(2)}) collective-permute-start(bf16[4,48,1152]{2,1,0:T(8,128)(2,1)S(1)} %get-tuple-element.153), channel_id=1, source_target_pairs={{0,4},{1,5},{2,6},{3,7},{4,0},{5,1},{6,2},{7,3},{8,12},{9,13},{10,... | collective-permute-start | bytes 1327112 | tf_op jit(solution)/shard_map/ppermute | solution.py:24
  332.4 12.6 %collective-permute-start.39 = (bf16[4,48,1152]{2,1,0:T(8,128)(2,1)S(1)}, bf16[4,48,1152]{2,1,0:T(8,128)(2,1)S(1)}, u32[]{:S(2)}, u32[]{:S(2)}) collective-permute-start(bf16[4,48,1152]{2,1,0:T(8,128)(2,1)S(1)} %get-tuple-element.154), channel_id=1, source_target_pairs={{0,2},{1,3},{2,0},{3,1},{4,6},{5,7},{6,4},{7,5},{8,10},{9,11},{10,... | collective-permute-start | bytes 1327112 | tf_op jit(solution)/shard_map/ppermute | solution.py:24
  347.0 34.4 %collective-permute-start.43 = (bf16[4,48,2304]{2,1,0:T(8,128)(2,1)}, bf16[4,48,2304]{2,1,0:T(8,128)(2,1)}, u32[]{:S(2)}, u32[]{:S(2)}) collective-permute-start(bf16[4,48,2304]{2,1,0:T(8,128)(2,1)} %get-tuple-element.164), channel_id=1, source_target_pairs={{0,2},{1,3},{2,0},{3,1},{4,6},{5,7},{6,4},{7,5},{8,10},{9,11},{10,... | collective-permute-start | bytes 2654216 | tf_op jit(solution)/shard_map/ppermute | solution.py:24
  347.5 33.8 %collective-permute-start.44 = (bf16[4,48,2304]{2,1,0:T(8,128)(2,1)}, bf16[4,48,2304]{2,1,0:T(8,128)(2,1)}, u32[]{:S(2)}, u32[]{:S(2)}) collective-permute-start(bf16[4,48,2304]{2,1,0:T(8,128)(2,1)} %get-tuple-element.165), channel_id=1, source_target_pairs={{0,4},{1,5},{2,6},{3,7},{4,0},{5,1},{6,2},{7,3},{8,12},{9,13},{10,... | collective-permute-start | bytes 2654216 | tf_op jit(solution)/shard_map/ppermute | solution.py:24
  350.2 16.9 %collective-permute-start.45 = (bf16[48,3072]{1,0:T(8,128)(2,1)}, bf16[48,3072]{1,0:T(8,128)(2,1)}, u32[]{:S(2)}, u32[]{:S(2)}) collective-permute-start(bf16[48,3072]{1,0:T(8,128)(2,1)} %get-tuple-element.211), channel_id=1, source_target_pairs={{0,8},{1,9},{2,10},{3,11},{4,12},{5,13},{6,14},{7,15},{8,0},{9,1},... | collective-permute-start | bytes 884744 | tf_op jit(solution)/shard_map/ppermute | solution.py:24
  358.4 22.9 %collective-permute-start.46 = (bf16[48,3072]{1,0:T(8,128)(2,1)}, bf16[48,3072]{1,0:T(8,128)(2,1)}, u32[]{:S(2)}, u32[]{:S(2)}) collective-permute-start(bf16[48,3072]{1,0:T(8,128)(2,1)} %get-tuple-element.210), channel_id=1, source_target_pairs={{0,16},{1,17},{2,18},{3,19},{4,20},{5,21},{6,22},{7,23},{8,24},{9,... | collective-permute-start | bytes 884744 | tf_op jit(solution)/shard_map/ppermute | solution.py:24
  360.3 21.0 %collective-permute-start.47 = (bf16[48,3072]{1,0:T(8,128)(2,1)}, bf16[48,3072]{1,0:T(8,128)(2,1)}, u32[]{:S(2)}, u32[]{:S(2)}) collective-permute-start(bf16[48,3072]{1,0:T(8,128)(2,1)} %get-tuple-element.209), channel_id=1, source_target_pairs={{0,24},{1,25},{2,26},{3,27},{4,28},{5,29},{6,30},{7,31},{8,16},{9,... | collective-permute-start | bytes 884744 | tf_op jit(solution)/shard_map/ppermute | solution.py:24
  388.8 19.7 %collective-permute-start.50 = (bf16[48,2304]{1,0:T(8,128)(2,1)}, bf16[48,2304]{1,0:T(8,128)(2,1)}, u32[]{:S(2)}, u32[]{:S(2)}) collective-permute-start(bf16[48,2304]{1,0:T(8,128)(2,1)} %get-tuple-element.214), channel_id=1, source_target_pairs={{0,8},{1,9},{2,10},{3,11},{4,12},{5,13},{6,14},{7,15},{8,0},{9,1},... | collective-permute-start | bytes 663560 | tf_op jit(solution)/shard_map/ppermute | solution.py:24
  392.6 17.9 %collective-permute-start.51 = (bf16[48,2304]{1,0:T(8,128)(2,1)}, bf16[48,2304]{1,0:T(8,128)(2,1)}, u32[]{:S(2)}, u32[]{:S(2)}) collective-permute-start(bf16[48,2304]{1,0:T(8,128)(2,1)} %get-tuple-element.213), channel_id=1, source_target_pairs={{0,16},{1,17},{2,18},{3,19},{4,20},{5,21},{6,22},{7,23},{8,24},{9,... | collective-permute-start | bytes 663560 | tf_op jit(solution)/shard_map/ppermute | solution.py:24
  394.4 16.1 %collective-permute-start.52 = (bf16[48,2304]{1,0:T(8,128)(2,1)}, bf16[48,2304]{1,0:T(8,128)(2,1)}, u32[]{:S(2)}, u32[]{:S(2)}) collective-permute-start(bf16[48,2304]{1,0:T(8,128)(2,1)} %get-tuple-element.212), channel_id=1, source_target_pairs={{0,24},{1,25},{2,26},{3,27},{4,28},{5,29},{6,30},{7,31},{8,16},{9,... | collective-permute-start | bytes 663560 | tf_op jit(solution)/shard_map/ppermute | solution.py:24
  395.9 2.0 collective-permute-start.49
  396.2 1.6 collective-permute-start.48
  411.9 1.4 collective-permute-start.53
  (37 other events, 150.7 us)
Sparse Core Ops, SparseCore 0:
  12.1 140.9 all-gather.1

commit v3 on v2

--- a/solution.py
+++ b/solution.py
@@ -56,59 +56,63 @@
 
 
 class Part:
-    def __init__(self, array, entries, first, own):
-        self.array, self.entries, self.first, self.own = array, entries, first, own
-
-
-def fetch(parts, refs, starts, targets, sems):
+    def __init__(self, array, entries, own):
+        self.array, self.entries, self.own = array, entries, own
+
+
+class Source:
+    def __init__(self, weights, starts):
+        self.weights, self.starts = weights, starts
+        self.natural = not isinstance(weights, list)
+        self.arrays = [weights] if self.natural else [part.array for part in weights]
+
+
+def fetch_parts(parts, refs, starts, targets, sems):
     index = lax.axis_index("dp")
     core, chip = index % 2, index // 2
     for part, ref in zip(parts, refs):
         half = core if part.own else 1 - core
-        last = part.first + part.array.shape[-1]
-        for name, target in targets.items():
-            begin = starts[name]
-            if name == "down":
-                pieces = [(begin + block * HALF, HALF, block) for block in range(4)]
-            else:
-                pieces = [(begin, target.shape[1] // 2, None)]
-            for start, width, block in pieces:
-                low, high = max(start, part.first), min(start + width, last)
-                if low >= high:
-                    continue
-                columns = pl.ds(pl.multiple_of(half * width + (low - start), 128), high - low)
-                for leading, code in part.entries:
-                    there = chip ^ code
+        for leading, code, first in part.entries:
+            last = first + part.array.shape[-1]
+            there = chip ^ code
+            for name, target in targets.items():
+                begin = starts[name]
+                if name == "down":
+                    pieces = [(begin + block * HALF, HALF, block) for block in range(4)]
+                else:
+                    pieces = [(begin, target.shape[1] // 2, None)]
+                for start, width, block in pieces:
+                    low, high = max(start, first), min(start + width, last)
+                    if low >= high:
+                        continue
+                    columns = pl.ds(pl.multiple_of(half * width + (low - start), 128), high - low)
                     row = there * SLAB if block is None else there * (4 * SLAB) + block * SLAB
                     pltpu.make_async_copy(
-                        ref.at[leading + (slice(None), pl.ds(low - part.first, high - low))],
+                        ref.at[leading + (slice(None), pl.ds(low - first, high - low))],
                         target.at[pl.ds(pl.multiple_of(row, SLAB), SLAB), columns],
                         sems[name],
                     ).start()
 
 
-NATURAL = {"qkv": 0, "out": 2304, "up": 3072, "down": 6144}
-
-
-def natural_pieces(array, name, whole):
-    if name == "down":
-        for block in range(4):
-            columns = pl.ds(NATURAL[name] + block * WIDTH, WIDTH)
-            yield array.at[:, columns], whole.at[pl.ds(block * WIDTH, WIDTH), :]
-    else:
-        yield array.at[:, pl.ds(NATURAL[name], whole.shape[1])], whole
-
-
-def start_fetch(weights, refs, starts, targets, sems):
-    if isinstance(weights, list):
-        return fetch(weights, refs, starts, targets, sems)
-    for name, target in targets.items():
-        for piece, place_of in natural_pieces(refs[0], name, target):
-            pltpu.make_async_copy(piece, place_of, sems[name]).start()
-
-
-def arrays_of(weights):
-    return [p.array for p in weights] if isinstance(weights, list) else [weights]
+def start_fetch(sources, refs, targets, sems):
+    for source in sources:
+        own, refs = refs[: len(source.arrays)], refs[len(source.arrays) :]
+        wanted = {name: targets[name] for name in source.starts if name in targets}
+        if not source.natural:
+            fetch_parts(source.weights, own, source.starts, wanted, sems)
+            continue
+        for name, target in wanted.items():
+            pieces = [(0, slice(None), target.shape[1])]
+            if name == "down":
+                pieces = [(b * WIDTH, pl.ds(b * WIDTH, WIDTH), WIDTH) for b in range(4)]
+            for shift, rows, width in pieces:
+                pltpu.make_async_copy(
+                    own[0].at[:, pl.ds(source.starts[name] + shift, width)], target.at[rows, :], sems[name]
+                ).start()
+
+
+def arrays_of(sources):
+    return [array for source in sources for array in source.arrays]
 
 
 def arrived(target, sem):
@@ -146,7 +150,7 @@
     scores = dot(query, keys, (1, 1)) * (1.0 / math.sqrt(HEAD_DIM))
     masked = jnp.where(same, scores, -1e30)
     expo = jnp.exp(masked - jnp.max(masked, axis=-1, keepdims=True))
-    return expo / jnp.sum(expo, axis=-1, keepdims=True)
+    return expo * (1.0 / jnp.sum(expo, axis=-1, keepdims=True))
 
 
 def head_lanes(count):
@@ -157,71 +161,55 @@
     return pl.ds(pl.multiple_of(block * WIDTH + pair * PAIR, PAIR), PAIR)
 
 
-def attn_forward(hidden, row, docs, weights, starts):
-    arrays = arrays_of(weights)
+def attn_steps(hidden, row_ref, docs_refs, packed_ref, mixed_ref, qkv_ref, out_ref, named):
+    unit, _ = unit_of(hidden)
+    normed = (unit * spot(row_ref, "gain_a") + spot(row_ref, "shift_a")).astype(BF)
+    arrived(qkv_ref, named["qkv"])
+    for block in range(3):
+        columns = slice(block * WIDTH, (block + 1) * WIDTH)
+        packed_ref[:, columns] = (
+            dot(normed, qkv_ref[:, columns], (1, 0))
+            + row_ref[:, BIAS_AT + block * WIDTH : BIAS_AT + (block + 1) * WIDTH]
+        ).astype(BF)
+    same = docs_refs[0][...] == docs_refs[1][...]
+    first_head = head_lanes(hidden.shape[0])
+    for pair in range(HEADS // 2):
+        query, keys, values = [packed_ref[:, pair_slice(pair, block)] for block in range(3)]
+        blank = jnp.zeros_like(query)
+        mixes = []
+        for own in (jnp.where(first_head, query, blank), jnp.where(first_head, blank, query)):
+            mixes.append(dot(softmax_rows(own, keys, same).astype(BF), values, (1, 0)))
+        mixed_ref[:, pair_slice(pair, 0)] = jnp.where(first_head, mixes[0], mixes[1]).astype(BF)
+    arrived(out_ref, named["out"])
+    return hidden + dot(mixed_ref[...], out_ref[...], (1, 0)) + spot(row_ref, "out_b")
+
+
+def layer_forward(hidden, row, docs, sources):
+    arrays = arrays_of(sources)
     tokens = hidden.shape[0]
+    names = ("qkv", "out", "up", "down")
 
     def body(hidden_ref, row_ref, down_docs, across_docs, *rest):
         refs, rest = rest[: len(arrays)], rest[len(arrays) :]
-        packed_ref, mixed_ref, middle_ref, qkv_ref, out_ref, sems = rest
-        targets = {"qkv": qkv_ref, "out": out_ref}
-        named = {"qkv": sems.at[0], "out": sems.at[1]}
-        start_fetch(weights, refs, starts, targets, named)
-        unit, _ = unit_of(hidden_ref[...])
-        normed = (unit * spot(row_ref, "gain_a") + spot(row_ref, "shift_a")).astype(BF)
-        arrived(qkv_ref, named["qkv"])
-        for block in range(3):
-            columns = slice(block * WIDTH, (block + 1) * WIDTH)
-            packed_ref[:, columns] = (
-                dot(normed, qkv_ref[:, columns], (1, 0))
-                + row_ref[:, BIAS_AT + block * WIDTH : BIAS_AT + (block + 1) * WIDTH]
-            ).astype(BF)
-        same = down_docs[...] == across_docs[...]
-        first_head = head_lanes(tokens)
-
-        def one_pair(pair, carry):
-            query = packed_ref[:, pair_slice(pair, 0)]
-            keys = packed_ref[:, pair_slice(pair, 1)]
-            values = packed_ref[:, pair_slice(pair, 2)]
-            blank = jnp.zeros_like(query)
-            mixes = []
-            for own in (jnp.where(first_head, query, blank), jnp.where(first_head, blank, query)):
-                mixes.append(dot(softmax_rows(own, keys, same).astype(BF), values, (1, 0)))
-            mixed_ref[:, pair_slice(pair, 0)] = jnp.where(first_head, mixes[0], mixes[1]).astype(BF)
-            return carry
-
-        lax.fori_loop(0, HEADS // 2, one_pair, 0)
-        arrived(out_ref, named["out"])
-        middle_ref[...] = hidden_ref[...] + dot(mixed_ref[...], out_ref[...], (1, 0)) + spot(row_ref, "out_b")
-
-    return pl.pallas_call(
-        body,
-        out_shape=[
-            jax.ShapeDtypeStruct((tokens, 3 * WIDTH), BF),
-            jax.ShapeDtypeStruct((tokens, WIDTH), BF),
-            jax.ShapeDtypeStruct((tokens, WIDTH), F32),
-        ],
-        in_specs=[WHOLE] * 4 + [ANY] * len(arrays),
-        out_specs=[WHOLE] * 3,
-        scratch_shapes=[pltpu.VMEM(SHAPES["qkv"], BF), pltpu.VMEM(SHAPES["out"], BF), pltpu.SemaphoreType.DMA((2,))],
-        compiler_params=pltpu.CompilerParams(vmem_limit_bytes=40 * 2**20),
-        cost_estimate=pl.CostEstimate(flops=1, bytes_accessed=1, transcendentals=1),
-        name="attn_forward",
-    )(hidden, row, docs.reshape(-1, 1), docs.reshape(1, -1), *arrays)
-
-
-def mlp_forward(middle, row, weights, starts):
-    arrays = arrays_of(weights)
-    tokens = middle.shape[0]
-
-    def body(middle_ref, row_ref, *rest):
-        refs, rest = rest[: len(arrays)], rest[len(arrays) :]
-        top_ref, up_ref, down_ref, sems = rest
-        named = {"up": sems.at[0], "down": sems.at[1]}
-        start_fetch(weights, refs, starts, {"up": up_ref, "down": down_ref}, named)
-        unit, _ = unit_of(middle_ref[...])
+        packed_ref, mixed_ref, middle_ref, top_ref = rest[:4]
+        targets, sems = dict(zip(names, rest[4:8])), rest[8]
+        named = {name: sems.at[n] for n, name in enumerate(names)}
+        start_fetch(sources, refs, targets, named)
+        middle = attn_steps(
+            hidden_ref[...],
+            row_ref,
+            (down_docs, across_docs),
+            packed_ref,
+            mixed_ref,
+            targets["qkv"],
+            targets["out"],
+            named,
+        )
+        middle_ref[...] = middle
+        unit, _ = unit_of(middle)
         normed = (unit * spot(row_ref, "gain_b") + spot(row_ref, "shift_b")).astype(BF)
-        total = middle_ref[...] + spot(row_ref, "down_b")
+        total = middle + spot(row_ref, "down_b")
+        up_ref, down_ref = targets["up"], targets["down"]
         arrived(up_ref, named["up"])
         arrived(down_ref, named["down"])
         for tile in range(4):
@@ -234,14 +222,19 @@
 
     return pl.pallas_call(
         body,
-        out_shape=jax.ShapeDtypeStruct((tokens, WIDTH), F32),
-        in_specs=[WHOLE] * 2 + [ANY] * len(arrays),
-        out_specs=WHOLE,
-        scratch_shapes=[pltpu.VMEM(SHAPES["up"], BF), pltpu.VMEM(SHAPES["down"], BF), pltpu.SemaphoreType.DMA((2,))],
-        compiler_params=pltpu.CompilerParams(vmem_limit_bytes=40 * 2**20),
+        out_shape=[
+            jax.ShapeDtypeStruct((tokens, 3 * WIDTH), BF),
+            jax.ShapeDtypeStruct((tokens, WIDTH), BF),
+            jax.ShapeDtypeStruct((tokens, WIDTH), F32),
+            jax.ShapeDtypeStruct((tokens, WIDTH), F32),
+        ],
+        in_specs=[WHOLE] * 4 + [ANY] * len(arrays),
+        out_specs=[WHOLE] * 4,
+        scratch_shapes=[pltpu.VMEM(SHAPES[name], BF) for name in names] + [pltpu.SemaphoreType.DMA((4,))],
+        compiler_params=pltpu.CompilerParams(vmem_limit_bytes=50 * 2**20),
         cost_estimate=pl.CostEstimate(flops=1, bytes_accessed=1, transcendentals=1),
-        name="mlp_forward",
-    )(middle, row, *arrays)
+        name="layer_forward",
+    )(hidden, row, docs.reshape(-1, 1), docs.reshape(1, -1), *arrays)
 
 
 def send_rows(source, rows, columns, targets, half, first, sem):
@@ -259,41 +252,54 @@
                 ).start()
 
 
-def mlp_backward(middle, grad_top, row, weights, starts, with_top):
-    natural = not isinstance(weights, list)
-    arrays = arrays_of(weights)
-    tokens = middle.shape[0]
-
-    def body(middle_ref, grad_ref, row_ref, *rest):
+def mlp_backward(hidden, grad_top, row, sources, docs=None):
+    natural = any(source.natural and "down" in source.starts for source in sources)
+    arrays = arrays_of(sources)
+    tokens = hidden.shape[0]
+    whole_layer = docs is not None
+    names = ("up", "down", "qkv", "out") if whole_layer else ("up", "down")
+    doc_operands = [docs.reshape(-1, 1), docs.reshape(1, -1)] if whole_layer else []
+
+    def body(hidden_ref, grad_ref, row_ref, *rest):
+        docs_refs, rest = rest[: len(doc_operands)], rest[len(doc_operands) :]
         refs, rest = rest[: len(arrays)], rest[len(arrays) :]
-        grads_ref, rest = rest[:2], rest[2:]
-        mid_ref, small_ref = rest[:2]
-        top_ref = rest[2] if with_top else None
-        up_ref, down_ref, up_stage, down_stage, sems = rest[-5:]
-        named = {"up": sems.at[0], "down": sems.at[1]}
-        tiles = [slice(tile * WIDTH, (tile + 1) * WIDTH) for tile in range(4)]
-        start_fetch(weights, refs, starts, {"up": up_ref, "down": down_ref}, named)
-        unit, inverse = unit_of(middle_ref[...])
-        normed = (unit * spot(row_ref, "gain_b") + spot(row_ref, "shift_b")).astype(BF)
+        grads_ref, (mid_ref, small_ref), rest = rest[:2], rest[2:4], rest[4:]
+        if whole_layer:
+            (packed_ref, mixed_ref, top_ref), rest = rest[:3], rest[3:]
+        targets, (up_stage, down_stage, sems) = dict(zip(names, rest[:-3])), rest[-3:]
+        named = {name: sems.at[n] for n, name in enumerate(names)}
+        up_sem, down_sem = sems.at[4], sems.at[5]
+        up_ref, down_ref = targets["up"], targets["down"]
+        start_fetch(sources, refs, targets, named)
+        middle = hidden_ref[...]
+        if whole_layer:
+            middle = attn_steps(
+                middle, row_ref, docs_refs, packed_ref, mixed_ref, targets["qkv"], targets["out"], named
+            )
+        unit, inverse = unit_of(middle)
+        normed = unit * spot(row_ref, "gain_b") + spot(row_ref, "shift_b")
+        normed_turned = normed.T.astype(BF)
+        normed = normed.astype(BF)
         grad_top_rows = grad_ref[...].astype(F32)
         grad_down = grad_top_rows.astype(BF)
         small_ref[:, HIDDEN : HIDDEN + WIDTH] = jnp.sum(grad_down.astype(F32), axis=0, keepdims=True)
         grad_nb = jnp.zeros((tokens, WIDTH), F32)
-        total = middle_ref[...] + spot(row_ref, "down_b") if with_top else None
+        total = middle + spot(row_ref, "down_b") if whole_layer else None
         arrived(up_ref, named["up"])
         arrived(down_ref, named["down"])
-        for tile, columns in enumerate(tiles):
+        for tile in range(4):
+            columns = slice(tile * WIDTH, (tile + 1) * WIDTH)
             lifted = dot(normed, up_ref[:, columns], (1, 0))
             lifted = lifted + row_ref[:, UP_AT + tile * WIDTH : UP_AT + (tile + 1) * WIDTH]
             active, slope = gelu_pair(lifted)
             active = active.astype(BF)
-            if with_top:
+            if whole_layer:
                 total = total + dot(active, down_ref[columns, :], (1, 0))
             grad_act = dot(grad_down, down_ref[columns, :], (1, 1))
             grad_lift = (grad_act * slope).astype(BF)
             small_ref[:, columns] = jnp.sum(grad_lift.astype(F32), axis=0, keepdims=True)
             grad_nb = grad_nb + dot(grad_lift, up_ref[:, columns], (1, 1))
-            up_stage[:, columns] = dot(normed, grad_lift, (0, 0)).astype(BF)
+            up_stage[:, columns] = dot(normed_turned, grad_lift, (1, 0)).astype(BF)
             down_stage[columns, :] = dot(active, grad_down, (0, 0)).astype(BF)
             send_rows(
                 up_stage,
@@ -302,7 +308,7 @@
                 grads_ref,
                 tile // 2,
                 tile % 2 * WIDTH,
-                sems.at[2],
+                up_sem,
             )
             if natural:
                 pieces = [(tile, [(there, tile * WIDTH + there * SLAB) for there in range(16)])]
@@ -318,38 +324,37 @@
                         grads_ref,
                         half,
                         4 * HALF + block * HALF,
-                        sems.at[3],
+                        down_sem,
                     )
-        if with_top:
+        if whole_layer:
             top_ref[...] = total.astype(BF)
         small_ref[:, HIDDEN + WIDTH : HIDDEN + 2 * WIDTH] = jnp.sum(grad_nb * unit, axis=0, keepdims=True)
         small_ref[:, HIDDEN + 2 * WIDTH :] = jnp.sum(grad_nb, axis=0, keepdims=True)
         mid_ref[...] = grad_top_rows + back_of_norm(grad_nb, unit, inverse, spot(row_ref, "gain_b"))
-        arrived(up_stage, sems.at[2])
-        arrived(down_stage, sems.at[3])
-
-    sums = [(16, SLAB, HIDDEN)] * 2
-    outs = [jax.ShapeDtypeStruct(shape, BF) for shape in sums] + [
+        arrived(up_stage, up_sem)
+        arrived(down_stage, down_sem)
+
+    outs = [jax.ShapeDtypeStruct((16, SLAB, HIDDEN), BF)] * 2 + [
         jax.ShapeDtypeStruct((tokens, WIDTH), F32),
         jax.ShapeDtypeStruct((1, HIDDEN + 3 * WIDTH), F32),
     ]
-    if with_top:
-        outs.append(jax.ShapeDtypeStruct((tokens, WIDTH), BF))
+    if whole_layer:
+        outs += [jax.ShapeDtypeStruct((tokens, count * WIDTH), BF) for count in (3, 1, 1)]
     return pl.pallas_call(
         body,
         out_shape=outs,
-        in_specs=[WHOLE] * 3 + [ANY] * len(arrays),
-        out_specs=[ANY] * len(sums) + [WHOLE] * (len(outs) - len(sums)),
-        scratch_shapes=[pltpu.VMEM(SHAPES["up"], BF), pltpu.VMEM(SHAPES["down"], BF)] * 2
-        + [pltpu.SemaphoreType.DMA((4,))],
-        compiler_params=pltpu.CompilerParams(vmem_limit_bytes=50 * 2**20),
+        in_specs=[WHOLE] * (3 + len(doc_operands)) + [ANY] * len(arrays),
+        out_specs=[ANY] * 2 + [WHOLE] * (len(outs) - 2),
+        scratch_shapes=[pltpu.VMEM(SHAPES[name], BF) for name in names + ("up", "down")]
+        + [pltpu.SemaphoreType.DMA((6,))],
+        compiler_params=pltpu.CompilerParams(vmem_limit_bytes=54 * 2**20),
         cost_estimate=pl.CostEstimate(flops=1, bytes_accessed=1, transcendentals=1),
-        name="mlp_backward",
-    )(middle, grad_top, row, *arrays)
-
-
-def attn_backward(hidden, grad_mid, packed, mixed, row, docs, weights, starts, steps):
-    arrays = arrays_of(weights)
+        name="top_layer" if whole_layer else "mlp_backward",
+    )(hidden, grad_top, row, *doc_operands, *arrays)
+
+
+def attn_backward(hidden, grad_mid, packed, mixed, row, docs, sources, steps):
+    arrays = arrays_of(sources)
     tokens = hidden.shape[0]
     scale = 1.0 / math.sqrt(HEAD_DIM)
 
@@ -361,7 +366,7 @@
         in_ref, small_ref = rest[:2]
         qkv_ref, out_ref, qkv_stage, out_stage, gm_ref, gp_ref, sems = rest[2:9]
         named = {"qkv": sems.at[0], "out": sems.at[1]}
-        start_fetch(weights, refs, starts, {"qkv": qkv_ref, "out": out_ref}, named)
+        start_fetch(sources, refs, {"qkv": qkv_ref, "out": out_ref}, named)
         unit, inverse = unit_of(hidden_ref[...])
         normed = (unit * spot(row_ref, "gain_a") + spot(row_ref, "shift_a")).astype(BF)
         grad_branch = mid_ref[...].astype(BF)
@@ -381,28 +386,26 @@
             values = packed_ref[:, pair_slice(pair, 2)]
             grad_mixed = gm_ref[:, pair_slice(pair, 0)]
             blank = jnp.zeros_like(query)
-            results = []
+            query_turned = query.astype(F32).T.astype(BF)
+            mixed_turned = grad_mixed.astype(F32).T.astype(BF)
+            by_query, by_key, by_value = [], [], []
             for head in range(2):
+                rows_of = slice(head * HEAD_DIM, (head + 1) * HEAD_DIM)
                 lanes = first_head if head == 0 else jnp.logical_not(first_head)
                 probs = softmax_rows(jnp.where(lanes, query, blank), keys, same)
                 low = probs.astype(BF)
                 grad_probs = dot(jnp.where(lanes, grad_mixed, blank), values, (1, 1))
                 grad_scores = probs * (grad_probs - jnp.sum(probs * grad_probs, axis=-1, keepdims=True))
                 scores_low = grad_scores.astype(BF)
-                results.append(
-                    (
-                        dot(scores_low, keys, (1, 0)) * scale,
-                        dot(scores_low, query, (0, 0)) * scale,
-                        dot(low, grad_mixed, (0, 0)),
-                    )
-                )
-            for block in range(3):
-                gp_ref[:, pair_slice(pair, block)] = jnp.where(
-                    first_head, results[0][block], results[1][block]
-                ).astype(BF)
+                by_query.append(dot(scores_low, keys, (1, 0)))
+                by_key.append(dot(query_turned[rows_of], scores_low, (1, 0)))
+                by_value.append(dot(mixed_turned[rows_of], low, (1, 0)))
+            gp_ref[:, pair_slice(pair, 0)] = (jnp.where(first_head, *by_query) * scale).astype(BF)
+            gp_ref[:, pair_slice(pair, 1)] = (jnp.concatenate(by_key, axis=0).T * scale).astype(BF)
+            gp_ref[:, pair_slice(pair, 2)] = jnp.concatenate(by_value, axis=0).T.astype(BF)
             return carry
 
-        lax.fori_loop(0, HEADS // 2, one_pair, 0)
+        lax.fori_loop(0, HEADS // 2, one_pair, 0, unroll=True)
         arrived(qkv_ref, named["qkv"])
         grad_na = jnp.zeros((tokens, WIDTH), F32)
         for block in range(3):
@@ -473,23 +476,23 @@
     )(*operands, *arrays)
 
 
-def lay_extra(parts, first):
+def lay_extra(source):
     def body(*rest):
-        refs, (extra_ref, sems) = rest[: len(parts)], rest[len(parts) :]
+        refs, (extra_ref, sems) = rest[: len(source.arrays)], rest[len(source.arrays) :]
         named = {"extra": sems.at[0]}
-        fetch(parts, refs, {"extra": first}, {"extra": extra_ref}, named)
+        start_fetch([source], refs, {"extra": extra_ref}, named)
         arrived(extra_ref, named["extra"])
 
     return pl.pallas_call(
         body,
         out_shape=jax.ShapeDtypeStruct(SHAPES["extra"], BF),
-        in_specs=[ANY] * len(parts),
+        in_specs=[ANY] * len(source.arrays),
         out_specs=WHOLE,
         scratch_shapes=[pltpu.SemaphoreType.DMA((1,))],
         compiler_params=pltpu.CompilerParams(vmem_limit_bytes=16 * 2**20),
         cost_estimate=pl.CostEstimate(flops=1, bytes_accessed=1, transcendentals=1),
         name="lay_extra",
-    )(*[p.array for p in parts])
+    )(*source.arrays)
 
 
 def is_middle():
@@ -581,6 +584,37 @@
 
 def direct_line(levels):
     return [swap(levels[k], ALONG_Z * k) for k in (1, 2, 3)]
+
+
+def half_line(levels):
+    return swap(levels[2:], MIDDLE)
+
+
+def line_end(levels, came):
+    return swap(total(levels[1], came[0]).astype(BF), ALONG_Z)
+
+
+def line_sum(levels, came, last):
+    return total(levels[0], came[1], last)
+
+
+def along_both(low, high):
+    return swap(low, ALONG_Y), swap(high, ALONG_X)
+
+
+def line_ends(levels):
+    return [swap_from(levels[k], ALONG_Z, (0, 3)) for k in (3, 2)]
+
+
+def line_middles(levels, ends):
+    return [
+        swap_from(total(levels[2], ends[0]).astype(BF), MIDDLE, (1, 2)),
+        swap_from(total(levels[3], ends[1]).astype(BF), MIDDLE, (1, 2)),
+    ]
+
+
+def line_last(levels, middles):
+    return swap(total(levels[1], middles[0]).astype(BF), ALONG_Z)
 
 
 def total(*values):
@@ -742,6 +776,7 @@
         {"qkv": qkv_weight[0], "out": out_weight[0], "up": up_weight[0], "down": down_weight[0]}, extra
     )
     starts = {"qkv": 0, "out": 1152, "up": 1536, "down": 3072, "extra": 4608}
+    upper_starts = {"qkv": 0, "out": 3 * WIDTH, "up": 4 * WIDTH, "down": 8 * WIDTH}
     upper = lax.all_gather(upper_share, "dp", axis=0, tiled=True)
 
     block1, block3_middle = line_first(lower_share)
@@ -752,10 +787,11 @@
     for distance, block in enumerate(blocks):
         by_x, by_y = along_each(block, block)
         plane = jnp.stack([block, by_x, by_y, jnp.concatenate(diagonal(by_x, by_y), axis=1)])
-        entries = [((step,), 4 * distance + step) for step in range(4)]
-        parts += [Part(plane, entries, 0, True), Part(swap(plane, CORE), entries, 0, False)]
-
-    all_extra = lay_extra(parts, starts["extra"])
+        entries = [((step,), 4 * distance + step, 0) for step in range(4)]
+        parts += [Part(plane, entries, True), Part(swap(plane, CORE), entries, False)]
+    source0, source1 = Source(parts, starts), Source(upper, upper_starts)
+
+    all_extra = lay_extra(source0)
     small_all = all_extra[32::SLAB].reshape(16, 2, 2, HALF).transpose(1, 0, 2, 3).reshape(2, TUNED, HALF)
     rows = [spread_smalls(small_all[layer], layer) for layer in range(2)]
     owner = steps // 32
@@ -767,31 +803,34 @@
     of_doc = [(docs == s)[:, None] for s in range(doc_count)]
     start = embedded.astype(F32) + sum(jnp.where(of_doc[s], doc_rows[s][None], 0.0) for s in range(doc_count))
 
-    packed0, mixed0, middle0 = attn_forward(start, rows[0], docs, parts, starts)
-    between = mlp_forward(middle0, rows[0], parts, starts)
-    packed1, mixed1, middle1 = attn_forward(between, rows[1], docs, upper, None)
-
-    kept_m, sent_m, mid1, small_mlp1, block_output = mlp_backward(middle1, cotangent, rows[1], upper, None, True)
+    start, rows = gate((start, rows))
+    packed0, mixed0, middle0, between = layer_forward(start, rows[0], docs, [source0])
+
+    kept_m, sent_m, mid1, small_mlp1, packed1, mixed1, block_output = mlp_backward(
+        between, cotangent, rows[1], [source1], docs
+    )
     came_m = swap(sent_m, CORE)
     kept_t, sent_t, in1, small_attn1 = attn_backward(
-        between, mid1, packed1, mixed1, rows[1], docs, upper, None, None
+        between, mid1, packed1, mixed1, rows[1], docs, [source1], None
     )
     in1, came_m, sent_t = gate((in1, came_m, sent_t))
+    sums_m = PlaneSums((kept_m, came_m))
+    in1, to_go, sent_t = gate((in1, sums_m.diagonals(), sent_t))
+    low_m = along_both(*to_go)
     came_t = swap(sent_t, CORE)
-    in1, came_t = gate((in1, came_t))
-    sums_a = PlaneSums((kept_m, came_m), (kept_t, came_t))
-    in1, to_go = gate((in1, sums_a.diagonals()))
-    low_a, high_a = swap(to_go[0], ALONG_Y), swap(to_go[1], ALONG_X)
-    kept_b, sent_b, mid0, small_mlp0 = mlp_backward(middle0, in1, rows[0], parts, starts, False)
-    mid0, low_a, high_a, sent_b = gate((mid0, low_a, high_a, sent_b))
-    mid0, to_go, sent_b, small_mlp1, small_attn1 = gate(
-        (mid0, sums_a.sides(low_a, high_a), sent_b, small_mlp1, small_attn1)
-    )
-    x_a, y_a = along_each(*to_go)
+    kept_b, sent_b, mid0, small_mlp0 = mlp_backward(middle0, in1, rows[0], [source0])
+    mid0, low_m, came_t, sent_b = gate((mid0, low_m, came_t, sent_b))
     came_b = swap(sent_b, CORE)
+    sums_t = PlaneSums((kept_t, came_t))
+    low_t = along_both(*sums_t.diagonals())
+    x_m = along_each(*sums_m.sides(*low_m))
+    mid0, to_go, small_mlp1, small_attn1 = gate((mid0, sums_t.sides(*low_t), small_mlp1, small_attn1))
+    x_t = along_each(*to_go)
     kept_c, sent_c, input_grad, small_attn0 = attn_backward(
-        start, mid0, packed0, mixed0, rows[0], docs, parts, starts, step_ids
-    )
+        start, mid0, packed0, mixed0, rows[0], docs, [source0], step_ids
+    )
+    input_grad, came_b, kept_c, sent_c, small_attn0 = gate((input_grad, came_b, kept_c, sent_c, small_attn0))
+    sums_b = PlaneSums((kept_b, came_b))
     small_grads = jnp.stack(
         [
             collect_smalls(jnp.concatenate([small_mlp0, small_attn0], axis=1), 0),
@@ -806,29 +845,37 @@
         )
         for v, side in ((kept_c, core), (sent_c, 1 - core))
     ]
-    sums_b = PlaneSums((kept_b, came_b))
-    input_grad, kept_c, sent_c, x_a, y_a, to_go = gate((input_grad, kept_c, sent_c, x_a, y_a, sums_b.diagonals()))
-    low_b, high_b = swap(to_go[0], ALONG_Y), swap(to_go[1], ALONG_X)
+    x_m, x_t, to_go, kept_c, sent_c = gate((x_m, x_t, sums_b.diagonals(), kept_c, sent_c))
+
+    low_b = along_both(*to_go)
     came_c = swap(sent_c, CORE)
-    levels_a = sums_a.levels(x_a, y_a)
-    low_b, high_b, levels_a = gate((low_b, high_b, levels_a))
-    to_go, levels_a = gate((sums_b.sides(low_b, high_b), levels_a))
-    x_b, y_b = along_each(*to_go)
-    back_a = direct_line(levels_a)
+    x_m, x_t, came_c = gate((x_m, x_t, came_c))
     sums_c = PlaneSums((kept_c, came_c))
-    x_b, y_b, to_go = gate((x_b, y_b, sums_c.diagonals()))
-    low_c, high_c = swap(to_go[0], ALONG_Y), swap(to_go[1], ALONG_X)
-    levels_b = sums_b.levels(x_b, y_b)
-    low_c, high_c, back_a, levels_b = gate((low_c, high_c, back_a, levels_b))
-    to_go, back_a, levels_b = gate((sums_c.sides(low_c, high_c), back_a, levels_b))
-    x_c, y_c = along_each(*to_go)
-    back_b = direct_line(levels_b)
-    x_c, y_c, back_b, back_a = gate((x_c, y_c, back_b, back_a))
-    levels_c = sums_c.levels(x_c, y_c)
-    back_c = direct_line(levels_c)
-    up_1, down_1, qkv_1, out_1 = own_rows(("up", "down_by_core", "qkv", "out"), total(levels_a[0], *back_a))
+    to_go = sums_c.diagonals()
+    low_c = along_both(*to_go)
+    levels_m = sums_m.levels(*x_m)
+    half_m = half_line(levels_m)
+    low_b, to_go = gate((low_b, to_go))
+    x_b = along_each(*sums_b.sides(*low_b))
+    low_c, half_m = gate((low_c, half_m))
+    x_c = along_each(*sums_c.sides(*low_c))
+    levels_t = sums_t.levels(*x_t)
+    half_t = half_line(levels_t)
+    levels_a = jnp.concatenate([levels_m, levels_t], axis=-1)
+    half_a = jnp.concatenate([half_m, half_t], axis=-1)
+    levels_b = sums_b.levels(*x_b)
+    half_b = half_line(levels_b)
+    levels_b, half_a = gate((levels_b, half_a))
+    last_a = line_end(levels_a, half_a)
+    half_b, last_a = gate((half_b, last_a))
+    last_b = line_end(levels_b, half_b)
+    levels_c = sums_c.levels(*x_c)
+    back_c = [swap(levels_c[k], ALONG_Z * k) for k in (1, 2, 3)]
+    up_1, down_1, qkv_1, out_1 = own_rows(
+        ("up", "down_by_core", "qkv", "out"), line_sum(levels_a, half_a, last_a)
+    )
     up_1 = up_1.reshape(24, 4, TUNED, 24).transpose(0, 2, 1, 3).reshape(24, HIDDEN)
-    up_0, down_0 = own_rows(("up", "down"), total(levels_b[0], *back_b))
+    up_0, down_0 = own_rows(("up", "down"), line_sum(levels_b, half_b, last_b))
     up, down = jnp.stack([up_0, up_1]), jnp.stack([down_0, down_1])
     up, down, qkv_1, out_1, back_c = gate((up, down, qkv_1, out_1, back_c))
     sum_c = total(levels_c[0], *back_c)

time: 431 us -> 410 us (0.951)
  waiting for transfers between devices: 162 us -> 150 us
  Pallas kernels: 88.4 us -> 78.5 us
  other arithmetic: 51.5 us -> 45.7 us
  local copies, waits for them, and re-layouts: 24.3 us -> 29.4 us
    ppermute x50 -> x53, waiting for transfers between devices: 146 us -> 135 us  [swap(): return lax.ppermute(value, 'dp', [(i, i ^ stride) for i in range(TUNED)])]
    add x6 -> x3, other arithmetic: 11.9 us -> 2.69 us  [total(): return sum((v.astype(F32) for v in values))]
    pallas_call x5 -> x3, Pallas kernels: 53.7 us -> 46.7 us  [the longest x2 34 us: mlp_backward(): pl.pallas_call(body, out_shape=outs, in_specs=[WHOLE] * (3 + len(doc_oper...]
    unnamed x104 -> x116, local copies, waits for them, and re-layouts: 4.43 us -> 10.2 us
    convert_element_type x2 -> x4, other arithmetic: 2.42 us -> 7.02 us  [diagonals(): self.pair(3, self.cut).astype(BF)]
    convert_element_type x3 -> x4, other arithmetic: 7.17 us -> 9.95 us  [levels(): return (self.pair(0) + total(by_x, by_y)).astype(BF)]
    ppermute x50 -> x53, starting transfers between devices: 63.5 us -> 64.8 us  [swap(): return lax.ppermute(value, 'dp', [(i, i ^ stride) for i in range(TUNED)])]
  transfers between devices with their start and end apart: 55 -> 58, of which waited for: 28 -> 27; matrix products, arithmetic and copies ran while one was open for 14% -> 17% of each run, Pallas kernels for 15% -> 15%
where the time goes in v3:
time: 410 us; the launch traced here: 403 us
  waiting for transfers between devices  150 us (37%)
  Pallas kernels  78.5 us (19%)
  starting transfers between devices  69.5 us (17%)
  other arithmetic  45.7 us (11%)
  local copies, waits for them, and re-layouts  29.4 us (7%)
  between operations  16.1 us (4%)
  matrix products  13.8 us (3%)
    ppermute x53, waiting for transfers between devices, swap(): return lax.ppermute(value, 'dp', [(i, i ^ stride) for i in range(TUNED)])  135 us
    ppermute x53, starting transfers between devices, swap(): return lax.ppermute(value, 'dp', [(i, i ^ stride) for i in range(TUNED)])  64.8 us
    pallas_call x2, Pallas kernels, mlp_backward(): pl.pallas_call(body, out_shape=outs, in_specs=[WHOLE] * (3 + len(doc_oper...  34 us
    pallas_call x2, Pallas kernels, attn_backward(): pl.pallas_call(body, out_shape=outs, in_specs=[WHOLE] * len(operands) + [...  29.5 us
    ppermute x4, waiting for transfers between devices, swap_from(): lax.ppermute(value, 'dp', [(i, i ^ stride) for i in range(TUNED) if i //...  14.9 us
    pallas_call x1, Pallas kernels, layer_forward(): pl.pallas_call(body, out_shape=[jax.ShapeDtypeStruct((tokens, 3 * WIDTH),...  12.7 us
    unnamed x116, local copies, waits for them, and re-layouts  10.2 us
    convert_element_type x4, other arithmetic, levels(): return (self.pair(0) + total(by_x, by_y)).astype(BF)  9.95 us
  transfers between devices with their start and end apart: 58, of which 27 were waited for; matrix products, arithmetic and copies ran while one was open for 17% of the time, Pallas kernels for 15%

profile of v3, /device:TPU:0, one launch (start us, length us, event | category | flops | bytes accessed | tf_op | source)
XLA Modules:
  0.0 403.4 jit_solution(7446191710518629399)
XLA Ops:
  15.3 3.0 collective-permute-start.2
  18.3 1.5 collective-permute-start.1
  19.8 1.6 collective-permute-start.6
  21.4 1.4 collective-permute-start.13
  22.8 10.7 %collective-permute-done.2 = bf16[48,5376]{1,0:T(8,128)(2,1)S(1)} collective-permute-done((bf16[48,5376]{1,0:T(8,128)(2,1)S(1)}, bf16[48,5376]{1,0:T(8,128)(2,1)S(1)}, u32[]{:S(2)}, u32[]{:S(2)}) %collective-permute-start.2) | collective-permute-done | bytes 516128 | tf_op jit(solution)/shard_map/ppermute | solution.py:24
  33.5 1.8 collective-permute-start.4
  35.3 1.6 collective-permute-start.3
  36.9 3.5 collective-permute-done.6
  45.3 14.4 %collective-permute-done.8 = bf16[48,5376]{1,0:T(8,128)(2,1)S(1)} collective-permute-done((bf16[48,5376]{1,0:T(8,128)(2,1)}, bf16[48,5376]{1,0:T(8,128)(2,1)S(1)}, u32[]{:S(2)}, u32[]{:S(2)}) %collective-permute-start.8) | collective-permute-done | bytes 516128 | tf_op jit(solution)/shard_map/ppermute | solution.py:24
  59.8 2.4 collective-permute-start.9
  62.3 8.2 %collective-permute-done.14 = bf16[48,5376]{1,0:T(8,128)(2,1)S(1)} collective-permute-done((bf16[48,5376]{1,0:T(8,128)(2,1)}, bf16[48,5376]{1,0:T(8,128)(2,1)S(1)}, u32[]{:S(2)}, u32[]{:S(2)}) %collective-permute-start.14) | collective-permute-done | bytes 516128 | tf_op jit(solution)/shard_map/ppermute | solution.py:28
  70.9 1.7 collective-permute-start.15
  74.0 2.6 pad_maximum_fusion.1.rest_2_.rest_3_
  76.5 3.5 collective-permute-done.16
  80.0 3.9 collective-permute-start.18
  85.0 6.8 %collective-permute-done.20 = bf16[48,5376]{1,0:T(8,128)(2,1)S(1)} collective-permute-done((bf16[48,5376]{1,0:T(8,128)(2,1)S(1)}, bf16[48,5376]{1,0:T(8,128)(2,1)S(1)}, u32[]{:S(2)}, u32[]{:S(2)}) %collective-permute-start.20) | collective-permute-done | bytes 516128 | tf_op jit(solution)/shard_map/ppermute | solution.py:28
  93.4 21.6 %collective-permute-done.22 = bf16[48,5376]{1,0:T(8,128)(2,1)S(1)} collective-permute-done((bf16[48,5376]{1,0:T(8,128)(2,1)S(1)}, bf16[48,5376]{1,0:T(8,128)(2,1)S(1)}, u32[]{:S(2)}, u32[]{:S(2)}) %collective-permute-start.22) | collective-permute-done | bytes 516128 | tf_op jit(solution)/shard_map/ppermute | solution.py:24
  116.0 2.3 collective-permute-start.23
  118.3 1.6 pad_maximum_fusion.2.rest_4_.rest_5_
  119.9 7.0 %collective-permute-done.24 = bf16[48,2688]{1,0:T(8,128)(2,1)S(1)} collective-permute-done((bf16[48,2688]{1,0:T(8,128)(2,1)S(1)}, bf16[48,2688]{1,0:T(8,128)(2,1)S(1)}, u32[]{:S(2)}, u32[]{:S(2)}) %collective-permute-start.24) | collective-permute-done | bytes 258080 | tf_op jit(solution)/shard_map/ppermute | solution.py:24
  128.2 1.6 pad_maximum_fusion.3.rest_6_.rest_7_
  130.0 4.2 %collective-permute-done.25.rest_7_.rest_8_ = bf16[4,48,5376]{2,1,0:T(8,128)(2,1)} collective-permute-done((bf16[4,48,5376]{2,1,0:T(8,128)(2,1)}, bf16[4,48,5376]{2,1,0:T(8,128)(2,1)}, u32[]{:S(2)}, u32[]{:S(2)}) %collective-permute-start.25) | collective-permute-done | bytes 2064416 | tf_op jit(solution)/shard_map/ppermute | solution.py:24
  134.2 2.2 lay_extra.1
  136.4 1.4 copy-done.1
  137.8 1.7 slice.503
  139.6 2.1 fusion.59
  142.0 3.0 fusion.21
  145.7 3.0 fusion.20
  149.1 12.7 %layer_forward.1 = (bf16[256,2304]{1,0:T(8,128)(2,1)S(1)}, bf16[256,768]{1,0:T(8,128)(2,1)S(1)}, f32[256,768]{1,0:T(8,128)S(1)}, f32[256,768]{1,0:T(8,128)S(1)}) custom-call(f32[256,768]{1,0:T(8,128)S(1)} %add_add_fusion.hidden_ref, f32[1,9984]{1,0:T(1,128)S(1)} %broadcast_in_dim.132.row_ref, s32[256,1]{1,0:T(8,128)S(1)} %copy.84.down_docs.rest_0_, ...), custom_call_target="tpu_custom_call" | custom-call | flops 1 | bytes 1 | tf_op jit(solution)/shard_map/layer_forward/pallas_call | solution.py:223
  164.4 19.5 %top_layer.1 = (bf16[16,48,3072]{2,1,0:T(8,128)(2,1)}, bf16[16,48,3072]{2,1,0:T(8,128)(2,1)}, f32[256,768]{1,0:T(8,128)}, f32[1,5376]{1,0:T(1,128)}, bf16[256,23...) custom-call(f32[256,768]{1,0:T(8,128)} %copy-done.4, bf16[256,768]{1,0:T(8,128)(2,1)} %grad_ref.1, ...), custom_call_target="tpu_custom_call" | custom-call | flops 1 | bytes 1 | tf_op jit(solution)/shard_map/top_layer/pallas_call | solution.py:343
  187.6 13.2 %attn_backward.2 = (bf16[16,48,1536]{2,1,0:T(8,128)(2,1)}, bf16[16,48,1536]{2,1,0:T(8,128)(2,1)}, f32[256,768]{1,0:T(8,128)S(1)}, f32[1,3840]{1,0:T(1,128)S(1)}) custom-call(f32[256,768]{1,0:T(8,128)S(1)} %copy-done.5, f32[256,768]{1,0:T(8,128)S(1)} %copy-done.9, bf16[256,2304]{1,0:T(8,128)(2,1)S(1)} %copy-done.6, bf16[256,768]{1,0:T(8,128)(2,1)S(1)} %copy-done.15, ...), custom_call_target="tpu_custom_call" | custom-call | flops 1 | bytes 1 | tf_op jit(solution)/shard_map/attn_backward/pallas_call | solution.py:467
  201.7 2.4 fusion.32
  204.2 1.8 collective-permute-start.27
  206.7 14.5 %mlp_backward.1 = (bf16[16,48,3072]{2,1,0:T(8,128)(2,1)}, bf16[16,48,3072]{2,1,0:T(8,128)(2,1)}, f32[256,768]{1,0:T(8,128)}, f32[1,5376]{1,0:T(1,128)}) custom-call(f32[256,768]{1,0:T(8,128)} %copy-done.7, f32[256,768]{1,0:T(8,128)} %copy-done.8, f32[1,9984]{1,0:T(1,128)} %copy-done.11, bf16[4,48,5376]{2,1,0:T(8,128)(2,1)} %copy-done, ...), custom_call_target="tpu_custom_call" | custom-call | flops 1 | bytes 1 | tf_op jit(solution)/shard_map/mlp_backward/pallas_call | solution.py:343
  222.3 1.4 fusion.43
  225.2 4.8 %fusion.14 = (bf16[4,48,3072]{2,1,0:T(8,128)(2,1)}, bf16[4,48,3072]{2,1,0:T(8,128)(2,1)}) fusion(bf16[4,4,48,3072]{3,2,1,0:T(8,128)(2,1)} %bitcast.380, bf16[4,4,48,3072]{3,2,1,0:T(8,128)(2,1)} %bitcast.377, bf16[4,48,1536]{2,1,0:T(8,128)(2,1)S(1)} %collective-permute-done.28, bf16[4,48,1536]{2,1,0:T(8,128)(2,1)S(1)} %collective-permute-done.27), kind=kLoop, calls=%fused_computation.24 | loop fusion | flops 7077888 | bytes 8257536 | tf_op jit(solution)/shard_map/convert_element_type | solution.py:649
  230.0 1.7 collective-permute-start.34
  233.2 1.7 collective-permute-done.30
  234.9 2.6 fusion.23
  237.7 2.9 fusion.27
  241.5 16.3 %attn_backward.3 = (bf16[16,48,2304]{2,1,0:T(8,128)(2,1)}, bf16[16,48,2304]{2,1,0:T(8,128)(2,1)}, f32[256,768]{1,0:T(8,128)}, f32[1,3840]{1,0:T(1,128)S(1)}) custom-call(f32[256,768]{1,0:T(8,128)S(1)} %add_add_fusion.hidden_ref, f32[256,768]{1,0:T(8,128)S(1)} %copy-done.10, bf16[256,2304]{1,0:T(8,128)(2,1)S(1)} %get-tuple-element.120.packed_ref, ...), custom_call_target="tpu_custom_call" | custom-call | flops 1 | bytes 1 | tf_op jit(solution)/shard_map/attn_backward/pallas_call | solution.py:467
  257.9 2.8 fusion.28
  263.4 3.0 fusion.34
  266.4 5.8 %collective-permute-done.35 = bf16[4,48,1536]{2,1,0:T(8,128)(2,1)} collective-permute-done((bf16[4,48,1536]{2,1,0:T(8,128)(2,1)}, bf16[4,48,1536]{2,1,0:T(8,128)(2,1)}, u32[]{:S(2)}, u32[]{:S(2)}) %collective-permute-start.35) | collective-permute-done | bytes 589856 | tf_op jit(solution)/shard_map/ppermute | solution.py:24
  273.7 5.0 %collective-permute-done.37 = bf16[16,48,2304]{2,1,0:T(8,128)(2,1)S(1)} collective-permute-done((bf16[16,48,2304]{2,1,0:T(8,128)(2,1)}, bf16[16,48,2304]{2,1,0:T(8,128)(2,1)S(1)}, u32[]{:S(2)}, u32[]{:S(2)}) %collective-permute-start.37) | collective-permute-done | bytes 3538976 | tf_op jit(solution)/shard_map/ppermute | solution.py:24
  278.7 3.2 fusion.22
  282.0 4.5 %collective-permute-start.47 = (bf16[2,48,1536]{2,1,0:T(8,128)(2,1)S(1)}, bf16[2,48,1536]{2,1,0:T(8,128)(2,1)S(1)}, u32[]{:S(2)}, u32[]{:S(2)}) collective-permute-start(bf16[2,48,1536]{2,1,0:T(8,128)(2,1)S(1)} %slice.690), channel_id=1, source_target_pairs={{0,24},{1,25},{2,26},{3,27},{4,28},{5,29},{6,30},{7,31},{8,16},{9,... | collective-permute-start | bytes 884744 | tf_op jit(solution)/shard_map/ppermute | solution.py:24
  286.5 3.1 fusion.13
  292.2 2.6 fusion.11
  296.2 7.1 %collective-permute-done.39 = bf16[4,48,1152]{2,1,0:T(8,128)(2,1)S(1)} collective-permute-done((bf16[4,48,1152]{2,1,0:T(8,128)(2,1)S(1)}, bf16[4,48,1152]{2,1,0:T(8,128)(2,1)S(1)}, u32[]{:S(2)}, u32[]{:S(2)}) %collective-permute-start.39) | collective-permute-done | bytes 442400 | tf_op jit(solution)/shard_map/ppermute | solution.py:24
  304.5 2.1 collective-permute-done.40
  309.3 19.2 %collective-permute-done.45 = bf16[4,48,3072]{2,1,0:T(8,128)(2,1)S(1)} collective-permute-done((bf16[4,48,3072]{2,1,0:T(8,128)(2,1)S(1)}, bf16[4,48,3072]{2,1,0:T(8,128)(2,1)S(1)}, u32[]{:S(2)}, u32[]{:S(2)}) %collective-permute-start.45) | collective-permute-done | bytes 1179680 | tf_op jit(solution)/shard_map/ppermute | solution.py:24
  328.5 3.6 collective-permute-done.46
  332.2 2.0 fusion.12
  334.4 2.5 collective-permute-start.49
  338.2 8.2 %collective-permute-done.41 = bf16[4,48,2304]{2,1,0:T(8,128)(2,1)S(1)} collective-permute-done((bf16[4,48,2304]{2,1,0:T(8,128)(2,1)S(1)}, bf16[4,48,2304]{2,1,0:T(8,128)(2,1)S(1)}, u32[]{:S(2)}, u32[]{:S(2)}) %collective-permute-start.41) | collective-permute-done | bytes 884768 | tf_op jit(solution)/shard_map/ppermute | solution.py:24
  346.4 1.6 collective-permute-done.42
  347.9 1.6 fusion.18
  350.5 3.0 collective-permute-start.55
  353.5 1.8 collective-permute-start.54
  355.3 5.9 %collective-permute-done.48 = bf16[2,48,3072]{2,1,0:T(8,128)(2,1)S(1)} collective-permute-done((bf16[2,48,3072]{2,1,0:T(8,128)(2,1)S(1)}, bf16[2,48,3072]{2,1,0:T(8,128)(2,1)S(1)}, u32[]{:S(2)}, u32[]{:S(2)}) %collective-permute-start.48) | collective-permute-done | bytes 589856 | tf_op jit(solution)/shard_map/ppermute | solution.py:24
  363.1 10.7 %collective-permute-start.50 = (bf16[48,3072]{1,0:T(8,128)(2,1)}, bf16[48,3072]{1,0:T(8,128)(2,1)}, u32[]{:S(2)}, u32[]{:S(2)}) collective-permute-start(bf16[48,3072]{1,0:T(8,128)(2,1)} %fusion.44), channel_id=1, source_target_pairs={{0,8},{1,9},{2,10},{3,11},{4,12},{5,13},{6,14},{7,15},{8,0},{9,1},... | collective-permute-start | bytes 884744 | tf_op jit(solution)/shard_map/ppermute | solution.py:24
  377.4 1.8 stack_reshape.3
  381.1 3.4 collective-permute-done.50
  (353 shorter events, 66.9 us)
Async XLA Ops:
  7.2 157.2 %all-gather.2.cloned.1.call-start = ((), (), s32[]{:S(2)}) async-start(), calls=%async_computation | async-start | bytes 14598144 | tf_op jit(solution)/shard_map/all_gather | solution.py:780
  13.4 1.7 collective-permute-start
  15.3 18.2 %collective-permute-start.2 = (bf16[48,5376]{1,0:T(8,128)(2,1)S(1)}, bf16[48,5376]{1,0:T(8,128)(2,1)S(1)}, u32[]{:S(2)}, u32[]{:S(2)}) collective-permute-start(bf16[48,5376]{1,0:T(8,128)(2,1)S(1)} %constant_dynamic-update-slice_fusion.2), channel_id=1, source_target_pairs={{0,4},{1,5},{2,6},{3,7},{4,0},{5,1},{6,2},{7,3},{8,12},{9,13},{10,... | collective-permute-start | bytes 1548296 | tf_op jit(solution)/shard_map/ppermute | solution.py:24
  18.3 17.0 %collective-permute-start.1 = (bf16[48,5376]{1,0:T(8,128)(2,1)S(1)}, bf16[48,5376]{1,0:T(8,128)(2,1)S(1)}, u32[]{:S(2)}, u32[]{:S(2)}) collective-permute-start(bf16[48,5376]{1,0:T(8,128)(2,1)S(1)} %constant_dynamic-update-slice_fusion.2), channel_id=1, source_target_pairs={{0,2},{1,3},{2,0},{3,1},{4,6},{5,7},{6,4},{7,5},{8,10},{9,11},{10,... | collective-permute-start | bytes 1548296 | tf_op jit(solution)/shard_map/ppermute | solution.py:24
  19.8 20.6 %collective-permute-start.6 = (bf16[48,5376]{1,0:T(8,128)(2,1)S(1)}, bf16[48,5376]{1,0:T(8,128)(2,1)}, u32[]{:S(2)}, u32[]{:S(2)}) collective-permute-start(bf16[48,5376]{1,0:T(8,128)(2,1)S(1)} %constant_dynamic-update-slice_fusion.2), channel_id=1, source_target_pairs={{0,8},{1,9},{2,10},{3,11},{4,12},{5,13},{6,14},{7,15},{8,0},{9,1},... | collective-permute-start | bytes 1548296 | tf_op jit(solution)/shard_map/ppermute | solution.py:24
  21.4 19.8 %collective-permute-start.13 = (bf16[48,5376]{1,0:T(8,128)(2,1)S(1)}, bf16[48,5376]{1,0:T(8,128)(2,1)}, u32[]{:S(2)}, u32[]{:S(2)}) collective-permute-start(bf16[48,5376]{1,0:T(8,128)(2,1)S(1)} %constant_dynamic-update-slice_fusion.2), channel_id=1, source_target_pairs={{8,16},{9,17},{10,18},{11,19},{12,20},{13,21},{14,22},{15,23},{16,... | collective-permute-start | bytes 1548296 | tf_op jit(solution)/shard_map/ppermute | solution.py:28
  33.5 7.7 %collective-permute-start.4 = (bf16[48,2688]{1,0:T(8,128)(2,1)S(1)}, bf16[48,2688]{1,0:T(8,128)(2,1)S(1)}, u32[]{:S(2)}, u32[]{:S(2)}) collective-permute-start(bf16[48,2688]{1,0:T(8,128)(2,1)S(1)} %slice.633), channel_id=1, source_target_pairs={{0,2},{1,3},{2,0},{3,1},{4,6},{5,7},{6,4},{7,5},{8,10},{9,11},{10,... | collective-permute-start | bytes 774152 | tf_op jit(solution)/shard_map/ppermute | solution.py:24
  35.3 8.6 %collective-permute-start.3 = (bf16[48,2688]{1,0:T(8,128)(2,1)S(1)}, bf16[48,2688]{1,0:T(8,128)(2,1)S(1)}, u32[]{:S(2)}, u32[]{:S(2)}) collective-permute-start(bf16[48,2688]{1,0:T(8,128)(2,1)S(1)} %slice.632), channel_id=1, source_target_pairs={{0,4},{1,5},{2,6},{3,7},{4,0},{5,1},{6,2},{7,3},{8,12},{9,13},{10,... | collective-permute-start | bytes 774152 | tf_op jit(solution)/shard_map/ppermute | solution.py:24
  40.4 30.1 %collective-permute-start.12 = (bf16[48,5376]{1,0:T(8,128)(2,1)}, bf16[48,5376]{1,0:T(8,128)(2,1)S(1)}, u32[]{:S(2)}, u32[]{:S(2)}) collective-permute-start(bf16[48,5376]{1,0:T(8,128)(2,1)} %collective-permute-done.6), channel_id=1, source_target_pairs={{8,16},{9,17},{10,18},{11,19},{12,20},{13,21},{14,22},{15,23},{16,... | collective-permute-start | bytes 1548296 | tf_op jit(solution)/shard_map/ppermute | solution.py:28
  41.1 18.6 %collective-permute-start.8 = (bf16[48,5376]{1,0:T(8,128)(2,1)}, bf16[48,5376]{1,0:T(8,128)(2,1)S(1)}, u32[]{:S(2)}, u32[]{:S(2)}) collective-permute-start(bf16[48,5376]{1,0:T(8,128)(2,1)} %collective-permute-done.6), channel_id=1, source_target_pairs={{0,4},{1,5},{2,6},{3,7},{4,0},{5,1},{6,2},{7,3},{8,12},{9,13},{10,... | collective-permute-start | bytes 1548296 | tf_op jit(solution)/shard_map/ppermute | solution.py:24
  41.1 18.7 %collective-permute-start.7 = (bf16[48,5376]{1,0:T(8,128)(2,1)}, bf16[48,5376]{1,0:T(8,128)(2,1)S(1)}, u32[]{:S(2)}, u32[]{:S(2)}) collective-permute-start(bf16[48,5376]{1,0:T(8,128)(2,1)} %collective-permute-done.6), channel_id=1, source_target_pairs={{0,2},{1,3},{2,0},{3,1},{4,6},{5,7},{6,4},{7,5},{8,10},{9,11},{10,... | collective-permute-start | bytes 1548296 | tf_op jit(solution)/shard_map/ppermute | solution.py:24
  41.2 29.2 %collective-permute-start.14 = (bf16[48,5376]{1,0:T(8,128)(2,1)}, bf16[48,5376]{1,0:T(8,128)(2,1)S(1)}, u32[]{:S(2)}, u32[]{:S(2)}) collective-permute-start(bf16[48,5376]{1,0:T(8,128)(2,1)} %collective-permute-done.13), channel_id=1, source_target_pairs={{8,0},{9,1},{10,2},{11,3},{12,4},{13,5},{14,6},{15,7},{16,24},{17,... | collective-permute-start | bytes 1548296 | tf_op jit(solution)/shard_map/ppermute | solution.py:28
  45.2 88.9 %copy-start = (bf16[4,48,5376]{2,1,0:T(8,128)(2,1)}, bf16[4,48,5376]{2,1,0:T(8,128)(2,1)S(1)}, u32[]{:S(2)}) copy-start(bf16[4,48,5376]{2,1,0:T(8,128)(2,1)S(1)} %pad_maximum_fusion.rest_0_.rest_1_) | copy-start | bytes 6193156
  45.3 84.7 %collective-permute-start.5 = (bf16[4,48,5376]{2,1,0:T(8,128)(2,1)S(1)}, bf16[4,48,5376]{2,1,0:T(8,128)(2,1)}, u32[]{:S(2)}, u32[]{:S(2)}) collective-permute-start(bf16[4,48,5376]{2,1,0:T(8,128)(2,1)S(1)} %pad_maximum_fusion.rest_0_.rest_1_), channel_id=1, source_target_pairs={{0,1},{1,0},{2,3},{3,2},{4,5},{5,4},{6,7},{7,6},{8,9},{9,8},{10,11... | collective-permute-start | bytes 6193160 | tf_op jit(solution)/shard_map/ppermute | solution.py:24
  59.7 12.9 %collective-permute-start.10 = (bf16[48,2688]{1,0:T(8,128)(2,1)S(1)}, bf16[48,2688]{1,0:T(8,128)(2,1)S(1)}, u32[]{:S(2)}, u32[]{:S(2)}) collective-permute-start(bf16[48,2688]{1,0:T(8,128)(2,1)S(1)} %slice.635), channel_id=1, source_target_pairs={{0,2},{1,3},{2,0},{3,1},{4,6},{5,7},{6,4},{7,5},{8,10},{9,11},{10,... | collective-permute-start | bytes 774152 | tf_op jit(solution)/shard_map/ppermute | solution.py:24
  59.8 14.1 %collective-permute-start.9 = (bf16[48,2688]{1,0:T(8,128)(2,1)S(1)}, bf16[48,2688]{1,0:T(8,128)(2,1)S(1)}, u32[]{:S(2)}, u32[]{:S(2)}) collective-permute-start(bf16[48,2688]{1,0:T(8,128)(2,1)S(1)} %slice.634), channel_id=1, source_target_pairs={{0,4},{1,5},{2,6},{3,7},{4,0},{5,1},{6,2},{7,3},{8,12},{9,13},{10,... | collective-permute-start | bytes 774152 | tf_op jit(solution)/shard_map/ppermute | solution.py:24
  70.5 9.5 %collective-permute-start.16 = (bf16[48,5376]{1,0:T(8,128)(2,1)S(1)}, bf16[48,5376]{1,0:T(8,128)(2,1)S(1)}, u32[]{:S(2)}, u32[]{:S(2)}) collective-permute-start(bf16[48,5376]{1,0:T(8,128)(2,1)S(1)} %broadcast_select_fusion.1), channel_id=1, source_target_pairs={{0,4},{1,5},{2,6},{3,7},{4,0},{5,1},{6,2},{7,3},{8,12},{9,13},{10,... | collective-permute-start | bytes 1548296 | tf_op jit(solution)/shard_map/ppermute | solution.py:24
  70.9 13.1 %collective-permute-start.15 = (bf16[48,5376]{1,0:T(8,128)(2,1)S(1)}, bf16[48,5376]{1,0:T(8,128)(2,1)S(1)}, u32[]{:S(2)}, u32[]{:S(2)}) collective-permute-start(bf16[48,5376]{1,0:T(8,128)(2,1)S(1)} %broadcast_select_fusion.1), channel_id=1, source_target_pairs={{0,2},{1,3},{2,0},{3,1},{4,6},{5,7},{6,4},{7,5},{8,10},{9,11},{10,... | collective-permute-start | bytes 1548296 | tf_op jit(solution)/shard_map/ppermute | solution.py:24
  72.6 19.2 %collective-permute-start.20 = (bf16[48,5376]{1,0:T(8,128)(2,1)S(1)}, bf16[48,5376]{1,0:T(8,128)(2,1)S(1)}, u32[]{:S(2)}, u32[]{:S(2)}) collective-permute-start(bf16[48,5376]{1,0:T(8,128)(2,1)S(1)} %collective-permute-done.12), channel_id=1, source_target_pairs={{8,0},{9,1},{10,2},{11,3},{12,4},{13,5},{14,6},{15,7},{16,24},{17,... | collective-permute-start | bytes 1548296 | tf_op jit(solution)/shard_map/ppermute | solution.py:28
  76.5 53.4 %collective-permute-start.11 = (bf16[4,48,5376]{2,1,0:T(8,128)(2,1)}, bf16[4,48,5376]{2,1,0:T(8,128)(2,1)}, u32[]{:S(2)}, u32[]{:S(2)}) collective-permute-start(bf16[4,48,5376]{2,1,0:T(8,128)(2,1)} %pad_maximum_fusion.1.rest_2_.rest_3_), channel_id=1, source_target_pairs={{0,1},{1,0},{2,3},{3,2},{4,5},{5,4},{6,7},{7,6},{8,9},{9,8},{10,11... | collective-permute-start | bytes 6193160 | tf_op jit(solution)/shard_map/ppermute | solution.py:24
  80.0 12.9 %collective-permute-start.18 = (bf16[48,2688]{1,0:T(8,128)(2,1)S(1)}, bf16[48,2688]{1,0:T(8,128)(2,1)S(1)}, u32[]{:S(2)}, u32[]{:S(2)}) collective-permute-start(bf16[48,2688]{1,0:T(8,128)(2,1)S(1)} %slice.637), channel_id=1, source_target_pairs={{0,2},{1,3},{2,0},{3,1},{4,6},{5,7},{6,4},{7,5},{8,10},{9,11},{10,... | collective-permute-start | bytes 774152 | tf_op jit(solution)/shard_map/ppermute | solution.py:24
  84.0 9.4 %collective-permute-start.17 = (bf16[48,2688]{1,0:T(8,128)(2,1)S(1)}, bf16[48,2688]{1,0:T(8,128)(2,1)S(1)}, u32[]{:S(2)}, u32[]{:S(2)}) collective-permute-start(bf16[48,2688]{1,0:T(8,128)(2,1)S(1)} %slice.636), channel_id=1, source_target_pairs={{0,4},{1,5},{2,6},{3,7},{4,0},{5,1},{6,2},{7,3},{8,12},{9,13},{10,... | collective-permute-start | bytes 774152 | tf_op jit(solution)/shard_map/ppermute | solution.py:24
  91.8 23.2 %collective-permute-start.22 = (bf16[48,5376]{1,0:T(8,128)(2,1)S(1)}, bf16[48,5376]{1,0:T(8,128)(2,1)S(1)}, u32[]{:S(2)}, u32[]{:S(2)}) collective-permute-start(bf16[48,5376]{1,0:T(8,128)(2,1)S(1)} %broadcast_select_fusion), channel_id=1, source_target_pairs={{0,4},{1,5},{2,6},{3,7},{4,0},{5,1},{6,2},{7,3},{8,12},{9,13},{10,... | collective-permute-start | bytes 1548296 | tf_op jit(solution)/shard_map/ppermute | solution.py:24
  93.0 23.0 %collective-permute-start.21 = (bf16[48,5376]{1,0:T(8,128)(2,1)S(1)}, bf16[48,5376]{1,0:T(8,128)(2,1)S(1)}, u32[]{:S(2)}, u32[]{:S(2)}) collective-permute-start(bf16[48,5376]{1,0:T(8,128)(2,1)S(1)} %broadcast_select_fusion), channel_id=1, source_target_pairs={{0,2},{1,3},{2,0},{3,1},{4,6},{5,7},{6,4},{7,5},{8,10},{9,11},{10,... | collective-permute-start | bytes 1548296 | tf_op jit(solution)/shard_map/ppermute | solution.py:24
  115.0 11.9 %collective-permute-start.24 = (bf16[48,2688]{1,0:T(8,128)(2,1)S(1)}, bf16[48,2688]{1,0:T(8,128)(2,1)S(1)}, u32[]{:S(2)}, u32[]{:S(2)}) collective-permute-start(bf16[48,2688]{1,0:T(8,128)(2,1)S(1)} %slice.639), channel_id=1, source_target_pairs={{0,2},{1,3},{2,0},{3,1},{4,6},{5,7},{6,4},{7,5},{8,10},{9,11},{10,... | collective-permute-start | bytes 774152 | tf_op jit(solution)/shard_map/ppermute | solution.py:24
  116.0 12.1 %collective-permute-start.23 = (bf16[48,2688]{1,0:T(8,128)(2,1)S(1)}, bf16[48,2688]{1,0:T(8,128)(2,1)S(1)}, u32[]{:S(2)}, u32[]{:S(2)}) collective-permute-start(bf16[48,2688]{1,0:T(8,128)(2,1)S(1)} %slice.638), channel_id=1, source_target_pairs={{0,4},{1,5},{2,6},{3,7},{4,0},{5,1},{6,2},{7,3},{8,12},{9,13},{10,... | collective-permute-start | bytes 774152 | tf_op jit(solution)/shard_map/ppermute | solution.py:24
  119.9 10.1 %collective-permute-start.19 = (bf16[4,48,5376]{2,1,0:T(8,128)(2,1)}, bf16[4,48,5376]{2,1,0:T(8,128)(2,1)}, u32[]{:S(2)}, u32[]{:S(2)}) collective-permute-start(bf16[4,48,5376]{2,1,0:T(8,128)(2,1)} %pad_maximum_fusion.2.rest_4_.rest_5_), channel_id=1, source_target_pairs={{0,1},{1,0},{2,3},{3,2},{4,5},{5,4},{6,7},{7,6},{8,9},{9,8},{10,11... | collective-permute-start | bytes 6193160 | tf_op jit(solution)/shard_map/ppermute | solution.py:24
  129.7 4.5 %collective-permute-start.25 = (bf16[4,48,5376]{2,1,0:T(8,128)(2,1)}, bf16[4,48,5376]{2,1,0:T(8,128)(2,1)}, u32[]{:S(2)}, u32[]{:S(2)}) collective-permute-start(bf16[4,48,5376]{2,1,0:T(8,128)(2,1)} %pad_maximum_fusion.3.rest_6_.rest_7_), channel_id=1, source_target_pairs={{0,1},{1,0},{2,3},{3,2},{4,5},{5,4},{6,7},{7,6},{8,9},{9,8},{10,11... | collective-permute-start | bytes 6193160 | tf_op jit(solution)/shard_map/ppermute | solution.py:24
  164.4 19.8 %copy-start.3 = (s32[256,1]{1,0:T(8,128)S(1)}, s32[256,1]{1,0:T(8,128)}, u32[]{:S(2)}) copy-start(s32[256,1]{1,0:T(8,128)} %copy-done.2) | copy-start | bytes 3076
  164.4 19.8 %copy-start.5 = (f32[256,768]{1,0:T(8,128)S(1)}, f32[256,768]{1,0:T(8,128)}, u32[]{:S(2)}) copy-start(f32[256,768]{1,0:T(8,128)} %copy-done.4) | copy-start | bytes 2359300
  164.4 19.8 %copy-start.16 = (f32[1,9984]{1,0:T(1,128)S(1)}, f32[1,9984]{1,0:T(1,128)}, u32[]{:S(2)}) copy-start(f32[1,9984]{1,0:T(1,128)} %broadcast_in_dim.133.row_ref) | copy-start | bytes 119812
  164.4 19.8 %copy-start.18 = (s32[1,256]{1,0:T(1,128)S(1)}, s32[1,256]{1,0:T(1,128)}, u32[]{:S(2)}) copy-start(s32[1,256]{1,0:T(1,128)} %across_docs.5) | copy-start | bytes 3076
  183.9 17.8 %collective-permute-start.26 = (bf16[16,48,3072]{2,1,0:T(8,128)(2,1)}, bf16[16,48,3072]{2,1,0:T(8,128)(2,1)S(1)}, u32[]{:S(2)}, u32[]{:S(2)}) collective-permute-start(bf16[16,48,3072]{2,1,0:T(8,128)(2,1)} %get-tuple-element.102), channel_id=1, source_target_pairs={{0,1},{1,0},{2,3},{3,2},{4,5},{5,4},{6,7},{7,6},{8,9},{9,8},{10,11... | collective-permute-start | bytes 14155784 | tf_op jit(solution)/shard_map/ppermute | solution.py:24
  204.1 17.4 %collective-permute-start.29 = (bf16[16,48,1536]{2,1,0:T(8,128)(2,1)}, bf16[16,48,1536]{2,1,0:T(8,128)(2,1)}, u32[]{:S(2)}, u32[]{:S(2)}) collective-permute-start(bf16[16,48,1536]{2,1,0:T(8,128)(2,1)} %get-tuple-element.112), channel_id=1, source_target_pairs={{0,1},{1,0},{2,3},{3,2},{4,5},{5,4},{6,7},{7,6},{8,9},{9,8},{10,11... | collective-permute-start | bytes 7077896 | tf_op jit(solution)/shard_map/ppermute | solution.py:24
  204.2 17.0 %collective-permute-start.27 = (bf16[4,48,1536]{2,1,0:T(8,128)(2,1)S(1)}, bf16[4,48,1536]{2,1,0:T(8,128)(2,1)S(1)}, u32[]{:S(2)}, u32[]{:S(2)}) collective-permute-start(bf16[4,48,1536]{2,1,0:T(8,128)(2,1)S(1)} %get-tuple-element.110), channel_id=1, source_target_pairs={{0,4},{1,5},{2,6},{3,7},{4,0},{5,1},{6,2},{7,3},{8,12},{9,13},{10,... | collective-permute-start | bytes 1769480 | tf_op jit(solution)/shard_map/ppermute | solution.py:24
  206.1 15.4 %collective-permute-start.28 = (bf16[4,48,1536]{2,1,0:T(8,128)(2,1)S(1)}, bf16[4,48,1536]{2,1,0:T(8,128)(2,1)S(1)}, u32[]{:S(2)}, u32[]{:S(2)}) collective-permute-start(bf16[4,48,1536]{2,1,0:T(8,128)(2,1)S(1)} %get-tuple-element.111), channel_id=1, source_target_pairs={{0,2},{1,3},{2,0},{3,1},{4,6},{5,7},{6,4},{7,5},{8,10},{9,11},{10,... | collective-permute-start | bytes 1769480 | tf_op jit(solution)/shard_map/ppermute | solution.py:24
  221.5 36.4 %collective-permute-start.32 = (bf16[16,48,3072]{2,1,0:T(8,128)(2,1)}, bf16[16,48,3072]{2,1,0:T(8,128)(2,1)}, u32[]{:S(2)}, u32[]{:S(2)}) collective-permute-start(bf16[16,48,3072]{2,1,0:T(8,128)(2,1)} %get-tuple-element.123), channel_id=1, source_target_pairs={{0,1},{1,0},{2,3},{3,2},{4,5},{5,4},{6,7},{7,6},{8,9},{9,8},{10,11... | collective-permute-start | bytes 14155784 | tf_op jit(solution)/shard_map/ppermute | solution.py:24
  223.7 9.5 %collective-permute-start.31 = (bf16[4,48,768]{2,1,0:T(8,128)(2,1)S(1)}, bf16[4,48,768]{2,1,0:T(8,128)(2,1)S(1)}, u32[]{:S(2)}, u32[]{:S(2)}) collective-permute-start(bf16[4,48,768]{2,1,0:T(8,128)(2,1)S(1)} %get-tuple-element.189), channel_id=1, source_target_pairs={{0,2},{1,3},{2,0},{3,1},{4,6},{5,7},{6,4},{7,5},{8,10},{9,11},{10,... | collective-permute-start | bytes 884744 | tf_op jit(solution)/shard_map/ppermute | solution.py:24
  225.0 9.9 %collective-permute-start.30 = (bf16[4,48,768]{2,1,0:T(8,128)(2,1)S(1)}, bf16[4,48,768]{2,1,0:T(8,128)(2,1)S(1)}, u32[]{:S(2)}, u32[]{:S(2)}) collective-permute-start(bf16[4,48,768]{2,1,0:T(8,128)(2,1)S(1)} %get-tuple-element.190), channel_id=1, source_target_pairs={{0,4},{1,5},{2,6},{3,7},{4,0},{5,1},{6,2},{7,3},{8,12},{9,13},{10,... | collective-permute-start | bytes 884744 | tf_op jit(solution)/shard_map/ppermute | solution.py:24
  230.0 42.2 %collective-permute-start.34 = (bf16[4,48,3072]{2,1,0:T(8,128)(2,1)}, bf16[4,48,3072]{2,1,0:T(8,128)(2,1)}, u32[]{:S(2)}, u32[]{:S(2)}) collective-permute-start(bf16[4,48,3072]{2,1,0:T(8,128)(2,1)} %get-tuple-element.179), channel_id=1, source_target_pairs={{0,4},{1,5},{2,6},{3,7},{4,0},{5,1},{6,2},{7,3},{8,12},{9,13},{10,... | collective-permute-start | bytes 3538952 | tf_op jit(solution)/shard_map/ppermute | solution.py:24
  231.8 40.4 %collective-permute-start.33 = (bf16[4,48,3072]{2,1,0:T(8,128)(2,1)}, bf16[4,48,3072]{2,1,0:T(8,128)(2,1)}, u32[]{:S(2)}, u32[]{:S(2)}) collective-permute-start(bf16[4,48,3072]{2,1,0:T(8,128)(2,1)} %get-tuple-element.180), channel_id=1, source_target_pairs={{0,2},{1,3},{2,0},{3,1},{4,6},{5,7},{6,4},{7,5},{8,10},{9,11},{10,... | collective-permute-start | bytes 3538952 | tf_op jit(solution)/shard_map/ppermute | solution.py:24
  240.7 31.5 %collective-permute-start.35 = (bf16[4,48,1536]{2,1,0:T(8,128)(2,1)}, bf16[4,48,1536]{2,1,0:T(8,128)(2,1)}, u32[]{:S(2)}, u32[]{:S(2)}) collective-permute-start(bf16[4,48,1536]{2,1,0:T(8,128)(2,1)} %get-tuple-element.130), channel_id=1, source_target_pairs={{0,2},{1,3},{2,0},{3,1},{4,6},{5,7},{6,4},{7,5},{8,10},{9,11},{10,... | collective-permute-start | bytes 1769480 | tf_op jit(solution)/shard_map/ppermute | solution.py:24
  241.5 30.7 %collective-permute-start.36 = (bf16[4,48,1536]{2,1,0:T(8,128)(2,1)}, bf16[4,48,1536]{2,1,0:T(8,128)(2,1)}, u32[]{:S(2)}, u32[]{:S(2)}) collective-permute-start(bf16[4,48,1536]{2,1,0:T(8,128)(2,1)} %get-tuple-element.131), channel_id=1, source_target_pairs={{0,4},{1,5},{2,6},{3,7},{4,0},{5,1},{6,2},{7,3},{8,12},{9,13},{10,... | collective-permute-start | bytes 1769480 | tf_op jit(solution)/shard_map/ppermute | solution.py:24
  272.2 6.5 %collective-permute-start.37 = (bf16[16,48,2304]{2,1,0:T(8,128)(2,1)}, bf16[16,48,2304]{2,1,0:T(8,128)(2,1)S(1)}, u32[]{:S(2)}, u32[]{:S(2)}) collective-permute-start(bf16[16,48,2304]{2,1,0:T(8,128)(2,1)} %bitcast_dynamic-update-slice_fusion), channel_id=1, source_target_pairs={{0,1},{1,0},{2,3},{3,2},{4,5},{5,4},{6,7},{7,6},{8,9},{9,8},{10,11... | collective-permute-start | bytes 10616840 | tf_op jit(solution)/shard_map/ppermute | solution.py:24
  272.3 18.8 %collective-permute-start.43 = (bf16[4,48,1536]{2,1,0:T(8,128)(2,1)}, bf16[4,48,1536]{2,1,0:T(8,128)(2,1)S(1)}, u32[]{:S(2)}, u32[]{:S(2)}) collective-permute-start(bf16[4,48,1536]{2,1,0:T(8,128)(2,1)} %get-tuple-element.151), channel_id=1, source_target_pairs={{0,4},{1,5},{2,6},{3,7},{4,0},{5,1},{6,2},{7,3},{8,12},{9,13},{10,... | collective-permute-start | bytes 1769480 | tf_op jit(solution)/shard_map/ppermute | solution.py:24
  272.9 19.4 %collective-permute-start.44 = (bf16[4,48,1536]{2,1,0:T(8,128)(2,1)}, bf16[4,48,1536]{2,1,0:T(8,128)(2,1)S(1)}, u32[]{:S(2)}, u32[]{:S(2)}) collective-permute-start(bf16[4,48,1536]{2,1,0:T(8,128)(2,1)} %get-tuple-element.152), channel_id=1, source_target_pairs={{0,2},{1,3},{2,0},{3,1},{4,6},{5,7},{6,4},{7,5},{8,10},{9,11},{10,... | collective-permute-start | bytes 1769480 | tf_op jit(solution)/shard_map/ppermute | solution.py:24
  278.7 27.9 %copy-start.20 = (bf16[16,48,2304]{2,1,0:T(8,128)(2,1)}, bf16[16,48,2304]{2,1,0:T(8,128)(2,1)S(1)}, u32[]{:S(2)}) copy-start(bf16[16,48,2304]{2,1,0:T(8,128)(2,1)S(1)} %collective-permute-done.37) | copy-start | bytes 10616836
  282.0 27.3 %collective-permute-start.47 = (bf16[2,48,1536]{2,1,0:T(8,128)(2,1)S(1)}, bf16[2,48,1536]{2,1,0:T(8,128)(2,1)S(1)}, u32[]{:S(2)}, u32[]{:S(2)}) collective-permute-start(bf16[2,48,1536]{2,1,0:T(8,128)(2,1)S(1)} %slice.690), channel_id=1, source_target_pairs={{0,24},{1,25},{2,26},{3,27},{4,28},{5,29},{6,30},{7,31},{8,16},{9,... | collective-permute-start | bytes 884744 | tf_op jit(solution)/shard_map/ppermute | solution.py:24
  289.6 17.0 %collective-permute-start.40 = (bf16[2,48,3072]{2,1,0:T(8,128)(2,1)S(1)}, bf16[2,48,3072]{2,1,0:T(8,128)(2,1)S(1)}, u32[]{:S(2)}, u32[]{:S(2)}) collective-permute-start(bf16[2,48,3072]{2,1,0:T(8,128)(2,1)S(1)} %slice.678), channel_id=1, source_target_pairs={{0,24},{1,25},{2,26},{3,27},{4,28},{5,29},{6,30},{7,31},{8,16},{9,... | collective-permute-start | bytes 1769480 | tf_op jit(solution)/shard_map/ppermute | solution.py:24
  290.1 13.1 %collective-permute-start.39 = (bf16[4,48,1152]{2,1,0:T(8,128)(2,1)S(1)}, bf16[4,48,1152]{2,1,0:T(8,128)(2,1)S(1)}, u32[]{:S(2)}, u32[]{:S(2)}) collective-permute-start(bf16[4,48,1152]{2,1,0:T(8,128)(2,1)S(1)} %get-tuple-element.185), channel_id=1, source_target_pairs={{0,2},{1,3},{2,0},{3,1},{4,6},{5,7},{6,4},{7,5},{8,10},{9,11},{10,... | collective-permute-start | bytes 1327112 | tf_op jit(solution)/shard_map/ppermute | solution.py:24
  291.2 13.4 %collective-permute-start.38 = (bf16[4,48,1152]{2,1,0:T(8,128)(2,1)S(1)}, bf16[4,48,1152]{2,1,0:T(8,128)(2,1)S(1)}, u32[]{:S(2)}, u32[]{:S(2)}) collective-permute-start(bf16[4,48,1152]{2,1,0:T(8,128)(2,1)S(1)} %get-tuple-element.186), channel_id=1, source_target_pairs={{0,4},{1,5},{2,6},{3,7},{4,0},{5,1},{6,2},{7,3},{8,12},{9,13},{10,... | collective-permute-start | bytes 1327112 | tf_op jit(solution)/shard_map/ppermute | solution.py:24
  294.8 33.7 %collective-permute-start.45 = (bf16[4,48,3072]{2,1,0:T(8,128)(2,1)S(1)}, bf16[4,48,3072]{2,1,0:T(8,128)(2,1)S(1)}, u32[]{:S(2)}, u32[]{:S(2)}) collective-permute-start(bf16[4,48,3072]{2,1,0:T(8,128)(2,1)S(1)} %get-tuple-element.175), channel_id=1, source_target_pairs={{0,2},{1,3},{2,0},{3,1},{4,6},{5,7},{6,4},{7,5},{8,10},{9,11},{10,... | collective-permute-start | bytes 3538952 | tf_op jit(solution)/shard_map/ppermute | solution.py:24
  303.2 28.9 %collective-permute-start.46 = (bf16[4,48,3072]{2,1,0:T(8,128)(2,1)S(1)}, bf16[4,48,3072]{2,1,0:T(8,128)(2,1)S(1)}, u32[]{:S(2)}, u32[]{:S(2)}) collective-permute-start(bf16[4,48,3072]{2,1,0:T(8,128)(2,1)S(1)} %get-tuple-element.176), channel_id=1, source_target_pairs={{0,4},{1,5},{2,6},{3,7},{4,0},{5,1},{6,2},{7,3},{8,12},{9,13},{10,... | collective-permute-start | bytes 3538952 | tf_op jit(solution)/shard_map/ppermute | solution.py:24
  307.2 39.2 %collective-permute-start.41 = (bf16[4,48,2304]{2,1,0:T(8,128)(2,1)S(1)}, bf16[4,48,2304]{2,1,0:T(8,128)(2,1)S(1)}, u32[]{:S(2)}, u32[]{:S(2)}) collective-permute-start(bf16[4,48,2304]{2,1,0:T(8,128)(2,1)S(1)} %get-tuple-element.183), channel_id=1, source_target_pairs={{0,2},{1,3},{2,0},{3,1},{4,6},{5,7},{6,4},{7,5},{8,10},{9,11},{10,... | collective-permute-start | bytes 2654216 | tf_op jit(solution)/shard_map/ppermute | solution.py:24
  308.2 39.7 %collective-permute-start.42 = (bf16[4,48,2304]{2,1,0:T(8,128)(2,1)S(1)}, bf16[4,48,2304]{2,1,0:T(8,128)(2,1)S(1)}, u32[]{:S(2)}, u32[]{:S(2)}) collective-permute-start(bf16[4,48,2304]{2,1,0:T(8,128)(2,1)S(1)} %get-tuple-element.184), channel_id=1, source_target_pairs={{0,4},{1,5},{2,6},{3,7},{4,0},{5,1},{6,2},{7,3},{8,12},{9,13},{10,... | collective-permute-start | bytes 2654216 | tf_op jit(solution)/shard_map/ppermute | solution.py:24
  334.4 20.9 %collective-permute-start.49 = (bf16[48,4608]{1,0:T(8,128)(2,1)S(1)}, bf16[48,4608]{1,0:T(8,128)(2,1)S(1)}, u32[]{:S(2)}, u32[]{:S(2)}) collective-permute-start(bf16[48,4608]{1,0:T(8,128)(2,1)S(1)} %fusion.39), channel_id=1, source_target_pairs={{0,8},{1,9},{2,10},{3,11},{4,12},{5,13},{6,14},{7,15},{8,0},{9,1},... | collective-permute-start | bytes 1327112 | tf_op jit(solution)/shard_map/ppermute | solution.py:24
  336.8 24.4 %collective-permute-start.48 = (bf16[2,48,3072]{2,1,0:T(8,128)(2,1)S(1)}, bf16[2,48,3072]{2,1,0:T(8,128)(2,1)S(1)}, u32[]{:S(2)}, u32[]{:S(2)}) collective-permute-start(bf16[2,48,3072]{2,1,0:T(8,128)(2,1)S(1)} %slice.691), channel_id=1, source_target_pairs={{0,24},{1,25},{2,26},{3,27},{4,28},{5,29},{6,30},{7,31},{8,16},{9,... | collective-permute-start | bytes 1769480 | tf_op jit(solution)/shard_map/ppermute | solution.py:24
  350.5 38.7 %collective-permute-start.55 = (bf16[48,2304]{1,0:T(8,128)(2,1)}, bf16[48,2304]{1,0:T(8,128)(2,1)}, u32[]{:S(2)}, u32[]{:S(2)}) collective-permute-start(bf16[48,2304]{1,0:T(8,128)(2,1)} %get-tuple-element.191), channel_id=1, source_target_pairs={{0,24},{1,25},{2,26},{3,27},{4,28},{5,29},{6,30},{7,31},{8,16},{9,... | collective-permute-start | bytes 663560 | tf_op jit(solution)/shard_map/ppermute | solution.py:24
  353.5 35.6 %collective-permute-start.54 = (bf16[48,2304]{1,0:T(8,128)(2,1)}, bf16[48,2304]{1,0:T(8,128)(2,1)}, u32[]{:S(2)}, u32[]{:S(2)}) collective-permute-start(bf16[48,2304]{1,0:T(8,128)(2,1)} %get-tuple-element.192), channel_id=1, source_target_pairs={{0,16},{1,17},{2,18},{3,19},{4,20},{5,21},{6,22},{7,23},{8,24},{9,... | collective-permute-start | bytes 663560 | tf_op jit(solution)/shard_map/ppermute | solution.py:24
  355.3 33.8 %collective-permute-start.53 = (bf16[48,2304]{1,0:T(8,128)(2,1)}, bf16[48,2304]{1,0:T(8,128)(2,1)}, u32[]{:S(2)}, u32[]{:S(2)}) collective-permute-start(bf16[48,2304]{1,0:T(8,128)(2,1)} %get-tuple-element.193), channel_id=1, source_target_pairs={{0,8},{1,9},{2,10},{3,11},{4,12},{5,13},{6,14},{7,15},{8,0},{9,1},... | collective-permute-start | bytes 663560 | tf_op jit(solution)/shard_map/ppermute | solution.py:24
  362.2 12.4 %collective-permute-start.52 = (bf16[24,4608]{1,0:T(8,128)(2,1)S(1)}, bf16[24,4608]{1,0:T(8,128)(2,1)S(1)}, u32[]{:S(2)}, u32[]{:S(2)}) collective-permute-start(bf16[24,4608]{1,0:T(8,128)(2,1)S(1)} %pad_maximum_fusion.9), channel_id=1, source_target_pairs={{0,1},{1,0},{2,3},{3,2},{4,5},{5,4},{6,7},{7,6},{8,9},{9,8},{10,11... | collective-permute-start | bytes 663560 | tf_op jit(solution)/shard_map/ppermute | solution.py:24
  363.1 21.3 %collective-permute-start.50 = (bf16[48,3072]{1,0:T(8,128)(2,1)}, bf16[48,3072]{1,0:T(8,128)(2,1)}, u32[]{:S(2)}, u32[]{:S(2)}) collective-permute-start(bf16[48,3072]{1,0:T(8,128)(2,1)} %fusion.44), channel_id=1, source_target_pairs={{0,8},{1,9},{2,10},{3,11},{4,12},{5,13},{6,14},{7,15},{8,0},{9,1},... | collective-permute-start | bytes 884744 | tf_op jit(solution)/shard_map/ppermute | solution.py:24
  385.8 1.4 collective-permute-start.51
  390.7 1.4 collective-permute-start.56
  (46 other events, 251.0 us)
Sparse Core Ops, SparseCore 0:
  13.0 141.6 all-gather.1

commit v4 on v3

--- a/solution.py
+++ b/solution.py
@@ -191,8 +191,9 @@
 
     def body(hidden_ref, row_ref, down_docs, across_docs, *rest):
         refs, rest = rest[: len(arrays)], rest[len(arrays) :]
-        packed_ref, mixed_ref, middle_ref, top_ref = rest[:4]
-        targets, sems = dict(zip(names, rest[4:8])), rest[8]
+        saved_at, top_ref = rest[:3], rest[3]
+        targets, sems, saved = dict(zip(names, rest[4:8])), rest[8], rest[9:]
+        packed_ref, mixed_ref, middle_ref = saved
         named = {name: sems.at[n] for n, name in enumerate(names)}
         start_fetch(sources, refs, targets, named)
         middle = attn_steps(
@@ -206,6 +207,9 @@
             named,
         )
         middle_ref[...] = middle
+        writes = [pltpu.make_async_copy(a, b, sems.at[4 + n]) for n, (a, b) in enumerate(zip(saved, saved_at))]
+        for write in writes:
+            write.start()
         unit, _ = unit_of(middle)
         normed = (unit * spot(row_ref, "gain_b") + spot(row_ref, "shift_b")).astype(BF)
         total = middle + spot(row_ref, "down_b")
@@ -219,6 +223,8 @@
             active, _ = gelu_pair(lifted)
             total = total + dot(active.astype(BF), down_ref[columns, :], (1, 0))
         top_ref[...] = total
+        for write in writes:
+            write.wait()
 
     return pl.pallas_call(
         body,
@@ -229,8 +235,10 @@
             jax.ShapeDtypeStruct((tokens, WIDTH), F32),
         ],
         in_specs=[WHOLE] * 4 + [ANY] * len(arrays),
-        out_specs=[WHOLE] * 4,
-        scratch_shapes=[pltpu.VMEM(SHAPES[name], BF) for name in names] + [pltpu.SemaphoreType.DMA((4,))],
+        out_specs=[ANY] * 3 + [WHOLE],
+        scratch_shapes=[pltpu.VMEM(SHAPES[name], BF) for name in names]
+        + [pltpu.SemaphoreType.DMA((7,))]
+        + [pltpu.VMEM((tokens, 3 * WIDTH), BF), pltpu.VMEM((tokens, WIDTH), BF), pltpu.VMEM((tokens, WIDTH), F32)],
         compiler_params=pltpu.CompilerParams(vmem_limit_bytes=50 * 2**20),
         cost_estimate=pl.CostEstimate(flops=1, bytes_accessed=1, transcendentals=1),
         name="layer_forward",
@@ -265,7 +273,7 @@
         refs, rest = rest[: len(arrays)], rest[len(arrays) :]
         grads_ref, (mid_ref, small_ref), rest = rest[:2], rest[2:4], rest[4:]
         if whole_layer:
-            (packed_ref, mixed_ref, top_ref), rest = rest[:3], rest[3:]
+            (packed_at, mixed_at, top_ref), (packed_ref, mixed_ref), rest = rest[:3], rest[-2:], rest[3:-2]
         targets, (up_stage, down_stage, sems) = dict(zip(names, rest[:-3])), rest[-3:]
         named = {name: sems.at[n] for n, name in enumerate(names)}
         up_sem, down_sem = sems.at[4], sems.at[5]
@@ -276,6 +284,12 @@
             middle = attn_steps(
                 middle, row_ref, docs_refs, packed_ref, mixed_ref, targets["qkv"], targets["out"], named
             )
+            writes = [
+                pltpu.make_async_copy(packed_ref, packed_at, sems.at[6]),
+                pltpu.make_async_copy(mixed_ref, mixed_at, sems.at[7]),
+            ]
+            for write in writes:
+                write.start()
         unit, inverse = unit_of(middle)
         normed = unit * spot(row_ref, "gain_b") + spot(row_ref, "shift_b")
         normed_turned = normed.T.astype(BF)
@@ -328,6 +342,8 @@
                     )
         if whole_layer:
             top_ref[...] = total.astype(BF)
+            for write in writes:
+                write.wait()
         small_ref[:, HIDDEN + WIDTH : HIDDEN + 2 * WIDTH] = jnp.sum(grad_nb * unit, axis=0, keepdims=True)
         small_ref[:, HIDDEN + 2 * WIDTH :] = jnp.sum(grad_nb, axis=0, keepdims=True)
         mid_ref[...] = grad_top_rows + back_of_norm(grad_nb, unit, inverse, spot(row_ref, "gain_b"))
@@ -344,9 +360,10 @@
         body,
         out_shape=outs,
         in_specs=[WHOLE] * (3 + len(doc_operands)) + [ANY] * len(arrays),
-        out_specs=[ANY] * 2 + [WHOLE] * (len(outs) - 2),
+        out_specs=[ANY] * 2 + [WHOLE] * 2 + ([ANY, ANY, WHOLE] if whole_layer else []),
         scratch_shapes=[pltpu.VMEM(SHAPES[name], BF) for name in names + ("up", "down")]
-        + [pltpu.SemaphoreType.DMA((6,))],
+        + [pltpu.SemaphoreType.DMA((8,))]
+        + ([pltpu.VMEM((tokens, 3 * WIDTH), BF), pltpu.VMEM((tokens, WIDTH), BF)] if whole_layer else []),
         compiler_params=pltpu.CompilerParams(vmem_limit_bytes=54 * 2**20),
         cost_estimate=pl.CostEstimate(flops=1, bytes_accessed=1, transcendentals=1),
         name="top_layer" if whole_layer else "mlp_backward",
@@ -358,25 +375,33 @@
     tokens = hidden.shape[0]
     scale = 1.0 / math.sqrt(HEAD_DIM)
 
-    def body(hidden_ref, mid_ref, packed_ref, mixed_ref, row_ref, down_docs, across_docs, *rest):
+    def body(hidden_at, packed_at, mixed_at, mid_ref, row_ref, down_docs, across_docs, *rest):
         if steps is not None:
             steps_ref, rest = rest[0], rest[1:]
         refs, rest = rest[: len(arrays)], rest[len(arrays) :]
         grads_ref, rest = rest[:2], rest[2:]
         in_ref, small_ref = rest[:2]
         qkv_ref, out_ref, qkv_stage, out_stage, gm_ref, gp_ref, sems = rest[2:9]
+        hidden_ref, packed_ref, mixed_ref, rest = rest[9], rest[10], rest[11], rest[:9] + rest[12:]
+        saved = [(hidden_at, hidden_ref), (mixed_at, mixed_ref), (packed_at, packed_ref)]
+        saved = [pltpu.make_async_copy(*pair, sems.at[6 + n]) for n, pair in enumerate(saved)]
+        for copy in saved:
+            copy.start()
         named = {"qkv": sems.at[0], "out": sems.at[1]}
         start_fetch(sources, refs, {"qkv": qkv_ref, "out": out_ref}, named)
+        saved[0].wait()
         unit, inverse = unit_of(hidden_ref[...])
         normed = (unit * spot(row_ref, "gain_a") + spot(row_ref, "shift_a")).astype(BF)
         grad_branch = mid_ref[...].astype(BF)
         small_ref[:, 2 * WIDTH : 3 * WIDTH] = jnp.sum(grad_branch.astype(F32), axis=0, keepdims=True)
+        saved[1].wait()
         out_stage[...] = dot(mixed_ref[...], grad_branch, (0, 0)).astype(BF)
         chips = [(there, there * SLAB) for there in range(16)]
         for half in range(2):
             send_rows(out_stage, chips, pl.ds(half * HALF, HALF), grads_ref, half, 3 * HALF, sems.at[2])
         arrived(out_ref, named["out"])
         gm_ref[...] = dot(grad_branch, out_ref[...], (1, 1)).astype(BF)
+        saved[2].wait()
         same = down_docs[...] == across_docs[...]
         first_head = head_lanes(tokens)
 
@@ -455,11 +480,14 @@
         jax.ShapeDtypeStruct((tokens, WIDTH), F32),
         jax.ShapeDtypeStruct((1, 5 * WIDTH), F32),
     ]
-    operands = [hidden, grad_mid, packed, mixed, row, docs.reshape(-1, 1), docs.reshape(1, -1)]
+    operands = [hidden, packed, mixed, grad_mid, row, docs.reshape(-1, 1), docs.reshape(1, -1)]
     scratch = [pltpu.VMEM(SHAPES["qkv"], BF), pltpu.VMEM(SHAPES["out"], BF)] * 2 + [
         pltpu.VMEM((tokens, WIDTH), BF),
         pltpu.VMEM((tokens, 3 * WIDTH), BF),
-        pltpu.SemaphoreType.DMA((6,)),
+        pltpu.SemaphoreType.DMA((9,)),
+        pltpu.VMEM((tokens, WIDTH), F32),
+        pltpu.VMEM((tokens, 3 * WIDTH), BF),
+        pltpu.VMEM((tokens, WIDTH), BF),
     ]
     if steps is not None:
         operands.append(jnp.pad(steps, ((0, 0), (0, 8 - steps.shape[1])), constant_values=-2))
@@ -467,10 +495,10 @@
     return pl.pallas_call(
         body,
         out_shape=outs,
-        in_specs=[WHOLE] * len(operands) + [ANY] * len(arrays),
+        in_specs=[ANY] * 3 + [WHOLE] * (len(operands) - 3) + [ANY] * len(arrays),
         out_specs=[ANY] * len(sums) + [WHOLE] * (len(outs) - len(sums)),
         scratch_shapes=scratch,
-        compiler_params=pltpu.CompilerParams(vmem_limit_bytes=50 * 2**20),
+        compiler_params=pltpu.CompilerParams(vmem_limit_bytes=60 * 2**20),
         cost_estimate=pl.CostEstimate(flops=1, bytes_accessed=1, transcendentals=1),
         name="attn_backward",
     )(*operands, *arrays)
@@ -793,7 +821,7 @@
 
     all_extra = lay_extra(source0)
     small_all = all_extra[32::SLAB].reshape(16, 2, 2, HALF).transpose(1, 0, 2, 3).reshape(2, TUNED, HALF)
-    rows = [spread_smalls(small_all[layer], layer) for layer in range(2)]
+    rows = [spread_smalls(small_all[0], 0)]
     owner = steps // 32
     row_of = (owner // 2) * SLAB + steps % 32
     row_hot = (row_of[:, None] == jnp.arange(16 * SLAB, dtype=jnp.int32)[None, :]).astype(BF)
@@ -803,9 +831,10 @@
     of_doc = [(docs == s)[:, None] for s in range(doc_count)]
     start = embedded.astype(F32) + sum(jnp.where(of_doc[s], doc_rows[s][None], 0.0) for s in range(doc_count))
 
-    start, rows = gate((start, rows))
     packed0, mixed0, middle0, between = layer_forward(start, rows[0], docs, [source0])
 
+    between, small_1 = gate((between, small_all[1]))
+    rows.append(spread_smalls(small_1, 1))
     kept_m, sent_m, mid1, small_mlp1, packed1, mixed1, block_output = mlp_backward(
         between, cotangent, rows[1], [source1], docs
     )
@@ -857,7 +886,7 @@
     half_m = half_line(levels_m)
     low_b, to_go = gate((low_b, to_go))
     x_b = along_each(*sums_b.sides(*low_b))
-    low_c, half_m = gate((low_c, half_m))
+    low_c, half_m, x_t = gate((low_c, half_m, x_t))
     x_c = along_each(*sums_c.sides(*low_c))
     levels_t = sums_t.levels(*x_t)
     half_t = half_line(levels_t)
@@ -865,21 +894,19 @@
     half_a = jnp.concatenate([half_m, half_t], axis=-1)
     levels_b = sums_b.levels(*x_b)
     half_b = half_line(levels_b)
-    levels_b, half_a = gate((levels_b, half_a))
+    x_c, levels_b = gate((x_c, levels_b))
+    levels_c, half_a = gate((sums_c.levels(*x_c), half_a))
+    back_c = [swap(levels_c[k], ALONG_Z * k) for k in (1, 2, 3)]
     last_a = line_end(levels_a, half_a)
-    half_b, last_a = gate((half_b, last_a))
-    last_b = line_end(levels_b, half_b)
-    levels_c = sums_c.levels(*x_c)
-    back_c = [swap(levels_c[k], ALONG_Z * k) for k in (1, 2, 3)]
     up_1, down_1, qkv_1, out_1 = own_rows(
         ("up", "down_by_core", "qkv", "out"), line_sum(levels_a, half_a, last_a)
     )
     up_1 = up_1.reshape(24, 4, TUNED, 24).transpose(0, 2, 1, 3).reshape(24, HIDDEN)
+    half_b, back_c, up_1, down_1, qkv_1, out_1 = gate((half_b, back_c, up_1, down_1, qkv_1, out_1))
+    last_b = line_end(levels_b, half_b)
+    qkv_0, out_0, extra_0 = own_rows(("qkv", "out", "extra"), total(levels_c[0], *back_c))
     up_0, down_0 = own_rows(("up", "down"), line_sum(levels_b, half_b, last_b))
     up, down = jnp.stack([up_0, up_1]), jnp.stack([down_0, down_1])
-    up, down, qkv_1, out_1, back_c = gate((up, down, qkv_1, out_1, back_c))
-    sum_c = total(levels_c[0], *back_c)
-    qkv_0, out_0, extra_0 = own_rows(("qkv", "out", "extra"), sum_c)
     small_out = extra_0[32].reshape(2, HALF)
     out_b, gain_a, shift_a, down_b, gain_b, shift_b = [small_out[:, n * 24 : n * 24 + 24] for n in range(6)]
     return (

time: 410 us -> 404 us (0.985)
  starting transfers between devices: 69.5 us -> 64.9 us
    ppermute x53, starting transfers between devices: 64.8 us -> 60 us  [swap(): return lax.ppermute(value, 'dp', [(i, i ^ stride) for i in range(TUNED)])]
    unnamed x116 -> x106, local copies, waits for them, and re-layouts: 10.2 us -> 5.66 us
    convert_element_type x2 -> x3, other arithmetic: 7.46 us -> 10 us  [sides(): (self.pair(2) + high.astype(F32)).astype(BF)]
  transfers between devices with their start and end apart: 58 -> 58, of which waited for: 27 -> 26; matrix products, arithmetic and copies ran while one was open for 17% -> 18% of each run, Pallas kernels for 15% -> 16%
where the time goes in v4:
time: 404 us; the launch traced here: 399 us
  waiting for transfers between devices  149 us (37%)
  Pallas kernels  81.7 us (20%)
  starting transfers between devices  64.9 us (16%)
  other arithmetic  47.8 us (12%)
  local copies, waits for them, and re-layouts  26.1 us (6%)
  between operations  16.2 us (4%)
  matrix products  13.8 us (3%)
    ppermute x53, waiting for transfers between devices, swap(): return lax.ppermute(value, 'dp', [(i, i ^ stride) for i in range(TUNED)])  133 us
    ppermute x53, starting transfers between devices, swap(): return lax.ppermute(value, 'dp', [(i, i ^ stride) for i in range(TUNED)])  60 us
    pallas_call x2, Pallas kernels, mlp_backward(): pl.pallas_call(body, out_shape=outs, in_specs=[WHOLE] * (3 + len(doc_oper...  33.5 us
    pallas_call x2, Pallas kernels, attn_backward(): pl.pallas_call(body, out_shape=outs, in_specs=[ANY] * 3 + [WHOLE] * (len(...  33 us
    ppermute x4, waiting for transfers between devices, swap_from(): lax.ppermute(value, 'dp', [(i, i ^ stride) for i in range(TUNED) if i //...  15.1 us
    pallas_call x1, Pallas kernels, layer_forward(): pl.pallas_call(body, out_shape=[jax.ShapeDtypeStruct((tokens, 3 * WIDTH),...  13.6 us
    convert_element_type x3, other arithmetic, sides(): (self.pair(2) + high.astype(F32)).astype(BF)  10 us
    convert_element_type x4, other arithmetic, levels(): return (self.pair(0) + total(by_x, by_y)).astype(BF)  8.73 us
  transfers between devices with their start and end apart: 58, of which 26 were waited for; matrix products, arithmetic and copies ran while one was open for 18% of the time, Pallas kernels for 16%

profile of v4, /device:TPU:0, one launch (start us, length us, event | category | flops | bytes accessed | tf_op | source)
XLA Modules:
  0.0 399.1 jit_solution(17375523613481700186)
XLA Ops:
  15.3 3.0 collective-permute-start.2
  18.3 1.5 collective-permute-start.1
  19.8 1.6 collective-permute-start.6
  21.4 1.5 collective-permute-start.13
  22.8 10.7 %collective-permute-done.2 = bf16[48,5376]{1,0:T(8,128)(2,1)S(1)} collective-permute-done((bf16[48,5376]{1,0:T(8,128)(2,1)S(1)}, bf16[48,5376]{1,0:T(8,128)(2,1)S(1)}, u32[]{:S(2)}, u32[]{:S(2)}) %collective-permute-start.2) | collective-permute-done | bytes 516128 | tf_op jit(solution)/shard_map/ppermute | solution.py:24
  33.5 1.8 collective-permute-start.4
  35.3 1.6 collective-permute-start.3
  36.9 3.5 collective-permute-done.6
  45.3 14.4 %collective-permute-done.8 = bf16[48,5376]{1,0:T(8,128)(2,1)S(1)} collective-permute-done((bf16[48,5376]{1,0:T(8,128)(2,1)}, bf16[48,5376]{1,0:T(8,128)(2,1)S(1)}, u32[]{:S(2)}, u32[]{:S(2)}) %collective-permute-start.8) | collective-permute-done | bytes 516128 | tf_op jit(solution)/shard_map/ppermute | solution.py:24
  59.8 2.4 collective-permute-start.9
  62.3 8.2 %collective-permute-done.14 = bf16[48,5376]{1,0:T(8,128)(2,1)S(1)} collective-permute-done((bf16[48,5376]{1,0:T(8,128)(2,1)}, bf16[48,5376]{1,0:T(8,128)(2,1)S(1)}, u32[]{:S(2)}, u32[]{:S(2)}) %collective-permute-start.14) | collective-permute-done | bytes 516128 | tf_op jit(solution)/shard_map/ppermute | solution.py:28
  70.9 1.7 collective-permute-start.15
  72.6 1.5 collective-permute-start.20
  74.1 2.6 pad_maximum_fusion.1.rest_2_.rest_3_
  76.8 3.2 collective-permute-done.16
  80.0 3.7 collective-permute-start.18
  84.8 6.9 %collective-permute-done.20 = bf16[48,5376]{1,0:T(8,128)(2,1)S(1)} collective-permute-done((bf16[48,5376]{1,0:T(8,128)(2,1)S(1)}, bf16[48,5376]{1,0:T(8,128)(2,1)S(1)}, u32[]{:S(2)}, u32[]{:S(2)}) %collective-permute-start.20) | collective-permute-done | bytes 516128 | tf_op jit(solution)/shard_map/ppermute | solution.py:28
  93.4 21.1 %collective-permute-done.22 = bf16[48,5376]{1,0:T(8,128)(2,1)S(1)} collective-permute-done((bf16[48,5376]{1,0:T(8,128)(2,1)S(1)}, bf16[48,5376]{1,0:T(8,128)(2,1)S(1)}, u32[]{:S(2)}, u32[]{:S(2)}) %collective-permute-start.22) | collective-permute-done | bytes 516128 | tf_op jit(solution)/shard_map/ppermute | solution.py:24
  115.6 2.1 collective-permute-start.23
  117.7 1.6 pad_maximum_fusion.2.rest_4_.rest_5_
  119.2 7.2 %collective-permute-done.24 = bf16[48,2688]{1,0:T(8,128)(2,1)S(1)} collective-permute-done((bf16[48,2688]{1,0:T(8,128)(2,1)S(1)}, bf16[48,2688]{1,0:T(8,128)(2,1)S(1)}, u32[]{:S(2)}, u32[]{:S(2)}) %collective-permute-start.24) | collective-permute-done | bytes 258080 | tf_op jit(solution)/shard_map/ppermute | solution.py:24
  127.6 1.6 pad_maximum_fusion.3.rest_6_.rest_7_
  129.4 4.2 %collective-permute-done.25.rest_7_.rest_8_ = bf16[4,48,5376]{2,1,0:T(8,128)(2,1)} collective-permute-done((bf16[4,48,5376]{2,1,0:T(8,128)(2,1)}, bf16[4,48,5376]{2,1,0:T(8,128)(2,1)}, u32[]{:S(2)}, u32[]{:S(2)}) %collective-permute-start.25) | collective-permute-done | bytes 2064416 | tf_op jit(solution)/shard_map/ppermute | solution.py:24
  133.6 1.7 lay_extra.1
  136.7 1.7 slice.503
  138.5 2.1 fusion.59
  140.9 3.0 fusion.20
  144.3 13.6 %layer_forward.1 = (bf16[256,2304]{1,0:T(8,128)(2,1)S(1)}, bf16[256,768]{1,0:T(8,128)(2,1)S(1)}, f32[256,768]{1,0:T(8,128)S(1)}, f32[256,768]{1,0:T(8,128)S(1)}) custom-call(f32[256,768]{1,0:T(8,128)S(1)} %add_add_fusion.hidden_ref.hidden_at, f32[1,9984]{1,0:T(1,128)S(1)} %broadcast_in_dim.132.row_ref, s32[256,1]{1,0:T(8,128)S(1)} %copy.84.down_docs.rest_0_, ...), custom_call_target="tpu_custom_call" | custom-call | flops 1 | bytes 1 | tf_op jit(solution)/shard_map/layer_forward/pallas_call | solution.py:229
  159.9 3.0 fusion.21
  163.5 18.9 %top_layer.1 = (bf16[16,48,3072]{2,1,0:T(8,128)(2,1)}, bf16[16,48,3072]{2,1,0:T(8,128)(2,1)}, f32[256,768]{1,0:T(8,128)}, f32[1,5376]{1,0:T(1,128)}, bf16[256,23...) custom-call(f32[256,768]{1,0:T(8,128)} %copy-done.4, bf16[256,768]{1,0:T(8,128)(2,1)} %grad_ref.1, ...), custom_call_target="tpu_custom_call" | custom-call | flops 1 | bytes 1 | tf_op jit(solution)/shard_map/top_layer/pallas_call | solution.py:359
  182.7 15.7 %attn_backward.2 = (bf16[16,48,1536]{2,1,0:T(8,128)(2,1)}, bf16[16,48,1536]{2,1,0:T(8,128)(2,1)}, f32[256,768]{1,0:T(8,128)}, f32[1,3840]{1,0:T(1,128)}) custom-call(f32[256,768]{1,0:T(8,128)} %copy-done.4, bf16[256,2304]{1,0:T(8,128)(2,1)} %get-tuple-element.102.packed_at, bf16[256,768]{1,0:T(8,128)(2,1)} %get-tuple-element.103.mixed_at, ...), custom_call_target="tpu_custom_call" | custom-call | flops 1 | bytes 1 | tf_op jit(solution)/shard_map/attn_backward/pallas_call | solution.py:495
  198.5 2.1 fusion.32
  201.0 2.0 collective-permute-start.27
  204.1 14.6 %mlp_backward.1 = (bf16[16,48,3072]{2,1,0:T(8,128)(2,1)}, bf16[16,48,3072]{2,1,0:T(8,128)(2,1)}, f32[256,768]{1,0:T(8,128)}, f32[1,5376]{1,0:T(1,128)}) custom-call(f32[256,768]{1,0:T(8,128)} %copy-done.6, f32[256,768]{1,0:T(8,128)} %get-tuple-element.112.grad_ref, f32[1,9984]{1,0:T(1,128)} %copy-done.7, bf16[4,48,5376]{2,1,0:T(8,128)(2,1)} %copy-done, ...), custom_call_target="tpu_custom_call" | custom-call | flops 1 | bytes 1 | tf_op jit(solution)/shard_map/mlp_backward/pallas_call | solution.py:359
  222.6 4.9 %fusion.14 = (bf16[4,48,3072]{2,1,0:T(8,128)(2,1)}, bf16[4,48,3072]{2,1,0:T(8,128)(2,1)}) fusion(bf16[4,4,48,3072]{3,2,1,0:T(8,128)(2,1)} %bitcast.32, bf16[4,4,48,3072]{3,2,1,0:T(8,128)(2,1)} %bitcast.373, bf16[4,48,1536]{2,1,0:T(8,128)(2,1)} %collective-permute-done.28, bf16[4,48,1536]{2,1,0:T(8,128)(2,1)S(1)} %collective-permute-done.27), kind=kLoop, calls=%fused_computation.24 | loop fusion | flops 7077888 | bytes 8257536 | tf_op jit(solution)/shard_map/convert_element_type | solution.py:677
  227.5 1.9 collective-permute-start.34
  232.3 2.6 fusion.23
  235.1 2.9 fusion.27
  239.1 17.2 %attn_backward.3 = (bf16[16,48,2304]{2,1,0:T(8,128)(2,1)}, bf16[16,48,2304]{2,1,0:T(8,128)(2,1)}, f32[256,768]{1,0:T(8,128)}, f32[1,3840]{1,0:T(1,128)}) custom-call(f32[256,768]{1,0:T(8,128)} %copy-done.2, bf16[256,2304]{1,0:T(8,128)(2,1)} %copy-done.5, bf16[256,768]{1,0:T(8,128)(2,1)} %copy-done.8, f32[256,768]{1,0:T(8,128)} %get-tuple-element.123.mid_ref, ...), custom_call_target="tpu_custom_call" | custom-call | flops 1 | bytes 1 | tf_op jit(solution)/shard_map/attn_backward/pallas_call | solution.py:495
  257.2 2.8 fusion.28
  262.6 2.8 fusion.34
  265.4 4.5 %collective-permute-done.35 = bf16[4,48,1536]{2,1,0:T(8,128)(2,1)} collective-permute-done((bf16[4,48,1536]{2,1,0:T(8,128)(2,1)}, bf16[4,48,1536]{2,1,0:T(8,128)(2,1)}, u32[]{:S(2)}, u32[]{:S(2)}) %collective-permute-start.35) | collective-permute-done | bytes 589856 | tf_op jit(solution)/shard_map/ppermute | solution.py:24
  271.5 5.1 %collective-permute-done.37 = bf16[16,48,2304]{2,1,0:T(8,128)(2,1)} collective-permute-done((bf16[16,48,2304]{2,1,0:T(8,128)(2,1)}, bf16[16,48,2304]{2,1,0:T(8,128)(2,1)}, u32[]{:S(2)}, u32[]{:S(2)}) %collective-permute-start.37) | collective-permute-done | bytes 3538976 | tf_op jit(solution)/shard_map/ppermute | solution.py:24
  276.5 3.1 fusion.13
  279.7 5.6 %collective-permute-start.40 = (bf16[2,48,3072]{2,1,0:T(8,128)(2,1)S(1)}, bf16[2,48,3072]{2,1,0:T(8,128)(2,1)S(1)}, u32[]{:S(2)}, u32[]{:S(2)}) collective-permute-start(bf16[2,48,3072]{2,1,0:T(8,128)(2,1)S(1)} %slice.678), channel_id=1, source_target_pairs={{0,24},{1,25},{2,26},{3,27},{4,28},{5,29},{6,30},{7,31},{8,16},{9,... | collective-permute-start | bytes 1769480 | tf_op jit(solution)/shard_map/ppermute | solution.py:24
  285.2 1.6 fusion.38
  289.1 2.6 fusion.11
  291.7 1.6 collective-permute-start.45
  293.7 6.3 %collective-permute-done.39 = bf16[4,48,1152]{2,1,0:T(8,128)(2,1)S(1)} collective-permute-done((bf16[4,48,1152]{2,1,0:T(8,128)(2,1)S(1)}, bf16[4,48,1152]{2,1,0:T(8,128)(2,1)S(1)}, u32[]{:S(2)}, u32[]{:S(2)}) %collective-permute-start.39) | collective-permute-done | bytes 442400 | tf_op jit(solution)/shard_map/ppermute | solution.py:24
  300.9 1.7 fusion.22
  302.6 2.2 collective-permute-start.47
  304.8 2.5 fusion.16
  309.0 2.2 collective-permute-done.47
  311.3 13.9 %collective-permute-done.45 = bf16[4,48,3072]{2,1,0:T(8,128)(2,1)S(1)} collective-permute-done((bf16[4,48,3072]{2,1,0:T(8,128)(2,1)S(1)}, bf16[4,48,3072]{2,1,0:T(8,128)(2,1)S(1)}, u32[]{:S(2)}, u32[]{:S(2)}) %collective-permute-start.45) | collective-permute-done | bytes 1179680 | tf_op jit(solution)/shard_map/ppermute | solution.py:24
  326.1 2.0 fusion.12
  329.0 2.1 collective-permute-start.48
  331.1 12.5 %collective-permute-done.42 = bf16[4,48,2304]{2,1,0:T(8,128)(2,1)S(1)} collective-permute-done((bf16[4,48,2304]{2,1,0:T(8,128)(2,1)S(1)}, bf16[4,48,2304]{2,1,0:T(8,128)(2,1)S(1)}, u32[]{:S(2)}, u32[]{:S(2)}) %collective-permute-start.42) | collective-permute-done | bytes 884768 | tf_op jit(solution)/shard_map/ppermute | solution.py:24
  343.7 1.9 fusion.18
  345.7 4.5 %collective-permute-start.52 = (bf16[48,4608]{1,0:T(8,128)(2,1)S(1)}, bf16[48,4608]{1,0:T(8,128)(2,1)S(1)}, u32[]{:S(2)}, u32[]{:S(2)}) collective-permute-start(bf16[48,4608]{1,0:T(8,128)(2,1)S(1)} %fusion.39), channel_id=1, source_target_pairs={{0,8},{1,9},{2,10},{3,11},{4,12},{5,13},{6,14},{7,15},{8,0},{9,1},... | collective-permute-start | bytes 1327112 | tf_op jit(solution)/shard_map/ppermute | solution.py:24
  351.1 2.0 collective-permute-start.51
  353.0 2.4 collective-permute-start.49
  355.5 10.5 %collective-permute-done.52 = bf16[48,4608]{1,0:T(8,128)(2,1)S(1)} collective-permute-done((bf16[48,4608]{1,0:T(8,128)(2,1)S(1)}, bf16[48,4608]{1,0:T(8,128)(2,1)S(1)}, u32[]{:S(2)}, u32[]{:S(2)}) %collective-permute-start.52) | collective-permute-done | bytes 442400 | tf_op jit(solution)/shard_map/ppermute | solution.py:24
  371.4 1.8 reshape.616
  382.6 4.7 %collective-permute-done.55 = bf16[48,3072]{1,0:T(8,128)(2,1)S(1)} collective-permute-done((bf16[48,3072]{1,0:T(8,128)(2,1)S(1)}, bf16[48,3072]{1,0:T(8,128)(2,1)S(1)}, u32[]{:S(2)}, u32[]{:S(2)}) %collective-permute-start.55) | collective-permute-done | bytes 294944 | tf_op jit(solution)/shard_map/ppermute | solution.py:24
  (341 shorter events, 64.7 us)
Async XLA Ops:
  7.2 156.3 %all-gather.2.cloned.1.call-start = ((), (), s32[]{:S(2)}) async-start(), calls=%async_computation | async-start | bytes 14598144 | tf_op jit(solution)/shard_map/all_gather | solution.py:808
  13.4 1.7 collective-permute-start
  15.3 18.2 %collective-permute-start.2 = (bf16[48,5376]{1,0:T(8,128)(2,1)S(1)}, bf16[48,5376]{1,0:T(8,128)(2,1)S(1)}, u32[]{:S(2)}, u32[]{:S(2)}) collective-permute-start(bf16[48,5376]{1,0:T(8,128)(2,1)S(1)} %constant_dynamic-update-slice_fusion.2), channel_id=1, source_target_pairs={{0,4},{1,5},{2,6},{3,7},{4,0},{5,1},{6,2},{7,3},{8,12},{9,13},{10,... | collective-permute-start | bytes 1548296 | tf_op jit(solution)/shard_map/ppermute | solution.py:24
  18.3 17.0 %collective-permute-start.1 = (bf16[48,5376]{1,0:T(8,128)(2,1)S(1)}, bf16[48,5376]{1,0:T(8,128)(2,1)S(1)}, u32[]{:S(2)}, u32[]{:S(2)}) collective-permute-start(bf16[48,5376]{1,0:T(8,128)(2,1)S(1)} %constant_dynamic-update-slice_fusion.2), channel_id=1, source_target_pairs={{0,2},{1,3},{2,0},{3,1},{4,6},{5,7},{6,4},{7,5},{8,10},{9,11},{10,... | collective-permute-start | bytes 1548296 | tf_op jit(solution)/shard_map/ppermute | solution.py:24
  19.8 20.6 %collective-permute-start.6 = (bf16[48,5376]{1,0:T(8,128)(2,1)S(1)}, bf16[48,5376]{1,0:T(8,128)(2,1)}, u32[]{:S(2)}, u32[]{:S(2)}) collective-permute-start(bf16[48,5376]{1,0:T(8,128)(2,1)S(1)} %constant_dynamic-update-slice_fusion.2), channel_id=1, source_target_pairs={{0,8},{1,9},{2,10},{3,11},{4,12},{5,13},{6,14},{7,15},{8,0},{9,1},... | collective-permute-start | bytes 1548296 | tf_op jit(solution)/shard_map/ppermute | solution.py:24
  21.4 19.8 %collective-permute-start.13 = (bf16[48,5376]{1,0:T(8,128)(2,1)S(1)}, bf16[48,5376]{1,0:T(8,128)(2,1)}, u32[]{:S(2)}, u32[]{:S(2)}) collective-permute-start(bf16[48,5376]{1,0:T(8,128)(2,1)S(1)} %constant_dynamic-update-slice_fusion.2), channel_id=1, source_target_pairs={{8,16},{9,17},{10,18},{11,19},{12,20},{13,21},{14,22},{15,23},{16,... | collective-permute-start | bytes 1548296 | tf_op jit(solution)/shard_map/ppermute | solution.py:28
  33.5 7.7 %collective-permute-start.4 = (bf16[48,2688]{1,0:T(8,128)(2,1)S(1)}, bf16[48,2688]{1,0:T(8,128)(2,1)S(1)}, u32[]{:S(2)}, u32[]{:S(2)}) collective-permute-start(bf16[48,2688]{1,0:T(8,128)(2,1)S(1)} %slice.633), channel_id=1, source_target_pairs={{0,2},{1,3},{2,0},{3,1},{4,6},{5,7},{6,4},{7,5},{8,10},{9,11},{10,... | collective-permute-start | bytes 774152 | tf_op jit(solution)/shard_map/ppermute | solution.py:24
  35.3 8.6 %collective-permute-start.3 = (bf16[48,2688]{1,0:T(8,128)(2,1)S(1)}, bf16[48,2688]{1,0:T(8,128)(2,1)S(1)}, u32[]{:S(2)}, u32[]{:S(2)}) collective-permute-start(bf16[48,2688]{1,0:T(8,128)(2,1)S(1)} %slice.632), channel_id=1, source_target_pairs={{0,4},{1,5},{2,6},{3,7},{4,0},{5,1},{6,2},{7,3},{8,12},{9,13},{10,... | collective-permute-start | bytes 774152 | tf_op jit(solution)/shard_map/ppermute | solution.py:24
  40.4 30.1 %collective-permute-start.12 = (bf16[48,5376]{1,0:T(8,128)(2,1)}, bf16[48,5376]{1,0:T(8,128)(2,1)S(1)}, u32[]{:S(2)}, u32[]{:S(2)}) collective-permute-start(bf16[48,5376]{1,0:T(8,128)(2,1)} %collective-permute-done.6), channel_id=1, source_target_pairs={{8,16},{9,17},{10,18},{11,19},{12,20},{13,21},{14,22},{15,23},{16,... | collective-permute-start | bytes 1548296 | tf_op jit(solution)/shard_map/ppermute | solution.py:28
  41.1 18.6 %collective-permute-start.8 = (bf16[48,5376]{1,0:T(8,128)(2,1)}, bf16[48,5376]{1,0:T(8,128)(2,1)S(1)}, u32[]{:S(2)}, u32[]{:S(2)}) collective-permute-start(bf16[48,5376]{1,0:T(8,128)(2,1)} %collective-permute-done.6), channel_id=1, source_target_pairs={{0,4},{1,5},{2,6},{3,7},{4,0},{5,1},{6,2},{7,3},{8,12},{9,13},{10,... | collective-permute-start | bytes 1548296 | tf_op jit(solution)/shard_map/ppermute | solution.py:24
  41.1 18.7 %collective-permute-start.7 = (bf16[48,5376]{1,0:T(8,128)(2,1)}, bf16[48,5376]{1,0:T(8,128)(2,1)S(1)}, u32[]{:S(2)}, u32[]{:S(2)}) collective-permute-start(bf16[48,5376]{1,0:T(8,128)(2,1)} %collective-permute-done.6), channel_id=1, source_target_pairs={{0,2},{1,3},{2,0},{3,1},{4,6},{5,7},{6,4},{7,5},{8,10},{9,11},{10,... | collective-permute-start | bytes 1548296 | tf_op jit(solution)/shard_map/ppermute | solution.py:24
  41.2 29.2 %collective-permute-start.14 = (bf16[48,5376]{1,0:T(8,128)(2,1)}, bf16[48,5376]{1,0:T(8,128)(2,1)S(1)}, u32[]{:S(2)}, u32[]{:S(2)}) collective-permute-start(bf16[48,5376]{1,0:T(8,128)(2,1)} %collective-permute-done.13), channel_id=1, source_target_pairs={{8,0},{9,1},{10,2},{11,3},{12,4},{13,5},{14,6},{15,7},{16,24},{17,... | collective-permute-start | bytes 1548296 | tf_op jit(solution)/shard_map/ppermute | solution.py:28
  45.2 88.3 %copy-start = (bf16[4,48,5376]{2,1,0:T(8,128)(2,1)}, bf16[4,48,5376]{2,1,0:T(8,128)(2,1)S(1)}, u32[]{:S(2)}) copy-start(bf16[4,48,5376]{2,1,0:T(8,128)(2,1)S(1)} %pad_maximum_fusion.rest_0_.rest_1_) | copy-start | bytes 6193156
  45.3 84.1 %collective-permute-start.5 = (bf16[4,48,5376]{2,1,0:T(8,128)(2,1)S(1)}, bf16[4,48,5376]{2,1,0:T(8,128)(2,1)}, u32[]{:S(2)}, u32[]{:S(2)}) collective-permute-start(bf16[4,48,5376]{2,1,0:T(8,128)(2,1)S(1)} %pad_maximum_fusion.rest_0_.rest_1_), channel_id=1, source_target_pairs={{0,1},{1,0},{2,3},{3,2},{4,5},{5,4},{6,7},{7,6},{8,9},{9,8},{10,11... | collective-permute-start | bytes 6193160 | tf_op jit(solution)/shard_map/ppermute | solution.py:24
  59.7 12.9 %collective-permute-start.10 = (bf16[48,2688]{1,0:T(8,128)(2,1)S(1)}, bf16[48,2688]{1,0:T(8,128)(2,1)S(1)}, u32[]{:S(2)}, u32[]{:S(2)}) collective-permute-start(bf16[48,2688]{1,0:T(8,128)(2,1)S(1)} %slice.635), channel_id=1, source_target_pairs={{0,2},{1,3},{2,0},{3,1},{4,6},{5,7},{6,4},{7,5},{8,10},{9,11},{10,... | collective-permute-start | bytes 774152 | tf_op jit(solution)/shard_map/ppermute | solution.py:24
  59.8 14.3 %collective-permute-start.9 = (bf16[48,2688]{1,0:T(8,128)(2,1)S(1)}, bf16[48,2688]{1,0:T(8,128)(2,1)S(1)}, u32[]{:S(2)}, u32[]{:S(2)}) collective-permute-start(bf16[48,2688]{1,0:T(8,128)(2,1)S(1)} %slice.634), channel_id=1, source_target_pairs={{0,4},{1,5},{2,6},{3,7},{4,0},{5,1},{6,2},{7,3},{8,12},{9,13},{10,... | collective-permute-start | bytes 774152 | tf_op jit(solution)/shard_map/ppermute | solution.py:24
  70.5 9.5 %collective-permute-start.16 = (bf16[48,5376]{1,0:T(8,128)(2,1)S(1)}, bf16[48,5376]{1,0:T(8,128)(2,1)S(1)}, u32[]{:S(2)}, u32[]{:S(2)}) collective-permute-start(bf16[48,5376]{1,0:T(8,128)(2,1)S(1)} %broadcast_select_fusion.1), channel_id=1, source_target_pairs={{0,4},{1,5},{2,6},{3,7},{4,0},{5,1},{6,2},{7,3},{8,12},{9,13},{10,... | collective-permute-start | bytes 1548296 | tf_op jit(solution)/shard_map/ppermute | solution.py:24
  70.9 12.8 %collective-permute-start.15 = (bf16[48,5376]{1,0:T(8,128)(2,1)S(1)}, bf16[48,5376]{1,0:T(8,128)(2,1)S(1)}, u32[]{:S(2)}, u32[]{:S(2)}) collective-permute-start(bf16[48,5376]{1,0:T(8,128)(2,1)S(1)} %broadcast_select_fusion.1), channel_id=1, source_target_pairs={{0,2},{1,3},{2,0},{3,1},{4,6},{5,7},{6,4},{7,5},{8,10},{9,11},{10,... | collective-permute-start | bytes 1548296 | tf_op jit(solution)/shard_map/ppermute | solution.py:24
  72.6 19.2 %collective-permute-start.20 = (bf16[48,5376]{1,0:T(8,128)(2,1)S(1)}, bf16[48,5376]{1,0:T(8,128)(2,1)S(1)}, u32[]{:S(2)}, u32[]{:S(2)}) collective-permute-start(bf16[48,5376]{1,0:T(8,128)(2,1)S(1)} %collective-permute-done.12), channel_id=1, source_target_pairs={{8,0},{9,1},{10,2},{11,3},{12,4},{13,5},{14,6},{15,7},{16,24},{17,... | collective-permute-start | bytes 1548296 | tf_op jit(solution)/shard_map/ppermute | solution.py:28
  76.8 52.6 %collective-permute-start.11 = (bf16[4,48,5376]{2,1,0:T(8,128)(2,1)}, bf16[4,48,5376]{2,1,0:T(8,128)(2,1)}, u32[]{:S(2)}, u32[]{:S(2)}) collective-permute-start(bf16[4,48,5376]{2,1,0:T(8,128)(2,1)} %pad_maximum_fusion.1.rest_2_.rest_3_), channel_id=1, source_target_pairs={{0,1},{1,0},{2,3},{3,2},{4,5},{5,4},{6,7},{7,6},{8,9},{9,8},{10,11... | collective-permute-start | bytes 6193160 | tf_op jit(solution)/shard_map/ppermute | solution.py:24
  80.0 12.9 %collective-permute-start.18 = (bf16[48,2688]{1,0:T(8,128)(2,1)S(1)}, bf16[48,2688]{1,0:T(8,128)(2,1)S(1)}, u32[]{:S(2)}, u32[]{:S(2)}) collective-permute-start(bf16[48,2688]{1,0:T(8,128)(2,1)S(1)} %slice.637), channel_id=1, source_target_pairs={{0,2},{1,3},{2,0},{3,1},{4,6},{5,7},{6,4},{7,5},{8,10},{9,11},{10,... | collective-permute-start | bytes 774152 | tf_op jit(solution)/shard_map/ppermute | solution.py:24
  83.7 9.6 %collective-permute-start.17 = (bf16[48,2688]{1,0:T(8,128)(2,1)S(1)}, bf16[48,2688]{1,0:T(8,128)(2,1)S(1)}, u32[]{:S(2)}, u32[]{:S(2)}) collective-permute-start(bf16[48,2688]{1,0:T(8,128)(2,1)S(1)} %slice.636), channel_id=1, source_target_pairs={{0,4},{1,5},{2,6},{3,7},{4,0},{5,1},{6,2},{7,3},{8,12},{9,13},{10,... | collective-permute-start | bytes 774152 | tf_op jit(solution)/shard_map/ppermute | solution.py:24
  91.8 22.7 %collective-permute-start.22 = (bf16[48,5376]{1,0:T(8,128)(2,1)S(1)}, bf16[48,5376]{1,0:T(8,128)(2,1)S(1)}, u32[]{:S(2)}, u32[]{:S(2)}) collective-permute-start(bf16[48,5376]{1,0:T(8,128)(2,1)S(1)} %broadcast_select_fusion), channel_id=1, source_target_pairs={{0,4},{1,5},{2,6},{3,7},{4,0},{5,1},{6,2},{7,3},{8,12},{9,13},{10,... | collective-permute-start | bytes 1548296 | tf_op jit(solution)/shard_map/ppermute | solution.py:24
  93.0 22.6 %collective-permute-start.21 = (bf16[48,5376]{1,0:T(8,128)(2,1)S(1)}, bf16[48,5376]{1,0:T(8,128)(2,1)S(1)}, u32[]{:S(2)}, u32[]{:S(2)}) collective-permute-start(bf16[48,5376]{1,0:T(8,128)(2,1)S(1)} %broadcast_select_fusion), channel_id=1, source_target_pairs={{0,2},{1,3},{2,0},{3,1},{4,6},{5,7},{6,4},{7,5},{8,10},{9,11},{10,... | collective-permute-start | bytes 1548296 | tf_op jit(solution)/shard_map/ppermute | solution.py:24
  114.6 11.9 %collective-permute-start.24 = (bf16[48,2688]{1,0:T(8,128)(2,1)S(1)}, bf16[48,2688]{1,0:T(8,128)(2,1)S(1)}, u32[]{:S(2)}, u32[]{:S(2)}) collective-permute-start(bf16[48,2688]{1,0:T(8,128)(2,1)S(1)} %slice.639), channel_id=1, source_target_pairs={{0,2},{1,3},{2,0},{3,1},{4,6},{5,7},{6,4},{7,5},{8,10},{9,11},{10,... | collective-permute-start | bytes 774152 | tf_op jit(solution)/shard_map/ppermute | solution.py:24
  115.6 11.9 %collective-permute-start.23 = (bf16[48,2688]{1,0:T(8,128)(2,1)S(1)}, bf16[48,2688]{1,0:T(8,128)(2,1)S(1)}, u32[]{:S(2)}, u32[]{:S(2)}) collective-permute-start(bf16[48,2688]{1,0:T(8,128)(2,1)S(1)} %slice.638), channel_id=1, source_target_pairs={{0,4},{1,5},{2,6},{3,7},{4,0},{5,1},{6,2},{7,3},{8,12},{9,13},{10,... | collective-permute-start | bytes 774152 | tf_op jit(solution)/shard_map/ppermute | solution.py:24
  119.2 10.2 %collective-permute-start.19 = (bf16[4,48,5376]{2,1,0:T(8,128)(2,1)}, bf16[4,48,5376]{2,1,0:T(8,128)(2,1)}, u32[]{:S(2)}, u32[]{:S(2)}) collective-permute-start(bf16[4,48,5376]{2,1,0:T(8,128)(2,1)} %pad_maximum_fusion.2.rest_4_.rest_5_), channel_id=1, source_target_pairs={{0,1},{1,0},{2,3},{3,2},{4,5},{5,4},{6,7},{7,6},{8,9},{9,8},{10,11... | collective-permute-start | bytes 6193160 | tf_op jit(solution)/shard_map/ppermute | solution.py:24
  129.1 4.5 %collective-permute-start.25 = (bf16[4,48,5376]{2,1,0:T(8,128)(2,1)}, bf16[4,48,5376]{2,1,0:T(8,128)(2,1)}, u32[]{:S(2)}, u32[]{:S(2)}) collective-permute-start(bf16[4,48,5376]{2,1,0:T(8,128)(2,1)} %pad_maximum_fusion.3.rest_6_.rest_7_), channel_id=1, source_target_pairs={{0,1},{1,0},{2,3},{3,2},{4,5},{5,4},{6,7},{7,6},{8,9},{9,8},{10,11... | collective-permute-start | bytes 6193160 | tf_op jit(solution)/shard_map/ppermute | solution.py:24
  182.4 16.1 %collective-permute-start.26 = (bf16[16,48,3072]{2,1,0:T(8,128)(2,1)}, bf16[16,48,3072]{2,1,0:T(8,128)(2,1)}, u32[]{:S(2)}, u32[]{:S(2)}) collective-permute-start(bf16[16,48,3072]{2,1,0:T(8,128)(2,1)} %get-tuple-element.106), channel_id=1, source_target_pairs={{0,1},{1,0},{2,3},{3,2},{4,5},{5,4},{6,7},{7,6},{8,9},{9,8},{10,11... | collective-permute-start | bytes 14155784 | tf_op jit(solution)/shard_map/ppermute | solution.py:24
  200.9 17.9 %collective-permute-start.29 = (bf16[16,48,1536]{2,1,0:T(8,128)(2,1)S(1)}, bf16[16,48,1536]{2,1,0:T(8,128)(2,1)}, u32[]{:S(2)}, u32[]{:S(2)}) collective-permute-start(bf16[16,48,1536]{2,1,0:T(8,128)(2,1)S(1)} %copy-done.35), channel_id=1, source_target_pairs={{0,1},{1,0},{2,3},{3,2},{4,5},{5,4},{6,7},{7,6},{8,9},{9,8},{10,11... | collective-permute-start | bytes 7077896 | tf_op jit(solution)/shard_map/ppermute | solution.py:24
  201.0 17.7 %collective-permute-start.27 = (bf16[4,48,1536]{2,1,0:T(8,128)(2,1)S(1)}, bf16[4,48,1536]{2,1,0:T(8,128)(2,1)S(1)}, u32[]{:S(2)}, u32[]{:S(2)}) collective-permute-start(bf16[4,48,1536]{2,1,0:T(8,128)(2,1)S(1)} %get-tuple-element.114), channel_id=1, source_target_pairs={{0,4},{1,5},{2,6},{3,7},{4,0},{5,1},{6,2},{7,3},{8,12},{9,13},{10,... | collective-permute-start | bytes 1769480 | tf_op jit(solution)/shard_map/ppermute | solution.py:24
  203.1 15.6 %collective-permute-start.28 = (bf16[4,48,1536]{2,1,0:T(8,128)(2,1)S(1)}, bf16[4,48,1536]{2,1,0:T(8,128)(2,1)}, u32[]{:S(2)}, u32[]{:S(2)}) collective-permute-start(bf16[4,48,1536]{2,1,0:T(8,128)(2,1)S(1)} %get-tuple-element.115), channel_id=1, source_target_pairs={{0,2},{1,3},{2,0},{3,1},{4,6},{5,7},{6,4},{7,5},{8,10},{9,11},{10,... | collective-permute-start | bytes 1769480 | tf_op jit(solution)/shard_map/ppermute | solution.py:24
  204.1 16.0 %copy-start.11 = (bf16[16,48,1536]{2,1,0:T(8,128)(2,1)S(1)}, bf16[16,48,1536]{2,1,0:T(8,128)(2,1)}, u32[]{:S(2)}) copy-start(bf16[16,48,1536]{2,1,0:T(8,128)(2,1)} %get-tuple-element.119) | copy-start | bytes 7077892
  218.7 37.6 %collective-permute-start.32 = (bf16[16,48,3072]{2,1,0:T(8,128)(2,1)}, bf16[16,48,3072]{2,1,0:T(8,128)(2,1)}, u32[]{:S(2)}, u32[]{:S(2)}) collective-permute-start(bf16[16,48,3072]{2,1,0:T(8,128)(2,1)} %get-tuple-element.125), channel_id=1, source_target_pairs={{0,1},{1,0},{2,3},{3,2},{4,5},{5,4},{6,7},{7,6},{8,9},{9,8},{10,11... | collective-permute-start | bytes 14155784 | tf_op jit(solution)/shard_map/ppermute | solution.py:24
  221.4 9.5 %collective-permute-start.31 = (bf16[4,48,768]{2,1,0:T(8,128)(2,1)S(1)}, bf16[4,48,768]{2,1,0:T(8,128)(2,1)S(1)}, u32[]{:S(2)}, u32[]{:S(2)}) collective-permute-start(bf16[4,48,768]{2,1,0:T(8,128)(2,1)S(1)} %get-tuple-element.195), channel_id=1, source_target_pairs={{0,2},{1,3},{2,0},{3,1},{4,6},{5,7},{6,4},{7,5},{8,10},{9,11},{10,... | collective-permute-start | bytes 884744 | tf_op jit(solution)/shard_map/ppermute | solution.py:24
  222.4 9.8 %collective-permute-start.30 = (bf16[4,48,768]{2,1,0:T(8,128)(2,1)S(1)}, bf16[4,48,768]{2,1,0:T(8,128)(2,1)S(1)}, u32[]{:S(2)}, u32[]{:S(2)}) collective-permute-start(bf16[4,48,768]{2,1,0:T(8,128)(2,1)S(1)} %get-tuple-element.196), channel_id=1, source_target_pairs={{0,4},{1,5},{2,6},{3,7},{4,0},{5,1},{6,2},{7,3},{8,12},{9,13},{10,... | collective-permute-start | bytes 884744 | tf_op jit(solution)/shard_map/ppermute | solution.py:24
  227.5 42.4 %collective-permute-start.34 = (bf16[4,48,3072]{2,1,0:T(8,128)(2,1)}, bf16[4,48,3072]{2,1,0:T(8,128)(2,1)}, u32[]{:S(2)}, u32[]{:S(2)}) collective-permute-start(bf16[4,48,3072]{2,1,0:T(8,128)(2,1)} %get-tuple-element.185), channel_id=1, source_target_pairs={{0,4},{1,5},{2,6},{3,7},{4,0},{5,1},{6,2},{7,3},{8,12},{9,13},{10,... | collective-permute-start | bytes 3538952 | tf_op jit(solution)/shard_map/ppermute | solution.py:24
  229.3 40.5 %collective-permute-start.33 = (bf16[4,48,3072]{2,1,0:T(8,128)(2,1)}, bf16[4,48,3072]{2,1,0:T(8,128)(2,1)}, u32[]{:S(2)}, u32[]{:S(2)}) collective-permute-start(bf16[4,48,3072]{2,1,0:T(8,128)(2,1)} %get-tuple-element.186), channel_id=1, source_target_pairs={{0,2},{1,3},{2,0},{3,1},{4,6},{5,7},{6,4},{7,5},{8,10},{9,11},{10,... | collective-permute-start | bytes 3538952 | tf_op jit(solution)/shard_map/ppermute | solution.py:24
  238.0 31.9 %collective-permute-start.35 = (bf16[4,48,1536]{2,1,0:T(8,128)(2,1)}, bf16[4,48,1536]{2,1,0:T(8,128)(2,1)}, u32[]{:S(2)}, u32[]{:S(2)}) collective-permute-start(bf16[4,48,1536]{2,1,0:T(8,128)(2,1)} %get-tuple-element.132), channel_id=1, source_target_pairs={{0,2},{1,3},{2,0},{3,1},{4,6},{5,7},{6,4},{7,5},{8,10},{9,11},{10,... | collective-permute-start | bytes 1769480 | tf_op jit(solution)/shard_map/ppermute | solution.py:24
  239.1 30.8 %collective-permute-start.36 = (bf16[4,48,1536]{2,1,0:T(8,128)(2,1)}, bf16[4,48,1536]{2,1,0:T(8,128)(2,1)}, u32[]{:S(2)}, u32[]{:S(2)}) collective-permute-start(bf16[4,48,1536]{2,1,0:T(8,128)(2,1)} %get-tuple-element.133), channel_id=1, source_target_pairs={{0,4},{1,5},{2,6},{3,7},{4,0},{5,1},{6,2},{7,3},{8,12},{9,13},{10,... | collective-permute-start | bytes 1769480 | tf_op jit(solution)/shard_map/ppermute | solution.py:24
  239.1 18.0 %copy-start.41 = (s32[9216]{0:T(1024)S(1)}, s32[9216]{0:T(1024)}, u32[]{:S(2)}) copy-start(s32[9216]{0:T(1024)} %constant.186) | copy-start | bytes 110596
  239.1 18.0 %copy-start.42 = (s32[9216]{0:T(1024)S(1)}, s32[9216]{0:T(1024)}, u32[]{:S(2)}) copy-start(s32[9216]{0:T(1024)} %constant.185) | copy-start | bytes 110596
  262.6 26.5 %slice-start = ((s8[4718592]{0:T(1024)(128)(4,1)}), s8[524288]{0:T(1024)(128)(4,1)S(1)}, s32[]{:S(2)}) async-start(s8[4718592]{0:T(1024)(128)(4,1)} %bitcast.368), calls=%async_computation.1 | async-start | bytes 1048576
  269.9 6.6 %collective-permute-start.37 = (bf16[16,48,2304]{2,1,0:T(8,128)(2,1)}, bf16[16,48,2304]{2,1,0:T(8,128)(2,1)}, u32[]{:S(2)}, u32[]{:S(2)}) collective-permute-start(bf16[16,48,2304]{2,1,0:T(8,128)(2,1)} %bitcast_dynamic-update-slice_fusion), channel_id=1, source_target_pairs={{0,1},{1,0},{2,3},{3,2},{4,5},{5,4},{6,7},{7,6},{8,9},{9,8},{10,11... | collective-permute-start | bytes 10616840 | tf_op jit(solution)/shard_map/ppermute | solution.py:24
  270.0 19.1 %slice-start.1 = ((s8[4718592]{0:T(1024)(128)(4,1)}), s8[4194304]{0:T(1024)(128)(4,1)S(1)}, s32[]{:S(2)}) async-start(s8[4718592]{0:T(1024)(128)(4,1)} %bitcast.368), calls=%async_computation.2 | async-start | bytes 8388608
  270.0 19.1 %collective-permute-start.43 = (bf16[4,48,1536]{2,1,0:T(8,128)(2,1)}, bf16[4,48,1536]{2,1,0:T(8,128)(2,1)S(1)}, u32[]{:S(2)}, u32[]{:S(2)}) collective-permute-start(bf16[4,48,1536]{2,1,0:T(8,128)(2,1)} %get-tuple-element.155), channel_id=1, source_target_pairs={{0,4},{1,5},{2,6},{3,7},{4,0},{5,1},{6,2},{7,3},{8,12},{9,13},{10,... | collective-permute-start | bytes 1769480 | tf_op jit(solution)/shard_map/ppermute | solution.py:24
  270.4 18.7 %collective-permute-start.44 = (bf16[4,48,1536]{2,1,0:T(8,128)(2,1)S(1)}, bf16[4,48,1536]{2,1,0:T(8,128)(2,1)S(1)}, u32[]{:S(2)}, u32[]{:S(2)}) collective-permute-start(bf16[4,48,1536]{2,1,0:T(8,128)(2,1)S(1)} %get-tuple-element.156), channel_id=1, source_target_pairs={{0,2},{1,3},{2,0},{3,1},{4,6},{5,7},{6,4},{7,5},{8,10},{9,11},{10,... | collective-permute-start | bytes 1769480 | tf_op jit(solution)/shard_map/ppermute | solution.py:24
  279.7 21.2 %collective-permute-start.40 = (bf16[2,48,3072]{2,1,0:T(8,128)(2,1)S(1)}, bf16[2,48,3072]{2,1,0:T(8,128)(2,1)S(1)}, u32[]{:S(2)}, u32[]{:S(2)}) collective-permute-start(bf16[2,48,3072]{2,1,0:T(8,128)(2,1)S(1)} %slice.678), channel_id=1, source_target_pairs={{0,24},{1,25},{2,26},{3,27},{4,28},{5,29},{6,30},{7,31},{8,16},{9,... | collective-permute-start | bytes 1769480 | tf_op jit(solution)/shard_map/ppermute | solution.py:24
  286.8 13.1 %collective-permute-start.39 = (bf16[4,48,1152]{2,1,0:T(8,128)(2,1)S(1)}, bf16[4,48,1152]{2,1,0:T(8,128)(2,1)S(1)}, u32[]{:S(2)}, u32[]{:S(2)}) collective-permute-start(bf16[4,48,1152]{2,1,0:T(8,128)(2,1)S(1)} %get-tuple-element.191), channel_id=1, source_target_pairs={{0,2},{1,3},{2,0},{3,1},{4,6},{5,7},{6,4},{7,5},{8,10},{9,11},{10,... | collective-permute-start | bytes 1327112 | tf_op jit(solution)/shard_map/ppermute | solution.py:24
  287.8 13.1 %collective-permute-start.38 = (bf16[4,48,1152]{2,1,0:T(8,128)(2,1)S(1)}, bf16[4,48,1152]{2,1,0:T(8,128)(2,1)S(1)}, u32[]{:S(2)}, u32[]{:S(2)}) collective-permute-start(bf16[4,48,1152]{2,1,0:T(8,128)(2,1)S(1)} %get-tuple-element.192), channel_id=1, source_target_pairs={{0,4},{1,5},{2,6},{3,7},{4,0},{5,1},{6,2},{7,3},{8,12},{9,13},{10,... | collective-permute-start | bytes 1327112 | tf_op jit(solution)/shard_map/ppermute | solution.py:24
  291.7 33.5 %collective-permute-start.45 = (bf16[4,48,3072]{2,1,0:T(8,128)(2,1)S(1)}, bf16[4,48,3072]{2,1,0:T(8,128)(2,1)S(1)}, u32[]{:S(2)}, u32[]{:S(2)}) collective-permute-start(bf16[4,48,3072]{2,1,0:T(8,128)(2,1)S(1)} %get-tuple-element.181), channel_id=1, source_target_pairs={{0,2},{1,3},{2,0},{3,1},{4,6},{5,7},{6,4},{7,5},{8,10},{9,11},{10,... | collective-permute-start | bytes 3538952 | tf_op jit(solution)/shard_map/ppermute | solution.py:24
  293.3 32.8 %collective-permute-start.46 = (bf16[4,48,3072]{2,1,0:T(8,128)(2,1)S(1)}, bf16[4,48,3072]{2,1,0:T(8,128)(2,1)S(1)}, u32[]{:S(2)}, u32[]{:S(2)}) collective-permute-start(bf16[4,48,3072]{2,1,0:T(8,128)(2,1)S(1)} %get-tuple-element.182), channel_id=1, source_target_pairs={{0,4},{1,5},{2,6},{3,7},{4,0},{5,1},{6,2},{7,3},{8,12},{9,13},{10,... | collective-permute-start | bytes 3538952 | tf_op jit(solution)/shard_map/ppermute | solution.py:24
  302.6 8.6 %collective-permute-start.47 = (bf16[2,48,1536]{2,1,0:T(8,128)(2,1)S(1)}, bf16[2,48,1536]{2,1,0:T(8,128)(2,1)S(1)}, u32[]{:S(2)}, u32[]{:S(2)}) collective-permute-start(bf16[2,48,1536]{2,1,0:T(8,128)(2,1)S(1)} %slice.689), channel_id=1, source_target_pairs={{0,24},{1,25},{2,26},{3,27},{4,28},{5,29},{6,30},{7,31},{8,16},{9,... | collective-permute-start | bytes 884744 | tf_op jit(solution)/shard_map/ppermute | solution.py:24
  307.3 36.4 %collective-permute-start.42 = (bf16[4,48,2304]{2,1,0:T(8,128)(2,1)S(1)}, bf16[4,48,2304]{2,1,0:T(8,128)(2,1)S(1)}, u32[]{:S(2)}, u32[]{:S(2)}) collective-permute-start(bf16[4,48,2304]{2,1,0:T(8,128)(2,1)S(1)} %get-tuple-element.189), channel_id=1, source_target_pairs={{0,4},{1,5},{2,6},{3,7},{4,0},{5,1},{6,2},{7,3},{8,12},{9,13},{10,... | collective-permute-start | bytes 2654216 | tf_op jit(solution)/shard_map/ppermute | solution.py:24
  308.6 35.1 %collective-permute-start.41 = (bf16[4,48,2304]{2,1,0:T(8,128)(2,1)S(1)}, bf16[4,48,2304]{2,1,0:T(8,128)(2,1)S(1)}, u32[]{:S(2)}, u32[]{:S(2)}) collective-permute-start(bf16[4,48,2304]{2,1,0:T(8,128)(2,1)S(1)} %get-tuple-element.190), channel_id=1, source_target_pairs={{0,2},{1,3},{2,0},{3,1},{4,6},{5,7},{6,4},{7,5},{8,10},{9,11},{10,... | collective-permute-start | bytes 2654216 | tf_op jit(solution)/shard_map/ppermute | solution.py:24
  329.0 46.2 %collective-permute-start.48 = (bf16[2,48,3072]{2,1,0:T(8,128)(2,1)}, bf16[2,48,3072]{2,1,0:T(8,128)(2,1)}, u32[]{:S(2)}, u32[]{:S(2)}) collective-permute-start(bf16[2,48,3072]{2,1,0:T(8,128)(2,1)} %slice.690), channel_id=1, source_target_pairs={{0,24},{1,25},{2,26},{3,27},{4,28},{5,29},{6,30},{7,31},{8,16},{9,... | collective-permute-start | bytes 1769480 | tf_op jit(solution)/shard_map/ppermute | solution.py:24
  345.7 20.3 %collective-permute-start.52 = (bf16[48,4608]{1,0:T(8,128)(2,1)S(1)}, bf16[48,4608]{1,0:T(8,128)(2,1)S(1)}, u32[]{:S(2)}, u32[]{:S(2)}) collective-permute-start(bf16[48,4608]{1,0:T(8,128)(2,1)S(1)} %fusion.39), channel_id=1, source_target_pairs={{0,8},{1,9},{2,10},{3,11},{4,12},{5,13},{6,14},{7,15},{8,0},{9,1},... | collective-permute-start | bytes 1327112 | tf_op jit(solution)/shard_map/ppermute | solution.py:24
  351.1 23.2 %collective-permute-start.51 = (bf16[48,2304]{1,0:T(8,128)(2,1)}, bf16[48,2304]{1,0:T(8,128)(2,1)}, u32[]{:S(2)}, u32[]{:S(2)}) collective-permute-start(bf16[48,2304]{1,0:T(8,128)(2,1)} %get-tuple-element.199), channel_id=1, source_target_pairs={{0,24},{1,25},{2,26},{3,27},{4,28},{5,29},{6,30},{7,31},{8,16},{9,... | collective-permute-start | bytes 663560 | tf_op jit(solution)/shard_map/ppermute | solution.py:24
  353.0 22.2 %collective-permute-start.50 = (bf16[48,2304]{1,0:T(8,128)(2,1)}, bf16[48,2304]{1,0:T(8,128)(2,1)}, u32[]{:S(2)}, u32[]{:S(2)}) collective-permute-start(bf16[48,2304]{1,0:T(8,128)(2,1)} %get-tuple-element.200), channel_id=1, source_target_pairs={{0,16},{1,17},{2,18},{3,19},{4,20},{5,21},{6,22},{7,23},{8,24},{9,... | collective-permute-start | bytes 663560 | tf_op jit(solution)/shard_map/ppermute | solution.py:24
  353.0 22.2 %collective-permute-start.49 = (bf16[48,2304]{1,0:T(8,128)(2,1)}, bf16[48,2304]{1,0:T(8,128)(2,1)}, u32[]{:S(2)}, u32[]{:S(2)}) collective-permute-start(bf16[48,2304]{1,0:T(8,128)(2,1)} %get-tuple-element.201), channel_id=1, source_target_pairs={{0,8},{1,9},{2,10},{3,11},{4,12},{5,13},{6,14},{7,15},{8,0},{9,1},... | collective-permute-start | bytes 663560 | tf_op jit(solution)/shard_map/ppermute | solution.py:24
  366.4 1.6 collective-permute-start.53
  376.8 1.7 collective-permute-start.54
  377.9 9.5 %collective-permute-start.55 = (bf16[48,3072]{1,0:T(8,128)(2,1)S(1)}, bf16[48,3072]{1,0:T(8,128)(2,1)S(1)}, u32[]{:S(2)}, u32[]{:S(2)}) collective-permute-start(bf16[48,3072]{1,0:T(8,128)(2,1)S(1)} %fusion.44), channel_id=1, source_target_pairs={{0,8},{1,9},{2,10},{3,11},{4,12},{5,13},{6,14},{7,15},{8,0},{9,1},... | collective-permute-start | bytes 884744 | tf_op jit(solution)/shard_map/ppermute | solution.py:24
  388.7 1.4 collective-permute-start.56
  (41 other events, 204.1 us)
Sparse Core Ops, SparseCore 0:
  13.0 141.6 all-gather.1

commit v5 on v4

--- a/solution.py
+++ b/solution.py
@@ -389,9 +389,6 @@
             copy.start()
         named = {"qkv": sems.at[0], "out": sems.at[1]}
         start_fetch(sources, refs, {"qkv": qkv_ref, "out": out_ref}, named)
-        saved[0].wait()
-        unit, inverse = unit_of(hidden_ref[...])
-        normed = (unit * spot(row_ref, "gain_a") + spot(row_ref, "shift_a")).astype(BF)
         grad_branch = mid_ref[...].astype(BF)
         small_ref[:, 2 * WIDTH : 3 * WIDTH] = jnp.sum(grad_branch.astype(F32), axis=0, keepdims=True)
         saved[1].wait()
@@ -401,6 +398,9 @@
             send_rows(out_stage, chips, pl.ds(half * HALF, HALF), grads_ref, half, 3 * HALF, sems.at[2])
         arrived(out_ref, named["out"])
         gm_ref[...] = dot(grad_branch, out_ref[...], (1, 1)).astype(BF)
+        saved[0].wait()
+        unit, inverse = unit_of(hidden_ref[...])
+        normed = (unit * spot(row_ref, "gain_a") + spot(row_ref, "shift_a")).astype(BF)
         saved[2].wait()
         same = down_docs[...] == across_docs[...]
         first_head = head_lanes(tokens)

time: 404 us -> 405 us (level)
  no operation moved by 1% of the time
where the time goes in v5:
time: 405 us; the launch traced here: 400 us
  waiting for transfers between devices  148 us (37%)
  Pallas kernels  83 us (20%)
  starting transfers between devices  65 us (16%)
  other arithmetic  47.8 us (12%)
  local copies, waits for them, and re-layouts  26.1 us (6%)
  between operations  16.2 us (4%)
  matrix products  13.8 us (3%)
    ppermute x53, waiting for transfers between devices, swap(): return lax.ppermute(value, 'dp', [(i, i ^ stride) for i in range(TUNED)])  133 us
    ppermute x53, starting transfers between devices, swap(): return lax.ppermute(value, 'dp', [(i, i ^ stride) for i in range(TUNED)])  60.1 us
    pallas_call x2, Pallas kernels, attn_backward(): pl.pallas_call(body, out_shape=outs, in_specs=[ANY] * 3 + [WHOLE] * (len(...  34.3 us
    pallas_call x2, Pallas kernels, mlp_backward(): pl.pallas_call(body, out_shape=outs, in_specs=[WHOLE] * (3 + len(doc_oper...  33.5 us
    ppermute x4, waiting for transfers between devices, swap_from(): lax.ppermute(value, 'dp', [(i, i ^ stride) for i in range(TUNED) if i //...  15.1 us
    pallas_call x1, Pallas kernels, layer_forward(): pl.pallas_call(body, out_shape=[jax.ShapeDtypeStruct((tokens, 3 * WIDTH),...  13.6 us
    convert_element_type x3, other arithmetic, sides(): (self.pair(2) + high.astype(F32)).astype(BF)  10 us
    convert_element_type x4, other arithmetic, levels(): return (self.pair(0) + total(by_x, by_y)).astype(BF)  8.73 us
  transfers between devices with their start and end apart: 58, of which 26 were waited for; matrix products, arithmetic and copies ran while one was open for 18% of the time, Pallas kernels for 16%

profile of v5, /device:TPU:0, one launch (start us, length us, event | category | flops | bytes accessed | tf_op | source)
XLA Modules:
  0.0 399.8 jit_solution(3206951039463878396)
XLA Ops:
  15.3 3.0 collective-permute-start.2
  18.3 1.5 collective-permute-start.1
  19.8 1.6 collective-permute-start.6
  21.4 1.5 collective-permute-start.13
  22.8 10.7 %collective-permute-done.2 = bf16[48,5376]{1,0:T(8,128)(2,1)S(1)} collective-permute-done((bf16[48,5376]{1,0:T(8,128)(2,1)S(1)}, bf16[48,5376]{1,0:T(8,128)(2,1)S(1)}, u32[]{:S(2)}, u32[]{:S(2)}) %collective-permute-start.2) | collective-permute-done | bytes 516128 | tf_op jit(solution)/shard_map/ppermute | solution.py:24
  33.5 1.8 collective-permute-start.4
  35.3 1.6 collective-permute-start.3
  36.9 3.5 collective-permute-done.6
  45.3 14.4 %collective-permute-done.8 = bf16[48,5376]{1,0:T(8,128)(2,1)S(1)} collective-permute-done((bf16[48,5376]{1,0:T(8,128)(2,1)}, bf16[48,5376]{1,0:T(8,128)(2,1)S(1)}, u32[]{:S(2)}, u32[]{:S(2)}) %collective-permute-start.8) | collective-permute-done | bytes 516128 | tf_op jit(solution)/shard_map/ppermute | solution.py:24
  59.8 2.4 collective-permute-start.9
  62.3 8.2 %collective-permute-done.14 = bf16[48,5376]{1,0:T(8,128)(2,1)S(1)} collective-permute-done((bf16[48,5376]{1,0:T(8,128)(2,1)}, bf16[48,5376]{1,0:T(8,128)(2,1)S(1)}, u32[]{:S(2)}, u32[]{:S(2)}) %collective-permute-start.14) | collective-permute-done | bytes 516128 | tf_op jit(solution)/shard_map/ppermute | solution.py:28
  70.9 1.7 collective-permute-start.15
  72.6 1.5 collective-permute-start.20
  74.1 2.6 pad_maximum_fusion.1.rest_2_.rest_3_
  76.8 3.2 collective-permute-done.16
  80.0 3.7 collective-permute-start.18
  84.8 6.9 %collective-permute-done.20 = bf16[48,5376]{1,0:T(8,128)(2,1)S(1)} collective-permute-done((bf16[48,5376]{1,0:T(8,128)(2,1)S(1)}, bf16[48,5376]{1,0:T(8,128)(2,1)S(1)}, u32[]{:S(2)}, u32[]{:S(2)}) %collective-permute-start.20) | collective-permute-done | bytes 516128 | tf_op jit(solution)/shard_map/ppermute | solution.py:28
  93.4 21.1 %collective-permute-done.22 = bf16[48,5376]{1,0:T(8,128)(2,1)S(1)} collective-permute-done((bf16[48,5376]{1,0:T(8,128)(2,1)S(1)}, bf16[48,5376]{1,0:T(8,128)(2,1)S(1)}, u32[]{:S(2)}, u32[]{:S(2)}) %collective-permute-start.22) | collective-permute-done | bytes 516128 | tf_op jit(solution)/shard_map/ppermute | solution.py:24
  115.6 2.1 collective-permute-start.23
  117.7 1.6 pad_maximum_fusion.2.rest_4_.rest_5_
  119.2 7.2 %collective-permute-done.24 = bf16[48,2688]{1,0:T(8,128)(2,1)S(1)} collective-permute-done((bf16[48,2688]{1,0:T(8,128)(2,1)S(1)}, bf16[48,2688]{1,0:T(8,128)(2,1)S(1)}, u32[]{:S(2)}, u32[]{:S(2)}) %collective-permute-start.24) | collective-permute-done | bytes 258080 | tf_op jit(solution)/shard_map/ppermute | solution.py:24
  127.6 1.6 pad_maximum_fusion.3.rest_6_.rest_7_
  129.4 4.2 %collective-permute-done.25.rest_7_.rest_8_ = bf16[4,48,5376]{2,1,0:T(8,128)(2,1)} collective-permute-done((bf16[4,48,5376]{2,1,0:T(8,128)(2,1)}, bf16[4,48,5376]{2,1,0:T(8,128)(2,1)}, u32[]{:S(2)}, u32[]{:S(2)}) %collective-permute-start.25) | collective-permute-done | bytes 2064416 | tf_op jit(solution)/shard_map/ppermute | solution.py:24
  133.6 1.7 lay_extra.1
  136.7 1.7 slice.503
  138.5 2.1 fusion.59
  140.9 3.0 fusion.20
  144.3 13.6 %layer_forward.1 = (bf16[256,2304]{1,0:T(8,128)(2,1)S(1)}, bf16[256,768]{1,0:T(8,128)(2,1)S(1)}, f32[256,768]{1,0:T(8,128)S(1)}, f32[256,768]{1,0:T(8,128)S(1)}) custom-call(f32[256,768]{1,0:T(8,128)S(1)} %add_add_fusion.hidden_ref.hidden_at, f32[1,9984]{1,0:T(1,128)S(1)} %broadcast_in_dim.132.row_ref, s32[256,1]{1,0:T(8,128)S(1)} %copy.84.down_docs.rest_0_, ...), custom_call_target="tpu_custom_call" | custom-call | flops 1 | bytes 1 | tf_op jit(solution)/shard_map/layer_forward/pallas_call | solution.py:229
  159.9 3.0 fusion.21
  163.5 18.9 %top_layer.1 = (bf16[16,48,3072]{2,1,0:T(8,128)(2,1)}, bf16[16,48,3072]{2,1,0:T(8,128)(2,1)}, f32[256,768]{1,0:T(8,128)}, f32[1,5376]{1,0:T(1,128)}, bf16[256,23...) custom-call(f32[256,768]{1,0:T(8,128)} %copy-done.4, bf16[256,768]{1,0:T(8,128)(2,1)} %grad_ref.1, ...), custom_call_target="tpu_custom_call" | custom-call | flops 1 | bytes 1 | tf_op jit(solution)/shard_map/top_layer/pallas_call | solution.py:359
  182.7 16.5 %attn_backward.2 = (bf16[16,48,1536]{2,1,0:T(8,128)(2,1)}, bf16[16,48,1536]{2,1,0:T(8,128)(2,1)}, f32[256,768]{1,0:T(8,128)}, f32[1,3840]{1,0:T(1,128)}) custom-call(f32[256,768]{1,0:T(8,128)} %copy-done.4, bf16[256,2304]{1,0:T(8,128)(2,1)} %get-tuple-element.102.packed_at, bf16[256,768]{1,0:T(8,128)(2,1)} %get-tuple-element.103.mixed_at, ...), custom_call_target="tpu_custom_call" | custom-call | flops 1 | bytes 1 | tf_op jit(solution)/shard_map/attn_backward/pallas_call | solution.py:495
  199.2 2.1 fusion.32
  201.8 2.0 collective-permute-start.27
  204.8 14.6 %mlp_backward.1 = (bf16[16,48,3072]{2,1,0:T(8,128)(2,1)}, bf16[16,48,3072]{2,1,0:T(8,128)(2,1)}, f32[256,768]{1,0:T(8,128)}, f32[1,5376]{1,0:T(1,128)}) custom-call(f32[256,768]{1,0:T(8,128)} %copy-done.6, f32[256,768]{1,0:T(8,128)} %get-tuple-element.112.grad_ref, f32[1,9984]{1,0:T(1,128)} %copy-done.7, bf16[4,48,5376]{2,1,0:T(8,128)(2,1)} %copy-done, ...), custom_call_target="tpu_custom_call" | custom-call | flops 1 | bytes 1 | tf_op jit(solution)/shard_map/mlp_backward/pallas_call | solution.py:359
  223.3 4.9 %fusion.14 = (bf16[4,48,3072]{2,1,0:T(8,128)(2,1)}, bf16[4,48,3072]{2,1,0:T(8,128)(2,1)}) fusion(bf16[4,4,48,3072]{3,2,1,0:T(8,128)(2,1)} %bitcast.32, bf16[4,4,48,3072]{3,2,1,0:T(8,128)(2,1)} %bitcast.373, bf16[4,48,1536]{2,1,0:T(8,128)(2,1)} %collective-permute-done.28, bf16[4,48,1536]{2,1,0:T(8,128)(2,1)S(1)} %collective-permute-done.27), kind=kLoop, calls=%fused_computation.24 | loop fusion | flops 7077888 | bytes 8257536 | tf_op jit(solution)/shard_map/convert_element_type | solution.py:677
  228.2 1.9 collective-permute-start.34
  233.0 2.6 fusion.23
  235.8 2.9 fusion.27
  239.9 17.8 %attn_backward.3 = (bf16[16,48,2304]{2,1,0:T(8,128)(2,1)}, bf16[16,48,2304]{2,1,0:T(8,128)(2,1)}, f32[256,768]{1,0:T(8,128)}, f32[1,3840]{1,0:T(1,128)}) custom-call(f32[256,768]{1,0:T(8,128)} %copy-done.2, bf16[256,2304]{1,0:T(8,128)(2,1)} %copy-done.5, bf16[256,768]{1,0:T(8,128)(2,1)} %copy-done.8, f32[256,768]{1,0:T(8,128)} %get-tuple-element.123.mid_ref, ...), custom_call_target="tpu_custom_call" | custom-call | flops 1 | bytes 1 | tf_op jit(solution)/shard_map/attn_backward/pallas_call | solution.py:495
  258.5 2.8 fusion.28
  263.9 2.8 fusion.34
  266.7 3.9 collective-permute-done.35
  272.2 5.1 %collective-permute-done.37 = bf16[16,48,2304]{2,1,0:T(8,128)(2,1)} collective-permute-done((bf16[16,48,2304]{2,1,0:T(8,128)(2,1)}, bf16[16,48,2304]{2,1,0:T(8,128)(2,1)}, u32[]{:S(2)}, u32[]{:S(2)}) %collective-permute-start.37) | collective-permute-done | bytes 3538976 | tf_op jit(solution)/shard_map/ppermute | solution.py:24
  277.3 3.1 fusion.13
  280.4 5.6 %collective-permute-start.40 = (bf16[2,48,3072]{2,1,0:T(8,128)(2,1)S(1)}, bf16[2,48,3072]{2,1,0:T(8,128)(2,1)S(1)}, u32[]{:S(2)}, u32[]{:S(2)}) collective-permute-start(bf16[2,48,3072]{2,1,0:T(8,128)(2,1)S(1)} %slice.678), channel_id=1, source_target_pairs={{0,24},{1,25},{2,26},{3,27},{4,28},{5,29},{6,30},{7,31},{8,16},{9,... | collective-permute-start | bytes 1769480 | tf_op jit(solution)/shard_map/ppermute | solution.py:24
  286.0 1.6 fusion.38
  289.9 2.6 fusion.11
  292.4 1.6 collective-permute-start.45
  294.4 6.3 %collective-permute-done.39 = bf16[4,48,1152]{2,1,0:T(8,128)(2,1)S(1)} collective-permute-done((bf16[4,48,1152]{2,1,0:T(8,128)(2,1)S(1)}, bf16[4,48,1152]{2,1,0:T(8,128)(2,1)S(1)}, u32[]{:S(2)}, u32[]{:S(2)}) %collective-permute-start.39) | collective-permute-done | bytes 442400 | tf_op jit(solution)/shard_map/ppermute | solution.py:24
  301.6 1.7 fusion.22
  303.3 2.2 collective-permute-start.47
  305.5 2.5 fusion.16
  309.8 2.2 collective-permute-done.47
  312.0 13.9 %collective-permute-done.45 = bf16[4,48,3072]{2,1,0:T(8,128)(2,1)S(1)} collective-permute-done((bf16[4,48,3072]{2,1,0:T(8,128)(2,1)S(1)}, bf16[4,48,3072]{2,1,0:T(8,128)(2,1)S(1)}, u32[]{:S(2)}, u32[]{:S(2)}) %collective-permute-start.45) | collective-permute-done | bytes 1179680 | tf_op jit(solution)/shard_map/ppermute | solution.py:24
  326.9 2.0 fusion.12
  329.7 2.2 collective-permute-start.48
  331.9 12.5 %collective-permute-done.42 = bf16[4,48,2304]{2,1,0:T(8,128)(2,1)S(1)} collective-permute-done((bf16[4,48,2304]{2,1,0:T(8,128)(2,1)S(1)}, bf16[4,48,2304]{2,1,0:T(8,128)(2,1)S(1)}, u32[]{:S(2)}, u32[]{:S(2)}) %collective-permute-start.42) | collective-permute-done | bytes 884768 | tf_op jit(solution)/shard_map/ppermute | solution.py:24
  344.4 1.9 fusion.18
  346.4 4.5 %collective-permute-start.52 = (bf16[48,4608]{1,0:T(8,128)(2,1)S(1)}, bf16[48,4608]{1,0:T(8,128)(2,1)S(1)}, u32[]{:S(2)}, u32[]{:S(2)}) collective-permute-start(bf16[48,4608]{1,0:T(8,128)(2,1)S(1)} %fusion.39), channel_id=1, source_target_pairs={{0,8},{1,9},{2,10},{3,11},{4,12},{5,13},{6,14},{7,15},{8,0},{9,1},... | collective-permute-start | bytes 1327112 | tf_op jit(solution)/shard_map/ppermute | solution.py:24
  351.8 1.9 collective-permute-start.51
  353.7 2.4 collective-permute-start.49
  356.2 10.6 %collective-permute-done.52 = bf16[48,4608]{1,0:T(8,128)(2,1)S(1)} collective-permute-done((bf16[48,4608]{1,0:T(8,128)(2,1)S(1)}, bf16[48,4608]{1,0:T(8,128)(2,1)S(1)}, u32[]{:S(2)}, u32[]{:S(2)}) %collective-permute-start.52) | collective-permute-done | bytes 442400 | tf_op jit(solution)/shard_map/ppermute | solution.py:24
  372.3 1.8 reshape.616
  383.4 4.7 %collective-permute-done.55 = bf16[48,3072]{1,0:T(8,128)(2,1)S(1)} collective-permute-done((bf16[48,3072]{1,0:T(8,128)(2,1)S(1)}, bf16[48,3072]{1,0:T(8,128)(2,1)S(1)}, u32[]{:S(2)}, u32[]{:S(2)}) %collective-permute-start.55) | collective-permute-done | bytes 294944 | tf_op jit(solution)/shard_map/ppermute | solution.py:24
  (341 shorter events, 64.5 us)
Async XLA Ops:
  7.2 156.3 %all-gather.2.cloned.1.call-start = ((), (), s32[]{:S(2)}) async-start(), calls=%async_computation | async-start | bytes 14598144 | tf_op jit(solution)/shard_map/all_gather | solution.py:808
  13.4 1.7 collective-permute-start
  15.3 18.2 %collective-permute-start.2 = (bf16[48,5376]{1,0:T(8,128)(2,1)S(1)}, bf16[48,5376]{1,0:T(8,128)(2,1)S(1)}, u32[]{:S(2)}, u32[]{:S(2)}) collective-permute-start(bf16[48,5376]{1,0:T(8,128)(2,1)S(1)} %constant_dynamic-update-slice_fusion.2), channel_id=1, source_target_pairs={{0,4},{1,5},{2,6},{3,7},{4,0},{5,1},{6,2},{7,3},{8,12},{9,13},{10,... | collective-permute-start | bytes 1548296 | tf_op jit(solution)/shard_map/ppermute | solution.py:24
  18.3 17.0 %collective-permute-start.1 = (bf16[48,5376]{1,0:T(8,128)(2,1)S(1)}, bf16[48,5376]{1,0:T(8,128)(2,1)S(1)}, u32[]{:S(2)}, u32[]{:S(2)}) collective-permute-start(bf16[48,5376]{1,0:T(8,128)(2,1)S(1)} %constant_dynamic-update-slice_fusion.2), channel_id=1, source_target_pairs={{0,2},{1,3},{2,0},{3,1},{4,6},{5,7},{6,4},{7,5},{8,10},{9,11},{10,... | collective-permute-start | bytes 1548296 | tf_op jit(solution)/shard_map/ppermute | solution.py:24
  19.8 20.6 %collective-permute-start.6 = (bf16[48,5376]{1,0:T(8,128)(2,1)S(1)}, bf16[48,5376]{1,0:T(8,128)(2,1)}, u32[]{:S(2)}, u32[]{:S(2)}) collective-permute-start(bf16[48,5376]{1,0:T(8,128)(2,1)S(1)} %constant_dynamic-update-slice_fusion.2), channel_id=1, source_target_pairs={{0,8},{1,9},{2,10},{3,11},{4,12},{5,13},{6,14},{7,15},{8,0},{9,1},... | collective-permute-start | bytes 1548296 | tf_op jit(solution)/shard_map/ppermute | solution.py:24
  21.4 19.8 %collective-permute-start.13 = (bf16[48,5376]{1,0:T(8,128)(2,1)S(1)}, bf16[48,5376]{1,0:T(8,128)(2,1)}, u32[]{:S(2)}, u32[]{:S(2)}) collective-permute-start(bf16[48,5376]{1,0:T(8,128)(2,1)S(1)} %constant_dynamic-update-slice_fusion.2), channel_id=1, source_target_pairs={{8,16},{9,17},{10,18},{11,19},{12,20},{13,21},{14,22},{15,23},{16,... | collective-permute-start | bytes 1548296 | tf_op jit(solution)/shard_map/ppermute | solution.py:28
  33.5 7.7 %collective-permute-start.4 = (bf16[48,2688]{1,0:T(8,128)(2,1)S(1)}, bf16[48,2688]{1,0:T(8,128)(2,1)S(1)}, u32[]{:S(2)}, u32[]{:S(2)}) collective-permute-start(bf16[48,2688]{1,0:T(8,128)(2,1)S(1)} %slice.633), channel_id=1, source_target_pairs={{0,2},{1,3},{2,0},{3,1},{4,6},{5,7},{6,4},{7,5},{8,10},{9,11},{10,... | collective-permute-start | bytes 774152 | tf_op jit(solution)/shard_map/ppermute | solution.py:24
  35.3 8.6 %collective-permute-start.3 = (bf16[48,2688]{1,0:T(8,128)(2,1)S(1)}, bf16[48,2688]{1,0:T(8,128)(2,1)S(1)}, u32[]{:S(2)}, u32[]{:S(2)}) collective-permute-start(bf16[48,2688]{1,0:T(8,128)(2,1)S(1)} %slice.632), channel_id=1, source_target_pairs={{0,4},{1,5},{2,6},{3,7},{4,0},{5,1},{6,2},{7,3},{8,12},{9,13},{10,... | collective-permute-start | bytes 774152 | tf_op jit(solution)/shard_map/ppermute | solution.py:24
  40.4 30.1 %collective-permute-start.12 = (bf16[48,5376]{1,0:T(8,128)(2,1)}, bf16[48,5376]{1,0:T(8,128)(2,1)S(1)}, u32[]{:S(2)}, u32[]{:S(2)}) collective-permute-start(bf16[48,5376]{1,0:T(8,128)(2,1)} %collective-permute-done.6), channel_id=1, source_target_pairs={{8,16},{9,17},{10,18},{11,19},{12,20},{13,21},{14,22},{15,23},{16,... | collective-permute-start | bytes 1548296 | tf_op jit(solution)/shard_map/ppermute | solution.py:28
  41.1 18.6 %collective-permute-start.8 = (bf16[48,5376]{1,0:T(8,128)(2,1)}, bf16[48,5376]{1,0:T(8,128)(2,1)S(1)}, u32[]{:S(2)}, u32[]{:S(2)}) collective-permute-start(bf16[48,5376]{1,0:T(8,128)(2,1)} %collective-permute-done.6), channel_id=1, source_target_pairs={{0,4},{1,5},{2,6},{3,7},{4,0},{5,1},{6,2},{7,3},{8,12},{9,13},{10,... | collective-permute-start | bytes 1548296 | tf_op jit(solution)/shard_map/ppermute | solution.py:24
  41.1 18.7 %collective-permute-start.7 = (bf16[48,5376]{1,0:T(8,128)(2,1)}, bf16[48,5376]{1,0:T(8,128)(2,1)S(1)}, u32[]{:S(2)}, u32[]{:S(2)}) collective-permute-start(bf16[48,5376]{1,0:T(8,128)(2,1)} %collective-permute-done.6), channel_id=1, source_target_pairs={{0,2},{1,3},{2,0},{3,1},{4,6},{5,7},{6,4},{7,5},{8,10},{9,11},{10,... | collective-permute-start | bytes 1548296 | tf_op jit(solution)/shard_map/ppermute | solution.py:24
  41.2 29.2 %collective-permute-start.14 = (bf16[48,5376]{1,0:T(8,128)(2,1)}, bf16[48,5376]{1,0:T(8,128)(2,1)S(1)}, u32[]{:S(2)}, u32[]{:S(2)}) collective-permute-start(bf16[48,5376]{1,0:T(8,128)(2,1)} %collective-permute-done.13), channel_id=1, source_target_pairs={{8,0},{9,1},{10,2},{11,3},{12,4},{13,5},{14,6},{15,7},{16,24},{17,... | collective-permute-start | bytes 1548296 | tf_op jit(solution)/shard_map/ppermute | solution.py:28
  45.2 88.3 %copy-start = (bf16[4,48,5376]{2,1,0:T(8,128)(2,1)}, bf16[4,48,5376]{2,1,0:T(8,128)(2,1)S(1)}, u32[]{:S(2)}) copy-start(bf16[4,48,5376]{2,1,0:T(8,128)(2,1)S(1)} %pad_maximum_fusion.rest_0_.rest_1_) | copy-start | bytes 6193156
  45.3 84.1 %collective-permute-start.5 = (bf16[4,48,5376]{2,1,0:T(8,128)(2,1)S(1)}, bf16[4,48,5376]{2,1,0:T(8,128)(2,1)}, u32[]{:S(2)}, u32[]{:S(2)}) collective-permute-start(bf16[4,48,5376]{2,1,0:T(8,128)(2,1)S(1)} %pad_maximum_fusion.rest_0_.rest_1_), channel_id=1, source_target_pairs={{0,1},{1,0},{2,3},{3,2},{4,5},{5,4},{6,7},{7,6},{8,9},{9,8},{10,11... | collective-permute-start | bytes 6193160 | tf_op jit(solution)/shard_map/ppermute | solution.py:24
  59.7 12.9 %collective-permute-start.10 = (bf16[48,2688]{1,0:T(8,128)(2,1)S(1)}, bf16[48,2688]{1,0:T(8,128)(2,1)S(1)}, u32[]{:S(2)}, u32[]{:S(2)}) collective-permute-start(bf16[48,2688]{1,0:T(8,128)(2,1)S(1)} %slice.635), channel_id=1, source_target_pairs={{0,2},{1,3},{2,0},{3,1},{4,6},{5,7},{6,4},{7,5},{8,10},{9,11},{10,... | collective-permute-start | bytes 774152 | tf_op jit(solution)/shard_map/ppermute | solution.py:24
  59.8 14.3 %collective-permute-start.9 = (bf16[48,2688]{1,0:T(8,128)(2,1)S(1)}, bf16[48,2688]{1,0:T(8,128)(2,1)S(1)}, u32[]{:S(2)}, u32[]{:S(2)}) collective-permute-start(bf16[48,2688]{1,0:T(8,128)(2,1)S(1)} %slice.634), channel_id=1, source_target_pairs={{0,4},{1,5},{2,6},{3,7},{4,0},{5,1},{6,2},{7,3},{8,12},{9,13},{10,... | collective-permute-start | bytes 774152 | tf_op jit(solution)/shard_map/ppermute | solution.py:24
  70.5 9.5 %collective-permute-start.16 = (bf16[48,5376]{1,0:T(8,128)(2,1)S(1)}, bf16[48,5376]{1,0:T(8,128)(2,1)S(1)}, u32[]{:S(2)}, u32[]{:S(2)}) collective-permute-start(bf16[48,5376]{1,0:T(8,128)(2,1)S(1)} %broadcast_select_fusion.1), channel_id=1, source_target_pairs={{0,4},{1,5},{2,6},{3,7},{4,0},{5,1},{6,2},{7,3},{8,12},{9,13},{10,... | collective-permute-start | bytes 1548296 | tf_op jit(solution)/shard_map/ppermute | solution.py:24
  70.9 12.8 %collective-permute-start.15 = (bf16[48,5376]{1,0:T(8,128)(2,1)S(1)}, bf16[48,5376]{1,0:T(8,128)(2,1)S(1)}, u32[]{:S(2)}, u32[]{:S(2)}) collective-permute-start(bf16[48,5376]{1,0:T(8,128)(2,1)S(1)} %broadcast_select_fusion.1), channel_id=1, source_target_pairs={{0,2},{1,3},{2,0},{3,1},{4,6},{5,7},{6,4},{7,5},{8,10},{9,11},{10,... | collective-permute-start | bytes 1548296 | tf_op jit(solution)/shard_map/ppermute | solution.py:24
  72.6 19.2 %collective-permute-start.20 = (bf16[48,5376]{1,0:T(8,128)(2,1)S(1)}, bf16[48,5376]{1,0:T(8,128)(2,1)S(1)}, u32[]{:S(2)}, u32[]{:S(2)}) collective-permute-start(bf16[48,5376]{1,0:T(8,128)(2,1)S(1)} %collective-permute-done.12), channel_id=1, source_target_pairs={{8,0},{9,1},{10,2},{11,3},{12,4},{13,5},{14,6},{15,7},{16,24},{17,... | collective-permute-start | bytes 1548296 | tf_op jit(solution)/shard_map/ppermute | solution.py:28
  76.8 52.6 %collective-permute-start.11 = (bf16[4,48,5376]{2,1,0:T(8,128)(2,1)}, bf16[4,48,5376]{2,1,0:T(8,128)(2,1)}, u32[]{:S(2)}, u32[]{:S(2)}) collective-permute-start(bf16[4,48,5376]{2,1,0:T(8,128)(2,1)} %pad_maximum_fusion.1.rest_2_.rest_3_), channel_id=1, source_target_pairs={{0,1},{1,0},{2,3},{3,2},{4,5},{5,4},{6,7},{7,6},{8,9},{9,8},{10,11... | collective-permute-start | bytes 6193160 | tf_op jit(solution)/shard_map/ppermute | solution.py:24
  80.0 12.9 %collective-permute-start.18 = (bf16[48,2688]{1,0:T(8,128)(2,1)S(1)}, bf16[48,2688]{1,0:T(8,128)(2,1)S(1)}, u32[]{:S(2)}, u32[]{:S(2)}) collective-permute-start(bf16[48,2688]{1,0:T(8,128)(2,1)S(1)} %slice.637), channel_id=1, source_target_pairs={{0,2},{1,3},{2,0},{3,1},{4,6},{5,7},{6,4},{7,5},{8,10},{9,11},{10,... | collective-permute-start | bytes 774152 | tf_op jit(solution)/shard_map/ppermute | solution.py:24
  83.7 9.6 %collective-permute-start.17 = (bf16[48,2688]{1,0:T(8,128)(2,1)S(1)}, bf16[48,2688]{1,0:T(8,128)(2,1)S(1)}, u32[]{:S(2)}, u32[]{:S(2)}) collective-permute-start(bf16[48,2688]{1,0:T(8,128)(2,1)S(1)} %slice.636), channel_id=1, source_target_pairs={{0,4},{1,5},{2,6},{3,7},{4,0},{5,1},{6,2},{7,3},{8,12},{9,13},{10,... | collective-permute-start | bytes 774152 | tf_op jit(solution)/shard_map/ppermute | solution.py:24
  91.8 22.7 %collective-permute-start.22 = (bf16[48,5376]{1,0:T(8,128)(2,1)S(1)}, bf16[48,5376]{1,0:T(8,128)(2,1)S(1)}, u32[]{:S(2)}, u32[]{:S(2)}) collective-permute-start(bf16[48,5376]{1,0:T(8,128)(2,1)S(1)} %broadcast_select_fusion), channel_id=1, source_target_pairs={{0,4},{1,5},{2,6},{3,7},{4,0},{5,1},{6,2},{7,3},{8,12},{9,13},{10,... | collective-permute-start | bytes 1548296 | tf_op jit(solution)/shard_map/ppermute | solution.py:24
  93.0 22.6 %collective-permute-start.21 = (bf16[48,5376]{1,0:T(8,128)(2,1)S(1)}, bf16[48,5376]{1,0:T(8,128)(2,1)S(1)}, u32[]{:S(2)}, u32[]{:S(2)}) collective-permute-start(bf16[48,5376]{1,0:T(8,128)(2,1)S(1)} %broadcast_select_fusion), channel_id=1, source_target_pairs={{0,2},{1,3},{2,0},{3,1},{4,6},{5,7},{6,4},{7,5},{8,10},{9,11},{10,... | collective-permute-start | bytes 1548296 | tf_op jit(solution)/shard_map/ppermute | solution.py:24
  114.6 11.9 %collective-permute-start.24 = (bf16[48,2688]{1,0:T(8,128)(2,1)S(1)}, bf16[48,2688]{1,0:T(8,128)(2,1)S(1)}, u32[]{:S(2)}, u32[]{:S(2)}) collective-permute-start(bf16[48,2688]{1,0:T(8,128)(2,1)S(1)} %slice.639), channel_id=1, source_target_pairs={{0,2},{1,3},{2,0},{3,1},{4,6},{5,7},{6,4},{7,5},{8,10},{9,11},{10,... | collective-permute-start | bytes 774152 | tf_op jit(solution)/shard_map/ppermute | solution.py:24
  115.6 11.9 %collective-permute-start.23 = (bf16[48,2688]{1,0:T(8,128)(2,1)S(1)}, bf16[48,2688]{1,0:T(8,128)(2,1)S(1)}, u32[]{:S(2)}, u32[]{:S(2)}) collective-permute-start(bf16[48,2688]{1,0:T(8,128)(2,1)S(1)} %slice.638), channel_id=1, source_target_pairs={{0,4},{1,5},{2,6},{3,7},{4,0},{5,1},{6,2},{7,3},{8,12},{9,13},{10,... | collective-permute-start | bytes 774152 | tf_op jit(solution)/shard_map/ppermute | solution.py:24
  119.2 10.2 %collective-permute-start.19 = (bf16[4,48,5376]{2,1,0:T(8,128)(2,1)}, bf16[4,48,5376]{2,1,0:T(8,128)(2,1)}, u32[]{:S(2)}, u32[]{:S(2)}) collective-permute-start(bf16[4,48,5376]{2,1,0:T(8,128)(2,1)} %pad_maximum_fusion.2.rest_4_.rest_5_), channel_id=1, source_target_pairs={{0,1},{1,0},{2,3},{3,2},{4,5},{5,4},{6,7},{7,6},{8,9},{9,8},{10,11... | collective-permute-start | bytes 6193160 | tf_op jit(solution)/shard_map/ppermute | solution.py:24
  129.1 4.5 %collective-permute-start.25 = (bf16[4,48,5376]{2,1,0:T(8,128)(2,1)}, bf16[4,48,5376]{2,1,0:T(8,128)(2,1)}, u32[]{:S(2)}, u32[]{:S(2)}) collective-permute-start(bf16[4,48,5376]{2,1,0:T(8,128)(2,1)} %pad_maximum_fusion.3.rest_6_.rest_7_), channel_id=1, source_target_pairs={{0,1},{1,0},{2,3},{3,2},{4,5},{5,4},{6,7},{7,6},{8,9},{9,8},{10,11... | collective-permute-start | bytes 6193160 | tf_op jit(solution)/shard_map/ppermute | solution.py:24
  182.4 16.8 %collective-permute-start.26 = (bf16[16,48,3072]{2,1,0:T(8,128)(2,1)}, bf16[16,48,3072]{2,1,0:T(8,128)(2,1)}, u32[]{:S(2)}, u32[]{:S(2)}) collective-permute-start(bf16[16,48,3072]{2,1,0:T(8,128)(2,1)} %get-tuple-element.106), channel_id=1, source_target_pairs={{0,1},{1,0},{2,3},{3,2},{4,5},{5,4},{6,7},{7,6},{8,9},{9,8},{10,11... | collective-permute-start | bytes 14155784 | tf_op jit(solution)/shard_map/ppermute | solution.py:24
  201.6 17.9 %collective-permute-start.29 = (bf16[16,48,1536]{2,1,0:T(8,128)(2,1)S(1)}, bf16[16,48,1536]{2,1,0:T(8,128)(2,1)}, u32[]{:S(2)}, u32[]{:S(2)}) collective-permute-start(bf16[16,48,1536]{2,1,0:T(8,128)(2,1)S(1)} %copy-done.35), channel_id=1, source_target_pairs={{0,1},{1,0},{2,3},{3,2},{4,5},{5,4},{6,7},{7,6},{8,9},{9,8},{10,11... | collective-permute-start | bytes 7077896 | tf_op jit(solution)/shard_map/ppermute | solution.py:24
  201.8 17.7 %collective-permute-start.27 = (bf16[4,48,1536]{2,1,0:T(8,128)(2,1)S(1)}, bf16[4,48,1536]{2,1,0:T(8,128)(2,1)S(1)}, u32[]{:S(2)}, u32[]{:S(2)}) collective-permute-start(bf16[4,48,1536]{2,1,0:T(8,128)(2,1)S(1)} %get-tuple-element.114), channel_id=1, source_target_pairs={{0,4},{1,5},{2,6},{3,7},{4,0},{5,1},{6,2},{7,3},{8,12},{9,13},{10,... | collective-permute-start | bytes 1769480 | tf_op jit(solution)/shard_map/ppermute | solution.py:24
  203.8 15.6 %collective-permute-start.28 = (bf16[4,48,1536]{2,1,0:T(8,128)(2,1)S(1)}, bf16[4,48,1536]{2,1,0:T(8,128)(2,1)}, u32[]{:S(2)}, u32[]{:S(2)}) collective-permute-start(bf16[4,48,1536]{2,1,0:T(8,128)(2,1)S(1)} %get-tuple-element.115), channel_id=1, source_target_pairs={{0,2},{1,3},{2,0},{3,1},{4,6},{5,7},{6,4},{7,5},{8,10},{9,11},{10,... | collective-permute-start | bytes 1769480 | tf_op jit(solution)/shard_map/ppermute | solution.py:24
  204.8 16.0 %copy-start.11 = (bf16[16,48,1536]{2,1,0:T(8,128)(2,1)S(1)}, bf16[16,48,1536]{2,1,0:T(8,128)(2,1)}, u32[]{:S(2)}) copy-start(bf16[16,48,1536]{2,1,0:T(8,128)(2,1)} %get-tuple-element.119) | copy-start | bytes 7077892
  219.5 38.2 %collective-permute-start.32 = (bf16[16,48,3072]{2,1,0:T(8,128)(2,1)}, bf16[16,48,3072]{2,1,0:T(8,128)(2,1)}, u32[]{:S(2)}, u32[]{:S(2)}) collective-permute-start(bf16[16,48,3072]{2,1,0:T(8,128)(2,1)} %get-tuple-element.125), channel_id=1, source_target_pairs={{0,1},{1,0},{2,3},{3,2},{4,5},{5,4},{6,7},{7,6},{8,9},{9,8},{10,11... | collective-permute-start | bytes 14155784 | tf_op jit(solution)/shard_map/ppermute | solution.py:24
  222.1 9.5 %collective-permute-start.31 = (bf16[4,48,768]{2,1,0:T(8,128)(2,1)S(1)}, bf16[4,48,768]{2,1,0:T(8,128)(2,1)S(1)}, u32[]{:S(2)}, u32[]{:S(2)}) collective-permute-start(bf16[4,48,768]{2,1,0:T(8,128)(2,1)S(1)} %get-tuple-element.195), channel_id=1, source_target_pairs={{0,2},{1,3},{2,0},{3,1},{4,6},{5,7},{6,4},{7,5},{8,10},{9,11},{10,... | collective-permute-start | bytes 884744 | tf_op jit(solution)/shard_map/ppermute | solution.py:24
  223.2 9.8 %collective-permute-start.30 = (bf16[4,48,768]{2,1,0:T(8,128)(2,1)S(1)}, bf16[4,48,768]{2,1,0:T(8,128)(2,1)S(1)}, u32[]{:S(2)}, u32[]{:S(2)}) collective-permute-start(bf16[4,48,768]{2,1,0:T(8,128)(2,1)S(1)} %get-tuple-element.196), channel_id=1, source_target_pairs={{0,4},{1,5},{2,6},{3,7},{4,0},{5,1},{6,2},{7,3},{8,12},{9,13},{10,... | collective-permute-start | bytes 884744 | tf_op jit(solution)/shard_map/ppermute | solution.py:24
  228.2 42.4 %collective-permute-start.34 = (bf16[4,48,3072]{2,1,0:T(8,128)(2,1)}, bf16[4,48,3072]{2,1,0:T(8,128)(2,1)}, u32[]{:S(2)}, u32[]{:S(2)}) collective-permute-start(bf16[4,48,3072]{2,1,0:T(8,128)(2,1)} %get-tuple-element.185), channel_id=1, source_target_pairs={{0,4},{1,5},{2,6},{3,7},{4,0},{5,1},{6,2},{7,3},{8,12},{9,13},{10,... | collective-permute-start | bytes 3538952 | tf_op jit(solution)/shard_map/ppermute | solution.py:24
  230.1 40.5 %collective-permute-start.33 = (bf16[4,48,3072]{2,1,0:T(8,128)(2,1)}, bf16[4,48,3072]{2,1,0:T(8,128)(2,1)}, u32[]{:S(2)}, u32[]{:S(2)}) collective-permute-start(bf16[4,48,3072]{2,1,0:T(8,128)(2,1)} %get-tuple-element.186), channel_id=1, source_target_pairs={{0,2},{1,3},{2,0},{3,1},{4,6},{5,7},{6,4},{7,5},{8,10},{9,11},{10,... | collective-permute-start | bytes 3538952 | tf_op jit(solution)/shard_map/ppermute | solution.py:24
  238.8 31.9 %collective-permute-start.35 = (bf16[4,48,1536]{2,1,0:T(8,128)(2,1)}, bf16[4,48,1536]{2,1,0:T(8,128)(2,1)}, u32[]{:S(2)}, u32[]{:S(2)}) collective-permute-start(bf16[4,48,1536]{2,1,0:T(8,128)(2,1)} %get-tuple-element.132), channel_id=1, source_target_pairs={{0,2},{1,3},{2,0},{3,1},{4,6},{5,7},{6,4},{7,5},{8,10},{9,11},{10,... | collective-permute-start | bytes 1769480 | tf_op jit(solution)/shard_map/ppermute | solution.py:24
  239.9 30.8 %collective-permute-start.36 = (bf16[4,48,1536]{2,1,0:T(8,128)(2,1)}, bf16[4,48,1536]{2,1,0:T(8,128)(2,1)}, u32[]{:S(2)}, u32[]{:S(2)}) collective-permute-start(bf16[4,48,1536]{2,1,0:T(8,128)(2,1)} %get-tuple-element.133), channel_id=1, source_target_pairs={{0,4},{1,5},{2,6},{3,7},{4,0},{5,1},{6,2},{7,3},{8,12},{9,13},{10,... | collective-permute-start | bytes 1769480 | tf_op jit(solution)/shard_map/ppermute | solution.py:24
  239.9 18.6 %copy-start.41 = (s32[9216]{0:T(1024)S(1)}, s32[9216]{0:T(1024)}, u32[]{:S(2)}) copy-start(s32[9216]{0:T(1024)} %constant.186) | copy-start | bytes 110596
  239.9 18.6 %copy-start.42 = (s32[9216]{0:T(1024)S(1)}, s32[9216]{0:T(1024)}, u32[]{:S(2)}) copy-start(s32[9216]{0:T(1024)} %constant.185) | copy-start | bytes 110596
  263.9 25.9 %slice-start = ((s8[4718592]{0:T(1024)(128)(4,1)}), s8[524288]{0:T(1024)(128)(4,1)S(1)}, s32[]{:S(2)}) async-start(s8[4718592]{0:T(1024)(128)(4,1)} %bitcast.368), calls=%async_computation.1 | async-start | bytes 1048576
  270.6 6.6 %collective-permute-start.37 = (bf16[16,48,2304]{2,1,0:T(8,128)(2,1)}, bf16[16,48,2304]{2,1,0:T(8,128)(2,1)}, u32[]{:S(2)}, u32[]{:S(2)}) collective-permute-start(bf16[16,48,2304]{2,1,0:T(8,128)(2,1)} %bitcast_dynamic-update-slice_fusion), channel_id=1, source_target_pairs={{0,1},{1,0},{2,3},{3,2},{4,5},{5,4},{6,7},{7,6},{8,9},{9,8},{10,11... | collective-permute-start | bytes 10616840 | tf_op jit(solution)/shard_map/ppermute | solution.py:24
  270.8 19.1 %slice-start.1 = ((s8[4718592]{0:T(1024)(128)(4,1)}), s8[4194304]{0:T(1024)(128)(4,1)S(1)}, s32[]{:S(2)}) async-start(s8[4718592]{0:T(1024)(128)(4,1)} %bitcast.368), calls=%async_computation.2 | async-start | bytes 8388608
  270.8 19.1 %collective-permute-start.43 = (bf16[4,48,1536]{2,1,0:T(8,128)(2,1)}, bf16[4,48,1536]{2,1,0:T(8,128)(2,1)S(1)}, u32[]{:S(2)}, u32[]{:S(2)}) collective-permute-start(bf16[4,48,1536]{2,1,0:T(8,128)(2,1)} %get-tuple-element.155), channel_id=1, source_target_pairs={{0,4},{1,5},{2,6},{3,7},{4,0},{5,1},{6,2},{7,3},{8,12},{9,13},{10,... | collective-permute-start | bytes 1769480 | tf_op jit(solution)/shard_map/ppermute | solution.py:24
  271.2 18.7 %collective-permute-start.44 = (bf16[4,48,1536]{2,1,0:T(8,128)(2,1)S(1)}, bf16[4,48,1536]{2,1,0:T(8,128)(2,1)S(1)}, u32[]{:S(2)}, u32[]{:S(2)}) collective-permute-start(bf16[4,48,1536]{2,1,0:T(8,128)(2,1)S(1)} %get-tuple-element.156), channel_id=1, source_target_pairs={{0,2},{1,3},{2,0},{3,1},{4,6},{5,7},{6,4},{7,5},{8,10},{9,11},{10,... | collective-permute-start | bytes 1769480 | tf_op jit(solution)/shard_map/ppermute | solution.py:24
  280.4 21.2 %collective-permute-start.40 = (bf16[2,48,3072]{2,1,0:T(8,128)(2,1)S(1)}, bf16[2,48,3072]{2,1,0:T(8,128)(2,1)S(1)}, u32[]{:S(2)}, u32[]{:S(2)}) collective-permute-start(bf16[2,48,3072]{2,1,0:T(8,128)(2,1)S(1)} %slice.678), channel_id=1, source_target_pairs={{0,24},{1,25},{2,26},{3,27},{4,28},{5,29},{6,30},{7,31},{8,16},{9,... | collective-permute-start | bytes 1769480 | tf_op jit(solution)/shard_map/ppermute | solution.py:24
  287.6 13.1 %collective-permute-start.39 = (bf16[4,48,1152]{2,1,0:T(8,128)(2,1)S(1)}, bf16[4,48,1152]{2,1,0:T(8,128)(2,1)S(1)}, u32[]{:S(2)}, u32[]{:S(2)}) collective-permute-start(bf16[4,48,1152]{2,1,0:T(8,128)(2,1)S(1)} %get-tuple-element.191), channel_id=1, source_target_pairs={{0,2},{1,3},{2,0},{3,1},{4,6},{5,7},{6,4},{7,5},{8,10},{9,11},{10,... | collective-permute-start | bytes 1327112 | tf_op jit(solution)/shard_map/ppermute | solution.py:24
  288.5 13.1 %collective-permute-start.38 = (bf16[4,48,1152]{2,1,0:T(8,128)(2,1)S(1)}, bf16[4,48,1152]{2,1,0:T(8,128)(2,1)S(1)}, u32[]{:S(2)}, u32[]{:S(2)}) collective-permute-start(bf16[4,48,1152]{2,1,0:T(8,128)(2,1)S(1)} %get-tuple-element.192), channel_id=1, source_target_pairs={{0,4},{1,5},{2,6},{3,7},{4,0},{5,1},{6,2},{7,3},{8,12},{9,13},{10,... | collective-permute-start | bytes 1327112 | tf_op jit(solution)/shard_map/ppermute | solution.py:24
  292.4 33.5 %collective-permute-start.45 = (bf16[4,48,3072]{2,1,0:T(8,128)(2,1)S(1)}, bf16[4,48,3072]{2,1,0:T(8,128)(2,1)S(1)}, u32[]{:S(2)}, u32[]{:S(2)}) collective-permute-start(bf16[4,48,3072]{2,1,0:T(8,128)(2,1)S(1)} %get-tuple-element.181), channel_id=1, source_target_pairs={{0,2},{1,3},{2,0},{3,1},{4,6},{5,7},{6,4},{7,5},{8,10},{9,11},{10,... | collective-permute-start | bytes 3538952 | tf_op jit(solution)/shard_map/ppermute | solution.py:24
  294.1 32.8 %collective-permute-start.46 = (bf16[4,48,3072]{2,1,0:T(8,128)(2,1)S(1)}, bf16[4,48,3072]{2,1,0:T(8,128)(2,1)S(1)}, u32[]{:S(2)}, u32[]{:S(2)}) collective-permute-start(bf16[4,48,3072]{2,1,0:T(8,128)(2,1)S(1)} %get-tuple-element.182), channel_id=1, source_target_pairs={{0,4},{1,5},{2,6},{3,7},{4,0},{5,1},{6,2},{7,3},{8,12},{9,13},{10,... | collective-permute-start | bytes 3538952 | tf_op jit(solution)/shard_map/ppermute | solution.py:24
  303.3 8.6 %collective-permute-start.47 = (bf16[2,48,1536]{2,1,0:T(8,128)(2,1)S(1)}, bf16[2,48,1536]{2,1,0:T(8,128)(2,1)S(1)}, u32[]{:S(2)}, u32[]{:S(2)}) collective-permute-start(bf16[2,48,1536]{2,1,0:T(8,128)(2,1)S(1)} %slice.689), channel_id=1, source_target_pairs={{0,24},{1,25},{2,26},{3,27},{4,28},{5,29},{6,30},{7,31},{8,16},{9,... | collective-permute-start | bytes 884744 | tf_op jit(solution)/shard_map/ppermute | solution.py:24
  308.0 36.3 %collective-permute-start.42 = (bf16[4,48,2304]{2,1,0:T(8,128)(2,1)S(1)}, bf16[4,48,2304]{2,1,0:T(8,128)(2,1)S(1)}, u32[]{:S(2)}, u32[]{:S(2)}) collective-permute-start(bf16[4,48,2304]{2,1,0:T(8,128)(2,1)S(1)} %get-tuple-element.189), channel_id=1, source_target_pairs={{0,4},{1,5},{2,6},{3,7},{4,0},{5,1},{6,2},{7,3},{8,12},{9,13},{10,... | collective-permute-start | bytes 2654216 | tf_op jit(solution)/shard_map/ppermute | solution.py:24
  309.3 35.1 %collective-permute-start.41 = (bf16[4,48,2304]{2,1,0:T(8,128)(2,1)S(1)}, bf16[4,48,2304]{2,1,0:T(8,128)(2,1)S(1)}, u32[]{:S(2)}, u32[]{:S(2)}) collective-permute-start(bf16[4,48,2304]{2,1,0:T(8,128)(2,1)S(1)} %get-tuple-element.190), channel_id=1, source_target_pairs={{0,2},{1,3},{2,0},{3,1},{4,6},{5,7},{6,4},{7,5},{8,10},{9,11},{10,... | collective-permute-start | bytes 2654216 | tf_op jit(solution)/shard_map/ppermute | solution.py:24
  329.7 46.2 %collective-permute-start.48 = (bf16[2,48,3072]{2,1,0:T(8,128)(2,1)}, bf16[2,48,3072]{2,1,0:T(8,128)(2,1)}, u32[]{:S(2)}, u32[]{:S(2)}) collective-permute-start(bf16[2,48,3072]{2,1,0:T(8,128)(2,1)} %slice.690), channel_id=1, source_target_pairs={{0,24},{1,25},{2,26},{3,27},{4,28},{5,29},{6,30},{7,31},{8,16},{9,... | collective-permute-start | bytes 1769480 | tf_op jit(solution)/shard_map/ppermute | solution.py:24
  346.4 20.4 %collective-permute-start.52 = (bf16[48,4608]{1,0:T(8,128)(2,1)S(1)}, bf16[48,4608]{1,0:T(8,128)(2,1)S(1)}, u32[]{:S(2)}, u32[]{:S(2)}) collective-permute-start(bf16[48,4608]{1,0:T(8,128)(2,1)S(1)} %fusion.39), channel_id=1, source_target_pairs={{0,8},{1,9},{2,10},{3,11},{4,12},{5,13},{6,14},{7,15},{8,0},{9,1},... | collective-permute-start | bytes 1327112 | tf_op jit(solution)/shard_map/ppermute | solution.py:24
  351.8 23.3 %collective-permute-start.51 = (bf16[48,2304]{1,0:T(8,128)(2,1)}, bf16[48,2304]{1,0:T(8,128)(2,1)}, u32[]{:S(2)}, u32[]{:S(2)}) collective-permute-start(bf16[48,2304]{1,0:T(8,128)(2,1)} %get-tuple-element.199), channel_id=1, source_target_pairs={{0,24},{1,25},{2,26},{3,27},{4,28},{5,29},{6,30},{7,31},{8,16},{9,... | collective-permute-start | bytes 663560 | tf_op jit(solution)/shard_map/ppermute | solution.py:24
  353.7 22.2 %collective-permute-start.50 = (bf16[48,2304]{1,0:T(8,128)(2,1)}, bf16[48,2304]{1,0:T(8,128)(2,1)}, u32[]{:S(2)}, u32[]{:S(2)}) collective-permute-start(bf16[48,2304]{1,0:T(8,128)(2,1)} %get-tuple-element.200), channel_id=1, source_target_pairs={{0,16},{1,17},{2,18},{3,19},{4,20},{5,21},{6,22},{7,23},{8,24},{9,... | collective-permute-start | bytes 663560 | tf_op jit(solution)/shard_map/ppermute | solution.py:24
  353.7 22.2 %collective-permute-start.49 = (bf16[48,2304]{1,0:T(8,128)(2,1)}, bf16[48,2304]{1,0:T(8,128)(2,1)}, u32[]{:S(2)}, u32[]{:S(2)}) collective-permute-start(bf16[48,2304]{1,0:T(8,128)(2,1)} %get-tuple-element.201), channel_id=1, source_target_pairs={{0,8},{1,9},{2,10},{3,11},{4,12},{5,13},{6,14},{7,15},{8,0},{9,1},... | collective-permute-start | bytes 663560 | tf_op jit(solution)/shard_map/ppermute | solution.py:24
  367.2 1.6 collective-permute-start.53
  377.5 1.7 collective-permute-start.54
  378.6 9.5 %collective-permute-start.55 = (bf16[48,3072]{1,0:T(8,128)(2,1)S(1)}, bf16[48,3072]{1,0:T(8,128)(2,1)S(1)}, u32[]{:S(2)}, u32[]{:S(2)}) collective-permute-start(bf16[48,3072]{1,0:T(8,128)(2,1)S(1)} %fusion.44), channel_id=1, source_target_pairs={{0,8},{1,9},{2,10},{3,11},{4,12},{5,13},{6,14},{7,15},{8,0},{9,1},... | collective-permute-start | bytes 884744 | tf_op jit(solution)/shard_map/ppermute | solution.py:24
  389.4 1.4 collective-permute-start.56
  (41 other events, 204.1 us)
Sparse Core Ops, SparseCore 0:
  13.0 141.6 all-gather.1
